TPU v7x, 32 devices: a whole 2x2x4 slice. The times are simulated.
32 devices in a mesh: section: 2 (over x), rep: 4 (over y, core), fsdp: 4 (over z).
Axes of the slice: x: 2, y: 2, z: 4, core: 2. Of those that a mesh axis runs over, the one named last changes fastest.
Arguments:
- ends: bfloat16 [2, 2, 4, 1024, 1536], P('section', None, 'rep', 'fsdp'), may hold values from -6 to 6
- norm_gain: bfloat16 [2, 1536], P('section', 'fsdp'), may hold values from 0.5 to 1.5
- input_weight: bfloat16 [2, 1536, 6448], P('section', 'fsdp'), may hold values from -0.15625 to 0.15625
- conv_weight: bfloat16 [2, 3328, 4], P('section', 'fsdp'), may hold values from -3 to 3
- conv_bias: bfloat16 [2, 3328], P('section', 'fsdp'), may hold values from -3 to 3
- dt_bias: bfloat16 [2, 48], P('section', 'fsdp'), may hold values from -6 to -2
- a_log: bfloat16 [2, 48], P('section', 'fsdp'), may hold values from -1.5 to 0.5
- skip_gain: bfloat16 [2, 48], P('section', 'fsdp'), may hold values from 0.5 to 1.5
- gate_gain: bfloat16 [2, 3072], P('section', 'fsdp'), may hold values from 0.5 to 1.5
- output_weight: bfloat16 [2, 3072, 1536], P('section', 'fsdp'), may hold values from -0.109375 to 0.109375
Outputs:
- edges: bfloat16 [2, 2, 4, 1024, 1536], P('section', None, 'rep', 'fsdp')
- norm_gain_grad: float32 [2, 1536], P('section', 'fsdp')
- in_weight_grad: float32 [2, 1536, 6448], P('section', 'fsdp')
- conv_weight_grad: float32 [2, 3328, 4], P('section', 'fsdp')
- conv_bias_grad: float32 [2, 3328], P('section', 'fsdp')
- dt_bias_grad: float32 [2, 48], P('section', 'fsdp')
- a_log_grad: float32 [2, 48], P('section', 'fsdp')
- skip_gain_grad: float32 [2, 48], P('section', 'fsdp')
- gate_gain_grad: float32 [2, 3072], P('section', 'fsdp')
- out_weight_grad: float32 [2, 3072, 1536], P('section', 'fsdp')
All inputs are finite; a program needn't handle non-finite values.
Results may differ from a plain program's by a relative error of at most 0.025.
Values may be sent and summed in bfloat16 or wider, within the bound.
No kernel may reach another device: no remote copies, remote signals or barrier semaphores. Data moves between devices by JAX's collectives and lax.ppermute only.
A program may use at most 576 MiB of HBM per device.

v0:
```python
import jax
import jax.numpy as jnp
from jax import lax
from jax.sharding import PartitionSpec as P

HEADS = 48
HEAD_DIM = 64
STATE = 128
KERNEL = 4
INNER = 3072
CONV_CH = 3328


EPSILON = 1e-05
EXACT_MATMUL = lax.Precision.HIGHEST


def shifted(block, axis, distance):
    devices = range(lax.axis_size(axis))
    route = [(i - distance, i) for i in devices if i - distance in devices]
    return lax.ppermute(block, axis, route)


def prefix(value, axis, join, neutral):
    place = lax.axis_index(axis)
    gathered = jax.tree.map(
        lambda a, kind: lax.all_gather(a.astype(kind), axis), value, (jnp.bfloat16, jnp.bfloat16)
    )
    state = jax.tree.map(lambda a, e: jnp.zeros_like(a) + jnp.asarray(e, a.dtype), value, neutral)

    def one(turn, state):
        return join(
            state,
            jax.tree.map(
                lambda a, own: lax.dynamic_index_in_dim(a, turn, 0, False).astype(own.dtype),
                gathered,
                value,
            ),
        )

    return lax.fori_loop(0, place, one, state)


def prefix_2(value, axis, join, neutral):
    count = lax.axis_size(axis)
    place = lax.axis_index(axis)
    ahead = count - 1 - place
    gathered = jax.tree.map(
        lambda a, kind: lax.all_gather(a.astype(kind), axis),
        value,
        jax.tree.map(lambda a: jnp.bfloat16 if a.dtype == jnp.float32 else a.dtype, value),
    )
    state = jax.tree.map(lambda a, e: jnp.zeros_like(a) + jnp.asarray(e, a.dtype), value, neutral)

    def one(turn, state):
        source = count - 1 - turn
        return join(
            state,
            jax.tree.map(
                lambda a, own: lax.dynamic_index_in_dim(a, source, 0, False).astype(own.dtype),
                gathered,
                value,
            ),
        )

    return lax.fori_loop(0, ahead, one, state)


def rms_scale(values, scale_gain):
    return (
        values * lax.rsqrt(jnp.mean(values * values, axis=-1, keepdims=True) + EPSILON) * scale_gain
    )


def chain_rule(earlier, later_part):
    return (
        earlier[0] * later_part[0],
        later_part[1] + later_part[0][:, :, None, None] * earlier[1],
    )


def conv_features(widened, conv_weight, conv_bias, dt_raw, dt_bias, a_log):
    tap_count = conv_weight.shape[1]
    step_count = widened.shape[1] - tap_count + 1
    convolved = conv_bias
    for offset in range(tap_count):
        convolved = convolved + widened[:, offset : offset + step_count, :] * conv_weight[:, offset]
    activated = jax.nn.silu(convolved)
    x_heads = activated[..., :INNER]
    b_rows = activated[..., INNER : INNER + STATE]
    c_rows = activated[..., INNER + STATE :]
    dt_step = jax.nn.softplus(dt_raw + dt_bias)
    log_decay = jnp.cumsum(-jnp.exp(a_log) * dt_step, axis=1)
    return (x_heads, b_rows, c_rows, dt_step, log_decay)


def local_states(x_heads, b_rows, dt_step, log_decay):
    seq_count, length = (x_heads.shape[0], x_heads.shape[1])
    spread = x_heads.reshape(seq_count, length, HEADS, HEAD_DIM)
    weights = jnp.exp(log_decay[:, -1:, :] - log_decay) * dt_step
    weighted = spread * weights[..., None]
    states = jnp.einsum("sqhd,sqn->shdn", weighted, b_rows, precision=EXACT_MATMUL)
    return (jnp.exp(log_decay[:, -1]), states)


def gated_output(
    x_heads, b_rows, c_rows, dt_step, log_decay, prior_state, gate_z, skip_gain, gate_gain
):
    seq_count, length = (x_heads.shape[0], x_heads.shape[1])
    spread = x_heads.reshape(seq_count, length, HEADS, HEAD_DIM)
    scaled = spread * dt_step[..., None]
    by_head = jnp.transpose(log_decay, (0, 2, 1))
    differ = by_head[:, :, :, None] - by_head[:, :, None, :]
    causal = jnp.arange(length)[:, None] >= jnp.arange(length)[None, :]
    mixing = jnp.where(causal, jnp.exp(jnp.where(causal, differ, 0.0)), 0.0)
    intersections = jnp.einsum("sqn,skn->sqk", c_rows, b_rows, precision=EXACT_MATMUL)
    mixed_out = jnp.einsum(
        "shqk,skhd->sqhd", mixing * intersections[:, None], scaled, precision=EXACT_MATMUL
    )
    mixed_out = mixed_out + jnp.exp(log_decay)[..., None] * jnp.einsum(
        "sqn,shdn->sqhd", c_rows, prior_state, precision=EXACT_MATMUL
    )
    mixed_out = (mixed_out + skip_gain[:, None] * spread).reshape(seq_count, length, INNER)
    return rms_scale(mixed_out * jax.nn.silu(gate_z), gate_gain)


def layer_forward(hidden, weights):
    (
        norm_gain,
        input_weight,
        conv_weight,
        conv_bias,
        dt_bias,
        a_log,
        skip_gain,
        gate_gain,
        output_weight,
    ) = weights
    normalized_rows = rms_scale(hidden, norm_gain.astype(jnp.float32)).astype(jnp.bfloat16)
    projected_rows = jnp.einsum(
        "spd,de->spe", normalized_rows, input_weight, preferred_element_type=jnp.float32
    ).astype(jnp.bfloat16)
    length = hidden.shape[1]
    xbc_part = projected_rows[..., INNER : INNER + CONV_CH]
    border = shifted(xbc_part[:, length - KERNEL + 1 :, :], "fsdp", 1)
    widened = jnp.concatenate([border, xbc_part], axis=1)
    features = conv_features(
        widened.astype(jnp.float32),
        conv_weight.astype(jnp.float32),
        conv_bias.astype(jnp.float32),
        projected_rows[..., INNER + CONV_CH :].astype(jnp.float32),
        dt_bias.astype(jnp.float32),
        a_log.astype(jnp.float32),
    )
    decays, states = local_states(features[0], features[1], features[3], features[4])
    scanned = prefix(
        (decays, states), "fsdp", chain_rule, (jnp.ones_like(decays), jnp.zeros_like(states))
    )
    prior_state = scanned[1]
    gated_result = gated_output(
        features[0],
        features[1],
        features[2],
        features[3],
        features[4],
        prior_state,
        projected_rows[..., :INNER].astype(jnp.float32),
        skip_gain.astype(jnp.float32),
        gate_gain.astype(jnp.float32),
    )
    gated_low = gated_result.astype(jnp.bfloat16)
    final_result = hidden + jnp.einsum(
        "spi,id->spd", gated_low, output_weight, preferred_element_type=jnp.float32
    )
    return (
        final_result,
        (hidden, normalized_rows, projected_rows, widened, prior_state, gated_low),
    )


def layer_backward(gradient, kept_state, weights):
    hidden, normalized_rows, projected_rows, widened, prior_state, gated_low = kept_state
    (
        norm_gain,
        input_weight,
        conv_weight,
        conv_bias,
        dt_bias,
        a_log,
        skip_gain,
        gate_gain,
        output_weight,
    ) = weights
    grad_low = gradient.astype(jnp.bfloat16)
    grad_out_weight = jnp.einsum(
        "spi,spd->id", gated_low, grad_low, preferred_element_type=jnp.float32
    )
    grad_gated = jnp.einsum(
        "spd,id->spi", grad_low, output_weight, preferred_element_type=jnp.float32
    )
    features, pull_features = jax.vjp(
        conv_features,
        widened.astype(jnp.float32),
        conv_weight.astype(jnp.float32),
        conv_bias.astype(jnp.float32),
        projected_rows[..., INNER + CONV_CH :].astype(jnp.float32),
        dt_bias.astype(jnp.float32),
        a_log.astype(jnp.float32),
    )
    _, pull_gated = jax.vjp(
        gated_output,
        features[0],
        features[1],
        features[2],
        features[3],
        features[4],
        prior_state,
        projected_rows[..., :INNER].astype(jnp.float32),
        skip_gain.astype(jnp.float32),
        gate_gain.astype(jnp.float32),
    )
    grads_gated = pull_gated(grad_gated)
    decay_states, pull_states = jax.vjp(
        local_states, features[0], features[1], features[3], features[4]
    )
    decays = decay_states[0]
    later_state = prefix_2(
        (decays, grads_gated[5]),
        "fsdp",
        chain_rule,
        (jnp.ones_like(decays), jnp.zeros_like(grads_gated[5])),
    )
    grad_end = later_state[1]
    state_parts = pull_states((jnp.sum(grad_end * prior_state, axis=(2, 3)), grad_end))
    feature_grads = (
        grads_gated[0] + state_parts[0],
        grads_gated[1] + state_parts[1],
        grads_gated[2],
        grads_gated[3] + state_parts[2],
        grads_gated[4] + state_parts[3],
    )
    grad_wide, grad_conv_w, grad_conv_b, grad_dt_raw, grad_dt_bias, grad_a_log = pull_features(
        feature_grads
    )
    margin = KERNEL - 1
    returned = shifted(grad_wide[:, :margin, :].astype(jnp.bfloat16), "fsdp", -1).astype(
        jnp.float32
    )
    own_rows = grad_wide[:, margin:, :]
    length = own_rows.shape[1]
    grad_xbc = jnp.concatenate(
        [own_rows[:, : length - margin], own_rows[:, length - margin :] + returned], axis=1
    )
    grad_proj = jnp.concatenate([grads_gated[6], grad_xbc, grad_dt_raw], axis=-1).astype(
        jnp.bfloat16
    )
    grad_in_weight = jnp.einsum(
        "spd,spe->de", normalized_rows, grad_proj, preferred_element_type=jnp.float32
    )
    grad_normed = jnp.einsum(
        "spe,de->spd", grad_proj, input_weight, preferred_element_type=jnp.float32
    )
    _, pull_norm = jax.vjp(rms_scale, hidden, norm_gain.astype(jnp.float32))
    grad_hidden, grad_norm_gain = pull_norm(grad_normed)
    return (
        gradient + grad_hidden,
        (
            grad_norm_gain,
            grad_in_weight,
            grad_conv_w,
            grad_conv_b,
            grad_dt_bias,
            grad_a_log,
            grads_gated[7],
            grads_gated[8],
            grad_out_weight,
        ),
    )


def shards(
    ends,
    norm_gain,
    input_weight,
    conv_weight,
    conv_bias,
    dt_bias,
    a_log,
    skip_gain,
    gate_gain,
    output_weight,
):
    gathered = (
        lax.all_gather(norm_gain, "fsdp", axis=1, tiled=True),
        lax.all_gather(input_weight, "fsdp", axis=1, tiled=True),
        lax.all_gather(conv_weight, "fsdp", axis=1, tiled=True),
        lax.all_gather(conv_bias, "fsdp", axis=1, tiled=True),
        lax.all_gather(dt_bias, "fsdp", axis=1, tiled=True),
        lax.all_gather(a_log, "fsdp", axis=1, tiled=True),
        lax.all_gather(skip_gain, "fsdp", axis=1, tiled=True),
        lax.all_gather(gate_gain, "fsdp", axis=1, tiled=True),
        lax.all_gather(output_weight, "fsdp", axis=1, tiled=True),
    )
    layer_weights = tuple((member[0] for member in gathered))
    leading = lax.axis_index("section") == 0
    local_data = ends[0].astype(jnp.float32)
    batches = local_data.shape[0]
    arrived = jnp.zeros(local_data.shape[1:], jnp.float32)
    stored = []
    produced = []
    for moment in range(batches + 1):
        source = jnp.where(leading, local_data[min(moment, batches - 1)], arrived)
        final_result, kept_state = layer_forward(source, layer_weights)
        stored.append(kept_state)
        produced.append(final_result)
        if moment < batches:
            arrived = shifted(final_result.astype(jnp.bfloat16), "section", 1).astype(jnp.float32)
    totals = None
    coming = jnp.zeros(local_data.shape[1:], jnp.float32)
    returned_grads = []
    for moment in range(batches + 1):
        gradient = jnp.where(leading, coming, local_data[min(moment, batches - 1)])
        kept_state = jax.tree.map(
            lambda upper_part, lower_part: jnp.where(leading, upper_part, lower_part),
            stored[max(moment - 1, 0)],
            stored[min(moment + 1, batches)],
        )
        grad_input, gradients = layer_backward(gradient, kept_state, layer_weights)
        active = jnp.where(leading, moment >= 1, moment < batches)
        masked = tuple((jnp.where(active, member, 0.0) for member in gradients))
        if totals is None:
            totals = masked
        else:
            totals = tuple((earlier_sum + member for earlier_sum, member in zip(totals, masked)))
        returned_grads.append(grad_input)
        if moment < batches:
            coming = shifted(grad_input.astype(jnp.bfloat16), "section", -1).astype(jnp.float32)
    boundary = jnp.stack(
        [
            jnp.where(leading, returned_grads[number + 1], produced[number + 1])
            for number in range(batches)
        ]
    )
    owned_parts = (
        lax.psum_scatter(
            totals[0][None].astype(jnp.bfloat16), "fsdp", scatter_dimension=1, tiled=True
        ).astype(jnp.float32),
        lax.psum_scatter(
            totals[1][None].astype(jnp.bfloat16), "fsdp", scatter_dimension=1, tiled=True
        ).astype(jnp.float32),
        lax.psum_scatter(
            totals[2][None].astype(jnp.bfloat16), "fsdp", scatter_dimension=1, tiled=True
        ).astype(jnp.float32),
        lax.psum_scatter(
            totals[3][None].astype(jnp.bfloat16), "fsdp", scatter_dimension=1, tiled=True
        ).astype(jnp.float32),
        lax.psum_scatter(
            totals[4][None].astype(jnp.bfloat16), "fsdp", scatter_dimension=1, tiled=True
        ).astype(jnp.float32),
        lax.psum_scatter(
            totals[5][None].astype(jnp.bfloat16), "fsdp", scatter_dimension=1, tiled=True
        ).astype(jnp.float32),
        lax.psum_scatter(
            totals[6][None].astype(jnp.bfloat16), "fsdp", scatter_dimension=1, tiled=True
        ).astype(jnp.float32),
        lax.psum_scatter(
            totals[7][None].astype(jnp.bfloat16), "fsdp", scatter_dimension=1, tiled=True
        ).astype(jnp.float32),
        lax.psum_scatter(
            totals[8][None].astype(jnp.bfloat16), "fsdp", scatter_dimension=1, tiled=True
        ).astype(jnp.float32),
    )
    summed = (
        lax.psum(owned_parts[0].astype(jnp.bfloat16), "rep").astype(jnp.float32),
        lax.psum(owned_parts[1].astype(jnp.bfloat16), "rep").astype(jnp.float32),
        lax.psum(owned_parts[2].astype(jnp.bfloat16), "rep").astype(jnp.float32),
        lax.psum(owned_parts[3].astype(jnp.bfloat16), "rep").astype(jnp.float32),
        lax.psum(owned_parts[4].astype(jnp.bfloat16), "rep").astype(jnp.float32),
        lax.psum(owned_parts[5].astype(jnp.bfloat16), "rep").astype(jnp.float32),
        lax.psum(owned_parts[6].astype(jnp.bfloat16), "rep").astype(jnp.float32),
        lax.psum(owned_parts[7].astype(jnp.bfloat16), "rep").astype(jnp.float32),
        lax.psum(owned_parts[8].astype(jnp.bfloat16), "rep").astype(jnp.float32),
    )
    return (
        boundary.astype(jnp.bfloat16)[None],
        summed[0],
        summed[1],
        summed[2],
        summed[3],
        summed[4],
        summed[5],
        summed[6],
        summed[7],
        summed[8],
    )


def solution(mesh):
    in_specs = (
        P("section", None, "rep", "fsdp", None),
        P("section", "fsdp"),
        P("section", "fsdp", None),
        P("section", "fsdp", None),
        P("section", "fsdp"),
        P("section", "fsdp"),
        P("section", "fsdp"),
        P("section", "fsdp"),
        P("section", "fsdp"),
        P("section", "fsdp", None),
    )
    out_specs = (
        P("section", None, "rep", "fsdp", None),
        P("section", "fsdp"),
        P("section", "fsdp", None),
        P("section", "fsdp", None),
        P("section", "fsdp"),
        P("section", "fsdp"),
        P("section", "fsdp"),
        P("section", "fsdp"),
        P("section", "fsdp"),
        P("section", "fsdp", None),
    )
    return jax.shard_map(shards, mesh=mesh, in_specs=in_specs, out_specs=out_specs, check_vma=False)
```

profile of v0, /device:TPU:1, one launch (start us, length us, event | category | flops | bytes accessed | tf_op | source)
XLA Modules:
  0.0 2630.0 jit_solution(584394799682908515)
XLA Ops:
  12.9 11.6 all-reduce.47
  25.7 56.3 %all_gather.90 = bf16[1,3328,4]{2,0,1:T(2,128)(2,1)S(1)} all-gather(bf16[1,832,4]{2,0,1:T(2,128)(2,1)} %copy.686), channel_id=1, replica_groups=mesh['section'=2,'rep'=4,'fsdp'=4] {'fsdp'}, dimensions={1}, use_global_device_ids=true | all-gather | bytes 33280 | tf_op jit(solution)/shard_map/all_gather | solution.py:296
  84.9 32.0 %all_gather.88 = bf16[1,1536]{1,0:T(2,128)(2,1)S(1)} all-gather(bf16[1,384]{1,0:T(2,128)(2,1)S(1)} %copy-done.251), channel_id=1, replica_groups=mesh['section'=2,'rep'=4,'fsdp'=4] {'fsdp'}, dimensions={1}, use_global_device_ids=true | all-gather | bytes 3840 | tf_op jit(solution)/shard_map/all_gather | solution.py:294
  123.8 251.6 %all-gather.15.cloned.1.call-done = bf16[1,1536,6448]{1,2,0:T(8,128)(2,1)} async-done(((bf16[1,384,6448]{1,2,0:T(8,128)(2,1)}), bf16[1,1536,6448]{1,2,0:T(8,128)(2,1)}) %all-gather.15.cloned.1.call-update) | async-done | bytes 19808272 | tf_op jit(solution)/shard_map/all_gather | solution.py:295
  375.4 11.6 fusion.62
  452.6 16.9 fusion.43
  469.5 18.1 all-gather.19.cloned.1.call-done
  508.8 146.2 %all-gather.17.cloned.1.call-done = bf16[1,3072,1536]{2,1,0:T(8,128)(2,1)} async-done(((bf16[1,768,1536]{2,1,0:T(8,128)(2,1)}), bf16[1,3072,1536]{2,1,0:T(8,128)(2,1)}) %all-gather.17.cloned.1.call-update) | async-done | bytes 9437200 | tf_op jit(solution)/shard_map/all_gather | solution.py:302
  664.9 16.4 collective-permute-done.1
  751.4 16.8 fusion.31
  768.2 31.0 %all-gather.21.cloned.1.call-done = bf16[192,64,128]{2,1,0:T(8,128)(2,1)} async-done(((bf16[48,64,128]{2,1,0:T(8,128)(2,1)}), bf16[192,64,128]{2,1,0:T(8,128)(2,1)}) %all-gather.21.cloned.1.call-update) | async-done | bytes 3145744 | tf_op jit(solution)/shard_map/all_gather | solution.py:27
  829.0 15.9 collective-permute-done.5
  848.3 11.9 fusion.68
  907.2 18.8 fusion.141
  983.2 13.5 all_gather.107
  1046.4 16.8 fusion.13
  1074.2 15.6 fusion.174
  1097.4 14.3 fusion.177
  1155.7 21.1 fusion.72
  1188.1 15.6 fusion.175
  1221.9 12.0 fusion.39
  1236.7 10.8 while.80
  1304.6 10.9 fusion.243
  1321.4 11.4 collective-permute-done.4
  1388.0 21.1 fusion.74
  1426.7 12.0 fusion.27
  1440.2 11.3 while.82
  1506.4 10.9 fusion.242
  1520.8 17.8 fusion.326
  1538.6 10.7 fusion.179
  1571.0 18.4 fusion.325
  1597.4 21.1 fusion.76
  1636.6 12.0 fusion.21
  1650.0 10.8 while.83
  1722.9 23.8 fusion
  1746.7 84.8 %copy.832 = bf16[1,1536,6448]{2,0,1:T(2,128)(2,1)} copy(bf16[1,1536,6448]{1,2,0:T(8,128)(2,1)} %fusion) | data formatting | bytes 39616512
  1831.5 27.4 %copy.862 = bf16[1536,1,6448]{2,0,1:T(8,128)(2,1)} copy(bf16[1536,1,6448]{2,1,0:T(2,128)(2,1)} %bitcast.1212) | data formatting | bytes 39616512
  1876.5 12.9 fusion.49
  1893.5 14.2 fusion.241
  1914.7 295.7 %reduce-scatter.24.cloned.1.call-done = bf16[384,6448]{1,0:T(8,128)(2,1)} async-done(((bf16[1536,6448]{1,0:T(8,128)(2,1)}), bf16[384,6448]{1,0:T(8,128)(2,1)}) %reduce-scatter.24.cloned.1.call-update) | async-done | bytes 4952080
  2218.1 21.5 copy.833
  2239.6 136.0 %reduce-scatter.20.cloned.1.call-done = bf16[1,768,1536]{2,1,0:T(8,128)(2,1)} async-done(((bf16[1,3072,1536]{2,1,0:T(8,128)(2,1)}), bf16[1,768,1536]{2,1,0:T(8,128)(2,1)}) %reduce-scatter.20.cloned.1.call-update) | async-done | bytes 2359312 | tf_op jit(solution)/shard_map/reduce_scatter | solution.py:369
  2376.9 24.2 reduce-scatter.30.cloned.1.call-done
  2411.5 15.9 reduce-scatter.28.cloned.1.call-done
  2438.3 10.6 reduce-scatter.22.cloned.1.call-done
  2449.9 24.3 reduce-scatter.26.cloned.1.call-done
  2475.9 11.5 all-reduce.48
  2491.2 121.8 %all-reduce.52.cloned.1.call-done = (bf16[1,384,6448]{1,2,0:T(8,128)(2,1)}, bf16[1,768,1536]{2,1,0:T(8,128)(2,1)}) async-done(((bf16[1,384,6448]{1,2,0:T(8,128)(2,1)}, bf16[1,768,1536]{2,1,0:T(8,128)(2,1)}), (bf16[1,384,6448]{1,2,0:T(8,128)(2,1)}, bf16[1,768,1536]{2,1,0:T(8,128)(2,1)})) %all-reduce.52.cloned.1.call-update) | async-done | bytes 7311376 | tf_op jit(solution)/shard_map/psum | solution.py:375
  (985 shorter events, 875.3 us)
Async XLA Ops:
  7.2 368.2 %all-gather.15.cloned.1.call-start = ((), (), s32[]{:S(2)}) async-start(), calls=%async_computation.6 | async-start | bytes 24760320 | tf_op jit(solution)/shard_map/all_gather | solution.py:295
  8.0 479.7 %all-gather.19.cloned.1.call-start = ((), (), s32[]{:S(2)}) async-start(), calls=%async_computation.9 | async-start | bytes 3932160 | tf_op jit(solution)/shard_map/all_gather | solution.py:27
  9.8 835.1 %copy-start.5 = (f32[1,2,1,256,1536]{4,3,2,1,0:T(8,128)}, f32[1,2,1,256,1536]{4,3,2,1,0:T(8,128)S(1)}, u32[]{:S(2)}) copy-start(f32[1,2,1,256,1536]{4,3,2,1,0:T(8,128)S(1)} %convert_element_type.731) | copy-start | bytes 9437188
  9.9 75.0 %copy-start.251 = (bf16[1,384]{1,0:T(2,128)(2,1)S(1)}, bf16[1,384]{1,0:T(2,128)(2,1)}, u32[]{:S(2)}) copy-start(bf16[1,384]{1,0:T(2,128)(2,1)} %param.24) | copy-start | bytes 2308
  24.5 92.6 %copy-start.252 = (bf16[48]{0:T(256)(128)(2,1)}, bf16[48]{0:T(256)(128)(2,1)S(1)}, u32[]{:S(2)}) copy-start(bf16[48]{0:T(256)(128)(2,1)S(1)} %get-tuple-element.765) | copy-start | bytes 292
  24.5 384.7 %copy-start.137 = (f32[3328]{0:T(1024)}, f32[3328]{0:T(1024)S(1)}, u32[]{:S(2)}) copy-start(f32[3328]{0:T(1024)S(1)} %convert_element_type.850) | copy-start | bytes 39940
  84.9 809.9 %copy-start.168 = (f32[48]{0:T(128)}, f32[48]{0:T(128)S(1)}, u32[]{:S(2)}) copy-start(f32[48]{0:T(128)S(1)} %convert_element_type.851) | copy-start | bytes 580
  116.9 730.2 %copy-start.81 = (f32[1536]{0:T(1024)}, f32[1536]{0:T(1024)S(1)}, u32[]{:S(2)}) copy-start(f32[1536]{0:T(1024)S(1)} %convert_reduce_fusion) | copy-start | bytes 18436
  117.2 747.2 %copy-start.200 = (f32[48]{0:T(128)}, f32[48]{0:T(128)S(1)}, u32[]{:S(2)}) copy-start(f32[48]{0:T(128)S(1)} %fusion.507) | copy-start | bytes 580
  117.2 258.2 %copy-start.112 = (f32[256]{0:T(256)}, f32[256]{0:T(256)S(1)}, u32[]{:S(2)}) copy-start(f32[256]{0:T(256)S(1)} %add_rsqrt_fusion.5) | copy-start | bytes 3076
  123.7 592.5 %copy-start.96 = (f32[3328]{0:T(1024)}, f32[3328]{0:T(1024)S(1)}, u32[]{:S(2)}) copy-start(f32[3328]{0:T(1024)S(1)} %get-tuple-element.696) | copy-start | bytes 39940
  123.8 592.5 %copy-start.100 = (f32[3328]{0:T(1024)}, f32[3328]{0:T(1024)S(1)}, u32[]{:S(2)}) copy-start(f32[3328]{0:T(1024)S(1)} %get-tuple-element.697) | copy-start | bytes 39940
  123.8 783.4 %copy-start.88 = (f32[3328]{0:T(1024)}, f32[3328]{0:T(1024)S(1)}, u32[]{:S(2)}) copy-start(f32[3328]{0:T(1024)S(1)} %get-tuple-element.694) | copy-start | bytes 39940
  123.8 783.4 %copy-start.92 = (f32[3328]{0:T(1024)}, f32[3328]{0:T(1024)S(1)}, u32[]{:S(2)}) copy-start(f32[3328]{0:T(1024)S(1)} %get-tuple-element.695) | copy-start | bytes 39940
  391.0 16.4 collective-permute-start
  424.3 230.7 %all-gather.17.cloned.1.call-start = ((), (), s32[]{:S(2)}) async-start(), calls=%async_computation.7 | async-start | bytes 11796480 | tf_op jit(solution)/shard_map/all_gather | solution.py:302
  425.0 374.2 %all-gather.21.cloned.1.call-start = ((), (), s32[]{:S(2)}) async-start(), calls=%async_computation.10 | async-start | bytes 3932160 | tf_op jit(solution)/shard_map/all_gather | solution.py:27
  435.2 380.7 %copy-start.114 = (f32[1,3072]{1,0:T(1,128)}, f32[1,3072]{1,0:T(1,128)S(1)}, u32[]{:S(2)}) copy-start(f32[1,3072]{1,0:T(1,128)S(1)} %convert_element_type.848) | copy-start | bytes 36868
  435.3 365.7 %copy-start.202 = (f32[48]{0:T(128)}, f32[48]{0:T(128)S(1)}, u32[]{:S(2)}) copy-start(f32[48]{0:T(128)S(1)} %convert_element_type.852) | copy-start | bytes 580
  661.7 19.5 collective-permute-start.1
  698.3 15.1 collective-permute-start.2
  735.2 328.0 %all-gather.25.cloned.1.call-start = ((), (), s32[]{:S(2)}) async-start(), calls=%async_computation.12 | async-start | bytes 3932160 | tf_op jit(solution)/shard_map/all_gather | solution.py:27
  825.7 19.2 collective-permute-start.5
  862.7 32.1 %copy-start.43 = (bf16[256,6448]{1,0:T(8,128)(2,1)S(1)}, bf16[256,6448]{1,0:T(8,128)(2,1)}, u32[]{:S(2)}) copy-start(bf16[256,6448]{1,0:T(8,128)(2,1)} %fusion.68) | copy-start | bytes 9904132
  883.6 18.3 collective-permute-start.6
  939.0 296.4 %all-gather.23.cloned.1.call-start = ((), (), s32[]{:S(2)}) async-start(), calls=%async_computation.11 | async-start | bytes 3932160 | tf_op jit(solution)/shard_map/all_gather | solution.py:49
  979.5 43.1 %copy-start.153 = (f32[1,48,2,128]{3,2,1,0:T(2,128)S(1)}, f32[1,48,2,128]{3,2,1,0:T(2,128)}, u32[]{:S(2)}) copy-start(f32[1,48,2,128]{3,2,1,0:T(2,128)} %copy.704) | copy-start | bytes 147460
  979.5 44.5 %copy-start.152 = (f32[1,48,2,128]{3,2,1,0:T(2,128)S(1)}, f32[1,48,2,128]{3,2,1,0:T(2,128)}, u32[]{:S(2)}) copy-start(f32[1,48,2,128]{3,2,1,0:T(2,128)} %copy.747) | copy-start | bytes 147460
  979.5 46.0 %copy-start.151 = (f32[1,48,2,128]{3,2,1,0:T(2,128)S(1)}, f32[1,48,2,128]{3,2,1,0:T(2,128)}, u32[]{:S(2)}) copy-start(f32[1,48,2,128]{3,2,1,0:T(2,128)} %copy.810) | copy-start | bytes 147460
  979.5 47.4 %copy-start.16 = (f32[1,256,3328]{2,1,0:T(8,128)S(1)}, f32[1,256,3328]{2,1,0:T(8,128)}, u32[]{:S(2)}) copy-start(f32[1,256,3328]{2,1,0:T(8,128)} %get-tuple-element.893) | copy-start | bytes 10223620
  1155.7 283.1 %all-gather.27.cloned.1.call-start = ((), (), s32[]{:S(2)}) async-start(), calls=%async_computation.13 | async-start | bytes 3932160 | tf_op jit(solution)/shard_map/all_gather | solution.py:49
  1292.7 9.3 collective-permute-start.3
  1317.2 62.2 %copy-start.224 = (f32[256]{0:T(256)}, f32[256]{0:T(256)S(1)}, u32[]{:S(2)}) copy-start(f32[256]{0:T(256)S(1)} %get-tuple-element.801) | copy-start | bytes 3076
  1317.2 15.6 collective-permute-start.4
  1321.4 53.0 %copy-start.222 = (f32[256]{0:T(256)}, f32[256]{0:T(256)S(1)}, u32[]{:S(2)}) copy-start(f32[256]{0:T(256)S(1)} %multiply_reduce_fusion.20) | copy-start | bytes 3076
  1362.6 286.0 %all-gather.29.cloned.1.call-start = ((), (), s32[]{:S(2)}) async-start(), calls=%async_computation.14 | async-start | bytes 3932160 | tf_op jit(solution)/shard_map/all_gather | solution.py:49
  1494.5 9.2 collective-permute-start.7
  1519.3 19.2 collective-permute-start.8
  1570.9 639.5 %reduce-scatter.24.cloned.1.call-start = ((), (), s32[]{:S(2)}) async-start(), calls=%async_computation.16 | async-start | bytes 25067520
  1706.3 12.9 collective-permute-start.9
  1858.9 516.7 %reduce-scatter.20.cloned.1.call-start = ((), (), s32[]{:S(2)}) async-start(), calls=%async_computation.8 | async-start | bytes 11796480 | tf_op jit(solution)/shard_map/reduce_scatter | solution.py:369
  1889.6 511.5 %reduce-scatter.30.cloned.1.call-start = ((), (), s32[]{:S(2)}) async-start(), calls=%async_computation.19 | async-start | bytes 983040
  1891.8 535.7 %reduce-scatter.28.cloned.1.call-start = ((), (), s32[]{:S(2)}) async-start(), calls=%async_computation.18 | async-start | bytes 1064960
  1893.4 555.5 %reduce-scatter.22.cloned.1.call-start = ((), (), s32[]{:S(2)}) async-start(), calls=%async_computation.15 | async-start | bytes 491520
  1908.8 565.4 %reduce-scatter.26.cloned.1.call-start = ((), (), s32[]{:S(2)}) async-start(), calls=%async_computation.17 | async-start | bytes 1064960
  1914.6 698.4 %all-reduce.52.cloned.1.call-start = ((), (), s32[]{:S(2)}) async-start(), calls=%async_computation.20 | async-start | bytes 14622720 | tf_op jit(solution)/shard_map/psum | solution.py:375
  2375.6 26.6 %copy-start.244 = (f32[48]{0:T(128)S(1)}, f32[48]{0:T(128)}, u32[]{:S(2)}) copy-start(f32[48]{0:T(128)} %get-tuple-element.698) | copy-start | bytes 580
  2375.6 26.6 %copy-start.245 = (f32[48]{0:T(128)S(1)}, f32[48]{0:T(128)}, u32[]{:S(2)}) copy-start(f32[48]{0:T(128)} %get-tuple-element.699) | copy-start | bytes 580
  (236 other events, 1675.2 us)
Sparse Core Ops, SparseCore 0:
  9.6 365.6 all-gather.14
  424.4 63.2 all-gather.18
  489.2 165.6 all-gather.16
  735.4 63.8 all-gather.20
  939.1 71.3 all-gather.24
  1155.8 79.5 all-gather.22
  1362.7 68.3 all-gather.26
  1571.1 71.5 all-gather.28
  1859.0 351.3 reduce-scatter.23
  2213.2 162.3 reduce-scatter.19
  2377.9 23.1 reduce-scatter.29
  2403.3 24.1 reduce-scatter.27
  2429.8 19.0 reduce-scatter.21
  2451.1 23.0 reduce-scatter.25
  2476.6 136.4 all-reduce.51
where the time goes:
time: 2650 us; the launch traced here: 2630 us
  waiting for transfers between devices  1120 us (42%)
  matrix products  564 us (21%)
  local copies, waits for them, and re-layouts  413 us (16%)
  other arithmetic  302 us (11%)
  blocking collectives  182 us (7%)
    unnamed x20, waiting for transfers between devices  372 us
    all_gather x1, waiting for transfers between devices, shards(): lax.all_gather(input_weight, 'fsdp', axis=1, tiled=True)  252 us
    dot_general x12, matrix products, gated_output(): jnp.einsum('shqk,skhd->sqhd', mixing * intersections[:, None], scaled, pr...  195 us
    unnamed x545, local copies, waits for them, and re-layouts  168 us
    all_gather x1, waiting for transfers between devices, shards(): lax.all_gather(output_weight, 'fsdp', axis=1, tiled=True)  146 us
    reduce_scatter x1, waiting for transfers between devices, shards(): lax.psum_scatter(totals[8][None].astype(jnp.bfloat16), 'fsdp', scatter_di...  136 us
    psum x1, waiting for transfers between devices, shards(): lax.psum(owned_parts[1].astype(jnp.bfloat16), 'rep').astype(jnp.float32)  122 us
    dot_general x12, matrix products, gated_output(): jnp.einsum('sqn,shdn->sqhd', c_rows, prior_state, precision=EXACT_MATMUL)  73.5 us
  transfers between devices with their start and end apart: 25, of which 15 were waited for; matrix products, arithmetic and copies ran while one was open for 23% of the time, Pallas kernels for 0%

commit v1 on v0

--- a/solution.py
+++ b/solution.py
@@ -1,18 +1,1239 @@
+import functools
+
 import jax
 import jax.numpy as jnp
 from jax import lax
+from jax.experimental import pallas as pl
+from jax.experimental.pallas import tpu as pltpu
+from jax.sharding import Mesh
 from jax.sharding import PartitionSpec as P
 
+D = 1536
 HEADS = 48
 HEAD_DIM = 64
 STATE = 128
 KERNEL = 4
 INNER = 3072
 CONV_CH = 3328
-
+LANES = 128
+
+OWN = INNER // 2
+OWN_HEADS = HEADS // 2
+OWN_CONV = OWN + 2 * STATE
+X_AT = OWN
+BC_AT = 2 * OWN
+DT_AT = 2 * OWN + 2 * STATE
+OWN_PROJ = DT_AT + 2 * LANES
+PAIRS = OWN // LANES
 
 EPSILON = 1e-05
 EXACT_MATMUL = lax.Precision.HIGHEST
+F32 = jnp.float32
+BF16 = jnp.bfloat16
+FORWARD_VMEM = 24
+BACKWARD_VMEM = 30
+JOIN_VMEM = 12
+
+
+def dot(a, b):
+    return lax.dot_general(a, b, (((1,), (0,)), ((), ())), preferred_element_type=F32)
+
+
+def dot_nt(a, b):
+    return lax.dot_general(a, b, (((1,), (1,)), ((), ())), preferred_element_type=F32)
+
+
+def dot_tn(a, b):
+    return lax.dot_general(a, b, (((0,), (0,)), ((), ())), preferred_element_type=F32)
+
+
+def split(v, parts):
+    pieces = []
+    for _ in range(parts):
+        piece = v.astype(BF16)
+        pieces.append(piece)
+        v = v - piece.astype(F32)
+    return pieces
+
+
+def sigmoid(v):
+    return 0.5 * jnp.tanh(0.5 * v) + 0.5
+
+
+def softplus(v):
+    return jnp.maximum(v, 0.0) + jnp.log1p(jnp.exp(-jnp.abs(v)))
+
+
+def step_sizes(dt_raw, headp):
+    t = dt_raw.shape[0]
+    biased = dt_raw + headp[0:1]
+    dt = softplus(biased)
+    rows = lax.broadcasted_iota(jnp.int32, (t, t), 0)
+    cols = lax.broadcasted_iota(jnp.int32, (t, t), 1)
+    tri = jnp.where(rows >= cols, 1.0, 0.0).astype(BF16)
+    ld = sum(dot(tri, part) for part in split(dt * headp[1:2], 3))
+    return dt, ld, biased
+
+
+def at_head(v, pair):
+    turned = pltpu.roll(v, lax.rem(LANES - 2 * pair, LANES), 1)
+    return [jnp.broadcast_to(turned[:, i : i + 1], v.shape) for i in range(2)]
+
+
+def decay_blocks(col, row, swapped):
+    n = col.shape[0] // 2
+    rows = lax.broadcasted_iota(jnp.int32, (n, n), 0)
+    cols = lax.broadcasted_iota(jnp.int32, (n, n), 1)
+    keep = rows <= cols if swapped else rows >= cols
+
+    def block(i, j):
+        down, along = col[i * n : (i + 1) * n], row[:, j * n : (j + 1) * n]
+        differ = along - down if swapped else down - along
+        return jnp.exp(jnp.where(keep, differ, -1e30) if i == j else differ)
+
+    return block(0, 0), block(0, 1) if swapped else block(1, 0), block(1, 1)
+
+
+def convolve(xw, sl, convp, t):
+    out = convp[4:5, sl] + xw[5 : 5 + t, sl] * convp[0:1, sl]
+    for k in range(1, KERNEL):
+        out = out + xw[5 + k : 5 + k + t, sl] * convp[k : k + 1, sl]
+    return out
+
+
+def pair_loop(step):
+    def two(turn, _):
+        step(2 * turn)
+        step(2 * turn + 1)
+        return 0
+
+    lax.fori_loop(0, PAIRS // 2, two, 0)
+
+
+def aligned(value):
+    return pl.multiple_of(value, LANES)
+
+
+def fetch(source, target, sem):
+    copy = pltpu.make_async_copy(source, target, sem)
+    copy.start()
+    return copy
+
+
+def fetch_one_of(first, one, other, target, sem):
+    @pl.when(first)
+    def _():
+        pltpu.make_async_copy(one, target, sem).start()
+
+    @pl.when(jnp.logical_not(first))
+    def _():
+        pltpu.make_async_copy(other, target, sem).start()
+
+    return pltpu.make_async_copy(other, target, sem)
+
+
+def forward_kernel(row, sc, *refs):
+    @pl.when(sc[row, VALID] == 1)
+    def _():
+        forward_chunk(row, sc, *refs)
+
+
+def forward_chunk(
+    row, sc, got_hbm, other_hbm, x_hbm, ng_ref, convp, headp, chanp, st_ref, tail_ref, win, wout, *rest
+):
+    p, h, st_out, tail_out = rest[-22:-18]
+    h_hbm, n_hbm, pr_hbm, mx_hbm, q_hbm, st_hbm, tl_hbm = rest[-18:-11]
+    normed, pr, mx, q, sti, tl, xw, ldt, ss, g_ref, sem = rest[-11:]
+    t = h.shape[0]
+    half = t // 2
+    slot = sc[row, SLOT]
+    first = sc[row, FIRST] == 1
+    leading = sc[row, LEADING] == 1
+    core = sc[row, CORE]
+
+    @pl.when(leading)
+    def _():
+        fetch(x_hbm, h, sem.at[0]).wait()
+
+    @pl.when(jnp.logical_not(leading))
+    def _():
+        mine = h.at[pl.ds(aligned(core * half), half)]
+        theirs = h.at[pl.ds(aligned((1 - core) * half), half)]
+        copies = fetch(got_hbm, mine, sem.at[0]), fetch(other_hbm, theirs, sem.at[1])
+        for copy in copies:
+            copy.wait()
+
+    stores = [fetch(h, h_hbm.at[slot], sem.at[0])]
+    hf = h[...].astype(F32)
+    r = lax.rsqrt(jnp.mean(hf * hf, axis=1, keepdims=True) + EPSILON)
+    normed[...] = (hf * r * ng_ref[...]).astype(BF16)
+    stores.append(fetch(normed, n_hbm.at[slot], sem.at[1]))
+
+    sti[...] = jnp.where(first, 0.0, st_ref[...])
+    tl[...] = jnp.where(first, 0.0, tail_ref[...])
+    stores.append(fetch(sti, st_hbm.at[slot], sem.at[2]))
+    stores.append(fetch(tl, tl_hbm.at[slot], sem.at[3]))
+    xw[0:8, :] = tl[...]
+
+    for at in range(0, OWN_PROJ, 512):
+        cols = slice(at, min(at + 512, OWN_PROJ))
+        pr[:, cols] = dot_nt(normed[...], win[cols, :]).astype(BF16)
+    stores.append(fetch(pr, pr_hbm.at[slot], sem.at[4]))
+    tail_out[...] = pr[t - 8 : t, X_AT : X_AT + OWN_CONV].astype(F32)
+
+    bc = pl.ds(OWN, 2 * STATE)
+    xw[8 : 8 + t, OWN:OWN_CONV] = pr[:, BC_AT:DT_AT].astype(F32)
+    conv_bc = convolve(xw, bc, convp, t)
+    act = (conv_bc * sigmoid(conv_bc)).astype(BF16)
+    b, c = act[:, :STATE], act[:, STATE:]
+    g_ref[...] = dot_nt(c, b)
+    b_turned = act[:, :STATE].astype(F32).T.astype(BF16)
+    dt, ld, _ = step_sizes(pr[:, DT_AT : DT_AT + LANES].astype(F32), headp[...])
+    ldt[...] = ld.T
+    left = lax.broadcasted_iota(jnp.int32, (t, LANES), 1) < HEAD_DIM
+    ss[...] = jnp.zeros_like(ss)
+
+    def pair_step(pair):
+        at = pl.multiple_of(pair * LANES, LANES)
+        sl = pl.ds(at, LANES)
+        xw[8 : 8 + t, sl] = pr[:, pl.ds(X_AT + at, LANES)].astype(F32)
+        conv = convolve(xw, sl, convp, t)
+        x = conv * sigmoid(conv)
+        cols = at_head(ld, pair)
+        u = jnp.where(left, *at_head(dt, pair)) * x
+        ld_p = jnp.where(left, *cols)
+        top = jnp.zeros((half, LANES), F32)
+        bottom = top
+        for i in range(2):
+            u_i = jnp.where(left if i == 0 else jnp.logical_not(left), u, 0.0).astype(BF16)
+            d00, d10, d11 = decay_blocks(cols[i], ldt[pl.ds(2 * pair + i, 1), :], False)
+            m00 = (g_ref[:half, :half] * d00).astype(BF16)
+            m10 = (g_ref[half:, :half] * d10).astype(BF16)
+            m11 = (g_ref[half:, half:] * d11).astype(BF16)
+            top = top + dot(m00, u_i[:half])
+            bottom = bottom + dot(jnp.concatenate([m10, m11], axis=1), u_i)
+        eld = jnp.exp(ld_p)
+        st = sti[:, sl]
+        y = jnp.concatenate([top, bottom], axis=0) + eld * dot(c, st.astype(BF16))
+        weighted = (u * jnp.exp(ld_p[t - 1 : t] - ld_p)).astype(BF16)
+        st_out[:, sl] = eld[t - 1 : t] * st + dot(b_turned, weighted)
+        mixed = y + chanp[0:1, sl] * x
+        mx[:, sl] = mixed
+        z = pr[:, sl].astype(F32)
+        gated = mixed * (z * sigmoid(z))
+        ss[...] += gated * gated
+        q[:, sl] = (gated * chanp[1:2, sl]).astype(BF16)
+
+    pair_loop(pair_step)
+    stores.append(fetch(mx, mx_hbm.at[slot], sem.at[5]))
+    stores.append(fetch(q, q_hbm.at[slot], sem.at[6]))
+    total = jnp.sum(ss[...], axis=1, keepdims=True)
+    high = total.astype(BF16).astype(F32)
+    lane = lax.broadcasted_iota(jnp.int32, (t, LANES), 1)
+    p[:, D:] = jnp.where(lane == 0, high, jnp.where(lane == 1, total - high, 0.0)).astype(BF16)
+    for at in range(0, D, 512):
+        p[:, at : at + 512] = dot(q[...], wout[:, at : at + 512]).astype(BF16)
+    for store in stores:
+        store.wait()
+
+
+def backward_kernel(row, sc, *refs):
+    acc_ref, acc_out = refs[15], refs[-20]
+
+    @pl.when(sc[row, VALID] == 1)
+    def _():
+        backward_chunk(row, sc, *refs)
+
+    @pl.when(sc[row, VALID] == 0)
+    def _():
+        acc_out[...] = acc_ref[...]
+
+
+def backward_chunk(
+    row,
+    sc,
+    arrived_hbm,
+    cot_hbm,
+    h_hbm,
+    pr_hbm,
+    mx_hbm,
+    st_hbm,
+    tl_hbm,
+    y_hbm,
+    ri_hbm,
+    convp,
+    headp,
+    chanp,
+    dst_ref,
+    dc_ref,
+    val_ref,
+    acc_ref,
+    win,
+    wout,
+    *rest,
+):
+    gn, g_ref, h_out, dst_out, dc_out, val_out, acc_out, gp_hbm, gs_hbm = rest[-26:-17]
+    pr, mx, st_ref, tl, y_ref, ri, gp, gs = rest[-17:-9]
+    xw, dw, ldt, gw, gt, dgt, dci, dbi, sem = rest[-9:]
+    t = g_ref.shape[0]
+    half = t // 2
+    slot = sc[row, SLOT]
+    last = sc[row, FIRST] == 1
+    g_copy = fetch_one_of(sc[row, LEADING] == 1, arrived_hbm, cot_hbm, g_ref, sem.at[0])
+    y_copy = fetch(y_hbm.at[slot], y_ref, sem.at[1])
+    ri_copy = fetch(ri_hbm.at[slot], ri, sem.at[2])
+    pr_copy = fetch(pr_hbm.at[slot], pr, sem.at[3])
+    tl_copy = fetch(tl_hbm.at[slot], tl, sem.at[4])
+    mx_copy = fetch(mx_hbm.at[slot], mx, sem.at[5])
+    st_copy = fetch(st_hbm.at[slot], st_ref, sem.at[6])
+    h_copy = fetch(h_hbm.at[slot], h_out, sem.at[8])
+
+    acc_out[...] = acc_ref[...]
+    dw[t : t + 8, :] = jnp.where(last, 0.0, dc_ref[...])
+    dgt[...] = jnp.zeros_like(dgt)
+    dci[...] = jnp.zeros_like(dci)
+    dbi[...] = jnp.zeros_like(dbi)
+    g_copy.wait()
+    for at in range(0, OWN, 512):
+        gw[:, at : at + 512] = dot_nt(g_ref[...], wout[at : at + 512, :])
+    y_copy.wait()
+    ri_copy.wait()
+    rinv = ri[:, 0:1]
+    mean = jnp.sum(g_ref[...].astype(F32) * y_ref[...].astype(F32), axis=1, keepdims=True)
+    lean = rinv * rinv * (mean * (1.0 / INNER))
+    gs[...] = (g_ref[...].astype(F32) * rinv).astype(BF16)
+    gs_store = fetch(gs, gs_hbm.at[sc[row, WRITE]], sem.at[7])
+    pr_copy.wait()
+    tl_copy.wait()
+    xw[0:8, :] = tl[...]
+
+    bc = pl.ds(OWN, 2 * STATE)
+    xw[8 : 8 + t, OWN:OWN_CONV] = pr[:, BC_AT:DT_AT].astype(F32)
+    conv_bc = convolve(xw, bc, convp, t)
+    sig_bc = sigmoid(conv_bc)
+    act = (conv_bc * sig_bc).astype(BF16)
+    b, c = act[:, :STATE], act[:, STATE:]
+    c_turned = c.astype(F32).T.astype(BF16)
+    gt[...] = dot_nt(b, c)
+    dt, ld, biased = step_sizes(pr[:, DT_AT : DT_AT + LANES].astype(F32), headp[...])
+    ldt[...] = ld.T
+    left = lax.broadcasted_iota(jnp.int32, (t, LANES), 1) < HEAD_DIM
+
+    def add(line, sl, v):
+        acc_out[line : line + 1, sl] += v
+
+    def conv_back(dact, conv, sig, sl):
+        dconv = dact * (sig * (1.0 + conv * (1.0 - sig)))
+        dw[0:t, sl] = dconv
+        add(4, sl, jnp.sum(dconv, axis=0, keepdims=True))
+        for k in range(KERNEL):
+            add(k, sl, jnp.sum(dconv * xw[5 + k : 5 + k + t, sl], axis=0, keepdims=True))
+        dx = dconv * convp[KERNEL - 1 : KERNEL, sl]
+        for k in range(KERNEL - 1):
+            ahead = KERNEL - 1 - k
+            dx = dx + dw[ahead : ahead + t, sl] * convp[k : k + 1, sl]
+        return dx.astype(BF16)
+
+    lane_head = lax.rem(lax.broadcasted_iota(jnp.int32, (2 * LANES, LANES), 0), LANES) // HEAD_DIM
+    head_lane = lax.broadcasted_iota(jnp.int32, (2 * LANES, LANES), 1)
+    mx_copy.wait()
+    st_copy.wait()
+
+    def pair_step(pair, carry):
+        ddt, dld, dval = carry
+        at = pl.multiple_of(pair * LANES, LANES)
+        sl = pl.ds(at, LANES)
+        xsl = pl.ds(X_AT + at, LANES)
+        xw[8 : 8 + t, sl] = pr[:, xsl].astype(F32)
+        conv = convolve(xw, sl, convp, t)
+        sig = sigmoid(conv)
+        x = conv * sig
+        z = pr[:, sl].astype(F32)
+        sig_z = sigmoid(z)
+        s = z * sig_z
+        mixed = mx[:, sl]
+        gated = mixed * s
+        scaled = gw[:, sl] * rinv
+        add(6, sl, jnp.sum(scaled * gated, axis=0, keepdims=True))
+        dgated = chanp[1:2, sl] * scaled - gated * lean
+        dy = dgated * s
+        gp[:, sl] = (dgated * mixed * (sig_z * (1.0 + z * (1.0 - sig_z)))).astype(BF16)
+        skip = chanp[0:1, sl]
+        add(5, sl, jnp.sum(dy * x, axis=0, keepdims=True))
+        y = mixed - skip * x
+
+        cols = at_head(ld, pair)
+        ld_p = jnp.where(left, *cols)
+        eld = jnp.exp(ld_p)
+        wend = jnp.exp(ld_p[t - 1 : t] - ld_p)
+        dt_p = jnp.where(left, *at_head(dt, pair))
+        u = dt_p * x
+        u_low = u.astype(BF16)
+        dy_low = dy.astype(BF16)
+        dst = jnp.where(last, 0.0, dst_ref[:, sl])
+        dst_low = dst.astype(BF16)
+        top = jnp.zeros((half, LANES), F32)
+        bottom = top
+        for i in range(2):
+            side = left if i == 0 else jnp.logical_not(left)
+            d00, d01, d11 = decay_blocks(cols[i], ldt[pl.ds(2 * pair + i, 1), :], True)
+            m00 = (gt[:half, :half] * d00).astype(BF16)
+            m01 = (gt[:half, half:] * d01).astype(BF16)
+            m11 = (gt[half:, half:] * d11).astype(BF16)
+            dy_i = jnp.where(side, dy, 0.0).astype(BF16)
+            top = top + dot(jnp.concatenate([m00, m01], axis=1), dy_i)
+            bottom = bottom + dot(m11, dy_i[half:])
+            u_i = jnp.where(side, u, 0.0).astype(BF16)
+            dm = dot_nt(u_i[:half], dy_low)
+            dgt[:half, :half] += dm[:, :half] * d00
+            dgt[:half, half:] += dm[:, half:] * d01
+            dgt[half:, half:] += dot_nt(u_i[half:], dy_low[half:]) * d11
+        du = jnp.concatenate([top, bottom], axis=0) + wend * dot(b, dst_low)
+        st = st_ref[:, sl]
+        dyl = (eld * dy).astype(BF16)
+        dst_new = eld[t - 1 : t] * dst + dot(c_turned, dyl)
+        dst_out[:, sl] = dst_new
+        val_out[:, sl] = jnp.broadcast_to(
+            jnp.sum(dst_new * st, axis=0, keepdims=True), (8, LANES)
+        )
+        dci[...] += dot_nt(dyl, st.astype(BF16))
+        dbi[...] += dot_nt((wend * u).astype(BF16), dst_low)
+
+        pick = jnp.where(lane_head + 2 * pair == head_lane, 1.0, 0.0).astype(BF16)
+
+
+        def by_head(v):
+            return dot(jnp.concatenate(split(v, 2), axis=1), pick)
+
+        ddt = ddt + by_head(du * x)
+        dld = dld + by_head(dy_low.astype(F32) * y - u_low.astype(F32) * du)
+        dval = dval + by_head(jnp.where(last, 0.0, val_ref[:, sl]))
+        gp[:, xsl] = conv_back(dt_p * du + skip * dy, conv, sig, sl)
+        return ddt, dld, dval
+
+    zero = jnp.zeros((t, LANES), F32)
+    ddt, dld, dval = lax.fori_loop(
+        0,
+        PAIRS // 2,
+        lambda turn, carry: pair_step(2 * turn + 1, pair_step(2 * turn, carry)),
+        (zero, zero, jnp.zeros((8, LANES), F32)),
+    )
+
+    dgt_low = dgt[...].astype(BF16)
+    db = dbi[...] + dot(dgt_low, c)
+    dc = dci[...] + dot_tn(dgt_low, b)
+    gp[:, BC_AT:DT_AT] = conv_back(jnp.concatenate([db, dc], axis=1), conv_bc, sig_bc, bc)
+
+    rows = lax.broadcasted_iota(jnp.int32, (t, t), 0)
+    cols = lax.broadcasted_iota(jnp.int32, (t, t), 1)
+    upper = jnp.where(rows <= cols, 1.0, 0.0).astype(BF16)
+    da = sum(dot(upper, part) for part in split(dld, 3)) + dval[0:1]
+    rate = headp[1:2]
+    head = pl.ds(0, LANES)
+    add(8, head, jnp.sum(da * rate * dt, axis=0, keepdims=True))
+    ddt_raw = (ddt + rate * da) * sigmoid(biased)
+    add(7, head, jnp.sum(ddt_raw, axis=0, keepdims=True))
+    gp[:, DT_AT : DT_AT + LANES] = ddt_raw.astype(BF16)
+    gp[:, DT_AT + LANES :] = jnp.zeros((t, LANES), BF16)
+    gp_store = fetch(gp, gp_hbm.at[sc[row, WRITE]], sem.at[0])
+    dc_out[...] = dw[0:8, :]
+    for at in range(0, D, 512):
+        gn[:, at : at + 512] = dot(gp[...], win[:, at : at + 512]).astype(BF16)
+    gp_store.wait()
+    gs_store.wait()
+    h_copy.wait()
+
+
+def forward_join_kernel(row, sc, own_ref, other_ref, h_ref, *rest):
+    out, y_hbm, ri_hbm, e_hbm, y_v, ri_v, low_v, sem = rest[-8:]
+    half = out.shape[0]
+
+    @pl.when(sc[row, VALID] == 1)
+    def _():
+        copies = []
+        for k in range(2):
+            rows = slice(k * half, (k + 1) * half)
+            total = own_ref[rows].astype(F32) + other_ref[rows].astype(F32)
+            square = total[:, D : D + 1] + total[:, D + 1 : D + 2]
+            rinv = lax.rsqrt(square * (1.0 / INNER) + EPSILON)
+            y = total[:, :D] * rinv
+            y_v[rows] = y.astype(BF16)
+            ri_v[rows] = jnp.broadcast_to(rinv, (half, LANES))
+            low_v[rows] = (h_ref[rows].astype(F32) + y).astype(BF16)
+            pieces = ((y_v, y_hbm, SLOT), (ri_v, ri_hbm, SLOT), (low_v, e_hbm, EDGE))
+            for near_ref, far_ref, which in pieces:
+                target = far_ref.at[sc[row, which], pl.ds(k * half, half)]
+                copies.append(fetch(near_ref.at[pl.ds(k * half, half)], target, sem.at[len(copies)]))
+        out[...] = low_v[pl.ds(aligned(sc[row, CORE] * half), half), :]
+        for copy in copies:
+            copy.wait()
+
+
+def backward_join_kernel(row, sc, own_ref, other_ref, h_ref, g_ref, ng_ref, dng_ref, *rest):
+    out, dng_out, e_hbm, sem = rest[-4:]
+    half = out.shape[0] // 2
+    dng_out[...] = dng_ref[...]
+
+    @pl.when(sc[row, VALID] == 1)
+    def _():
+        copies = []
+        for k in range(2):
+            rows = slice(k * half, (k + 1) * half)
+            gn = own_ref[rows].astype(F32) + other_ref[rows].astype(F32)
+            h = h_ref[rows].astype(F32)
+            r = lax.rsqrt(jnp.mean(h * h, axis=1, keepdims=True) + EPSILON)
+            t = gn * ng_ref[...]
+            m = jnp.mean(h * t, axis=1, keepdims=True)
+            out[rows] = (g_ref[rows].astype(F32) + r * (t - h * (r * r * m))).astype(BF16)
+            target = e_hbm.at[sc[row, EDGE], pl.ds(k * half, half)]
+            copies.append(fetch(out.at[pl.ds(k * half, half)], target, sem.at[k]))
+            dng_out[...] += jnp.sum(gn * h * r, axis=0, keepdims=True)
+        for copy in copies:
+            copy.wait()
+
+
+def pick_kernel(first, sc, stack_hbm, out, sem):
+    fetch(stack_hbm.at[first + sc[0, CORE]], out, sem.at[0]).wait()
+
+
+ANY = pl.BlockSpec(memory_space=pl.ANY)
+NEAR = pl.BlockSpec(memory_space=pltpu.VMEM)
+SLOT, LEADING, FIRST, VALID, WRITE, EDGE, CORE = range(7)
+LITTLE = pl.CostEstimate(flops=1 << 20, bytes_accessed=1 << 16, transcendentals=0)
+
+
+def near(value):
+    return pltpu.with_memory_space_constraint(value, pltpu.VMEM)
+
+
+def away(value):
+    return pltpu.with_memory_space_constraint(value, pltpu.HBM)
+
+
+def chunk_call(kernel, table, free, far, close, close_outs, buffers, scratch, limit, name):
+    inputs = [table, *free, *(away(v) for v in far), *(near(v) for v in close)]
+    in_specs = [pl.BlockSpec(memory_space=pltpu.SMEM)]
+    in_specs += [ANY] * (len(free) + len(far)) + [NEAR] * len(close)
+    outs = [pltpu.VMEM(*o) for o in close_outs]
+    out_specs = [NEAR] * len(close_outs)
+    aliases = {}
+    for held, shape, dtype in buffers:
+        if held is not None:
+            aliases[len(inputs)] = len(outs)
+            inputs.append(away(held))
+            in_specs.append(ANY)
+        outs.append(pltpu.HBM(shape, dtype))
+        out_specs.append(ANY)
+    results = pl.pallas_call(
+        kernel,
+        in_specs=in_specs,
+        out_specs=out_specs,
+        out_shape=outs,
+        scratch_shapes=scratch,
+        input_output_aliases=aliases,
+        compiler_params=pltpu.CompilerParams(vmem_limit_bytes=limit << 20),
+        cost_estimate=LITTLE,
+        name=name,
+    )(*inputs)
+    return tuple(results[: len(close_outs)]), tuple(results[len(close_outs) :])
+
+
+def forward_call(table, row, slots, x, arrived, params, carry, held):
+    t = x.shape[0]
+    held = held or (None,) * 7
+    kinds = (
+        ((t, D), BF16),
+        ((t, D), BF16),
+        ((t, OWN_PROJ), BF16),
+        ((t, OWN), F32),
+        ((t, OWN), BF16),
+        ((STATE, OWN), F32),
+        ((8, OWN_CONV), F32),
+    )
+    gain, convp, headp, chanp, win, wout = params
+    outs, held = chunk_call(
+        functools.partial(forward_kernel, row),
+        table,
+        (*arrived, x),
+        (),
+        (gain, convp, headp, chanp, *carry, win, wout),
+        (((t, D + LANES), BF16), kinds[0], kinds[5], kinds[6]),
+        [(b, (slots,) + k, d) for b, (k, d) in zip(held, kinds)],
+        [pltpu.VMEM(*k) for k in kinds[1:]]
+        + [
+            pltpu.VMEM((t + 8, OWN_CONV), F32),
+            pltpu.VMEM((LANES, t), F32),
+            pltpu.VMEM((t, LANES), F32),
+            pltpu.VMEM((t, t), F32),
+            pltpu.SemaphoreType.DMA((8,)),
+        ],
+        FORWARD_VMEM,
+        "forward_chunk",
+    )
+    return outs[0], outs[1], outs[2:], held
+
+
+def backward_call(table, row, slots, cot, arrived, saved, params, carry, held):
+    t = arrived.shape[0]
+    held = held or (None, None)
+    _, convp, headp, chanp, win, wout = params
+    wide, projected = ((t, D), BF16), ((t, OWN_PROJ), BF16)
+    outs, held = chunk_call(
+        functools.partial(backward_kernel, row),
+        table,
+        (arrived, cot),
+        saved,
+        (convp, headp, chanp, *carry, win, wout),
+        [wide] * 3 + [(v.shape, v.dtype) for v in carry],
+        [(held[0], (slots, t, OWN_PROJ), BF16), (held[1], (slots, t, D), BF16)],
+        [
+            pltpu.VMEM(*projected),
+            pltpu.VMEM((t, OWN), F32),
+            pltpu.VMEM((STATE, OWN), F32),
+            pltpu.VMEM((8, OWN_CONV), F32),
+            pltpu.VMEM(*wide),
+            pltpu.VMEM((t, LANES), F32),
+            pltpu.VMEM(*projected),
+            pltpu.VMEM(*wide),
+            pltpu.VMEM((t + 8, OWN_CONV), F32),
+            pltpu.VMEM((t + 8, OWN_CONV), F32),
+            pltpu.VMEM((LANES, t), F32),
+            pltpu.VMEM((t, OWN), F32),
+            pltpu.VMEM((t, t), F32),
+            pltpu.VMEM((t, t), F32),
+            pltpu.VMEM((t, STATE), F32),
+            pltpu.VMEM((t, STATE), F32),
+            pltpu.SemaphoreType.DMA((9,)),
+        ],
+        BACKWARD_VMEM,
+        "backward_chunk",
+    )
+    return outs[:3], outs[3:], held
+
+
+def forward_join(table, row, slots, own, other, h, held):
+    t = h.shape[0]
+    held = held or (None,) * 3
+    wide, thin = ((t, D), BF16), ((t, LANES), F32)
+    outs, held = chunk_call(
+        functools.partial(forward_join_kernel, row),
+        table,
+        (),
+        (),
+        (own, other, h),
+        [((t // 2, D), BF16)],
+        [(b, (slots,) + k, d) for b, (k, d) in zip(held, (wide, thin, wide))],
+        [pltpu.VMEM(*k) for k in (wide, thin, wide)] + [pltpu.SemaphoreType.DMA((6,))],
+        JOIN_VMEM,
+        "forward_join",
+    )
+    return outs[0], held
+
+
+def backward_join(table, row, own, other, h, g, gain, dng, edge_held):
+    slots = edge_held.shape[0]
+    wide = (h.shape, BF16)
+    outs, held = chunk_call(
+        functools.partial(backward_join_kernel, row),
+        table,
+        (),
+        (),
+        (own, other, h, g, gain, dng),
+        [wide, ((1, D), F32)],
+        [(edge_held, (slots,) + h.shape, BF16)],
+        [pltpu.SemaphoreType.DMA((2,))],
+        JOIN_VMEM,
+        "backward_join",
+    )
+    return outs[0], outs[1], held[0]
+
+
+def pick(table, stack, first):
+    outs, _ = chunk_call(
+        functools.partial(pick_kernel, first),
+        table,
+        (),
+        (stack,),
+        (),
+        [(stack.shape[1:], stack.dtype)],
+        [],
+        [pltpu.SemaphoreType.DMA((1,))],
+        JOIN_VMEM,
+        "pick",
+    )
+    return outs[0]
+
+
+def own_of(values, core):
+    lead, width = values.shape[:-1], values.shape[-1]
+    blocks = values.reshape(lead + (4, 2, width // 8))
+    return lax.dynamic_index_in_dim(blocks, core, len(lead) + 1, False).reshape(
+        lead + (width // 2,)
+    )
+
+
+def woven(halves):
+    width = halves.shape[-1]
+    lead = halves.shape[1:-1]
+    blocks = halves.reshape((2,) + lead + (4, width // 4))
+    return jnp.moveaxis(blocks, 0, -2).reshape(lead + (2 * width,))
+
+
+def small_params(norm_gain, conv_weight, conv_bias, dt_bias, a_log, skip_gain, gate_gain, core):
+    own = functools.partial(own_of, core=core)
+    taps = jnp.concatenate([conv_weight.T, conv_bias[None]], axis=0).astype(F32)
+    taps = jnp.concatenate([own(taps[:, :INNER]), taps[:, INNER:]], axis=1)
+    convp = jnp.pad(taps, ((0, 3), (0, 0)))
+    heads = jnp.stack([own(dt_bias.astype(F32)), -jnp.exp(own(a_log.astype(F32)))])
+    headp = jnp.pad(heads, ((0, 6), (0, LANES - OWN_HEADS)))
+    skip = jnp.repeat(own(skip_gain.astype(F32)), HEAD_DIM)
+    chanp = jnp.pad(jnp.stack([skip, own(gate_gain.astype(F32))]), ((0, 6), (0, 0)))
+    return norm_gain.astype(F32)[None], convp, headp, chanp
+
+
+def own_steps(weight, core):
+    own = own_of(weight[INNER + CONV_CH :].T, core).T
+    return jnp.pad(own, ((0, 2 * LANES - OWN_HEADS), (0, 0)))
+
+
+HALF = OWN // 2
+BLOCK = HALF // 2
+PACKED_ROWS = HALF + HALF + 2 * STATE + 2 * BLOCK
+PARTS = (
+    ("in", HALF, X_AT, HALF),
+    ("in", HALF, 0, HALF),
+    ("in", 2 * STATE, BC_AT, 2 * STATE),
+    ("out", BLOCK, 0, HALF),
+    ("out", BLOCK, BLOCK, HALF),
+)
+
+
+def ring_place(position, count):
+    back = position >= count
+    return jnp.where(back, 1, 0), jnp.where(back, 2 * count - 1 - position, position)
+
+
+def ring_route(count, step):
+    def index(position):
+        return position if position < count else count + (2 * count - 1 - position)
+
+    size = 2 * count
+    return [(index(p), index((p + step) % size)) for p in range(size)]
+
+
+def pack_kernel(sc, w, steps, o, own, rest, sem):
+    core, side = sc[0], sc[1]
+    copies = []
+    for target, y in ((own, side), (rest, 1 - side)):
+        at = 0
+
+        def put(source, rows):
+            span = target.at[pl.ds(at, rows)]
+            copies.append(fetch(source, span, sem.at[len(copies)]))
+
+        for base in (INNER, 0):
+            for k in range(2):
+                first = aligned(base + (2 * y + k) * HALF + core * BLOCK)
+                put(w.at[pl.ds(first, BLOCK)], BLOCK)
+                at += BLOCK
+        bc = w.at[pl.ds(2 * INNER, 2 * STATE)]
+        span = target.at[pl.ds(at, 2 * STATE)]
+        copies.append(fetch_one_of(y == 0, bc, steps, span, sem.at[len(copies)]))
+        at += 2 * STATE
+        for k in range(2):
+            cols = pl.ds(aligned(y * HALF + k * BLOCK), BLOCK)
+            put(o.at[pl.ds(aligned(core * BLOCK), BLOCK), cols], BLOCK)
+            at += BLOCK
+    for copy in copies:
+        copy.wait()
+
+
+def pack_weights(scalars, w, steps, o):
+    return pl.pallas_call(
+        pack_kernel,
+        in_specs=[pl.BlockSpec(memory_space=pltpu.SMEM), ANY, ANY, ANY],
+        out_specs=[NEAR, NEAR],
+        out_shape=[pltpu.VMEM((PACKED_ROWS, BLOCK), BF16)] * 2,
+        scratch_shapes=[pltpu.SemaphoreType.DMA((14,))],
+        compiler_params=pltpu.CompilerParams(vmem_limit_bytes=4 << 20),
+        cost_estimate=LITTLE,
+        name="pack_weights",
+    )(scalars, away(w), steps, away(o))
+
+
+def place_kernel(sc, own, rest, *refs):
+    (near_z, inner_2, outer_2, inner_3, outer_3), (win, wout, sem) = (
+        [refs[2 * i : 2 * i + 2] for i in range(5)],
+        refs[-3:],
+    )
+    side, place = sc[1], sc[2]
+    inner = jnp.logical_and(place > 0, place < 3)
+    second = jnp.where(inner, 3 - place, jnp.where(place == 0, 2, 1))
+    third = jnp.where(place < 2, 3, 0)
+    used = []
+
+    def put(source, z, y, start):
+        lanes = pl.ds(aligned(z * BLOCK), BLOCK)
+        at = 0
+        for k, (matrix, rows, first, step) in enumerate(PARTS):
+            if matrix == "in":
+                target = win.at[pl.ds(aligned(first + y * step), rows), lanes]
+            else:
+                target = wout.at[lanes, pl.ds(aligned(first + y * step), BLOCK)]
+            copy = pltpu.make_async_copy(source.at[pl.ds(at, rows)], target, sem.at[start + k])
+            copy.start()
+            used.append(copy)
+            at += rows
+
+    put(own, place, side, 0)
+    put(rest, place, 1 - side, 5)
+    put(near_z[0], place + 1 - 2 * lax.rem(place, 2), side, 10)
+    put(near_z[1], place + 1 - 2 * lax.rem(place, 2), 1 - side, 15)
+    waits = list(used)
+
+    @pl.when(inner)
+    def _():
+        put(inner_2[0], second, side, 20)
+        put(inner_2[1], second, 1 - side, 25)
+        put(inner_3[0], third, side, 30)
+        put(inner_3[1], third, 1 - side, 35)
+        for copy in used[20:]:
+            copy.wait()
+        del used[20:]
+
+    @pl.when(jnp.logical_not(inner))
+    def _():
+        put(outer_2[0], second, side, 20)
+        put(outer_2[1], second, 1 - side, 25)
+        put(outer_3[0], third, side, 30)
+        put(outer_3[1], third, 1 - side, 35)
+        for copy in used[20:]:
+            copy.wait()
+
+    for copy in waits:
+        copy.wait()
+
+
+def place_weights(here, own, rest, pairs):
+    inputs = [own, rest, *sum(pairs, ())]
+    return pl.pallas_call(
+        place_kernel,
+        in_specs=[pl.BlockSpec(memory_space=pltpu.SMEM)] + [ANY] * len(inputs),
+        out_specs=[NEAR, NEAR],
+        out_shape=[pltpu.VMEM((OWN_PROJ, D), BF16), pltpu.VMEM((OWN, D), BF16)],
+        scratch_shapes=[pltpu.SemaphoreType.DMA((40,))],
+        compiler_params=pltpu.CompilerParams(vmem_limit_bytes=4 << 20),
+        cost_estimate=LITTLE,
+        name="place_weights",
+    )(here, *inputs)
+
+
+def line_gather(own, beside):
+    def along(value, hops):
+        route = [(y * 4 + a, y * 4 + b) for y in range(2) for a, b in hops]
+        return lax.ppermute(value, ("y", "fsdp"), route)
+
+    def across(value, places):
+        route = [(y * 4 + z, (1 - y) * 4 + z) for y in range(2) for z in places]
+        return lax.ppermute(value, ("y", "fsdp"), route)
+
+    outward, middle = [(1, 0), (2, 3)], [(1, 2), (2, 1)]
+    near_z = along(own, [(0, 1), (1, 0), (2, 3), (3, 2)])
+    inner_2 = along(own, middle)
+    near_z, inner_2, *beside = lax.optimization_barrier((near_z, inner_2, *beside))
+    outer_2 = along(inner_2, outward)
+    inner_3 = along(near_z, middle)
+    near_y = across(near_z, range(4))
+    outer_2, inner_3, near_y = lax.optimization_barrier((outer_2, inner_3, near_y))
+    outer_3 = along(inner_3, outward)
+    outer_2_y = across(outer_2, (0, 3))
+    inner_2_y = across(inner_2, (1, 2))
+    ready = near_y
+    outer_3, outer_2_y, inner_2_y = lax.optimization_barrier((outer_3, outer_2_y, inner_2_y))
+    outer_3_y = across(outer_3, (0, 3))
+    inner_3_y = across(inner_3, (1, 2))
+    return [
+        (near_z, near_y),
+        (inner_2, inner_2_y),
+        (outer_2, outer_2_y),
+        (inner_3, inner_3_y),
+        (outer_3, outer_3_y),
+    ], ready, beside
+
+
+GROUPS = (
+    (1, (HALF, X_AT, HALF), (LANES, BC_AT, 2 * STATE)),
+    (-1, (HALF, 0, HALF), (LANES, BC_AT + LANES, 2 * STATE)),
+)
+
+
+SMALL_ROWS = 16
+IN_ROWS = HALF + LANES
+GROUP_ROWS = IN_ROWS + BLOCK
+
+
+def block_grad_kernel(row, sc, normed_ref, q_ref, gs_ref, *refs):
+    out = refs[-1]
+    chunks = normed_ref.shape[0]
+    at = 0
+    for ref in refs[:2]:
+        width = ref.shape[2]
+        out[at : at + width, :] = sum(dot_tn(ref[k], normed_ref[k]) for k in range(chunks))
+        at += width
+    out[at:, :] = sum(dot_tn(q_ref[k], gs_ref[k]) for k in range(chunks))
+    if len(refs) > 3:
+
+        @pl.when(sc[row, 0] == 1)
+        def _():
+            out[HALF : HALF + SMALL_ROWS, :] = refs[2][0]
+
+
+def block_grad(table, row, group, normed_held, grads_held, q_held, gs_held, small):
+    slots, t, _ = normed_held.shape
+    number, (_, *parts) = group, GROUPS[group]
+
+    def block(width, index):
+        return pl.BlockSpec((slots - 1, t, width), lambda i, s: (0, 0, index(s)))
+
+    in_specs = [
+        block(BLOCK, lambda s: s[row, 1]),
+        block(BLOCK, lambda s: s[row, 1]),
+        block(BLOCK, lambda s: 2 * s[row, 0] + number),
+    ]
+    for width, first, step in parts:
+
+        def index(s, width=width, first=first, step=step):
+            return first // width + s[row, 0] * (step // width)
+
+        in_specs.append(block(width, index))
+    extra = []
+    if number == 1:
+        extra = [small]
+        in_specs.append(pl.BlockSpec((1, SMALL_ROWS, BLOCK), lambda i, s: (s[row, 1], 0, 0)))
+    return pl.pallas_call(
+        functools.partial(block_grad_kernel, row),
+        grid_spec=pltpu.PrefetchScalarGridSpec(
+            num_scalar_prefetch=1,
+            grid=(1,),
+            in_specs=in_specs,
+            out_specs=pl.BlockSpec((GROUP_ROWS, BLOCK), lambda i, s: (0, 0)),
+        ),
+        out_shape=jax.ShapeDtypeStruct((GROUP_ROWS, BLOCK), F32),
+        compiler_params=pltpu.CompilerParams(vmem_limit_bytes=24 << 20),
+        cost_estimate=LITTLE,
+        name="block_grad",
+    )(
+        table,
+        away(normed_held),
+        away(q_held),
+        away(gs_held),
+        *([away(grads_held)] * len(parts)),
+        *extra,
+    )
+
+
+def grads_kernel(sc, *refs):
+    in_hbm, out_hbm, small_out, in_v, out_v, sem = refs[-6:]
+    core, side = sc[0], sc[1]
+
+    def block(i, c, y, rows):
+        own, across, other = refs[3 * i : 3 * i + 3]
+        here = jnp.where(side == y, own[rows], across[rows])
+        there = jnp.where(side == y, other[0, rows], other[1, rows])
+        return jnp.where(core == c, here, there).astype(F32)
+
+    copies = []
+
+    def store(values, near_ref, far_ref, at):
+        near_ref[at : at + values.shape[0]] = values
+        span = pl.ds(at, values.shape[0])
+        copies.append(fetch(near_ref.at[span], far_ref.at[span], sem.at[len(copies)]))
+
+    for i, base in ((0, INNER), (1, 0)):
+        for c in range(2):
+            for y in range(2):
+                for k in range(2):
+                    rows = slice(k * BLOCK, (k + 1) * BLOCK)
+                    store(block(i, c, y, rows), in_v, in_hbm, base + (2 * y + k) * HALF + c * BLOCK)
+    rows = slice(HALF, HALF + STATE)
+    for i in range(2):
+        store(block(i, 0, 0, rows) + block(i, 1, 0, rows), in_v, in_hbm, 2 * INNER + i * STATE)
+    steps = [block(0, c, 1, slice(HALF, HALF + 32)) for c in range(2)]
+    steps = [steps[c][z * 6 : z * 6 + 6] for z in range(4) for c in range(2)]
+    store(jnp.concatenate(steps, axis=0), in_v, in_hbm, INNER + CONV_CH)
+    rows = slice(HALF, HALF + SMALL_ROWS)
+    small_out[...] = block(1, 0, 1, rows) + block(1, 1, 1, rows)
+    rows = slice(IN_ROWS, GROUP_ROWS)
+    for c in range(2):
+        values = [block(i, c, y, rows) for y in range(2) for i in range(2)]
+        store(jnp.concatenate(values, axis=1), out_v, out_hbm, c * BLOCK)
+    for copy in copies:
+        copy.wait()
+
+
+def join_grads(scalars, parts):
+    arrays = [near(a) for part in parts for a in part]
+    height = INNER + CONV_CH + HEADS
+    shapes = ((height, BLOCK), F32), ((2 * BLOCK, D), F32)
+    return pl.pallas_call(
+        grads_kernel,
+        in_specs=[pl.BlockSpec(memory_space=pltpu.SMEM)] + [NEAR] * len(arrays),
+        out_specs=[ANY, ANY, NEAR],
+        out_shape=[pltpu.HBM(*k) for k in shapes] + [pltpu.VMEM((SMALL_ROWS, BLOCK), F32)],
+        scratch_shapes=[pltpu.VMEM(*k) for k in shapes] + [pltpu.SemaphoreType.DMA((24,))],
+        compiler_params=pltpu.CompilerParams(vmem_limit_bytes=28 << 20),
+        cost_estimate=LITTLE,
+        name="join_grads",
+    )(scalars, *arrays)
+
+
+def swap(value, axis):
+    return lax.ppermute(value, axis, [(0, 1), (1, 0)])
+
+
+def sent_along(value, axis):
+    size = lax.axis_size(axis)
+    routes = [[(i, (i + k) % size) for i in range(size)] for k in range(1, size)]
+    return [lax.ppermute(value, axis, path) for path in routes]
+
+
+def in_order(value, others, axis):
+    size, place = len(others) + 1, lax.axis_index(axis)
+    ring = jnp.stack([*others[::-1], value] * 2)
+    return lax.dynamic_slice_in_dim(ring, (size - 1 - place) % size, size, 0)
+
+
+LAG = 2
+
+
+def relay_shards(
+    ends,
+    norm_gain,
+    input_weight,
+    conv_weight,
+    conv_bias,
+    dt_bias,
+    a_log,
+    skip_gain,
+    gate_gain,
+    output_weight,
+):
+    core = lax.axis_index("core")
+    place = lax.axis_index("fsdp")
+    side = lax.axis_index("y")
+    section = lax.axis_index("section")
+    leading = (section == 0).astype(jnp.int32)
+    local = ends[0][:, 0]
+    t = local.shape[1]
+    chunks = lax.axis_size("fsdp")
+    micro = place // 2
+
+    small = [norm_gain[0], conv_weight[0].reshape(-1), conv_bias[0], dt_bias[0], a_log[0]]
+    small += [skip_gain[0], gate_gain[0]]
+    packed = jnp.concatenate(small)
+    others = sent_along(packed, "fsdp")
+    w = input_weight[0].T
+    steps = own_steps(w, core)
+    here = jnp.stack([core, side, place]).astype(jnp.int32)
+    own, rest = pack_weights(here, w, steps, output_weight[0])
+    pairs, ready, others = line_gather(own, others)
+    packed = in_order(packed, others, "fsdp")
+    pieces, at = [], 0
+    for member in small:
+        pieces.append(packed[:, at : at + member.shape[0]].reshape(-1))
+        at += member.shape[0]
+    pieces[1] = pieces[1].reshape(CONV_CH, KERNEL)
+    gain, convp, headp, chanp = small_params(*pieces, core)
+    local, _ = lax.optimization_barrier((local, ready))
+
+    def route(first, m):
+        return [
+            (c * chunks + z, (z % 2) * chunks + 2 * m + c)
+            for c in range(2)
+            for z in (first, first + 1)
+        ]
+
+    def bring(first):
+        return [lax.ppermute(local[m], ("core", "fsdp"), route(first, m)) for m in range(2)]
+
+    def shared(got):
+        got = jnp.where(micro == 0, got[0], got[1])
+        other = swap(got, "core")
+        return [jnp.where(core == 0, got, other), jnp.where(core == 0, other, got)]
+
+    def give(piece, first):
+        return [
+            lax.ppermute(piece, ("core", "fsdp"), [(b, a) for a, b in route(first, m)])
+            for m in range(2)
+        ]
+
+    here, *got = lax.optimization_barrier((here, *bring(0), *bring(2)))
+    pieces = shared(got[:2]) + shared(got[2:])
+    win, wout = place_weights(here, own, rest, pairs)
+    params = (gain, convp, headp, chanp, win, wout)
+
+    def scalars(moment, lag, reverse):
+        begin = jnp.where(leading == 1, lag if reverse else 0, 0 if reverse else lag)
+        step = moment - begin
+        valid = jnp.logical_and(step >= 0, step < chunks)
+        inside = jnp.clip(step, 0, chunks - 1)
+        chunk = chunks - 1 - inside if reverse else inside
+        write = jnp.where(valid, chunk, chunks)
+        edge_here = leading == 1 if reverse else leading == 0
+        edge = jnp.where(jnp.logical_and(valid, edge_here), chunk, chunks)
+        values = [chunk if reverse else write, leading, step == 0, valid, write, edge, core]
+        return [jnp.asarray(v, jnp.int32) for v in values]
+
+    moments = chunks + LAG
+    table = [scalars(moment, LAG, False) for moment in range(moments)]
+    table += [scalars(moment, LAG, True) for moment in range(moments)]
+    table = jnp.stack(sum(table, [])).reshape(len(table), -1)
+
+    state, tail = jnp.zeros((STATE, OWN), F32), jnp.zeros((8, OWN_CONV), F32)
+    blank = jnp.zeros((t, D), BF16)
+    held, joined, result = None, None, None
+    moved, incoming = {}, {}
+    for moment in range(moments):
+        if moment > 0:
+            tail, result = lax.optimization_barrier((tail, result))
+            if moment - 1 < chunks:
+                moved[moment - 1] = lax.ppermute(result, "section", [(0, 1)])
+        arrived = incoming.get(moment - LAG, (blank[: t // 2],) * 2)
+        partial, h, (state, tail), held = forward_call(
+            table,
+            moment,
+            chunks + 1,
+            pieces[min(moment, chunks - 1)],
+            arrived,
+            params,
+            (state, tail),
+            held,
+        )
+        if moment - 1 in moved:
+            partial, got = lax.optimization_barrier((partial, moved[moment - 1]))
+            incoming[moment - 1] = (got, swap(got, "core"))
+        other = swap(partial, "core")
+        result, joined = forward_join(table, moment, chunks + 1, partial, other, h, joined)
+    h_held, normed_held, pr_held, mx_held, q_held, st_held, tl_held = held
+    y_held, ri_held, edge_held = joined
+    saved = (h_held, pr_held, mx_held, st_held, tl_held, y_held, ri_held)
+
+    def tokens(buffer):
+        return buffer[:chunks].reshape(chunks * t, buffer.shape[-1])
+
+    carry = (
+        jnp.zeros((STATE, OWN), F32),
+        jnp.zeros((8, OWN_CONV), F32),
+        jnp.zeros((8, OWN), F32),
+        jnp.zeros((16, OWN_CONV), F32),
+    )
+    dng = jnp.zeros((1, D), F32)
+    grads_held, edges_late = None, None
+    incoming = {}
+    for moment in range(moments):
+        if moment > 0:
+            *carry, acc = carry
+            acc, result = lax.optimization_barrier((acc, result))
+            if moment == moments - 1:
+                acc, edges_late = lax.optimization_barrier((acc, edges_late))
+            carry = (*carry, acc)
+            if moment - 1 < chunks:
+                incoming[moment - 1] = lax.ppermute(result, "section", [(1, 0)])
+        arrived = incoming.get(moment - LAG, blank)
+        cot = pieces[max(chunks - 1 - moment, 0)]
+        (partial, g, h), carry, grads_held = backward_call(
+            table, moments + moment, chunks + 1, cot, arrived, saved, params, carry, grads_held
+        )
+        if moment - 1 in incoming:
+            partial, incoming[moment - 1] = lax.optimization_barrier(
+                (partial, incoming[moment - 1])
+            )
+        other = swap(partial, "core")
+        result, dng, edge_held = backward_join(
+            table, moments + moment, partial, other, h, g, gain, dng, edge_held
+        )
+        if moment == LAG + 1:
+            edges_late = give(pick(table, edge_held, 2), 2)
+
+    def both(own, other, index):
+        return jnp.where(index == 0, jnp.stack([own, other]), jnp.stack([other, own]))
+
+    acc = carry[3]
+
+    def placed(own):
+        zero = jnp.zeros_like(own)
+        return woven(both(own, zero, core))
+
+    taps = jnp.concatenate([placed(acc[:5, :OWN]), acc[:5, OWN:]], axis=1)
+    taps = jnp.moveaxis(taps.reshape(KERNEL + 1, chunks, -1), 1, 0)
+    skip = acc[5, :OWN].reshape(OWN_HEADS, HEAD_DIM).sum(axis=1)
+    vectors = [
+        jnp.where(core == 0, dng[0], 0.0),
+        taps,
+        placed(acc[7, :OWN_HEADS]),
+        placed(acc[8, :OWN_HEADS]),
+        placed(skip),
+        placed(acc[6, :OWN]),
+    ]
+    vectors = [v.reshape(chunks, -1) for v in vectors]
+    small = jnp.concatenate(vectors, axis=1)
+    small = jnp.pad(small, ((0, 0), (0, SMALL_ROWS * BLOCK - small.shape[1])))
+    small = small.reshape(chunks, SMALL_ROWS, BLOCK)
+
+    size = 2 * chunks
+    onward, back = ring_route(chunks, 1), ring_route(chunks, -1)
+    position = jnp.where(side == 0, place, size - 1 - place).astype(jnp.int32)
+    owners = []
+    for direction in (1, -1):
+        for hop in range(size):
+            owners += ring_place((position - direction * (1 + hop)) % size, chunks)
+    owners = jnp.stack(owners).reshape(2 * size, 2).astype(jnp.int32)
+    grads_held, gs_held = grads_held
+    sums = [None] * len(GROUPS)
+    for hop in range(size):
+        if hop > 0:
+            owners, *sums = lax.optimization_barrier((owners, *sums))
+        for i, (direction, *_) in enumerate(GROUPS):
+            row = hop + (0 if direction == 1 else size)
+            block = block_grad(owners, row, i, normed_held, grads_held, q_held, gs_held, small)
+            if hop > 0:
+                path = onward if direction == 1 else back
+                block = block + lax.ppermute(sums[i], ("y", "fsdp"), path).astype(F32)
+            sums[i] = block.astype(BF16)
+        if hop == 3:
+            owners, edge_last = lax.optimization_barrier((owners, pick(table, edge_held, 0)))
+    *sums, edge_last = lax.optimization_barrier((*sums, edge_last))
+
+    edges = jnp.where(place < 2, jnp.stack(give(edge_last, 0)), jnp.stack(edges_late))
+    edges = edges[None, :, None]
+    parts = []
+    for i, own in enumerate(sums):
+        across = swap(own, "y")
+        if i == 1:
+            across, edges = lax.optimization_barrier((across, edges))
+        parts.append((own, across, swap(jnp.stack([own, across]), "core")))
+    here = jnp.stack([core, side]).astype(jnp.int32)
+    in_grad, out_grad, summed = join_grads(here, parts)
+    in_grad = in_grad.T
+    summed = summed.reshape(-1)
+    grads, at = [], 0
+    for v in vectors:
+        grads.append(summed[at : at + v.shape[1]][None])
+        at += v.shape[1]
+    taps = grads[1].reshape(KERNEL + 1, -1)
+    grads[1:2] = taps[:KERNEL].T[None], taps[KERNEL:]
+    return (
+        edges,
+        grads[0],
+        in_grad[None],
+        grads[1],
+        grads[2],
+        grads[3],
+        grads[4],
+        grads[5],
+        grads[6],
+        out_grad[None],
+    )
 
 
 def shifted(block, axis, distance):
@@ -396,28 +1617,19 @@
 
 
 def solution(mesh):
-    in_specs = (
-        P("section", None, "rep", "fsdp", None),
-        P("section", "fsdp"),
-        P("section", "fsdp", None),
-        P("section", "fsdp", None),
-        P("section", "fsdp"),
-        P("section", "fsdp"),
-        P("section", "fsdp"),
-        P("section", "fsdp"),
-        P("section", "fsdp"),
-        P("section", "fsdp", None),
-    )
-    out_specs = (
-        P("section", None, "rep", "fsdp", None),
-        P("section", "fsdp"),
-        P("section", "fsdp", None),
-        P("section", "fsdp", None),
-        P("section", "fsdp"),
-        P("section", "fsdp"),
-        P("section", "fsdp"),
-        P("section", "fsdp"),
-        P("section", "fsdp"),
-        P("section", "fsdp", None),
-    )
-    return jax.shard_map(shards, mesh=mesh, in_specs=in_specs, out_specs=out_specs, check_vma=False)
+    shape = mesh.shape
+    relay = shape["section"] == 2 and shape["rep"] == 4 and shape["fsdp"] == 4
+    if relay:
+        devices = mesh.devices.reshape(2, 2, 2, 4)
+        mesh = Mesh(devices, ("section", "y", "core", "fsdp"))
+    rep = ("y", "core") if relay else "rep"
+    data = P("section", None, rep, "fsdp", None)
+    vector, matrix = P("section", "fsdp"), P("section", "fsdp", None)
+    params = (vector, matrix, matrix, vector, vector, vector, vector, vector, matrix)
+    return jax.shard_map(
+        relay_shards if relay else shards,
+        mesh=mesh,
+        in_specs=(data, *params),
+        out_specs=(data, *params),
+        check_vma=False,
+    )

time: 2650 us -> 750 us (0.28)
  waiting for transfers between devices: 1120 us -> 311 us
  matrix products: 564 us -> 0 us
  local copies, waits for them, and re-layouts: 413 us -> 33.4 us
  other arithmetic: 302 us -> 12.2 us
  Pallas kernels: 0 us -> 261 us
  blocking collectives: 182 us -> 0 us
  starting transfers between devices: 24.5 us -> 122 us
    dot_general x63 -> x0, matrix products: 564 us -> none  [the longest x12 195 us: gated_output(): jnp.einsum('shqk,skhd->sqhd', mixing * intersections[:, None], scaled, pr...]
    all_gather x8 -> x0, waiting for transfers between devices: 448 us -> none  [the longest x1 252 us: shards(): lax.all_gather(input_weight, 'fsdp', axis=1, tiled=True)]
    unnamed x20 -> x0, waiting for transfers between devices: 372 us -> none
    ppermute x10 -> x65, waiting for transfers between devices: 43.7 us -> 311 us  [the longest x5 76.3 us: along(): return lax.ppermute(value, ('y', 'fsdp'), route)]
    pallas_call x0 -> x45, Pallas kernels: none -> 261 us  [the longest x26 177 us: chunk_call(): pl.pallas_call(kernel, in_specs=in_specs, out_specs=out_specs, out_shape=...]
    all_gather x9 -> x0, blocking collectives: 150 us -> none  [the longest x1 56.3 us: shards(): lax.all_gather(conv_weight, 'fsdp', axis=1, tiled=True)]
    unnamed x545 -> x75, local copies, waits for them, and re-layouts: 168 us -> 21.1 us
    reduce_scatter x1 -> x0, waiting for transfers between devices: 136 us -> none  [shards(): lax.psum_scatter(totals[8][None].astype(jnp.bfloat16), 'fsdp', scatter_di...]
  transfers between devices with their start and end apart: 25 -> 65, of which waited for: 15 -> 39; matrix products, arithmetic and copies ran while one was open for 23% -> 3% of each run, Pallas kernels for 0% -> 26%
where the time goes in v1:
time: 750 us; the launch traced here: 742 us
  waiting for transfers between devices  311 us (41%)
  Pallas kernels  261 us (35%)
  starting transfers between devices  122 us (16%)
  local copies, waits for them, and re-layouts  33.4 us (4%)
  other arithmetic  12.2 us (2%)
    pallas_call x26, Pallas kernels, chunk_call(): pl.pallas_call(kernel, in_specs=in_specs, out_specs=out_specs, out_shape=...  177 us
    ppermute x5, waiting for transfers between devices, along(): return lax.ppermute(value, ('y', 'fsdp'), route)  76.3 us
    ppermute x14, waiting for transfers between devices, relay_shards(): block = block + lax.ppermute(sums[i], ('y', 'fsdp'), path).astype(F32)  74 us
    pallas_call x16, Pallas kernels, block_grad(): pl.pallas_call(functools.partial(block_grad_kernel, row), grid_spec=pltpu...  70.1 us
    ppermute x4, waiting for transfers between devices, relay_shards(): incoming[moment - 1] = lax.ppermute(result, 'section', [(1, 0)])  48.6 us
    ppermute x22, starting transfers between devices, swap(): return lax.ppermute(value, axis, [(0, 1), (1, 0)])  46.4 us
    ppermute x3, waiting for transfers between devices, sent_along(): return [lax.ppermute(value, axis, path) for path in routes]  39.6 us
    ppermute x5, waiting for transfers between devices, across(): return lax.ppermute(value, ('y', 'fsdp'), route)  24.7 us
  transfers between devices with their start and end apart: 65, of which 39 were waited for; matrix products, arithmetic and copies ran while one was open for 3% of the time, Pallas kernels for 26%

profile of v1, /device:TPU:1, one launch (start us, length us, event | category | flops | bytes accessed | tf_op | source)
XLA Modules:
  0.0 742.3 jit_solution(4878866472044961241)
XLA Ops:
  15.2 37.1 %collective-permute-done.2 = bf16[5348]{0:T(1024)(128)(2,1)S(1)} collective-permute-done((bf16[5348]{0:T(1024)(128)(2,1)S(1)}, bf16[5348]{0:T(1024)(128)(2,1)S(1)}, u32[]{:S(2)}, u32[]{:S(2)}) %collective-permute-start.2) | collective-permute-done | bytes 10728 | tf_op jit(solution)/shard_map/ppermute | solution.py:997
  58.9 40.4 %collective-permute-done.5.refs_4_ = bf16[2560,384]{1,0:T(8,128)(2,1)} collective-permute-done((bf16[2560,384]{1,0:T(8,128)(2,1)}, bf16[2560,384]{1,0:T(8,128)(2,1)}, u32[]{:S(2)}, u32[]{:S(2)}) %collective-permute-start.5) | collective-permute-done | bytes 1966112 | tf_op jit(solution)/shard_map/ppermute | solution.py:834
  110.2 11.7 %collective-permute-start.8 = (bf16[256,1536]{1,0:T(8,128)(2,1)}, bf16[256,1536]{1,0:T(8,128)(2,1)}, u32[]{:S(2)}, u32[]{:S(2)}) collective-permute-start(bf16[256,1536]{1,0:T(8,128)(2,1)} %get-tuple-element.495), channel_id=1, source_target_pairs={{0,0},{1,4},{4,1},{5,5},{8,8},{9,12},{12,9},{13,13},{16,16},{17,20... | collective-permute-start | bytes 2359304 | tf_op jit(solution)/shard_map/ppermute | solution.py:1057
  124.9 35.9 %collective-permute-done.13.refs_8_ = bf16[2560,384]{1,0:T(8,128)(2,1)S(1)} collective-permute-done((bf16[2560,384]{1,0:T(8,128)(2,1)S(1)}, bf16[2560,384]{1,0:T(8,128)(2,1)S(1)}, u32[]{:S(2)}, u32[]{:S(2)}) %collective-permute-start.13) | collective-permute-done | bytes 1966112 | tf_op jit(solution)/shard_map/ppermute | solution.py:834
  177.2 5.6 collective-permute-start.12
  184.9 24.5 %collective-permute-done.17.refs_9_ = bf16[2560,384]{1,0:T(8,128)(2,1)} collective-permute-done((bf16[2560,384]{1,0:T(8,128)(2,1)}, bf16[2560,384]{1,0:T(8,128)(2,1)}, u32[]{:S(2)}, u32[]{:S(2)}) %collective-permute-start.17) | collective-permute-done | bytes 1966112 | tf_op jit(solution)/shard_map/ppermute | solution.py:838
  212.4 4.7 place_weights.1
  217.3 12.8 %forward_chunk.6 = (bf16[256,1664]{1,0:T(8,128)(2,1)S(1)}, bf16[256,1536]{1,0:T(8,128)(2,1)S(1)}, f32[128,1536]{1,0:T(8,128)S(1)}, f32[8,1792]{1,0:T(8,128)S(1)}...) custom-call(s32[12,7]{1,0:T(8,128)S(1)} %reshape.197.sc, ...), custom_call_target="tpu_custom_call" | custom-call | flops 1048576 | bytes 65536 | tf_op jit(solution)/shard_map/forward_chunk/pallas_call | solution.py:527
  230.1 8.3 %collective-permute-start.18 = (bf16[256,1664]{1,0:T(8,128)(2,1)S(1)}, bf16[256,1664]{1,0:T(8,128)(2,1)S(1)}, u32[]{:S(2)}, u32[]{:S(2)}) collective-permute-start(bf16[256,1664]{1,0:T(8,128)(2,1)S(1)} %get-tuple-element.271.own_ref), channel_id=1, source_target_pairs={{0,4},{4,0},{1,5},{5,1},{2,6},{6,2},{3,7},{7,3},{8,12},{12,8},{9,1... | collective-permute-start | bytes 2555912 | tf_op jit(solution)/shard_map/ppermute | solution.py:991
  243.9 12.2 %forward_chunk.7 = (bf16[256,1664]{1,0:T(8,128)(2,1)S(1)}, bf16[256,1536]{1,0:T(8,128)(2,1)S(1)}, f32[128,1536]{1,0:T(8,128)S(1)}, f32[8,1792]{1,0:T(8,128)S(1)}...) custom-call(s32[12,7]{1,0:T(8,128)S(1)} %reshape.197.sc, ...), custom_call_target="tpu_custom_call", output_to_operand_aliasing={{4}: (12, {}), {5}: (13, {}), {6}: (14, {}), {7}: (15, {}),... | custom-call | flops 1048576 | bytes 65536 | tf_op jit(solution)/shard_map/forward_chunk/pallas_call | solution.py:527
  262.2 12.3 %forward_chunk.8 = (bf16[256,1664]{1,0:T(8,128)(2,1)S(1)}, bf16[256,1536]{1,0:T(8,128)(2,1)S(1)}, f32[128,1536]{1,0:T(8,128)S(1)}, f32[8,1792]{1,0:T(8,128)S(1)}...) custom-call(s32[12,7]{1,0:T(8,128)S(1)} %reshape.197.sc, ...), custom_call_target="tpu_custom_call", output_to_operand_aliasing={{4}: (12, {}), {5}: (13, {}), {6}: (14, {}), {7}: (15, {}),... | custom-call | flops 1048576 | bytes 65536 | tf_op jit(solution)/shard_map/forward_chunk/pallas_call | solution.py:527
  276.9 13.7 %forward_join.8 = (bf16[128,1536]{1,0:T(8,128)(2,1)S(1)}, bf16[5,256,1536]{2,1,0:T(8,128)(2,1)}, f32[5,256,128]{2,1,0:T(8,128)}, bf16[5,256,1536]{2,1,0:T(8,128)(2,1)}) custom-call(s32[12,7]{1,0:T(8,128)S(1)} %reshape.197.sc, bf16[256,1664]{1,0:T(8,128)(2,1)S(1)} %get-tuple-element.308.own_ref, ...), custom_call_target="tpu_custom_call", output_to_operand_aliasing={{1}: (4, {}), {2}: (5, {}), {3}: (6, {})} | custom-call | flops 1048576 | bytes 65536 | tf_op jit(solution)/shard_map/forward_join/pallas_call | solution.py:527
  292.0 12.2 %forward_chunk.9 = (bf16[256,1664]{1,0:T(8,128)(2,1)S(1)}, bf16[256,1536]{1,0:T(8,128)(2,1)S(1)}, f32[128,1536]{1,0:T(8,128)S(1)}, f32[8,1792]{1,0:T(8,128)S(1)}...) custom-call(s32[12,7]{1,0:T(8,128)S(1)} %reshape.197.sc, ...), custom_call_target="tpu_custom_call", output_to_operand_aliasing={{4}: (12, {}), {5}: (13, {}), {6}: (14, {}), {7}: (15, {}),... | custom-call | flops 1048576 | bytes 65536 | tf_op jit(solution)/shard_map/forward_chunk/pallas_call | solution.py:527
  311.0 7.6 %collective-permute-done.29.refs_0_ = bf16[128,1536]{1,0:T(8,128)(2,1)S(1)} collective-permute-done((bf16[128,1536]{1,0:T(8,128)(2,1)S(1)}, bf16[128,1536]{1,0:T(8,128)(2,1)S(1)}, u32[]{:S(2)}, u32[]{:S(2)}) %collective-permute-start.29) | collective-permute-done | bytes 393248 | tf_op jit(solution)/shard_map/ppermute | solution.py:1100
  331.8 7.8 %backward_chunk.7 = (bf16[256,1536]{1,0:T(8,128)(2,1)S(1)}, bf16[256,1536]{1,0:T(8,128)(2,1)S(1)}, bf16[256,1536]{1,0:T(8,128)(2,1)S(1)}, f32[128,1536]{1,0:T(8,...) custom-call(s32[12,7]{1,0:T(8,128)S(1)} %reshape.197.sc, ...), custom_call_target="tpu_custom_call", output_to_operand_aliasing={{7}: (19, {}), {8}: (20, {})} | custom-call | flops 1048576 | bytes 65536 | tf_op jit(solution)/shard_map/backward_chunk/pallas_call | solution.py:527
  339.6 45.3 %collective-permute-done.34.refs_0_ = bf16[256,1536]{1,0:T(8,128)(2,1)S(1)} collective-permute-done((bf16[256,1536]{1,0:T(8,128)(2,1)S(1)}, bf16[256,1536]{1,0:T(8,128)(2,1)S(1)}, u32[]{:S(2)}, u32[]{:S(2)}) %collective-permute-start.34) | collective-permute-done | bytes 786464 | tf_op jit(solution)/shard_map/ppermute | solution.py:1141
  389.5 17.5 %backward_chunk.8 = (bf16[256,1536]{1,0:T(8,128)(2,1)S(1)}, bf16[256,1536]{1,0:T(8,128)(2,1)S(1)}, bf16[256,1536]{1,0:T(8,128)(2,1)S(1)}, f32[128,1536]{1,0:T(8,...) custom-call(s32[12,7]{1,0:T(8,128)S(1)} %reshape.197.sc, ...), custom_call_target="tpu_custom_call", output_to_operand_aliasing={{7}: (19, {}), {8}: (20, {})} | custom-call | flops 1048576 | bytes 65536 | tf_op jit(solution)/shard_map/backward_chunk/pallas_call | solution.py:527
  415.8 17.9 %backward_chunk.9 = (bf16[256,1536]{1,0:T(8,128)(2,1)S(1)}, bf16[256,1536]{1,0:T(8,128)(2,1)S(1)}, bf16[256,1536]{1,0:T(8,128)(2,1)S(1)}, f32[128,1536]{1,0:T(8,...) custom-call(s32[12,7]{1,0:T(8,128)S(1)} %reshape.197.sc, ...), custom_call_target="tpu_custom_call", output_to_operand_aliasing={{7}: (19, {}), {8}: (20, {})} | custom-call | flops 1048576 | bytes 65536 | tf_op jit(solution)/shard_map/backward_chunk/pallas_call | solution.py:527
  455.4 17.4 %backward_chunk.10 = (bf16[256,1536]{1,0:T(8,128)(2,1)S(1)}, bf16[256,1536]{1,0:T(8,128)(2,1)S(1)}, bf16[256,1536]{1,0:T(8,128)(2,1)S(1)}, f32[128,1536]{1,0:T(8...) custom-call(s32[12,7]{1,0:T(8,128)S(1)} %reshape.197.sc, ...), custom_call_target="tpu_custom_call", output_to_operand_aliasing={{7}: (19, {}), {8}: (20, {})} | custom-call | flops 1048576 | bytes 65536 | tf_op jit(solution)/shard_map/backward_chunk/pallas_call | solution.py:527
  475.6 19.8 %backward_chunk.11 = (bf16[256,1536]{1,0:T(8,128)(2,1)}, bf16[256,1536]{1,0:T(8,128)(2,1)S(1)}, bf16[256,1536]{1,0:T(8,128)(2,1)S(1)}, f32[128,1536]{1,0:T(8,128...) custom-call(s32[12,7]{1,0:T(8,128)S(1)} %reshape.197.sc, ...), custom_call_target="tpu_custom_call", output_to_operand_aliasing={{7}: (19, {}), {8}: (20, {})} | custom-call | flops 1048576 | bytes 65536 | tf_op jit(solution)/shard_map/backward_chunk/pallas_call | solution.py:527
  499.1 4.4 block_grad.16
  513.2 4.4 block_grad.17
  519.9 4.4 block_grad.19
  524.3 4.4 block_grad.18
  528.7 12.1 %collective-permute-done.46 = bf16[1280,384]{1,0:T(8,128)(2,1)S(1)} collective-permute-done((bf16[1280,384]{1,0:T(8,128)(2,1)S(1)}, bf16[1280,384]{1,0:T(8,128)(2,1)S(1)}, u32[]{:S(2)}, u32[]{:S(2)}) %collective-permute-start.46) | collective-permute-done | bytes 983072 | tf_op jit(solution)/shard_map/ppermute | solution.py:1201
  543.7 4.4 block_grad.21
  548.1 4.4 block_grad.20
  552.5 11.1 %collective-permute-done.48 = bf16[1280,384]{1,0:T(8,128)(2,1)S(1)} collective-permute-done((bf16[1280,384]{1,0:T(8,128)(2,1)S(1)}, bf16[1280,384]{1,0:T(8,128)(2,1)S(1)}, u32[]{:S(2)}, u32[]{:S(2)}) %collective-permute-start.48) | collective-permute-done | bytes 983072 | tf_op jit(solution)/shard_map/ppermute | solution.py:1201
  570.3 4.4 block_grad.23
  574.7 4.4 block_grad.22
  579.1 7.8 %collective-permute-done.50 = bf16[1280,384]{1,0:T(8,128)(2,1)S(1)} collective-permute-done((bf16[1280,384]{1,0:T(8,128)(2,1)S(1)}, bf16[1280,384]{1,0:T(8,128)(2,1)S(1)}, u32[]{:S(2)}, u32[]{:S(2)}) %collective-permute-start.50) | collective-permute-done | bytes 983072 | tf_op jit(solution)/shard_map/ppermute | solution.py:1201
  590.4 4.4 block_grad.25
  594.8 4.4 block_grad.24
  599.2 9.6 %collective-permute-done.52 = bf16[1280,384]{1,0:T(8,128)(2,1)S(1)} collective-permute-done((bf16[1280,384]{1,0:T(8,128)(2,1)S(1)}, bf16[1280,384]{1,0:T(8,128)(2,1)S(1)}, u32[]{:S(2)}, u32[]{:S(2)}) %collective-permute-start.52) | collective-permute-done | bytes 983072 | tf_op jit(solution)/shard_map/ppermute | solution.py:1201
  611.9 4.4 block_grad.27
  616.3 4.4 block_grad.26
  620.7 8.3 %collective-permute-done.54 = bf16[1280,384]{1,0:T(8,128)(2,1)S(1)} collective-permute-done((bf16[1280,384]{1,0:T(8,128)(2,1)S(1)}, bf16[1280,384]{1,0:T(8,128)(2,1)S(1)}, u32[]{:S(2)}, u32[]{:S(2)}) %collective-permute-start.54) | collective-permute-done | bytes 983072 | tf_op jit(solution)/shard_map/ppermute | solution.py:1201
  632.1 4.4 block_grad.29
  636.5 4.4 block_grad.28
  640.9 8.1 %collective-permute-done.56 = bf16[1280,384]{1,0:T(8,128)(2,1)S(1)} collective-permute-done((bf16[1280,384]{1,0:T(8,128)(2,1)S(1)}, bf16[1280,384]{1,0:T(8,128)(2,1)S(1)}, u32[]{:S(2)}, u32[]{:S(2)}) %collective-permute-start.56) | collective-permute-done | bytes 983072 | tf_op jit(solution)/shard_map/ppermute | solution.py:1201
  657.0 4.4 block_grad.30
  661.3 8.1 %collective-permute-done.58 = bf16[1280,384]{1,0:T(8,128)(2,1)S(1)} collective-permute-done((bf16[1280,384]{1,0:T(8,128)(2,1)S(1)}, bf16[1280,384]{1,0:T(8,128)(2,1)S(1)}, u32[]{:S(2)}, u32[]{:S(2)}) %collective-permute-start.58) | collective-permute-done | bytes 983072 | tf_op jit(solution)/shard_map/ppermute | solution.py:1201
  670.8 9.4 %collective-permute-start.60 = (bf16[256,1536]{1,0:T(8,128)(2,1)}, bf16[256,1536]{1,0:T(8,128)(2,1)}, u32[]{:S(2)}, u32[]{:S(2)}) collective-permute-start(bf16[256,1536]{1,0:T(8,128)(2,1)} %pick.3), channel_id=1, source_target_pairs={{0,0},{4,1},{1,4},{5,5},{8,8},{12,9},{9,12},{13,13},{16,16},{20,17... | collective-permute-start | bytes 2359304 | tf_op jit(solution)/shard_map/ppermute | solution.py:1066
  683.1 10.2 %collective-permute-done.60 = bf16[256,1536]{1,0:T(8,128)(2,1)} collective-permute-done((bf16[256,1536]{1,0:T(8,128)(2,1)}, bf16[256,1536]{1,0:T(8,128)(2,1)}, u32[]{:S(2)}, u32[]{:S(2)}) %collective-permute-start.60) | collective-permute-done | bytes 786464 | tf_op jit(solution)/shard_map/ppermute | solution.py:1066
  693.2 7.0 collective-permute-done.61
  703.7 17.5 %collective-permute-start.64 = (bf16[2,1280,384]{2,1,0:T(8,128)(2,1)S(1)}, bf16[2,1280,384]{2,1,0:T(8,128)(2,1)S(1)}, u32[]{:S(2)}, u32[]{:S(2)}) collective-permute-start(bf16[2,1280,384]{2,1,0:T(8,128)(2,1)S(1)} %pad_maximum_fusion.1), channel_id=1, source_target_pairs={{0,4},{4,0},{1,5},{5,1},{2,6},{6,2},{3,7},{7,3},{8,12},{12,8},{9,1... | collective-permute-start | bytes 5898248 | tf_op jit(solution)/shard_map/ppermute | solution.py:991
  722.6 5.8 collective-permute-start.63
  732.0 6.7 join_grads.1
  (322 shorter events, 187.4 us)
Async XLA Ops:
  5.7 49.1 %collective-permute-start = (bf16[2560,384]{1,0:T(8,128)(2,1)S(1)}, bf16[2560,384]{1,0:T(8,128)(2,1)}, u32[]{:S(2)}, u32[]{:S(2)}) collective-permute-start(bf16[2560,384]{1,0:T(8,128)(2,1)S(1)} %get-tuple-element.250.own), channel_id=1, source_target_pairs={{0,1},{1,0},{2,3},{3,2},{8,9},{9,8},{10,11},{11,10},{4,5},{5,4},{6... | collective-permute-start | bytes 5898248 | tf_op jit(solution)/shard_map/ppermute | solution.py:834
  7.8 46.9 %collective-permute-start.1 = (bf16[2560,384]{1,0:T(8,128)(2,1)S(1)}, bf16[2560,384]{1,0:T(8,128)(2,1)}, u32[]{:S(2)}, u32[]{:S(2)}) collective-permute-start(bf16[2560,384]{1,0:T(8,128)(2,1)S(1)} %get-tuple-element.250.own), channel_id=1, source_target_pairs={{1,2},{2,1},{9,10},{10,9},{5,6},{6,5},{13,14},{14,13},{17,18},{18,... | collective-permute-start | bytes 5898248 | tf_op jit(solution)/shard_map/ppermute | solution.py:834
  10.5 41.7 %collective-permute-start.2 = (bf16[5348]{0:T(1024)(128)(2,1)S(1)}, bf16[5348]{0:T(1024)(128)(2,1)S(1)}, u32[]{:S(2)}, u32[]{:S(2)}) collective-permute-start(bf16[5348]{0:T(1024)(128)(2,1)S(1)} %concatenate.29), channel_id=1, source_target_pairs={{0,1},{1,2},{2,3},{3,0},{4,5},{5,6},{6,7},{7,4},{8,9},{9,10},{10,1... | collective-permute-start | bytes 32096 | tf_op jit(solution)/shard_map/ppermute | solution.py:997
  13.0 41.7 %collective-permute-start.3 = (bf16[5348]{0:T(1024)(128)(2,1)S(1)}, bf16[5348]{0:T(1024)(128)(2,1)S(1)}, u32[]{:S(2)}, u32[]{:S(2)}) collective-permute-start(bf16[5348]{0:T(1024)(128)(2,1)S(1)} %concatenate.29), channel_id=1, source_target_pairs={{0,2},{1,3},{2,0},{3,1},{4,6},{5,7},{6,4},{7,5},{8,10},{9,11},{10,... | collective-permute-start | bytes 32096 | tf_op jit(solution)/shard_map/ppermute | solution.py:997
  13.0 41.7 %collective-permute-start.4 = (bf16[5348]{0:T(1024)(128)(2,1)S(1)}, bf16[5348]{0:T(1024)(128)(2,1)S(1)}, u32[]{:S(2)}, u32[]{:S(2)}) collective-permute-start(bf16[5348]{0:T(1024)(128)(2,1)S(1)} %concatenate.29), channel_id=1, source_target_pairs={{0,3},{1,0},{2,1},{3,2},{4,7},{5,4},{6,5},{7,6},{8,11},{9,8},{10,9... | collective-permute-start | bytes 32096 | tf_op jit(solution)/shard_map/ppermute | solution.py:997
  54.8 44.6 %collective-permute-start.5 = (bf16[2560,384]{1,0:T(8,128)(2,1)}, bf16[2560,384]{1,0:T(8,128)(2,1)}, u32[]{:S(2)}, u32[]{:S(2)}) collective-permute-start(bf16[2560,384]{1,0:T(8,128)(2,1)} %collective-permute-done.1.refs_2_), channel_id=1, source_target_pairs={{1,0},{2,3},{9,8},{10,11},{5,4},{6,7},{13,12},{14,15},{17,16},{18,... | collective-permute-start | bytes 5898248 | tf_op jit(solution)/shard_map/ppermute | solution.py:834
  56.1 43.3 %collective-permute-start.6 = (bf16[2560,384]{1,0:T(8,128)(2,1)}, bf16[2560,384]{1,0:T(8,128)(2,1)S(1)}, u32[]{:S(2)}, u32[]{:S(2)}) collective-permute-start(bf16[2560,384]{1,0:T(8,128)(2,1)} %collective-permute-done.refs_0_), channel_id=1, source_target_pairs={{1,2},{2,1},{9,10},{10,9},{5,6},{6,5},{13,14},{14,13},{17,18},{18,... | collective-permute-start | bytes 5898248 | tf_op jit(solution)/shard_map/ppermute | solution.py:834
  56.8 42.7 %collective-permute-start.7 = (bf16[2560,384]{1,0:T(8,128)(2,1)}, bf16[2560,384]{1,0:T(8,128)(2,1)S(1)}, u32[]{:S(2)}, u32[]{:S(2)}) collective-permute-start(bf16[2560,384]{1,0:T(8,128)(2,1)} %collective-permute-done.refs_0_), channel_id=1, source_target_pairs={{0,8},{1,9},{2,10},{3,11},{8,0},{9,1},{10,2},{11,3},{4,12},{5,13},... | collective-permute-start | bytes 5898248 | tf_op jit(solution)/shard_map/ppermute | solution.py:838
  58.1 63.8 %collective-permute-start.15 = (bf16[2560,384]{1,0:T(8,128)(2,1)}, bf16[2560,384]{1,0:T(8,128)(2,1)S(1)}, u32[]{:S(2)}, u32[]{:S(2)}) collective-permute-start(bf16[2560,384]{1,0:T(8,128)(2,1)} %collective-permute-done.1.refs_2_), channel_id=1, source_target_pairs={{1,9},{2,10},{9,1},{10,2},{5,13},{6,14},{13,5},{14,6},{17,25},{18,... | collective-permute-start | bytes 5898248 | tf_op jit(solution)/shard_map/ppermute | solution.py:838
  101.9 58.9 %collective-permute-start.13 = (bf16[2560,384]{1,0:T(8,128)(2,1)S(1)}, bf16[2560,384]{1,0:T(8,128)(2,1)S(1)}, u32[]{:S(2)}, u32[]{:S(2)}) collective-permute-start(bf16[2560,384]{1,0:T(8,128)(2,1)S(1)} %collective-permute-done.6.refs_6_), channel_id=1, source_target_pairs={{1,0},{2,3},{9,8},{10,11},{5,4},{6,7},{13,12},{14,15},{17,16},{18,... | collective-permute-start | bytes 5898248 | tf_op jit(solution)/shard_map/ppermute | solution.py:834
  103.1 65.0 %collective-permute-start.14 = (bf16[2560,384]{1,0:T(8,128)(2,1)}, bf16[2560,384]{1,0:T(8,128)(2,1)}, u32[]{:S(2)}, u32[]{:S(2)}) collective-permute-start(bf16[2560,384]{1,0:T(8,128)(2,1)} %collective-permute-done.5.refs_4_), channel_id=1, source_target_pairs={{0,8},{3,11},{8,0},{11,3},{4,12},{7,15},{12,4},{15,7},{16,24},{19,... | collective-permute-start | bytes 5898248 | tf_op jit(solution)/shard_map/ppermute | solution.py:838
  108.9 61.2 %collective-permute-start.10 = (bf16[256,1536]{1,0:T(8,128)(2,1)}, bf16[256,1536]{1,0:T(8,128)(2,1)}, u32[]{:S(2)}, u32[]{:S(2)}) collective-permute-start(bf16[256,1536]{1,0:T(8,128)(2,1)} %get-tuple-element.495), channel_id=1, source_target_pairs={{2,0},{3,4},{6,1},{7,5},{10,8},{11,12},{14,9},{15,13},{18,16},{19,... | collective-permute-start | bytes 2359304 | tf_op jit(solution)/shard_map/ppermute | solution.py:1057
  110.2 65.7 %collective-permute-start.8 = (bf16[256,1536]{1,0:T(8,128)(2,1)}, bf16[256,1536]{1,0:T(8,128)(2,1)}, u32[]{:S(2)}, u32[]{:S(2)}) collective-permute-start(bf16[256,1536]{1,0:T(8,128)(2,1)} %get-tuple-element.495), channel_id=1, source_target_pairs={{0,0},{1,4},{4,1},{5,5},{8,8},{9,12},{12,9},{13,13},{16,16},{17,20... | collective-permute-start | bytes 2359304 | tf_op jit(solution)/shard_map/ppermute | solution.py:1057
  123.3 50.5 %collective-permute-start.11 = (bf16[256,1536]{1,0:T(8,128)(2,1)}, bf16[256,1536]{1,0:T(8,128)(2,1)}, u32[]{:S(2)}, u32[]{:S(2)}) collective-permute-start(bf16[256,1536]{1,0:T(8,128)(2,1)} %get-tuple-element.494), channel_id=1, source_target_pairs={{2,2},{3,6},{6,3},{7,7},{10,10},{11,14},{14,11},{15,15},{18,18},{1... | collective-permute-start | bytes 2359304 | tf_op jit(solution)/shard_map/ppermute | solution.py:1057
  162.0 13.9 %collective-permute-start.9 = (bf16[256,1536]{1,0:T(8,128)(2,1)}, bf16[256,1536]{1,0:T(8,128)(2,1)}, u32[]{:S(2)}, u32[]{:S(2)}) collective-permute-start(bf16[256,1536]{1,0:T(8,128)(2,1)} %get-tuple-element.494), channel_id=1, source_target_pairs={{0,2},{1,6},{4,3},{5,7},{8,10},{9,14},{12,11},{13,15},{16,18},{17,... | collective-permute-start | bytes 2359304 | tf_op jit(solution)/shard_map/ppermute | solution.py:1057
  168.2 16.7 %collective-permute-start.16 = (bf16[2560,384]{1,0:T(8,128)(2,1)S(1)}, bf16[2560,384]{1,0:T(8,128)(2,1)}, u32[]{:S(2)}, u32[]{:S(2)}) collective-permute-start(bf16[2560,384]{1,0:T(8,128)(2,1)S(1)} %copy-done.9), channel_id=1, source_target_pairs={{1,9},{2,10},{9,1},{10,2},{5,13},{6,14},{13,5},{14,6},{17,25},{18,... | collective-permute-start | bytes 5898248 | tf_op jit(solution)/shard_map/ppermute | solution.py:838
  170.1 39.2 %collective-permute-start.17 = (bf16[2560,384]{1,0:T(8,128)(2,1)}, bf16[2560,384]{1,0:T(8,128)(2,1)}, u32[]{:S(2)}, u32[]{:S(2)}) collective-permute-start(bf16[2560,384]{1,0:T(8,128)(2,1)} %copy-done.14), channel_id=1, source_target_pairs={{0,8},{3,11},{8,0},{11,3},{4,12},{7,15},{12,4},{15,7},{16,24},{19,... | collective-permute-start | bytes 5898248 | tf_op jit(solution)/shard_map/ppermute | solution.py:838
  230.1 10.3 %collective-permute-start.18 = (bf16[256,1664]{1,0:T(8,128)(2,1)S(1)}, bf16[256,1664]{1,0:T(8,128)(2,1)S(1)}, u32[]{:S(2)}, u32[]{:S(2)}) collective-permute-start(bf16[256,1664]{1,0:T(8,128)(2,1)S(1)} %get-tuple-element.271.own_ref), channel_id=1, source_target_pairs={{0,4},{4,0},{1,5},{5,1},{2,6},{6,2},{3,7},{7,3},{8,12},{12,8},{9,1... | collective-permute-start | bytes 2555912 | tf_op jit(solution)/shard_map/ppermute | solution.py:991
  242.5 13.5 %collective-permute-start.19 = (bf16[128,1536]{1,0:T(8,128)(2,1)S(1)}, bf16[128,1536]{1,0:T(8,128)(2,1)S(1)}, u32[]{:S(2)}, u32[]{:S(2)}) collective-permute-start(bf16[128,1536]{1,0:T(8,128)(2,1)S(1)} %get-tuple-element.283), channel_id=1, source_target_pairs={{0,16},{1,17},{2,18},{3,19},{4,20},{5,21},{6,22},{7,23},{8,24},{9,... | collective-permute-start | bytes 1179656 | tf_op jit(solution)/shard_map/ppermute | solution.py:1100
  260.7 13.7 %collective-permute-start.23 = (bf16[128,1536]{1,0:T(8,128)(2,1)S(1)}, bf16[128,1536]{1,0:T(8,128)(2,1)S(1)}, u32[]{:S(2)}, u32[]{:S(2)}) collective-permute-start(bf16[128,1536]{1,0:T(8,128)(2,1)S(1)} %get-tuple-element.304), channel_id=1, source_target_pairs={{0,16},{1,17},{2,18},{3,19},{4,20},{5,21},{6,22},{7,23},{8,24},{9,... | collective-permute-start | bytes 1179656 | tf_op jit(solution)/shard_map/ppermute | solution.py:1100
  274.9 17.1 %collective-permute-start.24 = (bf16[128,1536]{1,0:T(8,128)(2,1)S(1)}, bf16[128,1536]{1,0:T(8,128)(2,1)S(1)}, u32[]{:S(2)}, u32[]{:S(2)}) collective-permute-start(bf16[128,1536]{1,0:T(8,128)(2,1)S(1)} %collective-permute-done.23.refs_0_), channel_id=1, source_target_pairs={{0,4},{4,0},{1,5},{5,1},{2,6},{6,2},{3,7},{7,3},{8,12},{12,8},{9,1... | collective-permute-start | bytes 1179656 | tf_op jit(solution)/shard_map/ppermute | solution.py:991
  290.7 13.5 %collective-permute-start.26 = (bf16[128,1536]{1,0:T(8,128)(2,1)S(1)}, bf16[128,1536]{1,0:T(8,128)(2,1)S(1)}, u32[]{:S(2)}, u32[]{:S(2)}) collective-permute-start(bf16[128,1536]{1,0:T(8,128)(2,1)S(1)} %get-tuple-element.323), channel_id=1, source_target_pairs={{0,16},{1,17},{2,18},{3,19},{4,20},{5,21},{6,22},{7,23},{8,24},{9,... | collective-permute-start | bytes 1179656 | tf_op jit(solution)/shard_map/ppermute | solution.py:1100
  330.5 54.4 %collective-permute-start.34 = (bf16[256,1536]{1,0:T(8,128)(2,1)S(1)}, bf16[256,1536]{1,0:T(8,128)(2,1)S(1)}, u32[]{:S(2)}, u32[]{:S(2)}) collective-permute-start(bf16[256,1536]{1,0:T(8,128)(2,1)S(1)} %get-tuple-element.385), channel_id=1, source_target_pairs={{16,0},{17,1},{18,2},{19,3},{20,4},{21,5},{22,6},{23,7},{24,8},{25... | collective-permute-start | bytes 2359304 | tf_op jit(solution)/shard_map/ppermute | solution.py:1141
  388.2 20.6 %collective-permute-start.36 = (bf16[256,1536]{1,0:T(8,128)(2,1)S(1)}, bf16[256,1536]{1,0:T(8,128)(2,1)S(1)}, u32[]{:S(2)}, u32[]{:S(2)}) collective-permute-start(bf16[256,1536]{1,0:T(8,128)(2,1)S(1)} %get-tuple-element.401), channel_id=1, source_target_pairs={{16,0},{17,1},{18,2},{19,3},{20,4},{21,5},{22,6},{23,7},{24,8},{25... | collective-permute-start | bytes 2359304 | tf_op jit(solution)/shard_map/ppermute | solution.py:1141
  414.5 20.6 %collective-permute-start.38 = (bf16[256,1536]{1,0:T(8,128)(2,1)S(1)}, bf16[256,1536]{1,0:T(8,128)(2,1)S(1)}, u32[]{:S(2)}, u32[]{:S(2)}) collective-permute-start(bf16[256,1536]{1,0:T(8,128)(2,1)S(1)} %get-tuple-element.417), channel_id=1, source_target_pairs={{16,0},{17,1},{18,2},{19,3},{20,4},{21,5},{22,6},{23,7},{24,8},{25... | collective-permute-start | bytes 2359304 | tf_op jit(solution)/shard_map/ppermute | solution.py:1141
  444.3 31.3 %collective-permute-start.41 = (bf16[256,1536]{1,0:T(8,128)(2,1)}, bf16[256,1536]{1,0:T(8,128)(2,1)S(1)}, u32[]{:S(2)}, u32[]{:S(2)}) collective-permute-start(bf16[256,1536]{1,0:T(8,128)(2,1)} %pick.2), channel_id=1, source_target_pairs={{0,2},{4,3},{1,6},{5,7},{8,10},{12,11},{9,14},{13,15},{16,18},{20,... | collective-permute-start | bytes 2359304 | tf_op jit(solution)/shard_map/ppermute | solution.py:1066
  445.6 29.9 %collective-permute-start.42 = (bf16[256,1536]{1,0:T(8,128)(2,1)}, bf16[256,1536]{1,0:T(8,128)(2,1)}, u32[]{:S(2)}, u32[]{:S(2)}) collective-permute-start(bf16[256,1536]{1,0:T(8,128)(2,1)} %pick.2), channel_id=1, source_target_pairs={{2,2},{6,3},{3,6},{7,7},{10,10},{14,11},{11,14},{15,15},{18,18},{2... | collective-permute-start | bytes 2359304 | tf_op jit(solution)/shard_map/ppermute | solution.py:1066
  447.2 28.4 %collective-permute-start.40 = (bf16[256,1536]{1,0:T(8,128)(2,1)}, bf16[256,1536]{1,0:T(8,128)(2,1)}, u32[]{:S(2)}, u32[]{:S(2)}) collective-permute-start(bf16[256,1536]{1,0:T(8,128)(2,1)} %get-tuple-element.433), channel_id=1, source_target_pairs={{16,0},{17,1},{18,2},{19,3},{20,4},{21,5},{22,6},{23,7},{24,8},{25... | collective-permute-start | bytes 2359304 | tf_op jit(solution)/shard_map/ppermute | solution.py:1141
  498.1 11.1 %collective-permute-start.43 = (bf16[256,1536]{1,0:T(8,128)(2,1)}, bf16[256,1536]{1,0:T(8,128)(2,1)S(1)}, u32[]{:S(2)}, u32[]{:S(2)}) collective-permute-start(bf16[256,1536]{1,0:T(8,128)(2,1)} %get-tuple-element.445.own_ref), channel_id=1, source_target_pairs={{0,4},{4,0},{1,5},{5,1},{2,6},{6,2},{3,7},{7,3},{8,12},{12,8},{9,1... | collective-permute-start | bytes 2359304 | tf_op jit(solution)/shard_map/ppermute | solution.py:991
  517.7 23.0 %collective-permute-start.46 = (bf16[1280,384]{1,0:T(8,128)(2,1)S(1)}, bf16[1280,384]{1,0:T(8,128)(2,1)S(1)}, u32[]{:S(2)}, u32[]{:S(2)}) collective-permute-start(bf16[1280,384]{1,0:T(8,128)(2,1)S(1)} %convert_element_type.184), channel_id=1, source_target_pairs={{0,8},{1,0},{2,1},{3,2},{11,3},{10,11},{9,10},{8,9},{4,12},{5,4},{... | collective-permute-start | bytes 2949128 | tf_op jit(solution)/shard_map/ppermute | solution.py:1201
  519.0 22.6 %collective-permute-start.45 = (bf16[1280,384]{1,0:T(8,128)(2,1)S(1)}, bf16[1280,384]{1,0:T(8,128)(2,1)S(1)}, u32[]{:S(2)}, u32[]{:S(2)}) collective-permute-start(bf16[1280,384]{1,0:T(8,128)(2,1)S(1)} %copy-done.26), channel_id=1, source_target_pairs={{0,1},{1,2},{2,3},{3,11},{11,10},{10,9},{9,8},{8,0},{4,5},{5,6},{6... | collective-permute-start | bytes 2949128 | tf_op jit(solution)/shard_map/ppermute | solution.py:1201
  541.9 21.8 %collective-permute-start.48 = (bf16[1280,384]{1,0:T(8,128)(2,1)S(1)}, bf16[1280,384]{1,0:T(8,128)(2,1)S(1)}, u32[]{:S(2)}, u32[]{:S(2)}) collective-permute-start(bf16[1280,384]{1,0:T(8,128)(2,1)S(1)} %add_convert_fusion.12), channel_id=1, source_target_pairs={{0,8},{1,0},{2,1},{3,2},{11,3},{10,11},{9,10},{8,9},{4,12},{5,4},{... | collective-permute-start | bytes 2949128 | tf_op jit(solution)/shard_map/ppermute | solution.py:1201
  543.7 22.0 %collective-permute-start.47 = (bf16[1280,384]{1,0:T(8,128)(2,1)S(1)}, bf16[1280,384]{1,0:T(8,128)(2,1)S(1)}, u32[]{:S(2)}, u32[]{:S(2)}) collective-permute-start(bf16[1280,384]{1,0:T(8,128)(2,1)S(1)} %add_convert_fusion.13), channel_id=1, source_target_pairs={{0,1},{1,2},{2,3},{3,11},{11,10},{10,9},{9,8},{8,0},{4,5},{5,6},{6... | collective-permute-start | bytes 2949128 | tf_op jit(solution)/shard_map/ppermute | solution.py:1201
  565.9 21.0 %collective-permute-start.50 = (bf16[1280,384]{1,0:T(8,128)(2,1)S(1)}, bf16[1280,384]{1,0:T(8,128)(2,1)S(1)}, u32[]{:S(2)}, u32[]{:S(2)}) collective-permute-start(bf16[1280,384]{1,0:T(8,128)(2,1)S(1)} %add_convert_fusion.10), channel_id=1, source_target_pairs={{0,8},{1,0},{2,1},{3,2},{11,3},{10,11},{9,10},{8,9},{4,12},{5,4},{... | collective-permute-start | bytes 2949128 | tf_op jit(solution)/shard_map/ppermute | solution.py:1201
  567.4 21.2 %collective-permute-start.49 = (bf16[1280,384]{1,0:T(8,128)(2,1)S(1)}, bf16[1280,384]{1,0:T(8,128)(2,1)S(1)}, u32[]{:S(2)}, u32[]{:S(2)}) collective-permute-start(bf16[1280,384]{1,0:T(8,128)(2,1)S(1)} %add_convert_fusion.11), channel_id=1, source_target_pairs={{0,1},{1,2},{2,3},{3,11},{11,10},{10,9},{9,8},{8,0},{4,5},{5,6},{6... | collective-permute-start | bytes 2949128 | tf_op jit(solution)/shard_map/ppermute | solution.py:1201
  588.8 20.0 %collective-permute-start.52 = (bf16[1280,384]{1,0:T(8,128)(2,1)S(1)}, bf16[1280,384]{1,0:T(8,128)(2,1)S(1)}, u32[]{:S(2)}, u32[]{:S(2)}) collective-permute-start(bf16[1280,384]{1,0:T(8,128)(2,1)S(1)} %add_convert_fusion.8), channel_id=1, source_target_pairs={{0,8},{1,0},{2,1},{3,2},{11,3},{10,11},{9,10},{8,9},{4,12},{5,4},{... | collective-permute-start | bytes 2949128 | tf_op jit(solution)/shard_map/ppermute | solution.py:1201
  590.4 19.8 %collective-permute-start.51 = (bf16[1280,384]{1,0:T(8,128)(2,1)S(1)}, bf16[1280,384]{1,0:T(8,128)(2,1)S(1)}, u32[]{:S(2)}, u32[]{:S(2)}) collective-permute-start(bf16[1280,384]{1,0:T(8,128)(2,1)S(1)} %add_convert_fusion.9), channel_id=1, source_target_pairs={{0,1},{1,2},{2,3},{3,11},{11,10},{10,9},{9,8},{8,0},{4,5},{5,6},{6... | collective-permute-start | bytes 2949128 | tf_op jit(solution)/shard_map/ppermute | solution.py:1201
  610.4 18.6 %collective-permute-start.54 = (bf16[1280,384]{1,0:T(8,128)(2,1)S(1)}, bf16[1280,384]{1,0:T(8,128)(2,1)S(1)}, u32[]{:S(2)}, u32[]{:S(2)}) collective-permute-start(bf16[1280,384]{1,0:T(8,128)(2,1)S(1)} %add_convert_fusion.6), channel_id=1, source_target_pairs={{0,8},{1,0},{2,1},{3,2},{11,3},{10,11},{9,10},{8,9},{4,12},{5,4},{... | collective-permute-start | bytes 2949128 | tf_op jit(solution)/shard_map/ppermute | solution.py:1201
  611.2 19.3 %collective-permute-start.53 = (bf16[1280,384]{1,0:T(8,128)(2,1)S(1)}, bf16[1280,384]{1,0:T(8,128)(2,1)S(1)}, u32[]{:S(2)}, u32[]{:S(2)}) collective-permute-start(bf16[1280,384]{1,0:T(8,128)(2,1)S(1)} %add_convert_fusion.7), channel_id=1, source_target_pairs={{0,1},{1,2},{2,3},{3,11},{11,10},{10,9},{9,8},{8,0},{4,5},{5,6},{6... | collective-permute-start | bytes 2949128 | tf_op jit(solution)/shard_map/ppermute | solution.py:1201
  630.6 18.4 %collective-permute-start.56 = (bf16[1280,384]{1,0:T(8,128)(2,1)S(1)}, bf16[1280,384]{1,0:T(8,128)(2,1)S(1)}, u32[]{:S(2)}, u32[]{:S(2)}) collective-permute-start(bf16[1280,384]{1,0:T(8,128)(2,1)S(1)} %add_convert_fusion.4), channel_id=1, source_target_pairs={{0,8},{1,0},{2,1},{3,2},{11,3},{10,11},{9,10},{8,9},{4,12},{5,4},{... | collective-permute-start | bytes 2949128 | tf_op jit(solution)/shard_map/ppermute | solution.py:1201
  631.2 19.5 %collective-permute-start.55 = (bf16[1280,384]{1,0:T(8,128)(2,1)S(1)}, bf16[1280,384]{1,0:T(8,128)(2,1)S(1)}, u32[]{:S(2)}, u32[]{:S(2)}) collective-permute-start(bf16[1280,384]{1,0:T(8,128)(2,1)S(1)} %add_convert_fusion.5), channel_id=1, source_target_pairs={{0,1},{1,2},{2,3},{3,11},{11,10},{10,9},{9,8},{8,0},{4,5},{5,6},{6... | collective-permute-start | bytes 2949128 | tf_op jit(solution)/shard_map/ppermute | solution.py:1201
  650.8 18.6 %collective-permute-start.58 = (bf16[1280,384]{1,0:T(8,128)(2,1)S(1)}, bf16[1280,384]{1,0:T(8,128)(2,1)S(1)}, u32[]{:S(2)}, u32[]{:S(2)}) collective-permute-start(bf16[1280,384]{1,0:T(8,128)(2,1)S(1)} %add_convert_fusion.2), channel_id=1, source_target_pairs={{0,8},{1,0},{2,1},{3,2},{11,3},{10,11},{9,10},{8,9},{4,12},{5,4},{... | collective-permute-start | bytes 2949128 | tf_op jit(solution)/shard_map/ppermute | solution.py:1201
  651.4 19.2 %collective-permute-start.57 = (bf16[1280,384]{1,0:T(8,128)(2,1)S(1)}, bf16[1280,384]{1,0:T(8,128)(2,1)S(1)}, u32[]{:S(2)}, u32[]{:S(2)}) collective-permute-start(bf16[1280,384]{1,0:T(8,128)(2,1)S(1)} %add_convert_fusion.3), channel_id=1, source_target_pairs={{0,1},{1,2},{2,3},{3,11},{11,10},{10,9},{9,8},{8,0},{4,5},{5,6},{6... | collective-permute-start | bytes 2949128 | tf_op jit(solution)/shard_map/ppermute | solution.py:1201
  670.8 22.4 %collective-permute-start.60 = (bf16[256,1536]{1,0:T(8,128)(2,1)}, bf16[256,1536]{1,0:T(8,128)(2,1)}, u32[]{:S(2)}, u32[]{:S(2)}) collective-permute-start(bf16[256,1536]{1,0:T(8,128)(2,1)} %pick.3), channel_id=1, source_target_pairs={{0,0},{4,1},{1,4},{5,5},{8,8},{12,9},{9,12},{13,13},{16,16},{20,17... | collective-permute-start | bytes 2359304 | tf_op jit(solution)/shard_map/ppermute | solution.py:1066
  680.2 20.0 %collective-permute-start.61 = (bf16[256,1536]{1,0:T(8,128)(2,1)}, bf16[256,1536]{1,0:T(8,128)(2,1)}, u32[]{:S(2)}, u32[]{:S(2)}) collective-permute-start(bf16[256,1536]{1,0:T(8,128)(2,1)} %pick.3), channel_id=1, source_target_pairs={{2,0},{6,1},{3,4},{7,5},{10,8},{14,9},{11,12},{15,13},{18,16},{22,... | collective-permute-start | bytes 2359304 | tf_op jit(solution)/shard_map/ppermute | solution.py:1066
  681.5 22.0 %collective-permute-start.59 = (bf16[1280,384]{1,0:T(8,128)(2,1)S(1)}, bf16[1280,384]{1,0:T(8,128)(2,1)S(1)}, u32[]{:S(2)}, u32[]{:S(2)}) collective-permute-start(bf16[1280,384]{1,0:T(8,128)(2,1)S(1)} %add_convert_fusion.refs_3_), channel_id=1, source_target_pairs={{0,8},{8,0},{1,9},{9,1},{2,10},{10,2},{3,11},{11,3},{4,12},{12,4},... | collective-permute-start | bytes 2949128 | tf_op jit(solution)/shard_map/ppermute | solution.py:991
  682.7 38.6 %collective-permute-start.62 = (bf16[1280,384]{1,0:T(8,128)(2,1)S(1)}, bf16[1280,384]{1,0:T(8,128)(2,1)}, u32[]{:S(2)}, u32[]{:S(2)}) collective-permute-start(bf16[1280,384]{1,0:T(8,128)(2,1)S(1)} %add_convert_fusion.1.refs_0_), channel_id=1, source_target_pairs={{0,8},{8,0},{1,9},{9,1},{2,10},{10,2},{3,11},{11,3},{4,12},{12,4},... | collective-permute-start | bytes 2949128 | tf_op jit(solution)/shard_map/ppermute | solution.py:991
  703.7 24.8 %collective-permute-start.64 = (bf16[2,1280,384]{2,1,0:T(8,128)(2,1)S(1)}, bf16[2,1280,384]{2,1,0:T(8,128)(2,1)S(1)}, u32[]{:S(2)}, u32[]{:S(2)}) collective-permute-start(bf16[2,1280,384]{2,1,0:T(8,128)(2,1)S(1)} %pad_maximum_fusion.1), channel_id=1, source_target_pairs={{0,4},{4,0},{1,5},{5,1},{2,6},{6,2},{3,7},{7,3},{8,12},{12,8},{9,1... | collective-permute-start | bytes 5898248 | tf_op jit(solution)/shard_map/ppermute | solution.py:991
  (52 other events, 871.1 us)

commit v2 on v1

--- a/solution.py
+++ b/solution.py
@@ -202,16 +202,18 @@
         cols = at_head(ld, pair)
         u = jnp.where(left, *at_head(dt, pair)) * x
         ld_p = jnp.where(left, *cols)
-        top = jnp.zeros((half, LANES), F32)
-        bottom = top
+        tops, bottoms, sides = [], [], []
         for i in range(2):
             u_i = jnp.where(left if i == 0 else jnp.logical_not(left), u, 0.0).astype(BF16)
             d00, d10, d11 = decay_blocks(cols[i], ldt[pl.ds(2 * pair + i, 1), :], False)
             m00 = (g_ref[:half, :half] * d00).astype(BF16)
             m10 = (g_ref[half:, :half] * d10).astype(BF16)
             m11 = (g_ref[half:, half:] * d11).astype(BF16)
-            top = top + dot(m00, u_i[:half])
-            bottom = bottom + dot(jnp.concatenate([m10, m11], axis=1), u_i)
+            tops.append(m00)
+            bottoms += [m10, m11]
+            sides.append(u_i)
+        top = dot(jnp.concatenate(tops, axis=1), jnp.concatenate([v[:half] for v in sides], axis=0))
+        bottom = dot(jnp.concatenate(bottoms, axis=1), jnp.concatenate(sides, axis=0))
         eld = jnp.exp(ld_p)
         st = sti[:, sl]
         y = jnp.concatenate([top, bottom], axis=0) + eld * dot(c, st.astype(BF16))
@@ -238,7 +240,7 @@
 
 
 def backward_kernel(row, sc, *refs):
-    acc_ref, acc_out = refs[15], refs[-20]
+    acc_ref, acc_out = refs[17], refs[-21]
 
     @pl.when(sc[row, VALID] == 1)
     def _():
@@ -253,8 +255,10 @@
     row,
     sc,
     arrived_hbm,
+    other_hbm,
     cot_hbm,
     h_hbm,
+    n_hbm,
     pr_hbm,
     mx_hbm,
     st_hbm,
@@ -272,14 +276,28 @@
     wout,
     *rest,
 ):
-    gn, g_ref, h_out, dst_out, dc_out, val_out, acc_out, gp_hbm, gs_hbm = rest[-26:-17]
-    pr, mx, st_ref, tl, y_ref, ri, gp, gs = rest[-17:-9]
+    gn, g_ref, h_out, dst_out, dc_out, val_out, acc_out, gp_hbm, gs_hbm = rest[-27:-18]
+    pr, mx, st_ref, tl, y_ref, ri, gp, gs, normed = rest[-18:-9]
     xw, dw, ldt, gw, gt, dgt, dci, dbi, sem = rest[-9:]
     t = g_ref.shape[0]
     half = t // 2
     slot = sc[row, SLOT]
     last = sc[row, FIRST] == 1
-    g_copy = fetch_one_of(sc[row, LEADING] == 1, arrived_hbm, cot_hbm, g_ref, sem.at[0])
+    leading = sc[row, LEADING] == 1
+    core = sc[row, CORE]
+    mine = g_ref.at[pl.ds(aligned(core * half), half)]
+    theirs = g_ref.at[pl.ds(aligned((1 - core) * half), half)]
+
+    @pl.when(leading)
+    def _():
+        copies = fetch(arrived_hbm, mine, sem.at[0]), fetch(other_hbm, theirs, sem.at[10])
+        for copy in copies:
+            copy.wait()
+
+    @pl.when(jnp.logical_not(leading))
+    def _():
+        fetch(cot_hbm, g_ref, sem.at[0]).wait()
+
     y_copy = fetch(y_hbm.at[slot], y_ref, sem.at[1])
     ri_copy = fetch(ri_hbm.at[slot], ri, sem.at[2])
     pr_copy = fetch(pr_hbm.at[slot], pr, sem.at[3])
@@ -287,13 +305,13 @@
     mx_copy = fetch(mx_hbm.at[slot], mx, sem.at[5])
     st_copy = fetch(st_hbm.at[slot], st_ref, sem.at[6])
     h_copy = fetch(h_hbm.at[slot], h_out, sem.at[8])
+    n_copy = fetch(n_hbm.at[slot], normed, sem.at[9])
 
     acc_out[...] = acc_ref[...]
     dw[t : t + 8, :] = jnp.where(last, 0.0, dc_ref[...])
     dgt[...] = jnp.zeros_like(dgt)
     dci[...] = jnp.zeros_like(dci)
     dbi[...] = jnp.zeros_like(dbi)
-    g_copy.wait()
     for at in range(0, OWN, 512):
         gw[:, at : at + 512] = dot_nt(g_ref[...], wout[at : at + 512, :])
     y_copy.wait()
@@ -437,8 +455,12 @@
     gp[:, DT_AT + LANES :] = jnp.zeros((t, LANES), BF16)
     gp_store = fetch(gp, gp_hbm.at[sc[row, WRITE]], sem.at[0])
     dc_out[...] = dw[0:8, :]
+    n_copy.wait()
     for at in range(0, D, 512):
-        gn[:, at : at + 512] = dot(gp[...], win[:, at : at + 512]).astype(BF16)
+        cols = slice(at, at + 512)
+        values = dot(gp[...], win[:, cols])
+        gn[:, cols] = values.astype(BF16)
+        add(9, cols, jnp.sum(values * normed[:, cols].astype(F32), axis=0, keepdims=True))
     gp_store.wait()
     gs_store.wait()
     h_copy.wait()
@@ -469,10 +491,9 @@
             copy.wait()
 
 
-def backward_join_kernel(row, sc, own_ref, other_ref, h_ref, g_ref, ng_ref, dng_ref, *rest):
-    out, dng_out, e_hbm, sem = rest[-4:]
-    half = out.shape[0] // 2
-    dng_out[...] = dng_ref[...]
+def backward_join_kernel(row, sc, own_ref, other_ref, h_ref, g_ref, ng_ref, *rest):
+    out, e_hbm, low_v, sem = rest[-4:]
+    half = out.shape[0]
 
     @pl.when(sc[row, VALID] == 1)
     def _():
@@ -484,10 +505,10 @@
             r = lax.rsqrt(jnp.mean(h * h, axis=1, keepdims=True) + EPSILON)
             t = gn * ng_ref[...]
             m = jnp.mean(h * t, axis=1, keepdims=True)
-            out[rows] = (g_ref[rows].astype(F32) + r * (t - h * (r * r * m))).astype(BF16)
+            low_v[rows] = (g_ref[rows].astype(F32) + r * (t - h * (r * r * m))).astype(BF16)
             target = e_hbm.at[sc[row, EDGE], pl.ds(k * half, half)]
-            copies.append(fetch(out.at[pl.ds(k * half, half)], target, sem.at[k]))
-            dng_out[...] += jnp.sum(gn * h * r, axis=0, keepdims=True)
+            copies.append(fetch(low_v.at[pl.ds(k * half, half)], target, sem.at[k]))
+        out[...] = low_v[pl.ds(aligned(sc[row, CORE] * half), half), :]
         for copy in copies:
             copy.wait()
 
@@ -574,14 +595,14 @@
 
 
 def backward_call(table, row, slots, cot, arrived, saved, params, carry, held):
-    t = arrived.shape[0]
+    t = cot.shape[0]
     held = held or (None, None)
     _, convp, headp, chanp, win, wout = params
     wide, projected = ((t, D), BF16), ((t, OWN_PROJ), BF16)
     outs, held = chunk_call(
         functools.partial(backward_kernel, row),
         table,
-        (arrived, cot),
+        (*arrived, cot),
         saved,
         (convp, headp, chanp, *carry, win, wout),
         [wide] * 3 + [(v.shape, v.dtype) for v in carry],
@@ -595,6 +616,7 @@
             pltpu.VMEM((t, LANES), F32),
             pltpu.VMEM(*projected),
             pltpu.VMEM(*wide),
+            pltpu.VMEM(*wide),
             pltpu.VMEM((t + 8, OWN_CONV), F32),
             pltpu.VMEM((t + 8, OWN_CONV), F32),
             pltpu.VMEM((LANES, t), F32),
@@ -603,7 +625,7 @@
             pltpu.VMEM((t, t), F32),
             pltpu.VMEM((t, STATE), F32),
             pltpu.VMEM((t, STATE), F32),
-            pltpu.SemaphoreType.DMA((9,)),
+            pltpu.SemaphoreType.DMA((11,)),
         ],
         BACKWARD_VMEM,
         "backward_chunk",
@@ -630,22 +652,21 @@
     return outs[0], held
 
 
-def backward_join(table, row, own, other, h, g, gain, dng, edge_held):
-    slots = edge_held.shape[0]
-    wide = (h.shape, BF16)
+def backward_join(table, row, own, other, h, g, gain, edge_held):
+    slots, t, _ = edge_held.shape
     outs, held = chunk_call(
         functools.partial(backward_join_kernel, row),
         table,
         (),
         (),
-        (own, other, h, g, gain, dng),
-        [wide, ((1, D), F32)],
-        [(edge_held, (slots,) + h.shape, BF16)],
-        [pltpu.SemaphoreType.DMA((2,))],
+        (own, other, h, g, gain),
+        [((t // 2, D), BF16)],
+        [(edge_held, (slots, t, D), BF16)],
+        [pltpu.VMEM((t, D), BF16), pltpu.SemaphoreType.DMA((2,))],
         JOIN_VMEM,
         "backward_join",
     )
-    return outs[0], outs[1], held[0]
+    return outs[0], held[0]
 
 
 def pick(table, stack, first):
@@ -848,8 +869,8 @@
     outer_3 = along(inner_3, outward)
     outer_2_y = across(outer_2, (0, 3))
     inner_2_y = across(inner_2, (1, 2))
-    ready = near_y
     outer_3, outer_2_y, inner_2_y = lax.optimization_barrier((outer_3, outer_2_y, inner_2_y))
+    ready = inner_2_y
     outer_3_y = across(outer_3, (0, 3))
     inner_3_y = across(inner_3, (1, 2))
     return [
@@ -878,14 +899,15 @@
     at = 0
     for ref in refs[:2]:
         width = ref.shape[2]
-        out[at : at + width, :] = sum(dot_tn(ref[k], normed_ref[k]) for k in range(chunks))
+        value = sum(dot_tn(ref[k], normed_ref[k]) for k in range(chunks))
+        out[at : at + width, :] = value.astype(BF16)
         at += width
-    out[at:, :] = sum(dot_tn(q_ref[k], gs_ref[k]) for k in range(chunks))
+    out[at:, :] = sum(dot_tn(q_ref[k], gs_ref[k]) for k in range(chunks)).astype(BF16)
     if len(refs) > 3:
 
         @pl.when(sc[row, 0] == 1)
         def _():
-            out[HALF : HALF + SMALL_ROWS, :] = refs[2][0]
+            out[HALF : HALF + SMALL_ROWS, :] = refs[2][0].astype(BF16)
 
 
 def block_grad(table, row, group, normed_held, grads_held, q_held, gs_held, small):
@@ -918,7 +940,7 @@
             in_specs=in_specs,
             out_specs=pl.BlockSpec((GROUP_ROWS, BLOCK), lambda i, s: (0, 0)),
         ),
-        out_shape=jax.ShapeDtypeStruct((GROUP_ROWS, BLOCK), F32),
+        out_shape=jax.ShapeDtypeStruct((GROUP_ROWS, BLOCK), BF16),
         compiler_params=pltpu.CompilerParams(vmem_limit_bytes=24 << 20),
         cost_estimate=LITTLE,
         name="block_grad",
@@ -937,9 +959,9 @@
     core, side = sc[0], sc[1]
 
     def block(i, c, y, rows):
-        own, across, other = refs[3 * i : 3 * i + 3]
+        own, across, other, far = refs[4 * i : 4 * i + 4]
         here = jnp.where(side == y, own[rows], across[rows])
-        there = jnp.where(side == y, other[0, rows], other[1, rows])
+        there = jnp.where(side == y, other[rows], far[rows])
         return jnp.where(core == c, here, there).astype(F32)
 
     copies = []
@@ -1067,7 +1089,9 @@
             for m in range(2)
         ]
 
-    here, *got = lax.optimization_barrier((here, *bring(0), *bring(2)))
+    last = (*pairs[3], *pairs[4])
+    here, *got = lax.optimization_barrier((here, *bring(0), *bring(2), *last))
+    got, pairs[3:] = got[:4], [tuple(got[4:6]), tuple(got[6:8])]
     pieces = shared(got[:2]) + shared(got[2:])
     win, wout = place_weights(here, own, rest, pairs)
     params = (gain, convp, headp, chanp, win, wout)
@@ -1088,6 +1112,14 @@
     table = [scalars(moment, LAG, False) for moment in range(moments)]
     table += [scalars(moment, LAG, True) for moment in range(moments)]
     table = jnp.stack(sum(table, [])).reshape(len(table), -1)
+    size = 2 * chunks
+    position = jnp.where(side == 0, place, size - 1 - place).astype(jnp.int32)
+    owners = []
+    for direction in (1, -1):
+        for hop in range(size):
+            owners += ring_place((position - direction * (1 + hop)) % size, chunks)
+    owners = jnp.stack(owners).reshape(2 * size, 2).astype(jnp.int32)
+    table, owners = lax.optimization_barrier((table, owners))
 
     state, tail = jnp.zeros((STATE, OWN), F32), jnp.zeros((8, OWN_CONV), F32)
     blank = jnp.zeros((t, D), BF16)
@@ -1116,7 +1148,7 @@
         result, joined = forward_join(table, moment, chunks + 1, partial, other, h, joined)
     h_held, normed_held, pr_held, mx_held, q_held, st_held, tl_held = held
     y_held, ri_held, edge_held = joined
-    saved = (h_held, pr_held, mx_held, st_held, tl_held, y_held, ri_held)
+    saved = (h_held, normed_held, pr_held, mx_held, st_held, tl_held, y_held, ri_held)
 
     def tokens(buffer):
         return buffer[:chunks].reshape(chunks * t, buffer.shape[-1])
@@ -1127,33 +1159,27 @@
         jnp.zeros((8, OWN), F32),
         jnp.zeros((16, OWN_CONV), F32),
     )
-    dng = jnp.zeros((1, D), F32)
-    grads_held, edges_late = None, None
-    incoming = {}
+    grads_held = None
+    moved, incoming = {}, {}
     for moment in range(moments):
         if moment > 0:
             *carry, acc = carry
             acc, result = lax.optimization_barrier((acc, result))
-            if moment == moments - 1:
-                acc, edges_late = lax.optimization_barrier((acc, edges_late))
             carry = (*carry, acc)
             if moment - 1 < chunks:
-                incoming[moment - 1] = lax.ppermute(result, "section", [(1, 0)])
-        arrived = incoming.get(moment - LAG, blank)
+                moved[moment - 1] = lax.ppermute(result, "section", [(1, 0)])
+        arrived = incoming.get(moment - LAG, (blank[: t // 2],) * 2)
         cot = pieces[max(chunks - 1 - moment, 0)]
         (partial, g, h), carry, grads_held = backward_call(
             table, moments + moment, chunks + 1, cot, arrived, saved, params, carry, grads_held
         )
-        if moment - 1 in incoming:
-            partial, incoming[moment - 1] = lax.optimization_barrier(
-                (partial, incoming[moment - 1])
-            )
+        if moment - 1 in moved:
+            partial, got = lax.optimization_barrier((partial, moved[moment - 1]))
+            incoming[moment - 1] = (got, swap(got, "core"))
         other = swap(partial, "core")
-        result, dng, edge_held = backward_join(
-            table, moments + moment, partial, other, h, g, gain, dng, edge_held
+        result, edge_held = backward_join(
+            table, moments + moment, partial, other, h, g, gain, edge_held
         )
-        if moment == LAG + 1:
-            edges_late = give(pick(table, edge_held, 2), 2)
 
     def both(own, other, index):
         return jnp.where(index == 0, jnp.stack([own, other]), jnp.stack([other, own]))
@@ -1168,7 +1194,7 @@
     taps = jnp.moveaxis(taps.reshape(KERNEL + 1, chunks, -1), 1, 0)
     skip = acc[5, :OWN].reshape(OWN_HEADS, HEAD_DIM).sum(axis=1)
     vectors = [
-        jnp.where(core == 0, dng[0], 0.0),
+        acc[9, :D] / gain[0],
         taps,
         placed(acc[7, :OWN_HEADS]),
         placed(acc[8, :OWN_HEADS]),
@@ -1180,14 +1206,7 @@
     small = jnp.pad(small, ((0, 0), (0, SMALL_ROWS * BLOCK - small.shape[1])))
     small = small.reshape(chunks, SMALL_ROWS, BLOCK)
 
-    size = 2 * chunks
     onward, back = ring_route(chunks, 1), ring_route(chunks, -1)
-    position = jnp.where(side == 0, place, size - 1 - place).astype(jnp.int32)
-    owners = []
-    for direction in (1, -1):
-        for hop in range(size):
-            owners += ring_place((position - direction * (1 + hop)) % size, chunks)
-    owners = jnp.stack(owners).reshape(2 * size, 2).astype(jnp.int32)
     grads_held, gs_held = grads_held
     sums = [None] * len(GROUPS)
     for hop in range(size):
@@ -1198,21 +1217,22 @@
             block = block_grad(owners, row, i, normed_held, grads_held, q_held, gs_held, small)
             if hop > 0:
                 path = onward if direction == 1 else back
-                block = block + lax.ppermute(sums[i], ("y", "fsdp"), path).astype(F32)
-            sums[i] = block.astype(BF16)
+                came = lax.ppermute(sums[i], ("y", "fsdp"), path).astype(F32)
+                block = (block.astype(F32) + came).astype(BF16)
+            sums[i] = block
         if hop == 3:
-            owners, edge_last = lax.optimization_barrier((owners, pick(table, edge_held, 0)))
-    *sums, edge_last = lax.optimization_barrier((*sums, edge_last))
-
-    edges = jnp.where(place < 2, jnp.stack(give(edge_last, 0)), jnp.stack(edges_late))
+            finished = pick(table, edge_held, 0), pick(table, edge_held, 2)
+            owners, *finished = lax.optimization_barrier((owners, *finished))
+    *sums, early, late = lax.optimization_barrier((*sums, *finished))
+
+    edges = jnp.where(place < 2, jnp.stack(give(early, 0)), jnp.stack(give(late, 2)))
     edges = edges[None, :, None]
     parts = []
-    for i, own in enumerate(sums):
+    for own in sums:
         across = swap(own, "y")
-        if i == 1:
-            across, edges = lax.optimization_barrier((across, edges))
-        parts.append((own, across, swap(jnp.stack([own, across]), "core")))
+        parts.append((own, across, swap(own, "core"), swap(across, "core")))
     here = jnp.stack([core, side]).astype(jnp.int32)
+    here, edges = lax.optimization_barrier((here, edges))
     in_grad, out_grad, summed = join_grads(here, parts)
     in_grad = in_grad.T
     summed = summed.reshape(-1)

time: 750 us -> 717 us (0.956)
  waiting for transfers between devices: 311 us -> 275 us
    ppermute x5, waiting for transfers between devices: 24.7 us -> 6.29 us  [across(): return lax.ppermute(value, ('y', 'fsdp'), route)]
    ppermute x18, waiting for transfers between devices: 123 us -> 108 us  [the longest x14 68.5 us: relay_shards(): came = lax.ppermute(sums[i], ('y', 'fsdp'), path).astype(F32)]
    ppermute x22 -> x28, starting transfers between devices: 46.4 us -> 35.9 us  [swap(): return lax.ppermute(value, axis, [(0, 1), (1, 0)])]
    unnamed x75 -> x73, local copies, waits for them, and re-layouts: 21.1 us -> 22.5 us
    ppermute x22 -> x28, waiting for transfers between devices: 20.8 us -> 20 us  [swap(): return lax.ppermute(value, axis, [(0, 1), (1, 0)])]
  transfers between devices with their start and end apart: 65 -> 71, of which waited for: 39 -> 37; matrix products, arithmetic and copies ran while one was open for 3% -> 2% of each run, Pallas kernels for 26% -> 29%
where the time goes in v2:
time: 717 us; the launch traced here: 708 us
  waiting for transfers between devices  275 us (38%)
  Pallas kernels  266 us (37%)
  starting transfers between devices  119 us (17%)
  local copies, waits for them, and re-layouts  36.8 us (5%)
  other arithmetic  9.6 us (1%)
    pallas_call x26, Pallas kernels, chunk_call(): pl.pallas_call(kernel, in_specs=in_specs, out_specs=out_specs, out_shape=...  180 us
    ppermute x5, waiting for transfers between devices, along(): return lax.ppermute(value, ('y', 'fsdp'), route)  72.8 us
    pallas_call x16, Pallas kernels, block_grad(): pl.pallas_call(functools.partial(block_grad_kernel, row), grid_spec=pltpu...  70.5 us
    ppermute x14, waiting for transfers between devices, relay_shards(): came = lax.ppermute(sums[i], ('y', 'fsdp'), path).astype(F32)  68.5 us
    ppermute x4, waiting for transfers between devices, relay_shards(): moved[moment - 1] = lax.ppermute(result, 'section', [(1, 0)])  39.9 us
    ppermute x3, waiting for transfers between devices, sent_along(): return [lax.ppermute(value, axis, path) for path in routes]  39.6 us
    ppermute x28, starting transfers between devices, swap(): return lax.ppermute(value, axis, [(0, 1), (1, 0)])  35.9 us
    unnamed x73, local copies, waits for them, and re-layouts  22.5 us
  transfers between devices with their start and end apart: 71, of which 37 were waited for; matrix products, arithmetic and copies ran while one was open for 2% of the time, Pallas kernels for 29%

profile of v2, /device:TPU:1, one launch (start us, length us, event | category | flops | bytes accessed | tf_op | source)
XLA Modules:
  0.0 708.4 jit_solution(5182066953925161793)
XLA Ops:
  15.1 37.0 %collective-permute-done.2 = bf16[5348]{0:T(1024)(128)(2,1)S(1)} collective-permute-done((bf16[5348]{0:T(1024)(128)(2,1)S(1)}, bf16[5348]{0:T(1024)(128)(2,1)S(1)}, u32[]{:S(2)}, u32[]{:S(2)}) %collective-permute-start.2) | collective-permute-done | bytes 10728 | tf_op jit(solution)/shard_map/ppermute | solution.py:1019
  58.9 40.3 %collective-permute-done.5.refs_4_ = bf16[2560,384]{1,0:T(8,128)(2,1)S(1)} collective-permute-done((bf16[2560,384]{1,0:T(8,128)(2,1)}, bf16[2560,384]{1,0:T(8,128)(2,1)S(1)}, u32[]{:S(2)}, u32[]{:S(2)}) %collective-permute-start.5) | collective-permute-done | bytes 1966112 | tf_op jit(solution)/shard_map/ppermute | solution.py:855
  109.8 32.5 %collective-permute-done.8.refs_8_ = bf16[2560,384]{1,0:T(8,128)(2,1)} collective-permute-done((bf16[2560,384]{1,0:T(8,128)(2,1)S(1)}, bf16[2560,384]{1,0:T(8,128)(2,1)}, u32[]{:S(2)}, u32[]{:S(2)}) %collective-permute-start.8) | collective-permute-done | bytes 1966112 | tf_op jit(solution)/shard_map/ppermute | solution.py:855
  152.4 9.0 %collective-permute-start.11 = (bf16[256,1536]{1,0:T(8,128)(2,1)}, bf16[256,1536]{1,0:T(8,128)(2,1)}, u32[]{:S(2)}, u32[]{:S(2)}) collective-permute-start(bf16[256,1536]{1,0:T(8,128)(2,1)} %get-tuple-element.495), channel_id=1, source_target_pairs={{0,0},{1,4},{4,1},{5,5},{8,8},{9,12},{12,9},{13,13},{16,16},{17,20... | collective-permute-start | bytes 2359304 | tf_op jit(solution)/shard_map/ppermute | solution.py:1079
  162.7 7.0 collective-permute-start.12
  179.8 6.1 collective-permute-done.12
  190.0 11.0 %collective-permute-start.17 = (bf16[256,1536]{1,0:T(8,128)(2,1)S(1)}, bf16[256,1536]{1,0:T(8,128)(2,1)S(1)}, u32[]{:S(2)}, u32[]{:S(2)}) collective-permute-start(bf16[256,1536]{1,0:T(8,128)(2,1)S(1)} %broadcast_select_fusion.1), channel_id=1, source_target_pairs={{0,4},{4,0},{1,5},{5,1},{2,6},{6,2},{3,7},{7,3},{8,12},{12,8},{9,1... | collective-permute-start | bytes 2359304 | tf_op jit(solution)/shard_map/ppermute | solution.py:1013
  210.4 4.3 place_weights.1
  214.9 12.7 %forward_chunk.6 = (bf16[256,1664]{1,0:T(8,128)(2,1)S(1)}, bf16[256,1536]{1,0:T(8,128)(2,1)S(1)}, f32[128,1536]{1,0:T(8,128)S(1)}, f32[8,1792]{1,0:T(8,128)S(1)}...) custom-call(s32[12,7]{1,0:T(8,128)S(1)} %reshape.193.sc, ...), custom_call_target="tpu_custom_call" | custom-call | flops 1048576 | bytes 65536 | tf_op jit(solution)/shard_map/forward_chunk/pallas_call | solution.py:548
  233.6 12.1 %forward_chunk.7 = (bf16[256,1664]{1,0:T(8,128)(2,1)S(1)}, bf16[256,1536]{1,0:T(8,128)(2,1)S(1)}, f32[128,1536]{1,0:T(8,128)S(1)}, f32[8,1792]{1,0:T(8,128)S(1)}...) custom-call(s32[12,7]{1,0:T(8,128)S(1)} %reshape.193.sc, ...), custom_call_target="tpu_custom_call", output_to_operand_aliasing={{4}: (12, {}), {5}: (13, {}), {6}: (14, {}), {7}: (15, {}),... | custom-call | flops 1048576 | bytes 65536 | tf_op jit(solution)/shard_map/forward_chunk/pallas_call | solution.py:548
  251.9 23.9 %forward_chunk.8 = (bf16[256,1664]{1,0:T(8,128)(2,1)S(1)}, bf16[256,1536]{1,0:T(8,128)(2,1)S(1)}, f32[128,1536]{1,0:T(8,128)S(1)}, f32[8,1792]{1,0:T(8,128)S(1)}...) custom-call(s32[12,7]{1,0:T(8,128)S(1)} %reshape.193.sc, ...), custom_call_target="tpu_custom_call", output_to_operand_aliasing={{4}: (12, {}), {5}: (13, {}), {6}: (14, {}), {7}: (15, {}),... | custom-call | flops 1048576 | bytes 65536 | tf_op jit(solution)/shard_map/forward_chunk/pallas_call | solution.py:548
  281.9 12.2 %forward_chunk.9 = (bf16[256,1664]{1,0:T(8,128)(2,1)S(1)}, bf16[256,1536]{1,0:T(8,128)(2,1)S(1)}, f32[128,1536]{1,0:T(8,128)S(1)}, f32[8,1792]{1,0:T(8,128)S(1)}...) custom-call(s32[12,7]{1,0:T(8,128)S(1)} %reshape.193.sc, ...), custom_call_target="tpu_custom_call", output_to_operand_aliasing={{4}: (12, {}), {5}: (13, {}), {6}: (14, {}), {7}: (15, {}),... | custom-call | flops 1048576 | bytes 65536 | tf_op jit(solution)/shard_map/forward_chunk/pallas_call | solution.py:548
  301.0 7.8 %collective-permute-done.29.refs_0_ = bf16[128,1536]{1,0:T(8,128)(2,1)S(1)} collective-permute-done((bf16[128,1536]{1,0:T(8,128)(2,1)S(1)}, bf16[128,1536]{1,0:T(8,128)(2,1)S(1)}, u32[]{:S(2)}, u32[]{:S(2)}) %collective-permute-start.29) | collective-permute-done | bytes 393248 | tf_op jit(solution)/shard_map/ppermute | solution.py:1132
  321.8 7.6 %backward_chunk.7 = (bf16[256,1536]{1,0:T(8,128)(2,1)S(1)}, bf16[256,1536]{1,0:T(8,128)(2,1)S(1)}, bf16[256,1536]{1,0:T(8,128)(2,1)S(1)}, f32[128,1536]{1,0:T(8,...) custom-call(s32[12,7]{1,0:T(8,128)S(1)} %reshape.193.sc, ...), custom_call_target="tpu_custom_call", output_to_operand_aliasing={{7}: (21, {}), {8}: (22, {})} | custom-call | flops 1048576 | bytes 65536 | tf_op jit(solution)/shard_map/backward_chunk/pallas_call | solution.py:548
  329.4 38.3 %collective-permute-done.34.refs_0_ = bf16[128,1536]{1,0:T(8,128)(2,1)S(1)} collective-permute-done((bf16[128,1536]{1,0:T(8,128)(2,1)S(1)}, bf16[128,1536]{1,0:T(8,128)(2,1)S(1)}, u32[]{:S(2)}, u32[]{:S(2)}) %collective-permute-start.34) | collective-permute-done | bytes 393248 | tf_op jit(solution)/shard_map/ppermute | solution.py:1170
  372.3 19.4 %backward_chunk.8 = (bf16[256,1536]{1,0:T(8,128)(2,1)S(1)}, bf16[256,1536]{1,0:T(8,128)(2,1)S(1)}, bf16[256,1536]{1,0:T(8,128)(2,1)S(1)}, f32[128,1536]{1,0:T(8,...) custom-call(s32[12,7]{1,0:T(8,128)S(1)} %reshape.193.sc, ...), custom_call_target="tpu_custom_call", output_to_operand_aliasing={{7}: (21, {}), {8}: (22, {})} | custom-call | flops 1048576 | bytes 65536 | tf_op jit(solution)/shard_map/backward_chunk/pallas_call | solution.py:548
  399.5 19.9 %backward_chunk.9 = (bf16[256,1536]{1,0:T(8,128)(2,1)S(1)}, bf16[256,1536]{1,0:T(8,128)(2,1)S(1)}, bf16[256,1536]{1,0:T(8,128)(2,1)S(1)}, f32[128,1536]{1,0:T(8,...) custom-call(s32[12,7]{1,0:T(8,128)S(1)} %reshape.193.sc, ...), custom_call_target="tpu_custom_call", output_to_operand_aliasing={{7}: (21, {}), {8}: (22, {})} | custom-call | flops 1048576 | bytes 65536 | tf_op jit(solution)/shard_map/backward_chunk/pallas_call | solution.py:548
  425.4 19.4 %backward_chunk.10 = (bf16[256,1536]{1,0:T(8,128)(2,1)S(1)}, bf16[256,1536]{1,0:T(8,128)(2,1)S(1)}, bf16[256,1536]{1,0:T(8,128)(2,1)S(1)}, f32[128,1536]{1,0:T(8...) custom-call(s32[12,7]{1,0:T(8,128)S(1)} %reshape.193.sc, ...), custom_call_target="tpu_custom_call", output_to_operand_aliasing={{7}: (21, {}), {8}: (22, {})} | custom-call | flops 1048576 | bytes 65536 | tf_op jit(solution)/shard_map/backward_chunk/pallas_call | solution.py:548
  447.5 20.9 %backward_chunk.11 = (bf16[256,1536]{1,0:T(8,128)(2,1)S(1)}, bf16[256,1536]{1,0:T(8,128)(2,1)S(1)}, bf16[256,1536]{1,0:T(8,128)(2,1)S(1)}, f32[128,1536]{1,0:T(8...) custom-call(s32[12,7]{1,0:T(8,128)S(1)} %reshape.193.sc, ...), custom_call_target="tpu_custom_call", output_to_operand_aliasing={{7}: (21, {}), {8}: (22, {})} | custom-call | flops 1048576 | bytes 65536 | tf_op jit(solution)/shard_map/backward_chunk/pallas_call | solution.py:548
  473.2 4.4 block_grad.16
  477.6 4.4 block_grad.17
  483.5 4.4 block_grad.19
  487.9 4.4 block_grad.18
  492.2 12.7 %collective-permute-done.46 = bf16[1280,384]{1,0:T(8,128)(2,1)S(1)} collective-permute-done((bf16[1280,384]{1,0:T(8,128)(2,1)S(1)}, bf16[1280,384]{1,0:T(8,128)(2,1)S(1)}, u32[]{:S(2)}, u32[]{:S(2)}) %collective-permute-start.46) | collective-permute-done | bytes 983072 | tf_op jit(solution)/shard_map/ppermute | solution.py:1220
  506.1 5.9 collective-permute-start.48
  512.0 4.4 block_grad.21
  516.4 4.4 block_grad.20
  520.8 11.8 %collective-permute-done.48 = bf16[1280,384]{1,0:T(8,128)(2,1)S(1)} collective-permute-done((bf16[1280,384]{1,0:T(8,128)(2,1)S(1)}, bf16[1280,384]{1,0:T(8,128)(2,1)S(1)}, u32[]{:S(2)}, u32[]{:S(2)}) %collective-permute-start.48) | collective-permute-done | bytes 983072 | tf_op jit(solution)/shard_map/ppermute | solution.py:1220
  550.6 4.4 block_grad.23
  555.0 4.4 block_grad.22
  562.5 4.4 block_grad.25
  566.9 4.5 block_grad.24
  571.4 11.6 %collective-permute-done.54 = bf16[1280,384]{1,0:T(8,128)(2,1)S(1)} collective-permute-done((bf16[1280,384]{1,0:T(8,128)(2,1)S(1)}, bf16[1280,384]{1,0:T(8,128)(2,1)S(1)}, u32[]{:S(2)}, u32[]{:S(2)}) %collective-permute-start.54) | collective-permute-done | bytes 983072 | tf_op jit(solution)/shard_map/ppermute | solution.py:1220
  585.5 4.4 block_grad.27
  589.8 4.4 block_grad.26
  594.3 10.4 %collective-permute-done.56 = bf16[1280,384]{1,0:T(8,128)(2,1)S(1)} collective-permute-done((bf16[1280,384]{1,0:T(8,128)(2,1)S(1)}, bf16[1280,384]{1,0:T(8,128)(2,1)S(1)}, u32[]{:S(2)}, u32[]{:S(2)}) %collective-permute-start.56) | collective-permute-done | bytes 983072 | tf_op jit(solution)/shard_map/ppermute | solution.py:1220
  606.8 4.6 block_grad.29
  611.4 4.4 block_grad.28
  615.8 9.0 %collective-permute-done.58 = bf16[1280,384]{1,0:T(8,128)(2,1)S(1)} collective-permute-done((bf16[1280,384]{1,0:T(8,128)(2,1)S(1)}, bf16[1280,384]{1,0:T(8,128)(2,1)S(1)}, u32[]{:S(2)}, u32[]{:S(2)}) %collective-permute-start.58) | collective-permute-done | bytes 983072 | tf_op jit(solution)/shard_map/ppermute | solution.py:1220
  627.3 4.4 block_grad.31
  631.7 4.4 block_grad.30
  636.1 8.8 %collective-permute-done.60 = bf16[1280,384]{1,0:T(8,128)(2,1)S(1)} collective-permute-done((bf16[1280,384]{1,0:T(8,128)(2,1)S(1)}, bf16[1280,384]{1,0:T(8,128)(2,1)S(1)}, u32[]{:S(2)}, u32[]{:S(2)}) %collective-permute-start.60) | collective-permute-done | bytes 983072 | tf_op jit(solution)/shard_map/ppermute | solution.py:1220
  647.5 8.6 %collective-permute-start.61 = (bf16[256,1536]{1,0:T(8,128)(2,1)S(1)}, bf16[256,1536]{1,0:T(8,128)(2,1)}, u32[]{:S(2)}, u32[]{:S(2)}) collective-permute-start(bf16[256,1536]{1,0:T(8,128)(2,1)S(1)} %pick.2), channel_id=1, source_target_pairs={{0,0},{4,1},{1,4},{5,5},{8,8},{12,9},{9,12},{13,13},{16,16},{20,17... | collective-permute-start | bytes 2359304 | tf_op jit(solution)/shard_map/ppermute | solution.py:1088
  657.4 6.2 collective-permute-start.63
  663.6 13.7 %collective-permute-done.61 = bf16[256,1536]{1,0:T(8,128)(2,1)} collective-permute-done((bf16[256,1536]{1,0:T(8,128)(2,1)S(1)}, bf16[256,1536]{1,0:T(8,128)(2,1)}, u32[]{:S(2)}, u32[]{:S(2)}) %collective-permute-start.61) | collective-permute-done | bytes 786464 | tf_op jit(solution)/shard_map/ppermute | solution.py:1088
  678.9 10.0 %collective-permute-start.66 = (bf16[1280,384]{1,0:T(8,128)(2,1)S(1)}, bf16[1280,384]{1,0:T(8,128)(2,1)}, u32[]{:S(2)}, u32[]{:S(2)}) collective-permute-start(bf16[1280,384]{1,0:T(8,128)(2,1)S(1)} %add_convert_fusion.1.refs_0_), channel_id=1, source_target_pairs={{0,4},{4,0},{1,5},{5,1},{2,6},{6,2},{3,7},{7,3},{8,12},{12,8},{9,1... | collective-permute-start | bytes 2949128 | tf_op jit(solution)/shard_map/ppermute | solution.py:1013
  689.7 3.8 collective-permute-start.70
  696.9 7.9 %join_grads.1 = (f32[6448,384]{1,0:T(8,128)}, f32[768,1536]{1,0:T(8,128)}, f32[16,384]{1,0:T(8,128)S(1)}) custom-call(s32[2]{0:T(128)S(1)} %pad_add_fusion.sc, bf16[1280,384]{1,0:T(8,128)(2,1)S(1)} %add_convert_fusion.1.refs_0_, bf16[1280,384]{1,0:T(8,128)(2,1)S(1)} %collective-permute-done.65.refs_1_, bf16[1280,384]{1,0:T(8,128)(2,1)} %collective-permute-done.66.refs_2_, ...), custom_call_target="tpu_custom_call" | custom-call | flops 1048576 | bytes 65536 | tf_op jit(solution)/shard_map/join_grads/pallas_call | solution.py:1000
  (326 shorter events, 173.1 us)
Async XLA Ops:
  5.7 49.0 %collective-permute-start = (bf16[2560,384]{1,0:T(8,128)(2,1)S(1)}, bf16[2560,384]{1,0:T(8,128)(2,1)}, u32[]{:S(2)}, u32[]{:S(2)}) collective-permute-start(bf16[2560,384]{1,0:T(8,128)(2,1)S(1)} %get-tuple-element.251.own), channel_id=1, source_target_pairs={{0,1},{1,0},{2,3},{3,2},{8,9},{9,8},{10,11},{11,10},{4,5},{5,4},{6... | collective-permute-start | bytes 5898248 | tf_op jit(solution)/shard_map/ppermute | solution.py:855
  7.8 46.9 %collective-permute-start.1 = (bf16[2560,384]{1,0:T(8,128)(2,1)S(1)}, bf16[2560,384]{1,0:T(8,128)(2,1)}, u32[]{:S(2)}, u32[]{:S(2)}) collective-permute-start(bf16[2560,384]{1,0:T(8,128)(2,1)S(1)} %get-tuple-element.251.own), channel_id=1, source_target_pairs={{1,2},{2,1},{9,10},{10,9},{5,6},{6,5},{13,14},{14,13},{17,18},{18,... | collective-permute-start | bytes 5898248 | tf_op jit(solution)/shard_map/ppermute | solution.py:855
  10.5 41.7 %collective-permute-start.2 = (bf16[5348]{0:T(1024)(128)(2,1)S(1)}, bf16[5348]{0:T(1024)(128)(2,1)S(1)}, u32[]{:S(2)}, u32[]{:S(2)}) collective-permute-start(bf16[5348]{0:T(1024)(128)(2,1)S(1)} %concatenate.29), channel_id=1, source_target_pairs={{0,1},{1,2},{2,3},{3,0},{4,5},{5,6},{6,7},{7,4},{8,9},{9,10},{10,1... | collective-permute-start | bytes 32096 | tf_op jit(solution)/shard_map/ppermute | solution.py:1019
  13.0 41.7 %collective-permute-start.3 = (bf16[5348]{0:T(1024)(128)(2,1)S(1)}, bf16[5348]{0:T(1024)(128)(2,1)S(1)}, u32[]{:S(2)}, u32[]{:S(2)}) collective-permute-start(bf16[5348]{0:T(1024)(128)(2,1)S(1)} %concatenate.29), channel_id=1, source_target_pairs={{0,2},{1,3},{2,0},{3,1},{4,6},{5,7},{6,4},{7,5},{8,10},{9,11},{10,... | collective-permute-start | bytes 32096 | tf_op jit(solution)/shard_map/ppermute | solution.py:1019
  13.0 41.7 %collective-permute-start.4 = (bf16[5348]{0:T(1024)(128)(2,1)S(1)}, bf16[5348]{0:T(1024)(128)(2,1)S(1)}, u32[]{:S(2)}, u32[]{:S(2)}) collective-permute-start(bf16[5348]{0:T(1024)(128)(2,1)S(1)} %concatenate.29), channel_id=1, source_target_pairs={{0,3},{1,0},{2,1},{3,2},{4,7},{5,4},{6,5},{7,6},{8,11},{9,8},{10,9... | collective-permute-start | bytes 32096 | tf_op jit(solution)/shard_map/ppermute | solution.py:1019
  54.7 44.4 %collective-permute-start.5 = (bf16[2560,384]{1,0:T(8,128)(2,1)}, bf16[2560,384]{1,0:T(8,128)(2,1)S(1)}, u32[]{:S(2)}, u32[]{:S(2)}) collective-permute-start(bf16[2560,384]{1,0:T(8,128)(2,1)} %collective-permute-done.1.refs_2_), channel_id=1, source_target_pairs={{1,0},{2,3},{9,8},{10,11},{5,4},{6,7},{13,12},{14,15},{17,16},{18,... | collective-permute-start | bytes 5898248 | tf_op jit(solution)/shard_map/ppermute | solution.py:855
  56.0 43.1 %collective-permute-start.6 = (bf16[2560,384]{1,0:T(8,128)(2,1)}, bf16[2560,384]{1,0:T(8,128)(2,1)S(1)}, u32[]{:S(2)}, u32[]{:S(2)}) collective-permute-start(bf16[2560,384]{1,0:T(8,128)(2,1)} %collective-permute-done.refs_0_), channel_id=1, source_target_pairs={{1,2},{2,1},{9,10},{10,9},{5,6},{6,5},{13,14},{14,13},{17,18},{18,... | collective-permute-start | bytes 5898248 | tf_op jit(solution)/shard_map/ppermute | solution.py:855
  56.8 42.6 %collective-permute-start.7 = (bf16[2560,384]{1,0:T(8,128)(2,1)}, bf16[2560,384]{1,0:T(8,128)(2,1)S(1)}, u32[]{:S(2)}, u32[]{:S(2)}) collective-permute-start(bf16[2560,384]{1,0:T(8,128)(2,1)} %collective-permute-done.refs_0_), channel_id=1, source_target_pairs={{0,8},{1,9},{2,10},{3,11},{8,0},{9,1},{10,2},{11,3},{4,12},{5,13},... | collective-permute-start | bytes 5898248 | tf_op jit(solution)/shard_map/ppermute | solution.py:859
  58.1 50.4 %collective-permute-start.10 = (bf16[2560,384]{1,0:T(8,128)(2,1)}, bf16[2560,384]{1,0:T(8,128)(2,1)S(1)}, u32[]{:S(2)}, u32[]{:S(2)}) collective-permute-start(bf16[2560,384]{1,0:T(8,128)(2,1)} %collective-permute-done.1.refs_2_), channel_id=1, source_target_pairs={{1,9},{2,10},{9,1},{10,2},{5,13},{6,14},{13,5},{14,6},{17,25},{18,... | collective-permute-start | bytes 5898248 | tf_op jit(solution)/shard_map/ppermute | solution.py:859
  100.7 41.6 %collective-permute-start.8 = (bf16[2560,384]{1,0:T(8,128)(2,1)S(1)}, bf16[2560,384]{1,0:T(8,128)(2,1)}, u32[]{:S(2)}, u32[]{:S(2)}) collective-permute-start(bf16[2560,384]{1,0:T(8,128)(2,1)S(1)} %collective-permute-done.6.refs_6_), channel_id=1, source_target_pairs={{1,0},{2,3},{9,8},{10,11},{5,4},{6,7},{13,12},{14,15},{17,16},{18,... | collective-permute-start | bytes 5898248 | tf_op jit(solution)/shard_map/ppermute | solution.py:855
  102.0 43.4 %collective-permute-start.9 = (bf16[2560,384]{1,0:T(8,128)(2,1)S(1)}, bf16[2560,384]{1,0:T(8,128)(2,1)S(1)}, u32[]{:S(2)}, u32[]{:S(2)}) collective-permute-start(bf16[2560,384]{1,0:T(8,128)(2,1)S(1)} %collective-permute-done.5.refs_4_), channel_id=1, source_target_pairs={{0,8},{3,11},{8,0},{11,3},{4,12},{7,15},{12,4},{15,7},{16,24},{19,... | collective-permute-start | bytes 5898248 | tf_op jit(solution)/shard_map/ppermute | solution.py:859
  106.5 63.2 %collective-permute-start.15 = (bf16[2560,384]{1,0:T(8,128)(2,1)S(1)}, bf16[2560,384]{1,0:T(8,128)(2,1)S(1)}, u32[]{:S(2)}, u32[]{:S(2)}) collective-permute-start(bf16[2560,384]{1,0:T(8,128)(2,1)S(1)} %collective-permute-done.6.refs_6_), channel_id=1, source_target_pairs={{1,9},{2,10},{9,1},{10,2},{5,13},{6,14},{13,5},{14,6},{17,25},{18,... | collective-permute-start | bytes 5898248 | tf_op jit(solution)/shard_map/ppermute | solution.py:859
  146.7 42.1 %collective-permute-start.16 = (bf16[2560,384]{1,0:T(8,128)(2,1)}, bf16[2560,384]{1,0:T(8,128)(2,1)}, u32[]{:S(2)}, u32[]{:S(2)}) collective-permute-start(bf16[2560,384]{1,0:T(8,128)(2,1)} %collective-permute-done.8.refs_8_), channel_id=1, source_target_pairs={{0,8},{3,11},{8,0},{11,3},{4,12},{7,15},{12,4},{15,7},{16,24},{19,... | collective-permute-start | bytes 5898248 | tf_op jit(solution)/shard_map/ppermute | solution.py:859
  152.4 27.3 %collective-permute-start.11 = (bf16[256,1536]{1,0:T(8,128)(2,1)}, bf16[256,1536]{1,0:T(8,128)(2,1)}, u32[]{:S(2)}, u32[]{:S(2)}) collective-permute-start(bf16[256,1536]{1,0:T(8,128)(2,1)} %get-tuple-element.495), channel_id=1, source_target_pairs={{0,0},{1,4},{4,1},{5,5},{8,8},{9,12},{12,9},{13,13},{16,16},{17,20... | collective-permute-start | bytes 2359304 | tf_op jit(solution)/shard_map/ppermute | solution.py:1079
  161.4 24.4 %collective-permute-start.13 = (bf16[256,1536]{1,0:T(8,128)(2,1)}, bf16[256,1536]{1,0:T(8,128)(2,1)S(1)}, u32[]{:S(2)}, u32[]{:S(2)}) collective-permute-start(bf16[256,1536]{1,0:T(8,128)(2,1)} %get-tuple-element.495), channel_id=1, source_target_pairs={{2,0},{3,4},{6,1},{7,5},{10,8},{11,12},{14,9},{15,13},{18,16},{19,... | collective-permute-start | bytes 2359304 | tf_op jit(solution)/shard_map/ppermute | solution.py:1079
  162.7 23.1 %collective-permute-start.12 = (bf16[256,1536]{1,0:T(8,128)(2,1)}, bf16[256,1536]{1,0:T(8,128)(2,1)}, u32[]{:S(2)}, u32[]{:S(2)}) collective-permute-start(bf16[256,1536]{1,0:T(8,128)(2,1)} %get-tuple-element.494), channel_id=1, source_target_pairs={{0,2},{1,6},{4,3},{5,7},{8,10},{9,14},{12,11},{13,15},{16,18},{17,... | collective-permute-start | bytes 2359304 | tf_op jit(solution)/shard_map/ppermute | solution.py:1079
  171.1 14.8 %collective-permute-start.14 = (bf16[256,1536]{1,0:T(8,128)(2,1)}, bf16[256,1536]{1,0:T(8,128)(2,1)}, u32[]{:S(2)}, u32[]{:S(2)}) collective-permute-start(bf16[256,1536]{1,0:T(8,128)(2,1)} %get-tuple-element.494), channel_id=1, source_target_pairs={{2,2},{3,6},{6,3},{7,7},{10,10},{11,14},{14,11},{15,15},{18,18},{1... | collective-permute-start | bytes 2359304 | tf_op jit(solution)/shard_map/ppermute | solution.py:1079
  190.0 24.7 %collective-permute-start.17 = (bf16[256,1536]{1,0:T(8,128)(2,1)S(1)}, bf16[256,1536]{1,0:T(8,128)(2,1)S(1)}, u32[]{:S(2)}, u32[]{:S(2)}) collective-permute-start(bf16[256,1536]{1,0:T(8,128)(2,1)S(1)} %broadcast_select_fusion.1), channel_id=1, source_target_pairs={{0,4},{4,0},{1,5},{5,1},{2,6},{6,2},{3,7},{7,3},{8,12},{12,8},{9,1... | collective-permute-start | bytes 2359304 | tf_op jit(solution)/shard_map/ppermute | solution.py:1013
  232.3 13.5 %collective-permute-start.19 = (bf16[128,1536]{1,0:T(8,128)(2,1)S(1)}, bf16[128,1536]{1,0:T(8,128)(2,1)S(1)}, u32[]{:S(2)}, u32[]{:S(2)}) collective-permute-start(bf16[128,1536]{1,0:T(8,128)(2,1)S(1)} %get-tuple-element.288), channel_id=1, source_target_pairs={{0,16},{1,17},{2,18},{3,19},{4,20},{5,21},{6,22},{7,23},{8,24},{9,... | collective-permute-start | bytes 1179656 | tf_op jit(solution)/shard_map/ppermute | solution.py:1132
  250.5 25.4 %collective-permute-start.23 = (bf16[128,1536]{1,0:T(8,128)(2,1)S(1)}, bf16[128,1536]{1,0:T(8,128)(2,1)S(1)}, u32[]{:S(2)}, u32[]{:S(2)}) collective-permute-start(bf16[128,1536]{1,0:T(8,128)(2,1)S(1)} %get-tuple-element.309), channel_id=1, source_target_pairs={{0,16},{1,17},{2,18},{3,19},{4,20},{5,21},{6,22},{7,23},{8,24},{9,... | collective-permute-start | bytes 1179656 | tf_op jit(solution)/shard_map/ppermute | solution.py:1132
  280.6 13.5 %collective-permute-start.26 = (bf16[128,1536]{1,0:T(8,128)(2,1)S(1)}, bf16[128,1536]{1,0:T(8,128)(2,1)S(1)}, u32[]{:S(2)}, u32[]{:S(2)}) collective-permute-start(bf16[128,1536]{1,0:T(8,128)(2,1)S(1)} %get-tuple-element.328), channel_id=1, source_target_pairs={{0,16},{1,17},{2,18},{3,19},{4,20},{5,21},{6,22},{7,23},{8,24},{9,... | collective-permute-start | bytes 1179656 | tf_op jit(solution)/shard_map/ppermute | solution.py:1132
  298.9 9.9 %collective-permute-start.29 = (bf16[128,1536]{1,0:T(8,128)(2,1)S(1)}, bf16[128,1536]{1,0:T(8,128)(2,1)S(1)}, u32[]{:S(2)}, u32[]{:S(2)}) collective-permute-start(bf16[128,1536]{1,0:T(8,128)(2,1)S(1)} %get-tuple-element.347), channel_id=1, source_target_pairs={{0,16},{1,17},{2,18},{3,19},{4,20},{5,21},{6,22},{7,23},{8,24},{9,... | collective-permute-start | bytes 1179656 | tf_op jit(solution)/shard_map/ppermute | solution.py:1132
  320.5 47.2 %collective-permute-start.34 = (bf16[128,1536]{1,0:T(8,128)(2,1)S(1)}, bf16[128,1536]{1,0:T(8,128)(2,1)S(1)}, u32[]{:S(2)}, u32[]{:S(2)}) collective-permute-start(bf16[128,1536]{1,0:T(8,128)(2,1)S(1)} %get-tuple-element.390), channel_id=1, source_target_pairs={{16,0},{17,1},{18,2},{19,3},{20,4},{21,5},{22,6},{23,7},{24,8},{25... | collective-permute-start | bytes 1179656 | tf_op jit(solution)/shard_map/ppermute | solution.py:1170
  371.0 22.3 %collective-permute-start.37 = (bf16[128,1536]{1,0:T(8,128)(2,1)S(1)}, bf16[128,1536]{1,0:T(8,128)(2,1)S(1)}, u32[]{:S(2)}, u32[]{:S(2)}) collective-permute-start(bf16[128,1536]{1,0:T(8,128)(2,1)S(1)} %get-tuple-element.405), channel_id=1, source_target_pairs={{16,0},{17,1},{18,2},{19,3},{20,4},{21,5},{22,6},{23,7},{24,8},{25... | collective-permute-start | bytes 1179656 | tf_op jit(solution)/shard_map/ppermute | solution.py:1170
  398.2 21.2 %collective-permute-start.40 = (bf16[128,1536]{1,0:T(8,128)(2,1)S(1)}, bf16[128,1536]{1,0:T(8,128)(2,1)S(1)}, u32[]{:S(2)}, u32[]{:S(2)}) collective-permute-start(bf16[128,1536]{1,0:T(8,128)(2,1)S(1)} %get-tuple-element.420), channel_id=1, source_target_pairs={{16,0},{17,1},{18,2},{19,3},{20,4},{21,5},{22,6},{23,7},{24,8},{25... | collective-permute-start | bytes 1179656 | tf_op jit(solution)/shard_map/ppermute | solution.py:1170
  424.1 21.7 %collective-permute-start.43 = (bf16[128,1536]{1,0:T(8,128)(2,1)S(1)}, bf16[128,1536]{1,0:T(8,128)(2,1)S(1)}, u32[]{:S(2)}, u32[]{:S(2)}) collective-permute-start(bf16[128,1536]{1,0:T(8,128)(2,1)S(1)} %get-tuple-element.435), channel_id=1, source_target_pairs={{16,0},{17,1},{18,2},{19,3},{20,4},{21,5},{22,6},{23,7},{24,8},{25... | collective-permute-start | bytes 1179656 | tf_op jit(solution)/shard_map/ppermute | solution.py:1170
  482.0 23.0 %collective-permute-start.46 = (bf16[1280,384]{1,0:T(8,128)(2,1)S(1)}, bf16[1280,384]{1,0:T(8,128)(2,1)S(1)}, u32[]{:S(2)}, u32[]{:S(2)}) collective-permute-start(bf16[1280,384]{1,0:T(8,128)(2,1)S(1)} %block_grad.17), channel_id=1, source_target_pairs={{0,8},{1,0},{2,1},{3,2},{11,3},{10,11},{9,10},{8,9},{4,12},{5,4},{... | collective-permute-start | bytes 2949128 | tf_op jit(solution)/shard_map/ppermute | solution.py:1220
  483.2 22.7 %collective-permute-start.45 = (bf16[1280,384]{1,0:T(8,128)(2,1)S(1)}, bf16[1280,384]{1,0:T(8,128)(2,1)S(1)}, u32[]{:S(2)}, u32[]{:S(2)}) collective-permute-start(bf16[1280,384]{1,0:T(8,128)(2,1)S(1)} %block_grad.16), channel_id=1, source_target_pairs={{0,1},{1,2},{2,3},{3,11},{11,10},{10,9},{9,8},{8,0},{4,5},{5,6},{6... | collective-permute-start | bytes 2949128 | tf_op jit(solution)/shard_map/ppermute | solution.py:1220
  506.1 26.5 %collective-permute-start.48 = (bf16[1280,384]{1,0:T(8,128)(2,1)S(1)}, bf16[1280,384]{1,0:T(8,128)(2,1)S(1)}, u32[]{:S(2)}, u32[]{:S(2)}) collective-permute-start(bf16[1280,384]{1,0:T(8,128)(2,1)S(1)} %add_convert_fusion.12), channel_id=1, source_target_pairs={{0,8},{1,0},{2,1},{3,2},{11,3},{10,11},{9,10},{8,9},{4,12},{5,4},{... | collective-permute-start | bytes 2949128 | tf_op jit(solution)/shard_map/ppermute | solution.py:1220
  512.0 21.8 %collective-permute-start.47 = (bf16[1280,384]{1,0:T(8,128)(2,1)S(1)}, bf16[1280,384]{1,0:T(8,128)(2,1)S(1)}, u32[]{:S(2)}, u32[]{:S(2)}) collective-permute-start(bf16[1280,384]{1,0:T(8,128)(2,1)S(1)} %add_convert_fusion.13), channel_id=1, source_target_pairs={{0,1},{1,2},{2,3},{3,11},{11,10},{10,9},{9,8},{8,0},{4,5},{5,6},{6... | collective-permute-start | bytes 2949128 | tf_op jit(solution)/shard_map/ppermute | solution.py:1220
  534.1 25.3 %collective-permute-start.52 = (bf16[1280,384]{1,0:T(8,128)(2,1)S(1)}, bf16[1280,384]{1,0:T(8,128)(2,1)S(1)}, u32[]{:S(2)}, u32[]{:S(2)}) collective-permute-start(bf16[1280,384]{1,0:T(8,128)(2,1)S(1)} %add_convert_fusion.10), channel_id=1, source_target_pairs={{0,8},{1,0},{2,1},{3,2},{11,3},{10,11},{9,10},{8,9},{4,12},{5,4},{... | collective-permute-start | bytes 2949128 | tf_op jit(solution)/shard_map/ppermute | solution.py:1220
  537.9 22.8 %collective-permute-start.51 = (bf16[1280,384]{1,0:T(8,128)(2,1)S(1)}, bf16[1280,384]{1,0:T(8,128)(2,1)S(1)}, u32[]{:S(2)}, u32[]{:S(2)}) collective-permute-start(bf16[1280,384]{1,0:T(8,128)(2,1)S(1)} %add_convert_fusion.11), channel_id=1, source_target_pairs={{0,1},{1,2},{2,3},{3,11},{11,10},{10,9},{9,8},{8,0},{4,5},{5,6},{6... | collective-permute-start | bytes 2949128 | tf_op jit(solution)/shard_map/ppermute | solution.py:1220
  561.0 21.9 %collective-permute-start.54 = (bf16[1280,384]{1,0:T(8,128)(2,1)S(1)}, bf16[1280,384]{1,0:T(8,128)(2,1)S(1)}, u32[]{:S(2)}, u32[]{:S(2)}) collective-permute-start(bf16[1280,384]{1,0:T(8,128)(2,1)S(1)} %add_convert_fusion.8), channel_id=1, source_target_pairs={{0,8},{1,0},{2,1},{3,2},{11,3},{10,11},{9,10},{8,9},{4,12},{5,4},{... | collective-permute-start | bytes 2949128 | tf_op jit(solution)/shard_map/ppermute | solution.py:1220
  562.1 21.6 %collective-permute-start.53 = (bf16[1280,384]{1,0:T(8,128)(2,1)S(1)}, bf16[1280,384]{1,0:T(8,128)(2,1)S(1)}, u32[]{:S(2)}, u32[]{:S(2)}) collective-permute-start(bf16[1280,384]{1,0:T(8,128)(2,1)S(1)} %add_convert_fusion.9), channel_id=1, source_target_pairs={{0,1},{1,2},{2,3},{3,11},{11,10},{10,9},{9,8},{8,0},{4,5},{5,6},{6... | collective-permute-start | bytes 2949128 | tf_op jit(solution)/shard_map/ppermute | solution.py:1220
  583.9 20.7 %collective-permute-start.56 = (bf16[1280,384]{1,0:T(8,128)(2,1)S(1)}, bf16[1280,384]{1,0:T(8,128)(2,1)S(1)}, u32[]{:S(2)}, u32[]{:S(2)}) collective-permute-start(bf16[1280,384]{1,0:T(8,128)(2,1)S(1)} %add_convert_fusion.6), channel_id=1, source_target_pairs={{0,8},{1,0},{2,1},{3,2},{11,3},{10,11},{9,10},{8,9},{4,12},{5,4},{... | collective-permute-start | bytes 2949128 | tf_op jit(solution)/shard_map/ppermute | solution.py:1220
  584.6 20.4 %collective-permute-start.55 = (bf16[1280,384]{1,0:T(8,128)(2,1)S(1)}, bf16[1280,384]{1,0:T(8,128)(2,1)S(1)}, u32[]{:S(2)}, u32[]{:S(2)}) collective-permute-start(bf16[1280,384]{1,0:T(8,128)(2,1)S(1)} %add_convert_fusion.7), channel_id=1, source_target_pairs={{0,1},{1,2},{2,3},{3,11},{11,10},{10,9},{9,8},{8,0},{4,5},{5,6},{6... | collective-permute-start | bytes 2949128 | tf_op jit(solution)/shard_map/ppermute | solution.py:1220
  605.2 19.5 %collective-permute-start.58 = (bf16[1280,384]{1,0:T(8,128)(2,1)S(1)}, bf16[1280,384]{1,0:T(8,128)(2,1)S(1)}, u32[]{:S(2)}, u32[]{:S(2)}) collective-permute-start(bf16[1280,384]{1,0:T(8,128)(2,1)S(1)} %add_convert_fusion.4), channel_id=1, source_target_pairs={{0,8},{1,0},{2,1},{3,2},{11,3},{10,11},{9,10},{8,9},{4,12},{5,4},{... | collective-permute-start | bytes 2949128 | tf_op jit(solution)/shard_map/ppermute | solution.py:1220
  606.1 19.5 %collective-permute-start.57 = (bf16[1280,384]{1,0:T(8,128)(2,1)S(1)}, bf16[1280,384]{1,0:T(8,128)(2,1)S(1)}, u32[]{:S(2)}, u32[]{:S(2)}) collective-permute-start(bf16[1280,384]{1,0:T(8,128)(2,1)S(1)} %add_convert_fusion.5), channel_id=1, source_target_pairs={{0,1},{1,2},{2,3},{3,11},{11,10},{10,9},{9,8},{8,0},{4,5},{5,6},{6... | collective-permute-start | bytes 2949128 | tf_op jit(solution)/shard_map/ppermute | solution.py:1220
  625.8 19.2 %collective-permute-start.60 = (bf16[1280,384]{1,0:T(8,128)(2,1)S(1)}, bf16[1280,384]{1,0:T(8,128)(2,1)S(1)}, u32[]{:S(2)}, u32[]{:S(2)}) collective-permute-start(bf16[1280,384]{1,0:T(8,128)(2,1)S(1)} %add_convert_fusion.2), channel_id=1, source_target_pairs={{0,8},{1,0},{2,1},{3,2},{11,3},{10,11},{9,10},{8,9},{4,12},{5,4},{... | collective-permute-start | bytes 2949128 | tf_op jit(solution)/shard_map/ppermute | solution.py:1220
  626.7 19.1 %collective-permute-start.59 = (bf16[1280,384]{1,0:T(8,128)(2,1)S(1)}, bf16[1280,384]{1,0:T(8,128)(2,1)S(1)}, u32[]{:S(2)}, u32[]{:S(2)}) collective-permute-start(bf16[1280,384]{1,0:T(8,128)(2,1)S(1)} %add_convert_fusion.3), channel_id=1, source_target_pairs={{0,1},{1,2},{2,3},{3,11},{11,10},{10,9},{9,8},{8,0},{4,5},{5,6},{6... | collective-permute-start | bytes 2949128 | tf_op jit(solution)/shard_map/ppermute | solution.py:1220
  646.0 42.9 %collective-permute-start.65 = (bf16[1280,384]{1,0:T(8,128)(2,1)S(1)}, bf16[1280,384]{1,0:T(8,128)(2,1)S(1)}, u32[]{:S(2)}, u32[]{:S(2)}) collective-permute-start(bf16[1280,384]{1,0:T(8,128)(2,1)S(1)} %add_convert_fusion.1.refs_0_), channel_id=1, source_target_pairs={{0,8},{8,0},{1,9},{9,1},{2,10},{10,2},{3,11},{11,3},{4,12},{12,4},... | collective-permute-start | bytes 2949128 | tf_op jit(solution)/shard_map/ppermute | solution.py:1013
  646.9 42.5 %collective-permute-start.68 = (bf16[1280,384]{1,0:T(8,128)(2,1)S(1)}, bf16[1280,384]{1,0:T(8,128)(2,1)}, u32[]{:S(2)}, u32[]{:S(2)}) collective-permute-start(bf16[1280,384]{1,0:T(8,128)(2,1)S(1)} %add_convert_fusion.refs_4_), channel_id=1, source_target_pairs={{0,8},{8,0},{1,9},{9,1},{2,10},{10,2},{3,11},{11,3},{4,12},{12,4},... | collective-permute-start | bytes 2949128 | tf_op jit(solution)/shard_map/ppermute | solution.py:1013
  647.5 29.8 %collective-permute-start.61 = (bf16[256,1536]{1,0:T(8,128)(2,1)S(1)}, bf16[256,1536]{1,0:T(8,128)(2,1)}, u32[]{:S(2)}, u32[]{:S(2)}) collective-permute-start(bf16[256,1536]{1,0:T(8,128)(2,1)S(1)} %pick.2), channel_id=1, source_target_pairs={{0,0},{4,1},{1,4},{5,5},{8,8},{12,9},{9,12},{13,13},{16,16},{20,17... | collective-permute-start | bytes 2359304 | tf_op jit(solution)/shard_map/ppermute | solution.py:1088
  656.1 22.7 %collective-permute-start.62 = (bf16[256,1536]{1,0:T(8,128)(2,1)S(1)}, bf16[256,1536]{1,0:T(8,128)(2,1)S(1)}, u32[]{:S(2)}, u32[]{:S(2)}) collective-permute-start(bf16[256,1536]{1,0:T(8,128)(2,1)S(1)} %pick.2), channel_id=1, source_target_pairs={{2,0},{6,1},{3,4},{7,5},{10,8},{14,9},{11,12},{15,13},{18,16},{22,... | collective-permute-start | bytes 2359304 | tf_op jit(solution)/shard_map/ppermute | solution.py:1088
  657.4 31.4 %collective-permute-start.63 = (bf16[256,1536]{1,0:T(8,128)(2,1)}, bf16[256,1536]{1,0:T(8,128)(2,1)S(1)}, u32[]{:S(2)}, u32[]{:S(2)}) collective-permute-start(bf16[256,1536]{1,0:T(8,128)(2,1)} %pick.3), channel_id=1, source_target_pairs={{0,2},{4,3},{1,6},{5,7},{8,10},{12,11},{9,14},{13,15},{16,18},{20,... | collective-permute-start | bytes 2359304 | tf_op jit(solution)/shard_map/ppermute | solution.py:1088
  677.3 16.3 %collective-permute-start.64 = (bf16[256,1536]{1,0:T(8,128)(2,1)}, bf16[256,1536]{1,0:T(8,128)(2,1)}, u32[]{:S(2)}, u32[]{:S(2)}) collective-permute-start(bf16[256,1536]{1,0:T(8,128)(2,1)} %pick.3), channel_id=1, source_target_pairs={{2,2},{6,3},{3,6},{7,7},{10,10},{14,11},{11,14},{15,15},{18,18},{2... | collective-permute-start | bytes 2359304 | tf_op jit(solution)/shard_map/ppermute | solution.py:1088
  678.9 18.0 %collective-permute-start.66 = (bf16[1280,384]{1,0:T(8,128)(2,1)S(1)}, bf16[1280,384]{1,0:T(8,128)(2,1)}, u32[]{:S(2)}, u32[]{:S(2)}) collective-permute-start(bf16[1280,384]{1,0:T(8,128)(2,1)S(1)} %add_convert_fusion.1.refs_0_), channel_id=1, source_target_pairs={{0,4},{4,0},{1,5},{5,1},{2,6},{6,2},{3,7},{7,3},{8,12},{12,8},{9,1... | collective-permute-start | bytes 2949128 | tf_op jit(solution)/shard_map/ppermute | solution.py:1013
  688.9 8.1 %collective-permute-start.69 = (bf16[1280,384]{1,0:T(8,128)(2,1)S(1)}, bf16[1280,384]{1,0:T(8,128)(2,1)}, u32[]{:S(2)}, u32[]{:S(2)}) collective-permute-start(bf16[1280,384]{1,0:T(8,128)(2,1)S(1)} %add_convert_fusion.refs_4_), channel_id=1, source_target_pairs={{0,4},{4,0},{1,5},{5,1},{2,6},{6,2},{3,7},{7,3},{8,12},{12,8},{9,1... | collective-permute-start | bytes 2949128 | tf_op jit(solution)/shard_map/ppermute | solution.py:1013
  (57 other events, 330.4 us)

commit v3 on v2

--- a/solution.py
+++ b/solution.py
@@ -290,13 +290,12 @@
 
     @pl.when(leading)
     def _():
-        copies = fetch(arrived_hbm, mine, sem.at[0]), fetch(other_hbm, theirs, sem.at[10])
-        for copy in copies:
-            copy.wait()
+        pltpu.make_async_copy(arrived_hbm, mine, sem.at[0]).start()
+        pltpu.make_async_copy(other_hbm, theirs, sem.at[10]).start()
 
     @pl.when(jnp.logical_not(leading))
     def _():
-        fetch(cot_hbm, g_ref, sem.at[0]).wait()
+        pltpu.make_async_copy(cot_hbm, g_ref, sem.at[0]).start()
 
     y_copy = fetch(y_hbm.at[slot], y_ref, sem.at[1])
     ri_copy = fetch(ri_hbm.at[slot], ri, sem.at[2])
@@ -304,14 +303,22 @@
     tl_copy = fetch(tl_hbm.at[slot], tl, sem.at[4])
     mx_copy = fetch(mx_hbm.at[slot], mx, sem.at[5])
     st_copy = fetch(st_hbm.at[slot], st_ref, sem.at[6])
-    h_copy = fetch(h_hbm.at[slot], h_out, sem.at[8])
-    n_copy = fetch(n_hbm.at[slot], normed, sem.at[9])
 
     acc_out[...] = acc_ref[...]
     dw[t : t + 8, :] = jnp.where(last, 0.0, dc_ref[...])
     dgt[...] = jnp.zeros_like(dgt)
     dci[...] = jnp.zeros_like(dci)
     dbi[...] = jnp.zeros_like(dbi)
+
+    @pl.when(leading)
+    def _():
+        pltpu.make_async_copy(arrived_hbm, mine, sem.at[0]).wait()
+        pltpu.make_async_copy(other_hbm, theirs, sem.at[10]).wait()
+
+    @pl.when(jnp.logical_not(leading))
+    def _():
+        pltpu.make_async_copy(cot_hbm, g_ref, sem.at[0]).wait()
+
     for at in range(0, OWN, 512):
         gw[:, at : at + 512] = dot_nt(g_ref[...], wout[at : at + 512, :])
     y_copy.wait()
@@ -356,6 +363,8 @@
     head_lane = lax.broadcasted_iota(jnp.int32, (2 * LANES, LANES), 1)
     mx_copy.wait()
     st_copy.wait()
+    h_copy = fetch(h_hbm.at[slot], h_out, sem.at[8])
+    n_copy = fetch(n_hbm.at[slot], normed, sem.at[9])
 
     def pair_step(pair, carry):
         ddt, dld, dval = carry
@@ -742,28 +751,40 @@
     return [(index(p), index((p + step) % size)) for p in range(size)]
 
 
-def pack_kernel(sc, w, steps, o, own, rest, sem):
+HALF_ROWS = PACKED_ROWS // 2
+
+
+def cut(at, rows):
+    spans = []
+    for i in range(2):
+        a, b = max(at, i * HALF_ROWS), min(at + rows, (i + 1) * HALF_ROWS)
+        if a < b:
+            spans.append((i, a - i * HALF_ROWS, a - at, b - a))
+    return spans
+
+
+def pack_kernel(sc, w, steps, o, own_a, own_b, rest_a, rest_b, sem):
     core, side = sc[0], sc[1]
     copies = []
-    for target, y in ((own, side), (rest, 1 - side)):
+    for targets, y in (((own_a, own_b), side), ((rest_a, rest_b), 1 - side)):
         at = 0
-
-        def put(source, rows):
-            span = target.at[pl.ds(at, rows)]
-            copies.append(fetch(source, span, sem.at[len(copies)]))
-
         for base in (INNER, 0):
             for k in range(2):
-                first = aligned(base + (2 * y + k) * HALF + core * BLOCK)
-                put(w.at[pl.ds(first, BLOCK)], BLOCK)
+                first = base + (2 * y + k) * HALF + core * BLOCK
+                for i, to, off, rows in cut(at, BLOCK):
+                    source = w.at[pl.ds(aligned(first + off), rows)]
+                    copies.append(fetch(source, targets[i].at[pl.ds(to, rows)], sem.at[len(copies)]))
                 at += BLOCK
         bc = w.at[pl.ds(2 * INNER, 2 * STATE)]
-        span = target.at[pl.ds(at, 2 * STATE)]
+        ((i, to, _, rows),) = cut(at, 2 * STATE)
+        span = targets[i].at[pl.ds(to, rows)]
         copies.append(fetch_one_of(y == 0, bc, steps, span, sem.at[len(copies)]))
         at += 2 * STATE
         for k in range(2):
+            ((i, to, _, rows),) = cut(at, BLOCK)
             cols = pl.ds(aligned(y * HALF + k * BLOCK), BLOCK)
-            put(o.at[pl.ds(aligned(core * BLOCK), BLOCK), cols], BLOCK)
+            source = o.at[pl.ds(aligned(core * BLOCK), BLOCK), cols]
+            copies.append(fetch(source, targets[i].at[pl.ds(to, rows)], sem.at[len(copies)]))
             at += BLOCK
     for copy in copies:
         copy.wait()
@@ -773,76 +794,67 @@
     return pl.pallas_call(
         pack_kernel,
         in_specs=[pl.BlockSpec(memory_space=pltpu.SMEM), ANY, ANY, ANY],
-        out_specs=[NEAR, NEAR],
-        out_shape=[pltpu.VMEM((PACKED_ROWS, BLOCK), BF16)] * 2,
-        scratch_shapes=[pltpu.SemaphoreType.DMA((14,))],
+        out_specs=[NEAR, NEAR, NEAR, NEAR],
+        out_shape=[pltpu.VMEM((HALF_ROWS, BLOCK), BF16)] * 4,
+        scratch_shapes=[pltpu.SemaphoreType.DMA((16,))],
         compiler_params=pltpu.CompilerParams(vmem_limit_bytes=4 << 20),
         cost_estimate=LITTLE,
         name="pack_weights",
     )(scalars, away(w), steps, away(o))
 
 
-def place_kernel(sc, own, rest, *refs):
-    (near_z, inner_2, outer_2, inner_3, outer_3), (win, wout, sem) = (
-        [refs[2 * i : 2 * i + 2] for i in range(5)],
-        refs[-3:],
-    )
+def place_kernel(sc, *refs):
+    blocks, (win, wout, sem) = [refs[2 * i : 2 * i + 2] for i in range(12)], refs[-3:]
     side, place = sc[1], sc[2]
     inner = jnp.logical_and(place > 0, place < 3)
     second = jnp.where(inner, 3 - place, jnp.where(place == 0, 2, 1))
     third = jnp.where(place < 2, 3, 0)
-    used = []
-
-    def put(source, z, y, start):
+
+    def put(number, block, z, y):
         lanes = pl.ds(aligned(z * BLOCK), BLOCK)
-        at = 0
-        for k, (matrix, rows, first, step) in enumerate(PARTS):
-            if matrix == "in":
-                target = win.at[pl.ds(aligned(first + y * step), rows), lanes]
-            else:
-                target = wout.at[lanes, pl.ds(aligned(first + y * step), BLOCK)]
-            copy = pltpu.make_async_copy(source.at[pl.ds(at, rows)], target, sem.at[start + k])
-            copy.start()
-            used.append(copy)
+        copies, at = [], 0
+        for matrix, rows, first, step in PARTS:
+            for i, to, off, count in cut(at, rows):
+                if matrix == "in":
+                    span = pl.ds(aligned(first + y * step + off), count)
+                    target = win.at[span, lanes]
+                else:
+                    target = wout.at[lanes, pl.ds(aligned(first + y * step), BLOCK)]
+                source = blocks[block][i].at[pl.ds(to, count)]
+                copies.append(fetch(source, target, sem.at[8 * number + len(copies)]))
             at += rows
-
-    put(own, place, side, 0)
-    put(rest, place, 1 - side, 5)
-    put(near_z[0], place + 1 - 2 * lax.rem(place, 2), side, 10)
-    put(near_z[1], place + 1 - 2 * lax.rem(place, 2), 1 - side, 15)
-    waits = list(used)
+        return copies
+
+    beside = place + 1 - 2 * lax.rem(place, 2)
+    always = put(0, 0, place, side) + put(1, 1, place, 1 - side)
+    always += put(2, 2, beside, side) + put(3, 3, beside, 1 - side)
+
+    def rest(first):
+        copies = put(4, first, second, side) + put(5, first + 1, second, 1 - side)
+        copies += put(6, first + 4, third, side) + put(7, first + 5, third, 1 - side)
+        for copy in copies:
+            copy.wait()
 
     @pl.when(inner)
     def _():
-        put(inner_2[0], second, side, 20)
-        put(inner_2[1], second, 1 - side, 25)
-        put(inner_3[0], third, side, 30)
-        put(inner_3[1], third, 1 - side, 35)
-        for copy in used[20:]:
-            copy.wait()
-        del used[20:]
+        rest(4)
 
     @pl.when(jnp.logical_not(inner))
     def _():
-        put(outer_2[0], second, side, 20)
-        put(outer_2[1], second, 1 - side, 25)
-        put(outer_3[0], third, side, 30)
-        put(outer_3[1], third, 1 - side, 35)
-        for copy in used[20:]:
-            copy.wait()
-
-    for copy in waits:
+        rest(6)
+
+    for copy in always:
         copy.wait()
 
 
-def place_weights(here, own, rest, pairs):
-    inputs = [own, rest, *sum(pairs, ())]
+def place_weights(here, blocks):
+    inputs = [away(half) for block in blocks for half in block]
     return pl.pallas_call(
         place_kernel,
         in_specs=[pl.BlockSpec(memory_space=pltpu.SMEM)] + [ANY] * len(inputs),
         out_specs=[NEAR, NEAR],
         out_shape=[pltpu.VMEM((OWN_PROJ, D), BF16), pltpu.VMEM((OWN, D), BF16)],
-        scratch_shapes=[pltpu.SemaphoreType.DMA((40,))],
+        scratch_shapes=[pltpu.SemaphoreType.DMA((64,))],
         compiler_params=pltpu.CompilerParams(vmem_limit_bytes=4 << 20),
         cost_estimate=LITTLE,
         name="place_weights",
@@ -851,35 +863,51 @@
 
 def line_gather(own, beside):
     def along(value, hops):
-        route = [(y * 4 + a, y * 4 + b) for y in range(2) for a, b in hops]
-        return lax.ppermute(value, ("y", "fsdp"), route)
+        path = [(y * 4 + a, y * 4 + b) for y in range(2) for a, b in hops]
+        return lax.ppermute(value, ("y", "fsdp"), path)
 
     def across(value, places):
-        route = [(y * 4 + z, (1 - y) * 4 + z) for y in range(2) for z in places]
-        return lax.ppermute(value, ("y", "fsdp"), route)
-
-    outward, middle = [(1, 0), (2, 3)], [(1, 2), (2, 1)]
-    near_z = along(own, [(0, 1), (1, 0), (2, 3), (3, 2)])
-    inner_2 = along(own, middle)
-    near_z, inner_2, *beside = lax.optimization_barrier((near_z, inner_2, *beside))
-    outer_2 = along(inner_2, outward)
-    inner_3 = along(near_z, middle)
-    near_y = across(near_z, range(4))
-    outer_2, inner_3, near_y = lax.optimization_barrier((outer_2, inner_3, near_y))
-    outer_3 = along(inner_3, outward)
-    outer_2_y = across(outer_2, (0, 3))
-    inner_2_y = across(inner_2, (1, 2))
-    outer_3, outer_2_y, inner_2_y = lax.optimization_barrier((outer_3, outer_2_y, inner_2_y))
-    ready = inner_2_y
-    outer_3_y = across(outer_3, (0, 3))
-    inner_3_y = across(inner_3, (1, 2))
-    return [
-        (near_z, near_y),
-        (inner_2, inner_2_y),
-        (outer_2, outer_2_y),
-        (inner_3, inner_3_y),
-        (outer_3, outer_3_y),
-    ], ready, beside
+        path = [(y * 4 + z, (1 - y) * 4 + z) for y in range(2) for z in places]
+        return lax.ppermute(value, ("y", "fsdp"), path)
+
+    pair, middle, outward = [(0, 1), (1, 0), (2, 3), (3, 2)], [(1, 2), (2, 1)], [(1, 0), (2, 3)]
+    inner, outer = (1, 2), (0, 3)
+    barrier = lax.optimization_barrier
+    a, b = own
+    near_a, in2_a = along(a, pair), along(a, middle)
+    near_a, in2_a, b, *beside = barrier((near_a, in2_a, b, *beside))
+    near_b, in2_b, near_ya = along(b, pair), along(b, middle), across(near_a, range(4))
+    near_a, in2_a, near_b, in2_b, near_ya = barrier((near_a, in2_a, near_b, in2_b, near_ya))
+    out2_a, in3_a, near_yb = along(in2_a, outward), along(near_a, middle), across(near_b, range(4))
+    out2_a, in3_a, near_yb, in2_a, near_b, in2_b = barrier(
+        (out2_a, in3_a, near_yb, in2_a, near_b, in2_b)
+    )
+    out2_b, in3_b = along(in2_b, outward), along(near_b, middle)
+    out2_ya, in2_ya = across(out2_a, outer), across(in2_a, inner)
+    out2_b, in3_b, out2_ya, in2_ya, in3_a, in2_b = barrier(
+        (out2_b, in3_b, out2_ya, in2_ya, in3_a, in2_b)
+    )
+    out3_a = along(in3_a, outward)
+    out2_yb, in2_yb = across(out2_b, outer), across(in2_b, inner)
+    out3_a, out2_yb, in2_yb, in3_a, in3_b = barrier((out3_a, out2_yb, in2_yb, in3_a, in3_b))
+    out3_b = along(in3_b, outward)
+    out3_ya, in3_ya = across(out3_a, outer), across(in3_a, inner)
+    ready = out2_yb
+    out3_b, out3_ya, in3_ya, in3_b = barrier((out3_b, out3_ya, in3_ya, in3_b))
+    out3_yb, in3_yb = across(out3_b, outer), across(in3_b, inner)
+    blocks = [
+        (near_a, near_b),
+        (near_ya, near_yb),
+        (in2_a, in2_b),
+        (in2_ya, in2_yb),
+        (out2_a, out2_b),
+        (out2_ya, out2_yb),
+        (in3_a, in3_b),
+        (in3_ya, in3_yb),
+        (out3_a, out3_b),
+        (out3_ya, out3_yb),
+    ]
+    return blocks, beside, ready
 
 
 GROUPS = (
@@ -1057,8 +1085,8 @@
     w = input_weight[0].T
     steps = own_steps(w, core)
     here = jnp.stack([core, side, place]).astype(jnp.int32)
-    own, rest = pack_weights(here, w, steps, output_weight[0])
-    pairs, ready, others = line_gather(own, others)
+    packed_halves = pack_weights(here, w, steps, output_weight[0])
+    blocks, others, ready = line_gather(packed_halves[:2], others)
     packed = in_order(packed, others, "fsdp")
     pieces, at = [], 0
     for member in small:
@@ -1089,11 +1117,12 @@
             for m in range(2)
         ]
 
-    last = (*pairs[3], *pairs[4])
+    last = (blocks[7][1], blocks[9][1])
     here, *got = lax.optimization_barrier((here, *bring(0), *bring(2), *last))
-    got, pairs[3:] = got[:4], [tuple(got[4:6]), tuple(got[6:8])]
-    pieces = shared(got[:2]) + shared(got[2:])
-    win, wout = place_weights(here, own, rest, pairs)
+    blocks[7], blocks[9] = (blocks[7][0], got[4]), (blocks[9][0], got[5])
+    pieces = shared(got[:2]) + shared(got[2:4])
+    blocks = [packed_halves[:2], packed_halves[2:], *blocks]
+    win, wout = place_weights(here, blocks)
     params = (gain, convp, headp, chanp, win, wout)
 
     def scalars(moment, lag, reverse):

time: 717 us -> 694 us (0.968)
  waiting for transfers between devices: 275 us -> 248 us
  starting transfers between devices: 119 us -> 142 us
  local copies, waits for them, and re-layouts: 36.8 us -> 19.6 us
    ppermute x3, waiting for transfers between devices: 39.6 us -> 18.5 us  [sent_along(): return [lax.ppermute(value, axis, path) for path in routes]]
    unnamed x73, local copies, waits for them, and re-layouts: 22.5 us -> 5.23 us
    ppermute x10 -> x20, starting transfers between devices: 16.5 us -> 28.9 us  [the longest x10 16 us: across(): return lax.ppermute(value, ('y', 'fsdp'), path)]
    ppermute x4, starting transfers between devices: 18.9 us -> 26.6 us  [bring(): lax.ppermute(local[m], ('core', 'fsdp'), route(first, m))]
    ppermute x10 -> x20, waiting for transfers between devices: 79.1 us -> 75.5 us  [the longest x10 54.1 us: along(): return lax.ppermute(value, ('y', 'fsdp'), path)]
  transfers between devices with their start and end apart: 71 -> 81, of which waited for: 37 -> 39; matrix products, arithmetic and copies ran while one was open for 2% -> 2% of each run, Pallas kernels for 29% -> 30%
where the time goes in v3:
time: 694 us; the launch traced here: 686 us
  Pallas kernels  263 us (38%)
  waiting for transfers between devices  248 us (36%)
  starting transfers between devices  142 us (20%)
  local copies, waits for them, and re-layouts  19.6 us (3%)
  other arithmetic  9.61 us (1%)
    pallas_call x26, Pallas kernels, chunk_call(): pl.pallas_call(kernel, in_specs=in_specs, out_specs=out_specs, out_shape=...  175 us
    pallas_call x16, Pallas kernels, block_grad(): pl.pallas_call(functools.partial(block_grad_kernel, row), grid_spec=pltpu...  70.6 us
    ppermute x14, waiting for transfers between devices, relay_shards(): came = lax.ppermute(sums[i], ('y', 'fsdp'), path).astype(F32)  67.7 us
    ppermute x10, waiting for transfers between devices, along(): return lax.ppermute(value, ('y', 'fsdp'), path)  54.1 us
    ppermute x28, starting transfers between devices, swap(): return lax.ppermute(value, axis, [(0, 1), (1, 0)])  42.2 us
    ppermute x4, waiting for transfers between devices, relay_shards(): moved[moment - 1] = lax.ppermute(result, 'section', [(1, 0)])  38.9 us
    ppermute x4, starting transfers between devices, bring(): lax.ppermute(local[m], ('core', 'fsdp'), route(first, m))  26.6 us
    ppermute x10, waiting for transfers between devices, across(): return lax.ppermute(value, ('y', 'fsdp'), path)  21.4 us
  transfers between devices with their start and end apart: 81, of which 39 were waited for; matrix products, arithmetic and copies ran while one was open for 2% of the time, Pallas kernels for 30%

profile of v3, /device:TPU:1, one launch (start us, length us, event | category | flops | bytes accessed | tf_op | source)
XLA Modules:
  0.0 686.2 jit_solution(258744423149104744)
XLA Ops:
  15.8 16.0 %collective-permute-done.2 = bf16[5348]{0:T(1024)(128)(2,1)S(1)} collective-permute-done((bf16[5348]{0:T(1024)(128)(2,1)S(1)}, bf16[5348]{0:T(1024)(128)(2,1)S(1)}, u32[]{:S(2)}, u32[]{:S(2)}) %collective-permute-start.2) | collective-permute-done | bytes 10728 | tf_op jit(solution)/shard_map/ppermute | solution.py:1047
  37.3 18.4 %collective-permute-done.5.refs_5_ = bf16[1280,384]{1,0:T(8,128)(2,1)S(1)} collective-permute-done((bf16[1280,384]{1,0:T(8,128)(2,1)S(1)}, bf16[1280,384]{1,0:T(8,128)(2,1)S(1)}, u32[]{:S(2)}, u32[]{:S(2)}) %collective-permute-start.5) | collective-permute-done | bytes 983072 | tf_op jit(solution)/shard_map/ppermute | solution.py:867
  61.0 17.4 %collective-permute-done.10.refs_7_ = bf16[1280,384]{1,0:T(8,128)(2,1)S(1)} collective-permute-done((bf16[1280,384]{1,0:T(8,128)(2,1)S(1)}, bf16[1280,384]{1,0:T(8,128)(2,1)S(1)}, u32[]{:S(2)}, u32[]{:S(2)}) %collective-permute-start.10) | collective-permute-done | bytes 983072 | tf_op jit(solution)/shard_map/ppermute | solution.py:871
  86.2 15.2 %collective-permute-done.11.refs_13_ = bf16[1280,384]{1,0:T(8,128)(2,1)S(1)} collective-permute-done((bf16[1280,384]{1,0:T(8,128)(2,1)S(1)}, bf16[1280,384]{1,0:T(8,128)(2,1)S(1)}, u32[]{:S(2)}, u32[]{:S(2)}) %collective-permute-start.11) | collective-permute-done | bytes 983072 | tf_op jit(solution)/shard_map/ppermute | solution.py:867
  107.6 18.5 %collective-permute-done.15.refs_20_ = bf16[1280,384]{1,0:T(8,128)(2,1)S(1)} collective-permute-done((bf16[1280,384]{1,0:T(8,128)(2,1)S(1)}, bf16[1280,384]{1,0:T(8,128)(2,1)S(1)}, u32[]{:S(2)}, u32[]{:S(2)}) %collective-permute-start.15) | collective-permute-done | bytes 983072 | tf_op jit(solution)/shard_map/ppermute | solution.py:867
  133.2 13.7 %collective-permute-start.18 = (bf16[256,1536]{1,0:T(8,128)(2,1)}, bf16[256,1536]{1,0:T(8,128)(2,1)}, u32[]{:S(2)}, u32[]{:S(2)}) collective-permute-start(bf16[256,1536]{1,0:T(8,128)(2,1)} %get-tuple-element.537), channel_id=1, source_target_pairs={{0,0},{1,4},{4,1},{5,5},{8,8},{9,12},{12,9},{13,13},{16,16},{17,20... | collective-permute-start | bytes 2359304 | tf_op jit(solution)/shard_map/ppermute | solution.py:1107
  153.0 10.1 %collective-permute-start.19 = (bf16[256,1536]{1,0:T(8,128)(2,1)}, bf16[256,1536]{1,0:T(8,128)(2,1)}, u32[]{:S(2)}, u32[]{:S(2)}) collective-permute-start(bf16[256,1536]{1,0:T(8,128)(2,1)} %get-tuple-element.536), channel_id=1, source_target_pairs={{0,2},{1,6},{4,3},{5,7},{8,10},{9,14},{12,11},{13,15},{16,18},{17,... | collective-permute-start | bytes 2359304 | tf_op jit(solution)/shard_map/ppermute | solution.py:1107
  172.7 4.9 collective-permute-done.20
  178.9 17.4 %collective-permute-start.27 = (bf16[256,1536]{1,0:T(8,128)(2,1)S(1)}, bf16[256,1536]{1,0:T(8,128)(2,1)S(1)}, u32[]{:S(2)}, u32[]{:S(2)}) collective-permute-start(bf16[256,1536]{1,0:T(8,128)(2,1)S(1)} %broadcast_select_fusion.1), channel_id=1, source_target_pairs={{0,4},{4,0},{1,5},{5,1},{2,6},{6,2},{3,7},{7,3},{8,12},{12,8},{9,1... | collective-permute-start | bytes 2359304 | tf_op jit(solution)/shard_map/ppermute | solution.py:1041
  196.4 6.6 place_weights.1
  203.3 12.7 %forward_chunk.6 = (bf16[256,1664]{1,0:T(8,128)(2,1)S(1)}, bf16[256,1536]{1,0:T(8,128)(2,1)S(1)}, f32[128,1536]{1,0:T(8,128)S(1)}, f32[8,1792]{1,0:T(8,128)S(1)}...) custom-call(s32[12,7]{1,0:T(8,128)S(1)} %reshape.193.sc, ...), custom_call_target="tpu_custom_call" | custom-call | flops 1048576 | bytes 65536 | tf_op jit(solution)/shard_map/forward_chunk/pallas_call | solution.py:557
  222.0 12.1 %forward_chunk.7 = (bf16[256,1664]{1,0:T(8,128)(2,1)S(1)}, bf16[256,1536]{1,0:T(8,128)(2,1)S(1)}, f32[128,1536]{1,0:T(8,128)S(1)}, f32[8,1792]{1,0:T(8,128)S(1)}...) custom-call(s32[12,7]{1,0:T(8,128)S(1)} %reshape.193.sc, ...), custom_call_target="tpu_custom_call", output_to_operand_aliasing={{4}: (12, {}), {5}: (13, {}), {6}: (14, {}), {7}: (15, {}),... | custom-call | flops 1048576 | bytes 65536 | tf_op jit(solution)/shard_map/forward_chunk/pallas_call | solution.py:557
  240.3 23.9 %forward_chunk.8 = (bf16[256,1664]{1,0:T(8,128)(2,1)S(1)}, bf16[256,1536]{1,0:T(8,128)(2,1)S(1)}, f32[128,1536]{1,0:T(8,128)S(1)}, f32[8,1792]{1,0:T(8,128)S(1)}...) custom-call(s32[12,7]{1,0:T(8,128)S(1)} %reshape.193.sc, ...), custom_call_target="tpu_custom_call", output_to_operand_aliasing={{4}: (12, {}), {5}: (13, {}), {6}: (14, {}), {7}: (15, {}),... | custom-call | flops 1048576 | bytes 65536 | tf_op jit(solution)/shard_map/forward_chunk/pallas_call | solution.py:557
  270.2 12.2 %forward_chunk.9 = (bf16[256,1664]{1,0:T(8,128)(2,1)S(1)}, bf16[256,1536]{1,0:T(8,128)(2,1)S(1)}, f32[128,1536]{1,0:T(8,128)S(1)}, f32[8,1792]{1,0:T(8,128)S(1)}...) custom-call(s32[12,7]{1,0:T(8,128)S(1)} %reshape.193.sc, ...), custom_call_target="tpu_custom_call", output_to_operand_aliasing={{4}: (12, {}), {5}: (13, {}), {6}: (14, {}), {7}: (15, {}),... | custom-call | flops 1048576 | bytes 65536 | tf_op jit(solution)/shard_map/forward_chunk/pallas_call | solution.py:557
  289.1 7.8 %collective-permute-done.39.refs_0_ = bf16[128,1536]{1,0:T(8,128)(2,1)S(1)} collective-permute-done((bf16[128,1536]{1,0:T(8,128)(2,1)S(1)}, bf16[128,1536]{1,0:T(8,128)(2,1)S(1)}, u32[]{:S(2)}, u32[]{:S(2)}) %collective-permute-start.39) | collective-permute-done | bytes 393248 | tf_op jit(solution)/shard_map/ppermute | solution.py:1161
  310.0 7.6 %backward_chunk.7 = (bf16[256,1536]{1,0:T(8,128)(2,1)S(1)}, bf16[256,1536]{1,0:T(8,128)(2,1)S(1)}, bf16[256,1536]{1,0:T(8,128)(2,1)S(1)}, f32[128,1536]{1,0:T(8,...) custom-call(s32[12,7]{1,0:T(8,128)S(1)} %reshape.193.sc, ...), custom_call_target="tpu_custom_call", output_to_operand_aliasing={{7}: (21, {}), {8}: (22, {})} | custom-call | flops 1048576 | bytes 65536 | tf_op jit(solution)/shard_map/backward_chunk/pallas_call | solution.py:557
  317.5 37.3 %collective-permute-done.44.refs_0_ = bf16[128,1536]{1,0:T(8,128)(2,1)S(1)} collective-permute-done((bf16[128,1536]{1,0:T(8,128)(2,1)S(1)}, bf16[128,1536]{1,0:T(8,128)(2,1)S(1)}, u32[]{:S(2)}, u32[]{:S(2)}) %collective-permute-start.44) | collective-permute-done | bytes 393248 | tf_op jit(solution)/shard_map/ppermute | solution.py:1199
  359.5 18.2 %backward_chunk.8 = (bf16[256,1536]{1,0:T(8,128)(2,1)S(1)}, bf16[256,1536]{1,0:T(8,128)(2,1)S(1)}, bf16[256,1536]{1,0:T(8,128)(2,1)S(1)}, f32[128,1536]{1,0:T(8,...) custom-call(s32[12,7]{1,0:T(8,128)S(1)} %reshape.193.sc, ...), custom_call_target="tpu_custom_call", output_to_operand_aliasing={{7}: (21, {}), {8}: (22, {})} | custom-call | flops 1048576 | bytes 65536 | tf_op jit(solution)/shard_map/backward_chunk/pallas_call | solution.py:557
  385.6 18.7 %backward_chunk.9 = (bf16[256,1536]{1,0:T(8,128)(2,1)S(1)}, bf16[256,1536]{1,0:T(8,128)(2,1)S(1)}, bf16[256,1536]{1,0:T(8,128)(2,1)S(1)}, f32[128,1536]{1,0:T(8,...) custom-call(s32[12,7]{1,0:T(8,128)S(1)} %reshape.193.sc, ...), custom_call_target="tpu_custom_call", output_to_operand_aliasing={{7}: (21, {}), {8}: (22, {})} | custom-call | flops 1048576 | bytes 65536 | tf_op jit(solution)/shard_map/backward_chunk/pallas_call | solution.py:557
  410.3 18.3 %backward_chunk.10 = (bf16[256,1536]{1,0:T(8,128)(2,1)S(1)}, bf16[256,1536]{1,0:T(8,128)(2,1)S(1)}, bf16[256,1536]{1,0:T(8,128)(2,1)S(1)}, f32[128,1536]{1,0:T(8...) custom-call(s32[12,7]{1,0:T(8,128)S(1)} %reshape.193.sc, ...), custom_call_target="tpu_custom_call", output_to_operand_aliasing={{7}: (21, {}), {8}: (22, {})} | custom-call | flops 1048576 | bytes 65536 | tf_op jit(solution)/shard_map/backward_chunk/pallas_call | solution.py:557
  430.4 19.8 %backward_chunk.11 = (bf16[256,1536]{1,0:T(8,128)(2,1)S(1)}, bf16[256,1536]{1,0:T(8,128)(2,1)S(1)}, bf16[256,1536]{1,0:T(8,128)(2,1)S(1)}, f32[128,1536]{1,0:T(8...) custom-call(s32[12,7]{1,0:T(8,128)S(1)} %reshape.193.sc, ...), custom_call_target="tpu_custom_call", output_to_operand_aliasing={{7}: (21, {}), {8}: (22, {})} | custom-call | flops 1048576 | bytes 65536 | tf_op jit(solution)/shard_map/backward_chunk/pallas_call | solution.py:557
  455.0 4.4 block_grad.16
  459.4 4.4 block_grad.17
  465.7 4.4 block_grad.19
  470.0 4.4 block_grad.18
  474.5 13.0 %collective-permute-done.56 = bf16[1280,384]{1,0:T(8,128)(2,1)S(1)} collective-permute-done((bf16[1280,384]{1,0:T(8,128)(2,1)S(1)}, bf16[1280,384]{1,0:T(8,128)(2,1)S(1)}, u32[]{:S(2)}, u32[]{:S(2)}) %collective-permute-start.56) | collective-permute-done | bytes 983072 | tf_op jit(solution)/shard_map/ppermute | solution.py:1249
  490.1 4.4 block_grad.21
  494.5 4.5 block_grad.20
  499.0 11.7 %collective-permute-done.58 = bf16[1280,384]{1,0:T(8,128)(2,1)S(1)} collective-permute-done((bf16[1280,384]{1,0:T(8,128)(2,1)S(1)}, bf16[1280,384]{1,0:T(8,128)(2,1)S(1)}, u32[]{:S(2)}, u32[]{:S(2)}) %collective-permute-start.58) | collective-permute-done | bytes 983072 | tf_op jit(solution)/shard_map/ppermute | solution.py:1249
  528.8 4.4 block_grad.23
  533.1 4.4 block_grad.22
  540.7 4.4 block_grad.25
  545.1 4.4 block_grad.24
  549.4 11.6 %collective-permute-done.64 = bf16[1280,384]{1,0:T(8,128)(2,1)S(1)} collective-permute-done((bf16[1280,384]{1,0:T(8,128)(2,1)S(1)}, bf16[1280,384]{1,0:T(8,128)(2,1)S(1)}, u32[]{:S(2)}, u32[]{:S(2)}) %collective-permute-start.64) | collective-permute-done | bytes 983072 | tf_op jit(solution)/shard_map/ppermute | solution.py:1249
  563.2 4.4 block_grad.27
  567.6 4.4 block_grad.26
  571.9 10.4 %collective-permute-done.66 = bf16[1280,384]{1,0:T(8,128)(2,1)S(1)} collective-permute-done((bf16[1280,384]{1,0:T(8,128)(2,1)S(1)}, bf16[1280,384]{1,0:T(8,128)(2,1)S(1)}, u32[]{:S(2)}, u32[]{:S(2)}) %collective-permute-start.66) | collective-permute-done | bytes 983072 | tf_op jit(solution)/shard_map/ppermute | solution.py:1249
  584.7 4.6 block_grad.29
  589.3 4.6 block_grad.28
  593.9 9.0 %collective-permute-done.68 = bf16[1280,384]{1,0:T(8,128)(2,1)S(1)} collective-permute-done((bf16[1280,384]{1,0:T(8,128)(2,1)S(1)}, bf16[1280,384]{1,0:T(8,128)(2,1)S(1)}, u32[]{:S(2)}, u32[]{:S(2)}) %collective-permute-start.68) | collective-permute-done | bytes 983072 | tf_op jit(solution)/shard_map/ppermute | solution.py:1249
  604.9 4.4 block_grad.31
  609.3 4.4 block_grad.30
  613.7 8.8 %collective-permute-done.70 = bf16[1280,384]{1,0:T(8,128)(2,1)S(1)} collective-permute-done((bf16[1280,384]{1,0:T(8,128)(2,1)S(1)}, bf16[1280,384]{1,0:T(8,128)(2,1)S(1)}, u32[]{:S(2)}, u32[]{:S(2)}) %collective-permute-start.70) | collective-permute-done | bytes 983072 | tf_op jit(solution)/shard_map/ppermute | solution.py:1249
  625.1 8.9 %collective-permute-start.71 = (bf16[256,1536]{1,0:T(8,128)(2,1)S(1)}, bf16[256,1536]{1,0:T(8,128)(2,1)}, u32[]{:S(2)}, u32[]{:S(2)}) collective-permute-start(bf16[256,1536]{1,0:T(8,128)(2,1)S(1)} %pick.2), channel_id=1, source_target_pairs={{0,0},{4,1},{1,4},{5,5},{8,8},{12,9},{9,12},{13,13},{16,16},{20,17... | collective-permute-start | bytes 2359304 | tf_op jit(solution)/shard_map/ppermute | solution.py:1116
  635.3 6.2 collective-permute-start.73
  641.5 13.8 %collective-permute-done.71 = bf16[256,1536]{1,0:T(8,128)(2,1)} collective-permute-done((bf16[256,1536]{1,0:T(8,128)(2,1)S(1)}, bf16[256,1536]{1,0:T(8,128)(2,1)}, u32[]{:S(2)}, u32[]{:S(2)}) %collective-permute-start.71) | collective-permute-done | bytes 786464 | tf_op jit(solution)/shard_map/ppermute | solution.py:1116
  656.9 9.4 %collective-permute-start.76 = (bf16[1280,384]{1,0:T(8,128)(2,1)S(1)}, bf16[1280,384]{1,0:T(8,128)(2,1)}, u32[]{:S(2)}, u32[]{:S(2)}) collective-permute-start(bf16[1280,384]{1,0:T(8,128)(2,1)S(1)} %add_convert_fusion.1.refs_0_), channel_id=1, source_target_pairs={{0,4},{4,0},{1,5},{5,1},{2,6},{6,2},{3,7},{7,3},{8,12},{12,8},{9,1... | collective-permute-start | bytes 2949128 | tf_op jit(solution)/shard_map/ppermute | solution.py:1041
  674.7 7.9 %join_grads.1 = (f32[6448,384]{1,0:T(8,128)}, f32[768,1536]{1,0:T(8,128)}, f32[16,384]{1,0:T(8,128)S(1)}) custom-call(s32[2]{0:T(128)S(1)} %pad_add_fusion.sc, bf16[1280,384]{1,0:T(8,128)(2,1)S(1)} %add_convert_fusion.1.refs_0_, bf16[1280,384]{1,0:T(8,128)(2,1)S(1)} %collective-permute-done.75.refs_1_, bf16[1280,384]{1,0:T(8,128)(2,1)} %collective-permute-done.76.refs_2_, ...), custom_call_target="tpu_custom_call" | custom-call | flops 1048576 | bytes 65536 | tf_op jit(solution)/shard_map/join_grads/pallas_call | solution.py:1028
  (346 shorter events, 174.7 us)
Async XLA Ops:
  6.4 28.0 %collective-permute-start = (bf16[1280,384]{1,0:T(8,128)(2,1)S(1)}, bf16[1280,384]{1,0:T(8,128)(2,1)}, u32[]{:S(2)}, u32[]{:S(2)}) collective-permute-start(bf16[1280,384]{1,0:T(8,128)(2,1)S(1)} %get-tuple-element.272.refs_0_), channel_id=1, source_target_pairs={{0,1},{1,0},{2,3},{3,2},{8,9},{9,8},{10,11},{11,10},{4,5},{5,4},{6... | collective-permute-start | bytes 2949128 | tf_op jit(solution)/shard_map/ppermute | solution.py:867
  8.5 25.9 %collective-permute-start.1 = (bf16[1280,384]{1,0:T(8,128)(2,1)S(1)}, bf16[1280,384]{1,0:T(8,128)(2,1)}, u32[]{:S(2)}, u32[]{:S(2)}) collective-permute-start(bf16[1280,384]{1,0:T(8,128)(2,1)S(1)} %get-tuple-element.272.refs_0_), channel_id=1, source_target_pairs={{1,2},{2,1},{9,10},{10,9},{5,6},{6,5},{13,14},{14,13},{17,18},{18,... | collective-permute-start | bytes 2949128 | tf_op jit(solution)/shard_map/ppermute | solution.py:867
  10.8 21.0 %collective-permute-start.2 = (bf16[5348]{0:T(1024)(128)(2,1)S(1)}, bf16[5348]{0:T(1024)(128)(2,1)S(1)}, u32[]{:S(2)}, u32[]{:S(2)}) collective-permute-start(bf16[5348]{0:T(1024)(128)(2,1)S(1)} %concatenate.29), channel_id=1, source_target_pairs={{0,1},{1,2},{2,3},{3,0},{4,5},{5,6},{6,7},{7,4},{8,9},{9,10},{10,1... | collective-permute-start | bytes 32096 | tf_op jit(solution)/shard_map/ppermute | solution.py:1047
  13.7 20.7 %collective-permute-start.3 = (bf16[5348]{0:T(1024)(128)(2,1)S(1)}, bf16[5348]{0:T(1024)(128)(2,1)S(1)}, u32[]{:S(2)}, u32[]{:S(2)}) collective-permute-start(bf16[5348]{0:T(1024)(128)(2,1)S(1)} %concatenate.29), channel_id=1, source_target_pairs={{0,2},{1,3},{2,0},{3,1},{4,6},{5,7},{6,4},{7,5},{8,10},{9,11},{10,... | collective-permute-start | bytes 32096 | tf_op jit(solution)/shard_map/ppermute | solution.py:1047
  13.7 20.7 %collective-permute-start.4 = (bf16[5348]{0:T(1024)(128)(2,1)S(1)}, bf16[5348]{0:T(1024)(128)(2,1)S(1)}, u32[]{:S(2)}, u32[]{:S(2)}) collective-permute-start(bf16[5348]{0:T(1024)(128)(2,1)S(1)} %concatenate.29), channel_id=1, source_target_pairs={{0,3},{1,0},{2,1},{3,2},{4,7},{5,4},{6,5},{7,6},{8,11},{9,8},{10,9... | collective-permute-start | bytes 32096 | tf_op jit(solution)/shard_map/ppermute | solution.py:1047
  34.3 21.3 %collective-permute-start.5 = (bf16[1280,384]{1,0:T(8,128)(2,1)S(1)}, bf16[1280,384]{1,0:T(8,128)(2,1)S(1)}, u32[]{:S(2)}, u32[]{:S(2)}) collective-permute-start(bf16[1280,384]{1,0:T(8,128)(2,1)S(1)} %get-tuple-element.276.refs_1_), channel_id=1, source_target_pairs={{0,1},{1,0},{2,3},{3,2},{8,9},{9,8},{10,11},{11,10},{4,5},{5,4},{6... | collective-permute-start | bytes 2949128 | tf_op jit(solution)/shard_map/ppermute | solution.py:867
  35.3 20.4 %collective-permute-start.6 = (bf16[1280,384]{1,0:T(8,128)(2,1)S(1)}, bf16[1280,384]{1,0:T(8,128)(2,1)S(1)}, u32[]{:S(2)}, u32[]{:S(2)}) collective-permute-start(bf16[1280,384]{1,0:T(8,128)(2,1)S(1)} %get-tuple-element.276.refs_1_), channel_id=1, source_target_pairs={{1,2},{2,1},{9,10},{10,9},{5,6},{6,5},{13,14},{14,13},{17,18},{18,... | collective-permute-start | bytes 2949128 | tf_op jit(solution)/shard_map/ppermute | solution.py:867
  36.0 21.8 %collective-permute-start.7 = (bf16[1280,384]{1,0:T(8,128)(2,1)}, bf16[1280,384]{1,0:T(8,128)(2,1)S(1)}, u32[]{:S(2)}, u32[]{:S(2)}) collective-permute-start(bf16[1280,384]{1,0:T(8,128)(2,1)} %collective-permute-done.refs_4_), channel_id=1, source_target_pairs={{0,8},{1,9},{2,10},{3,11},{8,0},{9,1},{10,2},{11,3},{4,12},{5,13},... | collective-permute-start | bytes 2949128 | tf_op jit(solution)/shard_map/ppermute | solution.py:871
  57.8 20.6 %collective-permute-start.10 = (bf16[1280,384]{1,0:T(8,128)(2,1)S(1)}, bf16[1280,384]{1,0:T(8,128)(2,1)S(1)}, u32[]{:S(2)}, u32[]{:S(2)}) collective-permute-start(bf16[1280,384]{1,0:T(8,128)(2,1)S(1)} %collective-permute-done.5.refs_5_), channel_id=1, source_target_pairs={{0,8},{1,9},{2,10},{3,11},{8,0},{9,1},{10,2},{11,3},{4,12},{5,13},... | collective-permute-start | bytes 2949128 | tf_op jit(solution)/shard_map/ppermute | solution.py:871
  59.0 21.3 %collective-permute-start.8 = (bf16[1280,384]{1,0:T(8,128)(2,1)}, bf16[1280,384]{1,0:T(8,128)(2,1)S(1)}, u32[]{:S(2)}, u32[]{:S(2)}) collective-permute-start(bf16[1280,384]{1,0:T(8,128)(2,1)} %collective-permute-done.1.refs_8_), channel_id=1, source_target_pairs={{1,0},{2,3},{9,8},{10,11},{5,4},{6,7},{13,12},{14,15},{17,16},{18,... | collective-permute-start | bytes 2949128 | tf_op jit(solution)/shard_map/ppermute | solution.py:867
  60.3 20.0 %collective-permute-start.9 = (bf16[1280,384]{1,0:T(8,128)(2,1)}, bf16[1280,384]{1,0:T(8,128)(2,1)S(1)}, u32[]{:S(2)}, u32[]{:S(2)}) collective-permute-start(bf16[1280,384]{1,0:T(8,128)(2,1)} %collective-permute-done.refs_4_), channel_id=1, source_target_pairs={{1,2},{2,1},{9,10},{10,9},{5,6},{6,5},{13,14},{14,13},{17,18},{18,... | collective-permute-start | bytes 2949128 | tf_op jit(solution)/shard_map/ppermute | solution.py:867
  80.3 21.1 %collective-permute-start.11 = (bf16[1280,384]{1,0:T(8,128)(2,1)S(1)}, bf16[1280,384]{1,0:T(8,128)(2,1)S(1)}, u32[]{:S(2)}, u32[]{:S(2)}) collective-permute-start(bf16[1280,384]{1,0:T(8,128)(2,1)S(1)} %collective-permute-done.6.refs_9_), channel_id=1, source_target_pairs={{1,0},{2,3},{9,8},{10,11},{5,4},{6,7},{13,12},{14,15},{17,16},{18,... | collective-permute-start | bytes 2949128 | tf_op jit(solution)/shard_map/ppermute | solution.py:867
  81.6 19.8 %collective-permute-start.12 = (bf16[1280,384]{1,0:T(8,128)(2,1)S(1)}, bf16[1280,384]{1,0:T(8,128)(2,1)}, u32[]{:S(2)}, u32[]{:S(2)}) collective-permute-start(bf16[1280,384]{1,0:T(8,128)(2,1)S(1)} %collective-permute-done.5.refs_5_), channel_id=1, source_target_pairs={{1,2},{2,1},{9,10},{10,9},{5,6},{6,5},{13,14},{14,13},{17,18},{18,... | collective-permute-start | bytes 2949128 | tf_op jit(solution)/shard_map/ppermute | solution.py:867
  83.3 20.1 %collective-permute-start.13 = (bf16[1280,384]{1,0:T(8,128)(2,1)S(1)}, bf16[1280,384]{1,0:T(8,128)(2,1)S(1)}, u32[]{:S(2)}, u32[]{:S(2)}) collective-permute-start(bf16[1280,384]{1,0:T(8,128)(2,1)S(1)} %collective-permute-done.8.refs_12_), channel_id=1, source_target_pairs={{0,8},{3,11},{8,0},{11,3},{4,12},{7,15},{12,4},{15,7},{16,24},{19,... | collective-permute-start | bytes 2949128 | tf_op jit(solution)/shard_map/ppermute | solution.py:871
  103.4 22.8 %collective-permute-start.15 = (bf16[1280,384]{1,0:T(8,128)(2,1)S(1)}, bf16[1280,384]{1,0:T(8,128)(2,1)S(1)}, u32[]{:S(2)}, u32[]{:S(2)}) collective-permute-start(bf16[1280,384]{1,0:T(8,128)(2,1)S(1)} %collective-permute-done.9.refs_16_), channel_id=1, source_target_pairs={{1,0},{2,3},{9,8},{10,11},{5,4},{6,7},{13,12},{14,15},{17,16},{18,... | collective-permute-start | bytes 2949128 | tf_op jit(solution)/shard_map/ppermute | solution.py:867
  104.6 21.5 %collective-permute-start.16 = (bf16[1280,384]{1,0:T(8,128)(2,1)S(1)}, bf16[1280,384]{1,0:T(8,128)(2,1)S(1)}, u32[]{:S(2)}, u32[]{:S(2)}) collective-permute-start(bf16[1280,384]{1,0:T(8,128)(2,1)S(1)} %collective-permute-done.11.refs_13_), channel_id=1, source_target_pairs={{0,8},{3,11},{8,0},{11,3},{4,12},{7,15},{12,4},{15,7},{16,24},{19,... | collective-permute-start | bytes 2949128 | tf_op jit(solution)/shard_map/ppermute | solution.py:871
  106.9 19.3 %collective-permute-start.17 = (bf16[1280,384]{1,0:T(8,128)(2,1)S(1)}, bf16[1280,384]{1,0:T(8,128)(2,1)S(1)}, u32[]{:S(2)}, u32[]{:S(2)}) collective-permute-start(bf16[1280,384]{1,0:T(8,128)(2,1)S(1)} %collective-permute-done.6.refs_9_), channel_id=1, source_target_pairs={{1,9},{2,10},{9,1},{10,2},{5,13},{6,14},{13,5},{14,6},{17,25},{18,... | collective-permute-start | bytes 2949128 | tf_op jit(solution)/shard_map/ppermute | solution.py:871
  126.2 20.7 %collective-permute-start.22 = (bf16[1280,384]{1,0:T(8,128)(2,1)}, bf16[1280,384]{1,0:T(8,128)(2,1)}, u32[]{:S(2)}, u32[]{:S(2)}) collective-permute-start(bf16[1280,384]{1,0:T(8,128)(2,1)} %collective-permute-done.12.refs_17_), channel_id=1, source_target_pairs={{1,0},{2,3},{9,8},{10,11},{5,4},{6,7},{13,12},{14,15},{17,16},{18,... | collective-permute-start | bytes 2949128 | tf_op jit(solution)/shard_map/ppermute | solution.py:867
  127.5 19.4 %collective-permute-start.23 = (bf16[1280,384]{1,0:T(8,128)(2,1)S(1)}, bf16[1280,384]{1,0:T(8,128)(2,1)S(1)}, u32[]{:S(2)}, u32[]{:S(2)}) collective-permute-start(bf16[1280,384]{1,0:T(8,128)(2,1)S(1)} %collective-permute-done.15.refs_20_), channel_id=1, source_target_pairs={{0,8},{3,11},{8,0},{11,3},{4,12},{7,15},{12,4},{15,7},{16,24},{19,... | collective-permute-start | bytes 2949128 | tf_op jit(solution)/shard_map/ppermute | solution.py:871
  133.2 29.9 %collective-permute-start.18 = (bf16[256,1536]{1,0:T(8,128)(2,1)}, bf16[256,1536]{1,0:T(8,128)(2,1)}, u32[]{:S(2)}, u32[]{:S(2)}) collective-permute-start(bf16[256,1536]{1,0:T(8,128)(2,1)} %get-tuple-element.537), channel_id=1, source_target_pairs={{0,0},{1,4},{4,1},{5,5},{8,8},{9,12},{12,9},{13,13},{16,16},{17,20... | collective-permute-start | bytes 2359304 | tf_op jit(solution)/shard_map/ppermute | solution.py:1107
  147.0 30.6 %collective-permute-start.25 = (bf16[1280,384]{1,0:T(8,128)(2,1)}, bf16[1280,384]{1,0:T(8,128)(2,1)}, u32[]{:S(2)}, u32[]{:S(2)}) collective-permute-start(bf16[1280,384]{1,0:T(8,128)(2,1)} %collective-permute-done.12.refs_17_), channel_id=1, source_target_pairs={{1,9},{2,10},{9,1},{10,2},{5,13},{6,14},{13,5},{14,6},{17,25},{18,... | collective-permute-start | bytes 2949128 | tf_op jit(solution)/shard_map/ppermute | solution.py:871
  148.6 29.0 %collective-permute-start.26 = (bf16[1280,384]{1,0:T(8,128)(2,1)}, bf16[1280,384]{1,0:T(8,128)(2,1)}, u32[]{:S(2)}, u32[]{:S(2)}) collective-permute-start(bf16[1280,384]{1,0:T(8,128)(2,1)} %collective-permute-done.22.refs_21_), channel_id=1, source_target_pairs={{0,8},{3,11},{8,0},{11,3},{4,12},{7,15},{12,4},{15,7},{16,24},{19,... | collective-permute-start | bytes 2949128 | tf_op jit(solution)/shard_map/ppermute | solution.py:871
  151.7 25.9 %collective-permute-start.20 = (bf16[256,1536]{1,0:T(8,128)(2,1)}, bf16[256,1536]{1,0:T(8,128)(2,1)S(1)}, u32[]{:S(2)}, u32[]{:S(2)}) collective-permute-start(bf16[256,1536]{1,0:T(8,128)(2,1)} %get-tuple-element.537), channel_id=1, source_target_pairs={{2,0},{3,4},{6,1},{7,5},{10,8},{11,12},{14,9},{15,13},{18,16},{19,... | collective-permute-start | bytes 2359304 | tf_op jit(solution)/shard_map/ppermute | solution.py:1107
  153.0 19.7 %collective-permute-start.19 = (bf16[256,1536]{1,0:T(8,128)(2,1)}, bf16[256,1536]{1,0:T(8,128)(2,1)}, u32[]{:S(2)}, u32[]{:S(2)}) collective-permute-start(bf16[256,1536]{1,0:T(8,128)(2,1)} %get-tuple-element.536), channel_id=1, source_target_pairs={{0,2},{1,6},{4,3},{5,7},{8,10},{9,14},{12,11},{13,15},{16,18},{17,... | collective-permute-start | bytes 2359304 | tf_op jit(solution)/shard_map/ppermute | solution.py:1107
  178.9 24.2 %collective-permute-start.27 = (bf16[256,1536]{1,0:T(8,128)(2,1)S(1)}, bf16[256,1536]{1,0:T(8,128)(2,1)S(1)}, u32[]{:S(2)}, u32[]{:S(2)}) collective-permute-start(bf16[256,1536]{1,0:T(8,128)(2,1)S(1)} %broadcast_select_fusion.1), channel_id=1, source_target_pairs={{0,4},{4,0},{1,5},{5,1},{2,6},{6,2},{3,7},{7,3},{8,12},{12,8},{9,1... | collective-permute-start | bytes 2359304 | tf_op jit(solution)/shard_map/ppermute | solution.py:1041
  238.8 25.4 %collective-permute-start.33 = (bf16[128,1536]{1,0:T(8,128)(2,1)S(1)}, bf16[128,1536]{1,0:T(8,128)(2,1)S(1)}, u32[]{:S(2)}, u32[]{:S(2)}) collective-permute-start(bf16[128,1536]{1,0:T(8,128)(2,1)S(1)} %get-tuple-element.351), channel_id=1, source_target_pairs={{0,16},{1,17},{2,18},{3,19},{4,20},{5,21},{6,22},{7,23},{8,24},{9,... | collective-permute-start | bytes 1179656 | tf_op jit(solution)/shard_map/ppermute | solution.py:1161
  308.7 46.2 %collective-permute-start.44 = (bf16[128,1536]{1,0:T(8,128)(2,1)S(1)}, bf16[128,1536]{1,0:T(8,128)(2,1)S(1)}, u32[]{:S(2)}, u32[]{:S(2)}) collective-permute-start(bf16[128,1536]{1,0:T(8,128)(2,1)S(1)} %get-tuple-element.432), channel_id=1, source_target_pairs={{16,0},{17,1},{18,2},{19,3},{20,4},{21,5},{22,6},{23,7},{24,8},{25... | collective-permute-start | bytes 1179656 | tf_op jit(solution)/shard_map/ppermute | solution.py:1199
  358.2 21.2 %collective-permute-start.47 = (bf16[128,1536]{1,0:T(8,128)(2,1)S(1)}, bf16[128,1536]{1,0:T(8,128)(2,1)S(1)}, u32[]{:S(2)}, u32[]{:S(2)}) collective-permute-start(bf16[128,1536]{1,0:T(8,128)(2,1)S(1)} %get-tuple-element.447), channel_id=1, source_target_pairs={{16,0},{17,1},{18,2},{19,3},{20,4},{21,5},{22,6},{23,7},{24,8},{25... | collective-permute-start | bytes 1179656 | tf_op jit(solution)/shard_map/ppermute | solution.py:1199
  384.3 20.0 %collective-permute-start.50 = (bf16[128,1536]{1,0:T(8,128)(2,1)S(1)}, bf16[128,1536]{1,0:T(8,128)(2,1)S(1)}, u32[]{:S(2)}, u32[]{:S(2)}) collective-permute-start(bf16[128,1536]{1,0:T(8,128)(2,1)S(1)} %get-tuple-element.462), channel_id=1, source_target_pairs={{16,0},{17,1},{18,2},{19,3},{20,4},{21,5},{22,6},{23,7},{24,8},{25... | collective-permute-start | bytes 1179656 | tf_op jit(solution)/shard_map/ppermute | solution.py:1199
  409.0 19.6 %collective-permute-start.53 = (bf16[128,1536]{1,0:T(8,128)(2,1)S(1)}, bf16[128,1536]{1,0:T(8,128)(2,1)S(1)}, u32[]{:S(2)}, u32[]{:S(2)}) collective-permute-start(bf16[128,1536]{1,0:T(8,128)(2,1)S(1)} %get-tuple-element.477), channel_id=1, source_target_pairs={{16,0},{17,1},{18,2},{19,3},{20,4},{21,5},{22,6},{23,7},{24,8},{25... | collective-permute-start | bytes 1179656 | tf_op jit(solution)/shard_map/ppermute | solution.py:1199
  463.7 23.7 %collective-permute-start.56 = (bf16[1280,384]{1,0:T(8,128)(2,1)S(1)}, bf16[1280,384]{1,0:T(8,128)(2,1)S(1)}, u32[]{:S(2)}, u32[]{:S(2)}) collective-permute-start(bf16[1280,384]{1,0:T(8,128)(2,1)S(1)} %block_grad.17), channel_id=1, source_target_pairs={{0,8},{1,0},{2,1},{3,2},{11,3},{10,11},{9,10},{8,9},{4,12},{5,4},{... | collective-permute-start | bytes 2949128 | tf_op jit(solution)/shard_map/ppermute | solution.py:1249
  464.9 23.4 %collective-permute-start.55 = (bf16[1280,384]{1,0:T(8,128)(2,1)S(1)}, bf16[1280,384]{1,0:T(8,128)(2,1)S(1)}, u32[]{:S(2)}, u32[]{:S(2)}) collective-permute-start(bf16[1280,384]{1,0:T(8,128)(2,1)S(1)} %block_grad.16), channel_id=1, source_target_pairs={{0,1},{1,2},{2,3},{3,11},{11,10},{10,9},{9,8},{8,0},{4,5},{5,6},{6... | collective-permute-start | bytes 2949128 | tf_op jit(solution)/shard_map/ppermute | solution.py:1249
  488.6 22.1 %collective-permute-start.58 = (bf16[1280,384]{1,0:T(8,128)(2,1)S(1)}, bf16[1280,384]{1,0:T(8,128)(2,1)S(1)}, u32[]{:S(2)}, u32[]{:S(2)}) collective-permute-start(bf16[1280,384]{1,0:T(8,128)(2,1)S(1)} %add_convert_fusion.12), channel_id=1, source_target_pairs={{0,8},{1,0},{2,1},{3,2},{11,3},{10,11},{9,10},{8,9},{4,12},{5,4},{... | collective-permute-start | bytes 2949128 | tf_op jit(solution)/shard_map/ppermute | solution.py:1249
  489.9 21.5 %collective-permute-start.57 = (bf16[1280,384]{1,0:T(8,128)(2,1)S(1)}, bf16[1280,384]{1,0:T(8,128)(2,1)S(1)}, u32[]{:S(2)}, u32[]{:S(2)}) collective-permute-start(bf16[1280,384]{1,0:T(8,128)(2,1)S(1)} %add_convert_fusion.13), channel_id=1, source_target_pairs={{0,1},{1,2},{2,3},{3,11},{11,10},{10,9},{9,8},{8,0},{4,5},{5,6},{6... | collective-permute-start | bytes 2949128 | tf_op jit(solution)/shard_map/ppermute | solution.py:1249
  511.7 25.8 %collective-permute-start.62 = (bf16[1280,384]{1,0:T(8,128)(2,1)S(1)}, bf16[1280,384]{1,0:T(8,128)(2,1)S(1)}, u32[]{:S(2)}, u32[]{:S(2)}) collective-permute-start(bf16[1280,384]{1,0:T(8,128)(2,1)S(1)} %add_convert_fusion.10), channel_id=1, source_target_pairs={{0,8},{1,0},{2,1},{3,2},{11,3},{10,11},{9,10},{8,9},{4,12},{5,4},{... | collective-permute-start | bytes 2949128 | tf_op jit(solution)/shard_map/ppermute | solution.py:1249
  516.1 22.8 %collective-permute-start.61 = (bf16[1280,384]{1,0:T(8,128)(2,1)S(1)}, bf16[1280,384]{1,0:T(8,128)(2,1)S(1)}, u32[]{:S(2)}, u32[]{:S(2)}) collective-permute-start(bf16[1280,384]{1,0:T(8,128)(2,1)S(1)} %add_convert_fusion.11), channel_id=1, source_target_pairs={{0,1},{1,2},{2,3},{3,11},{11,10},{10,9},{9,8},{8,0},{4,5},{5,6},{6... | collective-permute-start | bytes 2949128 | tf_op jit(solution)/shard_map/ppermute | solution.py:1249
  539.2 21.9 %collective-permute-start.64 = (bf16[1280,384]{1,0:T(8,128)(2,1)S(1)}, bf16[1280,384]{1,0:T(8,128)(2,1)S(1)}, u32[]{:S(2)}, u32[]{:S(2)}) collective-permute-start(bf16[1280,384]{1,0:T(8,128)(2,1)S(1)} %add_convert_fusion.8), channel_id=1, source_target_pairs={{0,8},{1,0},{2,1},{3,2},{11,3},{10,11},{9,10},{8,9},{4,12},{5,4},{... | collective-permute-start | bytes 2949128 | tf_op jit(solution)/shard_map/ppermute | solution.py:1249
  539.8 21.6 %collective-permute-start.63 = (bf16[1280,384]{1,0:T(8,128)(2,1)S(1)}, bf16[1280,384]{1,0:T(8,128)(2,1)S(1)}, u32[]{:S(2)}, u32[]{:S(2)}) collective-permute-start(bf16[1280,384]{1,0:T(8,128)(2,1)S(1)} %add_convert_fusion.9), channel_id=1, source_target_pairs={{0,1},{1,2},{2,3},{3,11},{11,10},{10,9},{9,8},{8,0},{4,5},{5,6},{6... | collective-permute-start | bytes 2949128 | tf_op jit(solution)/shard_map/ppermute | solution.py:1249
  561.7 20.7 %collective-permute-start.66 = (bf16[1280,384]{1,0:T(8,128)(2,1)S(1)}, bf16[1280,384]{1,0:T(8,128)(2,1)S(1)}, u32[]{:S(2)}, u32[]{:S(2)}) collective-permute-start(bf16[1280,384]{1,0:T(8,128)(2,1)S(1)} %add_convert_fusion.6), channel_id=1, source_target_pairs={{0,8},{1,0},{2,1},{3,2},{11,3},{10,11},{9,10},{8,9},{4,12},{5,4},{... | collective-permute-start | bytes 2949128 | tf_op jit(solution)/shard_map/ppermute | solution.py:1249
  562.3 20.6 %collective-permute-start.65 = (bf16[1280,384]{1,0:T(8,128)(2,1)S(1)}, bf16[1280,384]{1,0:T(8,128)(2,1)S(1)}, u32[]{:S(2)}, u32[]{:S(2)}) collective-permute-start(bf16[1280,384]{1,0:T(8,128)(2,1)S(1)} %add_convert_fusion.7), channel_id=1, source_target_pairs={{0,1},{1,2},{2,3},{3,11},{11,10},{10,9},{9,8},{8,0},{4,5},{5,6},{6... | collective-permute-start | bytes 2949128 | tf_op jit(solution)/shard_map/ppermute | solution.py:1249
  583.1 19.8 %collective-permute-start.68 = (bf16[1280,384]{1,0:T(8,128)(2,1)S(1)}, bf16[1280,384]{1,0:T(8,128)(2,1)S(1)}, u32[]{:S(2)}, u32[]{:S(2)}) collective-permute-start(bf16[1280,384]{1,0:T(8,128)(2,1)S(1)} %add_convert_fusion.4), channel_id=1, source_target_pairs={{0,8},{1,0},{2,1},{3,2},{11,3},{10,11},{9,10},{8,9},{4,12},{5,4},{... | collective-permute-start | bytes 2949128 | tf_op jit(solution)/shard_map/ppermute | solution.py:1249
  583.9 19.3 %collective-permute-start.67 = (bf16[1280,384]{1,0:T(8,128)(2,1)S(1)}, bf16[1280,384]{1,0:T(8,128)(2,1)S(1)}, u32[]{:S(2)}, u32[]{:S(2)}) collective-permute-start(bf16[1280,384]{1,0:T(8,128)(2,1)S(1)} %add_convert_fusion.5), channel_id=1, source_target_pairs={{0,1},{1,2},{2,3},{3,11},{11,10},{10,9},{9,8},{8,0},{4,5},{5,6},{6... | collective-permute-start | bytes 2949128 | tf_op jit(solution)/shard_map/ppermute | solution.py:1249
  604.0 19.4 %collective-permute-start.69 = (bf16[1280,384]{1,0:T(8,128)(2,1)S(1)}, bf16[1280,384]{1,0:T(8,128)(2,1)S(1)}, u32[]{:S(2)}, u32[]{:S(2)}) collective-permute-start(bf16[1280,384]{1,0:T(8,128)(2,1)S(1)} %add_convert_fusion.3), channel_id=1, source_target_pairs={{0,1},{1,2},{2,3},{3,11},{11,10},{10,9},{9,8},{8,0},{4,5},{5,6},{6... | collective-permute-start | bytes 2949128 | tf_op jit(solution)/shard_map/ppermute | solution.py:1249
  623.6 42.8 %collective-permute-start.75 = (bf16[1280,384]{1,0:T(8,128)(2,1)S(1)}, bf16[1280,384]{1,0:T(8,128)(2,1)S(1)}, u32[]{:S(2)}, u32[]{:S(2)}) collective-permute-start(bf16[1280,384]{1,0:T(8,128)(2,1)S(1)} %add_convert_fusion.1.refs_0_), channel_id=1, source_target_pairs={{0,8},{8,0},{1,9},{9,1},{2,10},{10,2},{3,11},{11,3},{4,12},{12,4},... | collective-permute-start | bytes 2949128 | tf_op jit(solution)/shard_map/ppermute | solution.py:1041
  624.2 42.6 %collective-permute-start.78 = (bf16[1280,384]{1,0:T(8,128)(2,1)S(1)}, bf16[1280,384]{1,0:T(8,128)(2,1)}, u32[]{:S(2)}, u32[]{:S(2)}) collective-permute-start(bf16[1280,384]{1,0:T(8,128)(2,1)S(1)} %add_convert_fusion.refs_4_), channel_id=1, source_target_pairs={{0,8},{8,0},{1,9},{9,1},{2,10},{10,2},{3,11},{11,3},{4,12},{12,4},... | collective-permute-start | bytes 2949128 | tf_op jit(solution)/shard_map/ppermute | solution.py:1041
  625.1 30.2 %collective-permute-start.71 = (bf16[256,1536]{1,0:T(8,128)(2,1)S(1)}, bf16[256,1536]{1,0:T(8,128)(2,1)}, u32[]{:S(2)}, u32[]{:S(2)}) collective-permute-start(bf16[256,1536]{1,0:T(8,128)(2,1)S(1)} %pick.2), channel_id=1, source_target_pairs={{0,0},{4,1},{1,4},{5,5},{8,8},{12,9},{9,12},{13,13},{16,16},{20,17... | collective-permute-start | bytes 2359304 | tf_op jit(solution)/shard_map/ppermute | solution.py:1116
  634.0 22.8 %collective-permute-start.72 = (bf16[256,1536]{1,0:T(8,128)(2,1)S(1)}, bf16[256,1536]{1,0:T(8,128)(2,1)S(1)}, u32[]{:S(2)}, u32[]{:S(2)}) collective-permute-start(bf16[256,1536]{1,0:T(8,128)(2,1)S(1)} %pick.2), channel_id=1, source_target_pairs={{2,0},{6,1},{3,4},{7,5},{10,8},{14,9},{11,12},{15,13},{18,16},{22,... | collective-permute-start | bytes 2359304 | tf_op jit(solution)/shard_map/ppermute | solution.py:1116
  635.3 31.0 %collective-permute-start.73 = (bf16[256,1536]{1,0:T(8,128)(2,1)}, bf16[256,1536]{1,0:T(8,128)(2,1)S(1)}, u32[]{:S(2)}, u32[]{:S(2)}) collective-permute-start(bf16[256,1536]{1,0:T(8,128)(2,1)} %pick.3), channel_id=1, source_target_pairs={{0,2},{4,3},{1,6},{5,7},{8,10},{12,11},{9,14},{13,15},{16,18},{20,... | collective-permute-start | bytes 2359304 | tf_op jit(solution)/shard_map/ppermute | solution.py:1116
  (67 other events, 1143.8 us)

commit v4 on v3

--- a/solution.py
+++ b/solution.py
@@ -803,62 +803,75 @@
     )(scalars, away(w), steps, away(o))
 
 
-def place_kernel(sc, *refs):
-    blocks, (win, wout, sem) = [refs[2 * i : 2 * i + 2] for i in range(12)], refs[-3:]
+def put_block(sc, halves, z, y, win, wout, sem, start):
+    lanes = pl.ds(aligned(z * BLOCK), BLOCK)
+    copies, at = [], 0
+    for matrix, rows, first, step in PARTS:
+        for i, to, off, count in cut(at, rows):
+            if matrix == "in":
+                target = win.at[pl.ds(aligned(first + y * step + off), count), lanes]
+            else:
+                target = wout.at[lanes, pl.ds(aligned(first + y * step), BLOCK)]
+            source = halves[i].at[pl.ds(to, count)]
+            copies.append(fetch(source, target, sem.at[start + len(copies)]))
+        at += rows
+    return copies
+
+
+def place_kernel(which, sc, *refs):
+    win, wout, sem = refs[-3:]
+    blocks = [refs[2 * i : 2 * i + 2] for i in range(8 if which == 0 else 4)]
     side, place = sc[1], sc[2]
     inner = jnp.logical_and(place > 0, place < 3)
-    second = jnp.where(inner, 3 - place, jnp.where(place == 0, 2, 1))
-    third = jnp.where(place < 2, 3, 0)
 
     def put(number, block, z, y):
-        lanes = pl.ds(aligned(z * BLOCK), BLOCK)
-        copies, at = [], 0
-        for matrix, rows, first, step in PARTS:
-            for i, to, off, count in cut(at, rows):
-                if matrix == "in":
-                    span = pl.ds(aligned(first + y * step + off), count)
-                    target = win.at[span, lanes]
-                else:
-                    target = wout.at[lanes, pl.ds(aligned(first + y * step), BLOCK)]
-                source = blocks[block][i].at[pl.ds(to, count)]
-                copies.append(fetch(source, target, sem.at[8 * number + len(copies)]))
-            at += rows
-        return copies
-
-    beside = place + 1 - 2 * lax.rem(place, 2)
-    always = put(0, 0, place, side) + put(1, 1, place, 1 - side)
-    always += put(2, 2, beside, side) + put(3, 3, beside, 1 - side)
-
-    def rest(first):
-        copies = put(4, first, second, side) + put(5, first + 1, second, 1 - side)
-        copies += put(6, first + 4, third, side) + put(7, first + 5, third, 1 - side)
+        return put_block(sc, blocks[block], z, y, win, wout, sem, 8 * number)
+
+    always = []
+    if which == 0:
+        beside = place + 1 - 2 * lax.rem(place, 2)
+        always += put(0, 0, place, side) + put(1, 1, place, 1 - side)
+        always += put(2, 2, beside, side) + put(3, 3, beside, 1 - side)
+        from_z, first = jnp.where(inner, 3 - place, jnp.where(place == 0, 2, 1)), 4
+    else:
+        from_z, first = jnp.where(place < 2, 3, 0), 0
+
+    def rest(block):
+        copies = put(4, block, from_z, side) + put(5, block + 1, from_z, 1 - side)
         for copy in copies:
             copy.wait()
 
     @pl.when(inner)
     def _():
-        rest(4)
+        rest(first)
 
     @pl.when(jnp.logical_not(inner))
     def _():
-        rest(6)
+        rest(first + 2)
 
     for copy in always:
         copy.wait()
 
 
-def place_weights(here, blocks):
-    inputs = [away(half) for block in blocks for half in block]
+def place_weights(here, blocks, held):
+    inputs = [here] + [away(half) for block in blocks for half in block]
+    in_specs = [pl.BlockSpec(memory_space=pltpu.SMEM)] + [ANY] * (len(inputs) - 1)
+    aliases = {}
+    if held is not None:
+        aliases = {len(inputs): 0, len(inputs) + 1: 1}
+        inputs += [near(v) for v in held]
+        in_specs += [NEAR, NEAR]
     return pl.pallas_call(
-        place_kernel,
-        in_specs=[pl.BlockSpec(memory_space=pltpu.SMEM)] + [ANY] * len(inputs),
+        functools.partial(place_kernel, 0 if held is None else 1),
+        in_specs=in_specs,
         out_specs=[NEAR, NEAR],
         out_shape=[pltpu.VMEM((OWN_PROJ, D), BF16), pltpu.VMEM((OWN, D), BF16)],
-        scratch_shapes=[pltpu.SemaphoreType.DMA((64,))],
+        scratch_shapes=[pltpu.SemaphoreType.DMA((48,))],
+        input_output_aliases=aliases,
         compiler_params=pltpu.CompilerParams(vmem_limit_bytes=4 << 20),
         cost_estimate=LITTLE,
         name="place_weights",
-    )(here, *inputs)
+    )(*inputs)
 
 
 def line_gather(own, beside):
@@ -875,9 +888,11 @@
     barrier = lax.optimization_barrier
     a, b = own
     near_a, in2_a = along(a, pair), along(a, middle)
-    near_a, in2_a, b, *beside = barrier((near_a, in2_a, b, *beside))
+    near_a, in2_a, b = barrier((near_a, in2_a, b))
     near_b, in2_b, near_ya = along(b, pair), along(b, middle), across(near_a, range(4))
-    near_a, in2_a, near_b, in2_b, near_ya = barrier((near_a, in2_a, near_b, in2_b, near_ya))
+    near_a, in2_a, near_b, in2_b, near_ya, *beside = barrier(
+        (near_a, in2_a, near_b, in2_b, near_ya, *beside)
+    )
     out2_a, in3_a, near_yb = along(in2_a, outward), along(near_a, middle), across(near_b, range(4))
     out2_a, in3_a, near_yb, in2_a, near_b, in2_b = barrier(
         (out2_a, in3_a, near_yb, in2_a, near_b, in2_b)
@@ -887,12 +902,12 @@
     out2_b, in3_b, out2_ya, in2_ya, in3_a, in2_b = barrier(
         (out2_b, in3_b, out2_ya, in2_ya, in3_a, in2_b)
     )
+    ready = in2_ya
     out3_a = along(in3_a, outward)
     out2_yb, in2_yb = across(out2_b, outer), across(in2_b, inner)
     out3_a, out2_yb, in2_yb, in3_a, in3_b = barrier((out3_a, out2_yb, in2_yb, in3_a, in3_b))
     out3_b = along(in3_b, outward)
     out3_ya, in3_ya = across(out3_a, outer), across(in3_a, inner)
-    ready = out2_yb
     out3_b, out3_ya, in3_ya, in3_b = barrier((out3_b, out3_ya, in3_ya, in3_b))
     out3_yb, in3_yb = across(out3_b, outer), across(in3_b, inner)
     blocks = [
@@ -1117,12 +1132,12 @@
             for m in range(2)
         ]
 
+    matrices = place_weights(here, [packed_halves[:2], packed_halves[2:], *blocks[:6]], None)
     last = (blocks[7][1], blocks[9][1])
-    here, *got = lax.optimization_barrier((here, *bring(0), *bring(2), *last))
+    here, *got = lax.optimization_barrier((here, *bring(0), *bring(2), *last, *matrices))
     blocks[7], blocks[9] = (blocks[7][0], got[4]), (blocks[9][0], got[5])
     pieces = shared(got[:2]) + shared(got[2:4])
-    blocks = [packed_halves[:2], packed_halves[2:], *blocks]
-    win, wout = place_weights(here, blocks)
+    win, wout = place_weights(here, blocks[6:], got[6:])
     params = (gain, convp, headp, chanp, win, wout)
 
     def scalars(moment, lag, reverse):

time: 694 us -> 693 us (level)
  transfers between devices with their start and end apart: 81 -> 81, of which waited for: 39 -> 37; matrix products, arithmetic and copies ran while one was open for 2% -> 3% of each run, Pallas kernels for 30% -> 30%
where the time goes in v4:
time: 693 us; the launch traced here: 685 us
  Pallas kernels  265 us (38%)
  waiting for transfers between devices  243 us (35%)
  starting transfers between devices  141 us (20%)
  local copies, waits for them, and re-layouts  21.9 us (3%)
  other arithmetic  10.3 us (1%)
    pallas_call x26, Pallas kernels, chunk_call(): pl.pallas_call(kernel, in_specs=in_specs, out_specs=out_specs, out_shape=...  175 us
    pallas_call x16, Pallas kernels, block_grad(): pl.pallas_call(functools.partial(block_grad_kernel, row), grid_spec=pltpu...  70.5 us
    ppermute x14, waiting for transfers between devices, relay_shards(): came = lax.ppermute(sums[i], ('y', 'fsdp'), path).astype(F32)  67.6 us
    ppermute x10, waiting for transfers between devices, along(): return lax.ppermute(value, ('y', 'fsdp'), path)  57.5 us
    ppermute x4, waiting for transfers between devices, relay_shards(): moved[moment - 1] = lax.ppermute(result, 'section', [(1, 0)])  39 us
    ppermute x28, starting transfers between devices, swap(): return lax.ppermute(value, axis, [(0, 1), (1, 0)])  38.9 us
    ppermute x4, starting transfers between devices, bring(): lax.ppermute(local[m], ('core', 'fsdp'), route(first, m))  26.9 us
    ppermute x28, waiting for transfers between devices, swap(): return lax.ppermute(value, axis, [(0, 1), (1, 0)])  20.3 us
  transfers between devices with their start and end apart: 81, of which 37 were waited for; matrix products, arithmetic and copies ran while one was open for 3% of the time, Pallas kernels for 30%

profile of v4, /device:TPU:1, one launch (start us, length us, event | category | flops | bytes accessed | tf_op | source)
XLA Modules:
  0.0 684.7 jit_solution(7330676836032534982)
XLA Ops:
  10.1 19.9 %collective-permute-done.refs_4_ = bf16[1280,384]{1,0:T(8,128)(2,1)} collective-permute-done((bf16[1280,384]{1,0:T(8,128)(2,1)S(1)}, bf16[1280,384]{1,0:T(8,128)(2,1)}, u32[]{:S(2)}, u32[]{:S(2)}) %collective-permute-start) | collective-permute-done | bytes 983072 | tf_op jit(solution)/shard_map/ppermute | solution.py:880
  40.1 16.1 %collective-permute-done.5 = bf16[5348]{0:T(1024)(128)(2,1)S(1)} collective-permute-done((bf16[5348]{0:T(1024)(128)(2,1)S(1)}, bf16[5348]{0:T(1024)(128)(2,1)S(1)}, u32[]{:S(2)}, u32[]{:S(2)}) %collective-permute-start.5) | collective-permute-done | bytes 10728 | tf_op jit(solution)/shard_map/ppermute | solution.py:1062
  62.4 16.1 %collective-permute-done.10.refs_7_ = bf16[1280,384]{1,0:T(8,128)(2,1)S(1)} collective-permute-done((bf16[1280,384]{1,0:T(8,128)(2,1)}, bf16[1280,384]{1,0:T(8,128)(2,1)S(1)}, u32[]{:S(2)}, u32[]{:S(2)}) %collective-permute-start.10) | collective-permute-done | bytes 983072 | tf_op jit(solution)/shard_map/ppermute | solution.py:884
  87.2 15.3 %collective-permute-done.11.refs_13_ = bf16[1280,384]{1,0:T(8,128)(2,1)S(1)} collective-permute-done((bf16[1280,384]{1,0:T(8,128)(2,1)}, bf16[1280,384]{1,0:T(8,128)(2,1)S(1)}, u32[]{:S(2)}, u32[]{:S(2)}) %collective-permute-start.11) | collective-permute-done | bytes 983072 | tf_op jit(solution)/shard_map/ppermute | solution.py:880
  108.4 19.4 %collective-permute-done.19.refs_4_ = bf16[1280,384]{1,0:T(8,128)(2,1)S(1)} collective-permute-done((bf16[1280,384]{1,0:T(8,128)(2,1)S(1)}, bf16[1280,384]{1,0:T(8,128)(2,1)S(1)}, u32[]{:S(2)}, u32[]{:S(2)}) %collective-permute-start.19) | collective-permute-done | bytes 983072 | tf_op jit(solution)/shard_map/ppermute | solution.py:880
  134.8 14.1 %collective-permute-start.15 = (bf16[256,1536]{1,0:T(8,128)(2,1)}, bf16[256,1536]{1,0:T(8,128)(2,1)}, u32[]{:S(2)}, u32[]{:S(2)}) collective-permute-start(bf16[256,1536]{1,0:T(8,128)(2,1)} %get-tuple-element.545), channel_id=1, source_target_pairs={{0,0},{1,4},{4,1},{5,5},{8,8},{9,12},{12,9},{13,13},{16,16},{17,20... | collective-permute-start | bytes 2359304 | tf_op jit(solution)/shard_map/ppermute | solution.py:1122
  154.9 10.0 %collective-permute-start.16 = (bf16[256,1536]{1,0:T(8,128)(2,1)}, bf16[256,1536]{1,0:T(8,128)(2,1)}, u32[]{:S(2)}, u32[]{:S(2)}) collective-permute-start(bf16[256,1536]{1,0:T(8,128)(2,1)} %get-tuple-element.544), channel_id=1, source_target_pairs={{0,2},{1,6},{4,3},{5,7},{8,10},{9,14},{12,11},{13,15},{16,18},{17,... | collective-permute-start | bytes 2359304 | tf_op jit(solution)/shard_map/ppermute | solution.py:1122
  175.8 5.4 place_weights.2
  182.5 15.3 %collective-permute-start.27 = (bf16[256,1536]{1,0:T(8,128)(2,1)S(1)}, bf16[256,1536]{1,0:T(8,128)(2,1)S(1)}, u32[]{:S(2)}, u32[]{:S(2)}) collective-permute-start(bf16[256,1536]{1,0:T(8,128)(2,1)S(1)} %broadcast_select_fusion.1), channel_id=1, source_target_pairs={{0,4},{4,0},{1,5},{5,1},{2,6},{6,2},{3,7},{7,3},{8,12},{12,8},{9,1... | collective-permute-start | bytes 2359304 | tf_op jit(solution)/shard_map/ppermute | solution.py:1056
  201.9 12.7 %forward_chunk.6 = (bf16[256,1664]{1,0:T(8,128)(2,1)S(1)}, bf16[256,1536]{1,0:T(8,128)(2,1)S(1)}, f32[128,1536]{1,0:T(8,128)S(1)}, f32[8,1792]{1,0:T(8,128)S(1)}...) custom-call(s32[12,7]{1,0:T(8,128)S(1)} %reshape.193.sc, ...), custom_call_target="tpu_custom_call" | custom-call | flops 1048576 | bytes 65536 | tf_op jit(solution)/shard_map/forward_chunk/pallas_call | solution.py:557
  220.6 12.1 %forward_chunk.7 = (bf16[256,1664]{1,0:T(8,128)(2,1)S(1)}, bf16[256,1536]{1,0:T(8,128)(2,1)S(1)}, f32[128,1536]{1,0:T(8,128)S(1)}, f32[8,1792]{1,0:T(8,128)S(1)}...) custom-call(s32[12,7]{1,0:T(8,128)S(1)} %reshape.193.sc, ...), custom_call_target="tpu_custom_call", output_to_operand_aliasing={{4}: (12, {}), {5}: (13, {}), {6}: (14, {}), {7}: (15, {}),... | custom-call | flops 1048576 | bytes 65536 | tf_op jit(solution)/shard_map/forward_chunk/pallas_call | solution.py:557
  238.8 23.9 %forward_chunk.8 = (bf16[256,1664]{1,0:T(8,128)(2,1)S(1)}, bf16[256,1536]{1,0:T(8,128)(2,1)S(1)}, f32[128,1536]{1,0:T(8,128)S(1)}, f32[8,1792]{1,0:T(8,128)S(1)}...) custom-call(s32[12,7]{1,0:T(8,128)S(1)} %reshape.193.sc, ...), custom_call_target="tpu_custom_call", output_to_operand_aliasing={{4}: (12, {}), {5}: (13, {}), {6}: (14, {}), {7}: (15, {}),... | custom-call | flops 1048576 | bytes 65536 | tf_op jit(solution)/shard_map/forward_chunk/pallas_call | solution.py:557
  268.8 12.2 %forward_chunk.9 = (bf16[256,1664]{1,0:T(8,128)(2,1)S(1)}, bf16[256,1536]{1,0:T(8,128)(2,1)S(1)}, f32[128,1536]{1,0:T(8,128)S(1)}, f32[8,1792]{1,0:T(8,128)S(1)}...) custom-call(s32[12,7]{1,0:T(8,128)S(1)} %reshape.193.sc, ...), custom_call_target="tpu_custom_call", output_to_operand_aliasing={{4}: (12, {}), {5}: (13, {}), {6}: (14, {}), {7}: (15, {}),... | custom-call | flops 1048576 | bytes 65536 | tf_op jit(solution)/shard_map/forward_chunk/pallas_call | solution.py:557
  287.7 7.8 %collective-permute-done.39.refs_0_ = bf16[128,1536]{1,0:T(8,128)(2,1)S(1)} collective-permute-done((bf16[128,1536]{1,0:T(8,128)(2,1)S(1)}, bf16[128,1536]{1,0:T(8,128)(2,1)S(1)}, u32[]{:S(2)}, u32[]{:S(2)}) %collective-permute-start.39) | collective-permute-done | bytes 393248 | tf_op jit(solution)/shard_map/ppermute | solution.py:1176
  308.6 7.6 %backward_chunk.7 = (bf16[256,1536]{1,0:T(8,128)(2,1)S(1)}, bf16[256,1536]{1,0:T(8,128)(2,1)S(1)}, bf16[256,1536]{1,0:T(8,128)(2,1)S(1)}, f32[128,1536]{1,0:T(8,...) custom-call(s32[12,7]{1,0:T(8,128)S(1)} %reshape.193.sc, ...), custom_call_target="tpu_custom_call", output_to_operand_aliasing={{7}: (21, {}), {8}: (22, {})} | custom-call | flops 1048576 | bytes 65536 | tf_op jit(solution)/shard_map/backward_chunk/pallas_call | solution.py:557
  316.1 37.4 %collective-permute-done.44.refs_0_ = bf16[128,1536]{1,0:T(8,128)(2,1)S(1)} collective-permute-done((bf16[128,1536]{1,0:T(8,128)(2,1)S(1)}, bf16[128,1536]{1,0:T(8,128)(2,1)S(1)}, u32[]{:S(2)}, u32[]{:S(2)}) %collective-permute-start.44) | collective-permute-done | bytes 393248 | tf_op jit(solution)/shard_map/ppermute | solution.py:1214
  358.2 18.2 %backward_chunk.8 = (bf16[256,1536]{1,0:T(8,128)(2,1)S(1)}, bf16[256,1536]{1,0:T(8,128)(2,1)S(1)}, bf16[256,1536]{1,0:T(8,128)(2,1)S(1)}, f32[128,1536]{1,0:T(8,...) custom-call(s32[12,7]{1,0:T(8,128)S(1)} %reshape.193.sc, ...), custom_call_target="tpu_custom_call", output_to_operand_aliasing={{7}: (21, {}), {8}: (22, {})} | custom-call | flops 1048576 | bytes 65536 | tf_op jit(solution)/shard_map/backward_chunk/pallas_call | solution.py:557
  384.3 18.7 %backward_chunk.9 = (bf16[256,1536]{1,0:T(8,128)(2,1)S(1)}, bf16[256,1536]{1,0:T(8,128)(2,1)S(1)}, bf16[256,1536]{1,0:T(8,128)(2,1)S(1)}, f32[128,1536]{1,0:T(8,...) custom-call(s32[12,7]{1,0:T(8,128)S(1)} %reshape.193.sc, ...), custom_call_target="tpu_custom_call", output_to_operand_aliasing={{7}: (21, {}), {8}: (22, {})} | custom-call | flops 1048576 | bytes 65536 | tf_op jit(solution)/shard_map/backward_chunk/pallas_call | solution.py:557
  409.0 18.3 %backward_chunk.10 = (bf16[256,1536]{1,0:T(8,128)(2,1)S(1)}, bf16[256,1536]{1,0:T(8,128)(2,1)S(1)}, bf16[256,1536]{1,0:T(8,128)(2,1)S(1)}, f32[128,1536]{1,0:T(8...) custom-call(s32[12,7]{1,0:T(8,128)S(1)} %reshape.193.sc, ...), custom_call_target="tpu_custom_call", output_to_operand_aliasing={{7}: (21, {}), {8}: (22, {})} | custom-call | flops 1048576 | bytes 65536 | tf_op jit(solution)/shard_map/backward_chunk/pallas_call | solution.py:557
  429.1 19.8 %backward_chunk.11 = (bf16[256,1536]{1,0:T(8,128)(2,1)S(1)}, bf16[256,1536]{1,0:T(8,128)(2,1)S(1)}, bf16[256,1536]{1,0:T(8,128)(2,1)S(1)}, f32[128,1536]{1,0:T(8...) custom-call(s32[12,7]{1,0:T(8,128)S(1)} %reshape.193.sc, ...), custom_call_target="tpu_custom_call", output_to_operand_aliasing={{7}: (21, {}), {8}: (22, {})} | custom-call | flops 1048576 | bytes 65536 | tf_op jit(solution)/shard_map/backward_chunk/pallas_call | solution.py:557
  453.6 4.4 block_grad.16
  458.0 4.4 block_grad.17
  464.3 4.4 block_grad.19
  468.6 4.4 block_grad.18
  473.1 12.9 %collective-permute-done.56 = bf16[1280,384]{1,0:T(8,128)(2,1)S(1)} collective-permute-done((bf16[1280,384]{1,0:T(8,128)(2,1)S(1)}, bf16[1280,384]{1,0:T(8,128)(2,1)S(1)}, u32[]{:S(2)}, u32[]{:S(2)}) %collective-permute-start.56) | collective-permute-done | bytes 983072 | tf_op jit(solution)/shard_map/ppermute | solution.py:1264
  488.8 4.4 block_grad.21
  493.2 4.6 block_grad.20
  497.7 11.6 %collective-permute-done.58 = bf16[1280,384]{1,0:T(8,128)(2,1)S(1)} collective-permute-done((bf16[1280,384]{1,0:T(8,128)(2,1)S(1)}, bf16[1280,384]{1,0:T(8,128)(2,1)S(1)}, u32[]{:S(2)}, u32[]{:S(2)}) %collective-permute-start.58) | collective-permute-done | bytes 983072 | tf_op jit(solution)/shard_map/ppermute | solution.py:1264
  527.4 4.4 block_grad.23
  531.8 4.4 block_grad.22
  539.3 4.4 block_grad.25
  543.7 4.4 block_grad.24
  548.1 11.6 %collective-permute-done.64 = bf16[1280,384]{1,0:T(8,128)(2,1)S(1)} collective-permute-done((bf16[1280,384]{1,0:T(8,128)(2,1)S(1)}, bf16[1280,384]{1,0:T(8,128)(2,1)S(1)}, u32[]{:S(2)}, u32[]{:S(2)}) %collective-permute-start.64) | collective-permute-done | bytes 983072 | tf_op jit(solution)/shard_map/ppermute | solution.py:1264
  561.8 4.4 block_grad.27
  566.2 4.4 block_grad.26
  570.6 10.4 %collective-permute-done.66 = bf16[1280,384]{1,0:T(8,128)(2,1)S(1)} collective-permute-done((bf16[1280,384]{1,0:T(8,128)(2,1)S(1)}, bf16[1280,384]{1,0:T(8,128)(2,1)S(1)}, u32[]{:S(2)}, u32[]{:S(2)}) %collective-permute-start.66) | collective-permute-done | bytes 983072 | tf_op jit(solution)/shard_map/ppermute | solution.py:1264
  583.3 4.6 block_grad.29
  587.9 4.4 block_grad.28
  592.3 9.2 %collective-permute-done.68 = bf16[1280,384]{1,0:T(8,128)(2,1)S(1)} collective-permute-done((bf16[1280,384]{1,0:T(8,128)(2,1)S(1)}, bf16[1280,384]{1,0:T(8,128)(2,1)S(1)}, u32[]{:S(2)}, u32[]{:S(2)}) %collective-permute-start.68) | collective-permute-done | bytes 983072 | tf_op jit(solution)/shard_map/ppermute | solution.py:1264
  603.5 4.4 block_grad.31
  607.9 4.4 block_grad.30
  612.3 9.0 %collective-permute-done.70 = bf16[1280,384]{1,0:T(8,128)(2,1)S(1)} collective-permute-done((bf16[1280,384]{1,0:T(8,128)(2,1)S(1)}, bf16[1280,384]{1,0:T(8,128)(2,1)S(1)}, u32[]{:S(2)}, u32[]{:S(2)}) %collective-permute-start.70) | collective-permute-done | bytes 983072 | tf_op jit(solution)/shard_map/ppermute | solution.py:1264
  623.7 9.0 %collective-permute-start.71 = (bf16[256,1536]{1,0:T(8,128)(2,1)S(1)}, bf16[256,1536]{1,0:T(8,128)(2,1)S(1)}, u32[]{:S(2)}, u32[]{:S(2)}) collective-permute-start(bf16[256,1536]{1,0:T(8,128)(2,1)S(1)} %pick.2), channel_id=1, source_target_pairs={{0,0},{4,1},{1,4},{5,5},{8,8},{12,9},{9,12},{13,13},{16,16},{20,17... | collective-permute-start | bytes 2359304 | tf_op jit(solution)/shard_map/ppermute | solution.py:1131
  633.9 6.2 collective-permute-start.73
  640.1 14.8 %collective-permute-done.71 = bf16[256,1536]{1,0:T(8,128)(2,1)S(1)} collective-permute-done((bf16[256,1536]{1,0:T(8,128)(2,1)S(1)}, bf16[256,1536]{1,0:T(8,128)(2,1)S(1)}, u32[]{:S(2)}, u32[]{:S(2)}) %collective-permute-start.71) | collective-permute-done | bytes 786464 | tf_op jit(solution)/shard_map/ppermute | solution.py:1131
  656.4 7.9 %collective-permute-start.76 = (bf16[1280,384]{1,0:T(8,128)(2,1)S(1)}, bf16[1280,384]{1,0:T(8,128)(2,1)}, u32[]{:S(2)}, u32[]{:S(2)}) collective-permute-start(bf16[1280,384]{1,0:T(8,128)(2,1)S(1)} %add_convert_fusion.1.refs_0_), channel_id=1, source_target_pairs={{0,4},{4,0},{1,5},{5,1},{2,6},{6,2},{3,7},{7,3},{8,12},{12,8},{9,1... | collective-permute-start | bytes 2949128 | tf_op jit(solution)/shard_map/ppermute | solution.py:1056
  665.3 4.6 collective-permute-start.80
  673.3 7.9 %join_grads.1 = (f32[6448,384]{1,0:T(8,128)}, f32[768,1536]{1,0:T(8,128)}, f32[16,384]{1,0:T(8,128)S(1)}) custom-call(s32[2]{0:T(128)S(1)} %pad_add_fusion.sc, bf16[1280,384]{1,0:T(8,128)(2,1)S(1)} %add_convert_fusion.1.refs_0_, bf16[1280,384]{1,0:T(8,128)(2,1)S(1)} %collective-permute-done.75.refs_1_, bf16[1280,384]{1,0:T(8,128)(2,1)} %collective-permute-done.76.refs_2_, ...), custom_call_target="tpu_custom_call" | custom-call | flops 1048576 | bytes 65536 | tf_op jit(solution)/shard_map/join_grads/pallas_call | solution.py:1043
  (357 shorter events, 175.4 us)
Async XLA Ops:
  6.4 23.7 %collective-permute-start = (bf16[1280,384]{1,0:T(8,128)(2,1)S(1)}, bf16[1280,384]{1,0:T(8,128)(2,1)}, u32[]{:S(2)}, u32[]{:S(2)}) collective-permute-start(bf16[1280,384]{1,0:T(8,128)(2,1)S(1)} %get-tuple-element.276.refs_0_), channel_id=1, source_target_pairs={{0,1},{1,0},{2,3},{3,2},{8,9},{9,8},{10,11},{11,10},{4,5},{5,4},{6... | collective-permute-start | bytes 2949128 | tf_op jit(solution)/shard_map/ppermute | solution.py:880
  8.5 21.6 %collective-permute-start.1 = (bf16[1280,384]{1,0:T(8,128)(2,1)S(1)}, bf16[1280,384]{1,0:T(8,128)(2,1)}, u32[]{:S(2)}, u32[]{:S(2)}) collective-permute-start(bf16[1280,384]{1,0:T(8,128)(2,1)S(1)} %get-tuple-element.276.refs_0_), channel_id=1, source_target_pairs={{1,2},{2,1},{9,10},{10,9},{5,6},{6,5},{13,14},{14,13},{17,18},{18,... | collective-permute-start | bytes 2949128 | tf_op jit(solution)/shard_map/ppermute | solution.py:880
  30.1 29.0 %collective-permute-start.2 = (bf16[1280,384]{1,0:T(8,128)(2,1)S(1)}, bf16[1280,384]{1,0:T(8,128)(2,1)}, u32[]{:S(2)}, u32[]{:S(2)}) collective-permute-start(bf16[1280,384]{1,0:T(8,128)(2,1)S(1)} %get-tuple-element.280.refs_1_), channel_id=1, source_target_pairs={{0,1},{1,0},{2,3},{3,2},{8,9},{9,8},{10,11},{11,10},{4,5},{5,4},{6... | collective-permute-start | bytes 2949128 | tf_op jit(solution)/shard_map/ppermute | solution.py:880
  34.3 24.9 %collective-permute-start.3 = (bf16[1280,384]{1,0:T(8,128)(2,1)S(1)}, bf16[1280,384]{1,0:T(8,128)(2,1)}, u32[]{:S(2)}, u32[]{:S(2)}) collective-permute-start(bf16[1280,384]{1,0:T(8,128)(2,1)S(1)} %get-tuple-element.280.refs_1_), channel_id=1, source_target_pairs={{1,2},{2,1},{9,10},{10,9},{5,6},{6,5},{13,14},{14,13},{17,18},{18,... | collective-permute-start | bytes 2949128 | tf_op jit(solution)/shard_map/ppermute | solution.py:880
  35.9 23.3 %collective-permute-start.4 = (bf16[1280,384]{1,0:T(8,128)(2,1)}, bf16[1280,384]{1,0:T(8,128)(2,1)}, u32[]{:S(2)}, u32[]{:S(2)}) collective-permute-start(bf16[1280,384]{1,0:T(8,128)(2,1)} %collective-permute-done.refs_4_), channel_id=1, source_target_pairs={{0,8},{1,9},{2,10},{3,11},{8,0},{9,1},{10,2},{11,3},{4,12},{5,13},... | collective-permute-start | bytes 2949128 | tf_op jit(solution)/shard_map/ppermute | solution.py:884
  37.8 18.4 %collective-permute-start.5 = (bf16[5348]{0:T(1024)(128)(2,1)S(1)}, bf16[5348]{0:T(1024)(128)(2,1)S(1)}, u32[]{:S(2)}, u32[]{:S(2)}) collective-permute-start(bf16[5348]{0:T(1024)(128)(2,1)S(1)} %concatenate.29), channel_id=1, source_target_pairs={{0,1},{1,2},{2,3},{3,0},{4,5},{5,6},{6,7},{7,4},{8,9},{9,10},{10,1... | collective-permute-start | bytes 32096 | tf_op jit(solution)/shard_map/ppermute | solution.py:1062
  39.3 18.5 %collective-permute-start.6 = (bf16[5348]{0:T(1024)(128)(2,1)S(1)}, bf16[5348]{0:T(1024)(128)(2,1)S(1)}, u32[]{:S(2)}, u32[]{:S(2)}) collective-permute-start(bf16[5348]{0:T(1024)(128)(2,1)S(1)} %concatenate.29), channel_id=1, source_target_pairs={{0,2},{1,3},{2,0},{3,1},{4,6},{5,7},{6,4},{7,5},{8,10},{9,11},{10,... | collective-permute-start | bytes 32096 | tf_op jit(solution)/shard_map/ppermute | solution.py:1062
  59.2 19.4 %collective-permute-start.10 = (bf16[1280,384]{1,0:T(8,128)(2,1)}, bf16[1280,384]{1,0:T(8,128)(2,1)S(1)}, u32[]{:S(2)}, u32[]{:S(2)}) collective-permute-start(bf16[1280,384]{1,0:T(8,128)(2,1)} %collective-permute-done.2.refs_5_), channel_id=1, source_target_pairs={{0,8},{1,9},{2,10},{3,11},{8,0},{9,1},{10,2},{11,3},{4,12},{5,13},... | collective-permute-start | bytes 2949128 | tf_op jit(solution)/shard_map/ppermute | solution.py:884
  60.4 21.0 %collective-permute-start.8 = (bf16[1280,384]{1,0:T(8,128)(2,1)}, bf16[1280,384]{1,0:T(8,128)(2,1)S(1)}, u32[]{:S(2)}, u32[]{:S(2)}) collective-permute-start(bf16[1280,384]{1,0:T(8,128)(2,1)} %collective-permute-done.1.refs_8_), channel_id=1, source_target_pairs={{1,0},{2,3},{9,8},{10,11},{5,4},{6,7},{13,12},{14,15},{17,16},{18,... | collective-permute-start | bytes 2949128 | tf_op jit(solution)/shard_map/ppermute | solution.py:880
  61.7 19.7 %collective-permute-start.9 = (bf16[1280,384]{1,0:T(8,128)(2,1)}, bf16[1280,384]{1,0:T(8,128)(2,1)S(1)}, u32[]{:S(2)}, u32[]{:S(2)}) collective-permute-start(bf16[1280,384]{1,0:T(8,128)(2,1)} %collective-permute-done.refs_4_), channel_id=1, source_target_pairs={{1,2},{2,1},{9,10},{10,9},{5,6},{6,5},{13,14},{14,13},{17,18},{18,... | collective-permute-start | bytes 2949128 | tf_op jit(solution)/shard_map/ppermute | solution.py:880
  81.4 21.1 %collective-permute-start.11 = (bf16[1280,384]{1,0:T(8,128)(2,1)}, bf16[1280,384]{1,0:T(8,128)(2,1)S(1)}, u32[]{:S(2)}, u32[]{:S(2)}) collective-permute-start(bf16[1280,384]{1,0:T(8,128)(2,1)} %collective-permute-done.3.refs_9_), channel_id=1, source_target_pairs={{1,0},{2,3},{9,8},{10,11},{5,4},{6,7},{13,12},{14,15},{17,16},{18,... | collective-permute-start | bytes 2949128 | tf_op jit(solution)/shard_map/ppermute | solution.py:880
  82.7 19.8 %collective-permute-start.12 = (bf16[1280,384]{1,0:T(8,128)(2,1)}, bf16[1280,384]{1,0:T(8,128)(2,1)}, u32[]{:S(2)}, u32[]{:S(2)}) collective-permute-start(bf16[1280,384]{1,0:T(8,128)(2,1)} %collective-permute-done.2.refs_5_), channel_id=1, source_target_pairs={{1,2},{2,1},{9,10},{10,9},{5,6},{6,5},{13,14},{14,13},{17,18},{18,... | collective-permute-start | bytes 2949128 | tf_op jit(solution)/shard_map/ppermute | solution.py:880
  84.3 19.8 %collective-permute-start.13 = (bf16[1280,384]{1,0:T(8,128)(2,1)S(1)}, bf16[1280,384]{1,0:T(8,128)(2,1)S(1)}, u32[]{:S(2)}, u32[]{:S(2)}) collective-permute-start(bf16[1280,384]{1,0:T(8,128)(2,1)S(1)} %collective-permute-done.8.refs_12_), channel_id=1, source_target_pairs={{0,8},{3,11},{8,0},{11,3},{4,12},{7,15},{12,4},{15,7},{16,24},{19,... | collective-permute-start | bytes 2949128 | tf_op jit(solution)/shard_map/ppermute | solution.py:884
  104.1 23.6 %collective-permute-start.19 = (bf16[1280,384]{1,0:T(8,128)(2,1)S(1)}, bf16[1280,384]{1,0:T(8,128)(2,1)S(1)}, u32[]{:S(2)}, u32[]{:S(2)}) collective-permute-start(bf16[1280,384]{1,0:T(8,128)(2,1)S(1)} %collective-permute-done.9.refs_0_), channel_id=1, source_target_pairs={{1,0},{2,3},{9,8},{10,11},{5,4},{6,7},{13,12},{14,15},{17,16},{18,... | collective-permute-start | bytes 2949128 | tf_op jit(solution)/shard_map/ppermute | solution.py:880
  105.4 22.3 %collective-permute-start.20 = (bf16[1280,384]{1,0:T(8,128)(2,1)S(1)}, bf16[1280,384]{1,0:T(8,128)(2,1)S(1)}, u32[]{:S(2)}, u32[]{:S(2)}) collective-permute-start(bf16[1280,384]{1,0:T(8,128)(2,1)S(1)} %collective-permute-done.11.refs_13_), channel_id=1, source_target_pairs={{0,8},{3,11},{8,0},{11,3},{4,12},{7,15},{12,4},{15,7},{16,24},{19,... | collective-permute-start | bytes 2949128 | tf_op jit(solution)/shard_map/ppermute | solution.py:884
  107.6 20.1 %collective-permute-start.21 = (bf16[1280,384]{1,0:T(8,128)(2,1)}, bf16[1280,384]{1,0:T(8,128)(2,1)S(1)}, u32[]{:S(2)}, u32[]{:S(2)}) collective-permute-start(bf16[1280,384]{1,0:T(8,128)(2,1)} %collective-permute-done.3.refs_9_), channel_id=1, source_target_pairs={{1,9},{2,10},{9,1},{10,2},{5,13},{6,14},{13,5},{14,6},{17,25},{18,... | collective-permute-start | bytes 2949128 | tf_op jit(solution)/shard_map/ppermute | solution.py:884
  127.8 21.1 %collective-permute-start.22 = (bf16[1280,384]{1,0:T(8,128)(2,1)}, bf16[1280,384]{1,0:T(8,128)(2,1)}, u32[]{:S(2)}, u32[]{:S(2)}) collective-permute-start(bf16[1280,384]{1,0:T(8,128)(2,1)} %collective-permute-done.12.refs_1_), channel_id=1, source_target_pairs={{1,0},{2,3},{9,8},{10,11},{5,4},{6,7},{13,12},{14,15},{17,16},{18,... | collective-permute-start | bytes 2949128 | tf_op jit(solution)/shard_map/ppermute | solution.py:880
  129.1 19.8 %collective-permute-start.23 = (bf16[1280,384]{1,0:T(8,128)(2,1)S(1)}, bf16[1280,384]{1,0:T(8,128)(2,1)S(1)}, u32[]{:S(2)}, u32[]{:S(2)}) collective-permute-start(bf16[1280,384]{1,0:T(8,128)(2,1)S(1)} %collective-permute-done.19.refs_4_), channel_id=1, source_target_pairs={{0,8},{3,11},{8,0},{11,3},{4,12},{7,15},{12,4},{15,7},{16,24},{19,... | collective-permute-start | bytes 2949128 | tf_op jit(solution)/shard_map/ppermute | solution.py:884
  134.8 30.2 %collective-permute-start.15 = (bf16[256,1536]{1,0:T(8,128)(2,1)}, bf16[256,1536]{1,0:T(8,128)(2,1)}, u32[]{:S(2)}, u32[]{:S(2)}) collective-permute-start(bf16[256,1536]{1,0:T(8,128)(2,1)} %get-tuple-element.545), channel_id=1, source_target_pairs={{0,0},{1,4},{4,1},{5,5},{8,8},{9,12},{12,9},{13,13},{16,16},{17,20... | collective-permute-start | bytes 2359304 | tf_op jit(solution)/shard_map/ppermute | solution.py:1122
  148.9 32.3 %collective-permute-start.25 = (bf16[1280,384]{1,0:T(8,128)(2,1)}, bf16[1280,384]{1,0:T(8,128)(2,1)}, u32[]{:S(2)}, u32[]{:S(2)}) collective-permute-start(bf16[1280,384]{1,0:T(8,128)(2,1)} %collective-permute-done.12.refs_1_), channel_id=1, source_target_pairs={{1,9},{2,10},{9,1},{10,2},{5,13},{6,14},{13,5},{14,6},{17,25},{18,... | collective-permute-start | bytes 2949128 | tf_op jit(solution)/shard_map/ppermute | solution.py:884
  150.5 30.7 %collective-permute-start.26 = (bf16[1280,384]{1,0:T(8,128)(2,1)}, bf16[1280,384]{1,0:T(8,128)(2,1)}, u32[]{:S(2)}, u32[]{:S(2)}) collective-permute-start(bf16[1280,384]{1,0:T(8,128)(2,1)} %collective-permute-done.22.refs_5_), channel_id=1, source_target_pairs={{0,8},{3,11},{8,0},{11,3},{4,12},{7,15},{12,4},{15,7},{16,24},{19,... | collective-permute-start | bytes 2949128 | tf_op jit(solution)/shard_map/ppermute | solution.py:884
  153.6 27.6 %collective-permute-start.17 = (bf16[256,1536]{1,0:T(8,128)(2,1)}, bf16[256,1536]{1,0:T(8,128)(2,1)S(1)}, u32[]{:S(2)}, u32[]{:S(2)}) collective-permute-start(bf16[256,1536]{1,0:T(8,128)(2,1)} %get-tuple-element.545), channel_id=1, source_target_pairs={{2,0},{3,4},{6,1},{7,5},{10,8},{11,12},{14,9},{15,13},{18,16},{19,... | collective-permute-start | bytes 2359304 | tf_op jit(solution)/shard_map/ppermute | solution.py:1122
  154.9 26.3 %collective-permute-start.16 = (bf16[256,1536]{1,0:T(8,128)(2,1)}, bf16[256,1536]{1,0:T(8,128)(2,1)}, u32[]{:S(2)}, u32[]{:S(2)}) collective-permute-start(bf16[256,1536]{1,0:T(8,128)(2,1)} %get-tuple-element.544), channel_id=1, source_target_pairs={{0,2},{1,6},{4,3},{5,7},{8,10},{9,14},{12,11},{13,15},{16,18},{17,... | collective-permute-start | bytes 2359304 | tf_op jit(solution)/shard_map/ppermute | solution.py:1122
  182.5 19.1 %collective-permute-start.27 = (bf16[256,1536]{1,0:T(8,128)(2,1)S(1)}, bf16[256,1536]{1,0:T(8,128)(2,1)S(1)}, u32[]{:S(2)}, u32[]{:S(2)}) collective-permute-start(bf16[256,1536]{1,0:T(8,128)(2,1)S(1)} %broadcast_select_fusion.1), channel_id=1, source_target_pairs={{0,4},{4,0},{1,5},{5,1},{2,6},{6,2},{3,7},{7,3},{8,12},{12,8},{9,1... | collective-permute-start | bytes 2359304 | tf_op jit(solution)/shard_map/ppermute | solution.py:1056
  237.4 25.4 %collective-permute-start.33 = (bf16[128,1536]{1,0:T(8,128)(2,1)S(1)}, bf16[128,1536]{1,0:T(8,128)(2,1)S(1)}, u32[]{:S(2)}, u32[]{:S(2)}) collective-permute-start(bf16[128,1536]{1,0:T(8,128)(2,1)S(1)} %get-tuple-element.359), channel_id=1, source_target_pairs={{0,16},{1,17},{2,18},{3,19},{4,20},{5,21},{6,22},{7,23},{8,24},{9,... | collective-permute-start | bytes 1179656 | tf_op jit(solution)/shard_map/ppermute | solution.py:1176
  307.3 46.3 %collective-permute-start.44 = (bf16[128,1536]{1,0:T(8,128)(2,1)S(1)}, bf16[128,1536]{1,0:T(8,128)(2,1)S(1)}, u32[]{:S(2)}, u32[]{:S(2)}) collective-permute-start(bf16[128,1536]{1,0:T(8,128)(2,1)S(1)} %get-tuple-element.440), channel_id=1, source_target_pairs={{16,0},{17,1},{18,2},{19,3},{20,4},{21,5},{22,6},{23,7},{24,8},{25... | collective-permute-start | bytes 1179656 | tf_op jit(solution)/shard_map/ppermute | solution.py:1214
  356.9 21.2 %collective-permute-start.47 = (bf16[128,1536]{1,0:T(8,128)(2,1)S(1)}, bf16[128,1536]{1,0:T(8,128)(2,1)S(1)}, u32[]{:S(2)}, u32[]{:S(2)}) collective-permute-start(bf16[128,1536]{1,0:T(8,128)(2,1)S(1)} %get-tuple-element.455), channel_id=1, source_target_pairs={{16,0},{17,1},{18,2},{19,3},{20,4},{21,5},{22,6},{23,7},{24,8},{25... | collective-permute-start | bytes 1179656 | tf_op jit(solution)/shard_map/ppermute | solution.py:1214
  383.0 20.0 %collective-permute-start.50 = (bf16[128,1536]{1,0:T(8,128)(2,1)S(1)}, bf16[128,1536]{1,0:T(8,128)(2,1)S(1)}, u32[]{:S(2)}, u32[]{:S(2)}) collective-permute-start(bf16[128,1536]{1,0:T(8,128)(2,1)S(1)} %get-tuple-element.470), channel_id=1, source_target_pairs={{16,0},{17,1},{18,2},{19,3},{20,4},{21,5},{22,6},{23,7},{24,8},{25... | collective-permute-start | bytes 1179656 | tf_op jit(solution)/shard_map/ppermute | solution.py:1214
  407.7 19.6 %collective-permute-start.53 = (bf16[128,1536]{1,0:T(8,128)(2,1)S(1)}, bf16[128,1536]{1,0:T(8,128)(2,1)S(1)}, u32[]{:S(2)}, u32[]{:S(2)}) collective-permute-start(bf16[128,1536]{1,0:T(8,128)(2,1)S(1)} %get-tuple-element.485), channel_id=1, source_target_pairs={{16,0},{17,1},{18,2},{19,3},{20,4},{21,5},{22,6},{23,7},{24,8},{25... | collective-permute-start | bytes 1179656 | tf_op jit(solution)/shard_map/ppermute | solution.py:1214
  462.4 23.6 %collective-permute-start.56 = (bf16[1280,384]{1,0:T(8,128)(2,1)S(1)}, bf16[1280,384]{1,0:T(8,128)(2,1)S(1)}, u32[]{:S(2)}, u32[]{:S(2)}) collective-permute-start(bf16[1280,384]{1,0:T(8,128)(2,1)S(1)} %block_grad.17), channel_id=1, source_target_pairs={{0,8},{1,0},{2,1},{3,2},{11,3},{10,11},{9,10},{8,9},{4,12},{5,4},{... | collective-permute-start | bytes 2949128 | tf_op jit(solution)/shard_map/ppermute | solution.py:1264
  463.6 23.4 %collective-permute-start.55 = (bf16[1280,384]{1,0:T(8,128)(2,1)S(1)}, bf16[1280,384]{1,0:T(8,128)(2,1)S(1)}, u32[]{:S(2)}, u32[]{:S(2)}) collective-permute-start(bf16[1280,384]{1,0:T(8,128)(2,1)S(1)} %block_grad.16), channel_id=1, source_target_pairs={{0,1},{1,2},{2,3},{3,11},{11,10},{10,9},{9,8},{8,0},{4,5},{5,6},{6... | collective-permute-start | bytes 2949128 | tf_op jit(solution)/shard_map/ppermute | solution.py:1264
  487.3 22.1 %collective-permute-start.58 = (bf16[1280,384]{1,0:T(8,128)(2,1)S(1)}, bf16[1280,384]{1,0:T(8,128)(2,1)S(1)}, u32[]{:S(2)}, u32[]{:S(2)}) collective-permute-start(bf16[1280,384]{1,0:T(8,128)(2,1)S(1)} %add_convert_fusion.12), channel_id=1, source_target_pairs={{0,8},{1,0},{2,1},{3,2},{11,3},{10,11},{9,10},{8,9},{4,12},{5,4},{... | collective-permute-start | bytes 2949128 | tf_op jit(solution)/shard_map/ppermute | solution.py:1264
  488.5 21.5 %collective-permute-start.57 = (bf16[1280,384]{1,0:T(8,128)(2,1)S(1)}, bf16[1280,384]{1,0:T(8,128)(2,1)S(1)}, u32[]{:S(2)}, u32[]{:S(2)}) collective-permute-start(bf16[1280,384]{1,0:T(8,128)(2,1)S(1)} %add_convert_fusion.13), channel_id=1, source_target_pairs={{0,1},{1,2},{2,3},{3,11},{11,10},{10,9},{9,8},{8,0},{4,5},{5,6},{6... | collective-permute-start | bytes 2949128 | tf_op jit(solution)/shard_map/ppermute | solution.py:1264
  510.2 26.0 %collective-permute-start.62 = (bf16[1280,384]{1,0:T(8,128)(2,1)S(1)}, bf16[1280,384]{1,0:T(8,128)(2,1)S(1)}, u32[]{:S(2)}, u32[]{:S(2)}) collective-permute-start(bf16[1280,384]{1,0:T(8,128)(2,1)S(1)} %add_convert_fusion.10), channel_id=1, source_target_pairs={{0,8},{1,0},{2,1},{3,2},{11,3},{10,11},{9,10},{8,9},{4,12},{5,4},{... | collective-permute-start | bytes 2949128 | tf_op jit(solution)/shard_map/ppermute | solution.py:1264
  514.7 22.8 %collective-permute-start.61 = (bf16[1280,384]{1,0:T(8,128)(2,1)S(1)}, bf16[1280,384]{1,0:T(8,128)(2,1)S(1)}, u32[]{:S(2)}, u32[]{:S(2)}) collective-permute-start(bf16[1280,384]{1,0:T(8,128)(2,1)S(1)} %add_convert_fusion.11), channel_id=1, source_target_pairs={{0,1},{1,2},{2,3},{3,11},{11,10},{10,9},{9,8},{8,0},{4,5},{5,6},{6... | collective-permute-start | bytes 2949128 | tf_op jit(solution)/shard_map/ppermute | solution.py:1264
  537.8 21.9 %collective-permute-start.64 = (bf16[1280,384]{1,0:T(8,128)(2,1)S(1)}, bf16[1280,384]{1,0:T(8,128)(2,1)S(1)}, u32[]{:S(2)}, u32[]{:S(2)}) collective-permute-start(bf16[1280,384]{1,0:T(8,128)(2,1)S(1)} %add_convert_fusion.8), channel_id=1, source_target_pairs={{0,8},{1,0},{2,1},{3,2},{11,3},{10,11},{9,10},{8,9},{4,12},{5,4},{... | collective-permute-start | bytes 2949128 | tf_op jit(solution)/shard_map/ppermute | solution.py:1264
  538.4 21.6 %collective-permute-start.63 = (bf16[1280,384]{1,0:T(8,128)(2,1)S(1)}, bf16[1280,384]{1,0:T(8,128)(2,1)S(1)}, u32[]{:S(2)}, u32[]{:S(2)}) collective-permute-start(bf16[1280,384]{1,0:T(8,128)(2,1)S(1)} %add_convert_fusion.9), channel_id=1, source_target_pairs={{0,1},{1,2},{2,3},{3,11},{11,10},{10,9},{9,8},{8,0},{4,5},{5,6},{6... | collective-permute-start | bytes 2949128 | tf_op jit(solution)/shard_map/ppermute | solution.py:1264
  560.3 20.7 %collective-permute-start.66 = (bf16[1280,384]{1,0:T(8,128)(2,1)S(1)}, bf16[1280,384]{1,0:T(8,128)(2,1)S(1)}, u32[]{:S(2)}, u32[]{:S(2)}) collective-permute-start(bf16[1280,384]{1,0:T(8,128)(2,1)S(1)} %add_convert_fusion.6), channel_id=1, source_target_pairs={{0,8},{1,0},{2,1},{3,2},{11,3},{10,11},{9,10},{8,9},{4,12},{5,4},{... | collective-permute-start | bytes 2949128 | tf_op jit(solution)/shard_map/ppermute | solution.py:1264
  560.9 20.6 %collective-permute-start.65 = (bf16[1280,384]{1,0:T(8,128)(2,1)S(1)}, bf16[1280,384]{1,0:T(8,128)(2,1)S(1)}, u32[]{:S(2)}, u32[]{:S(2)}) collective-permute-start(bf16[1280,384]{1,0:T(8,128)(2,1)S(1)} %add_convert_fusion.7), channel_id=1, source_target_pairs={{0,1},{1,2},{2,3},{3,11},{11,10},{10,9},{9,8},{8,0},{4,5},{5,6},{6... | collective-permute-start | bytes 2949128 | tf_op jit(solution)/shard_map/ppermute | solution.py:1264
  581.8 19.8 %collective-permute-start.68 = (bf16[1280,384]{1,0:T(8,128)(2,1)S(1)}, bf16[1280,384]{1,0:T(8,128)(2,1)S(1)}, u32[]{:S(2)}, u32[]{:S(2)}) collective-permute-start(bf16[1280,384]{1,0:T(8,128)(2,1)S(1)} %add_convert_fusion.4), channel_id=1, source_target_pairs={{0,8},{1,0},{2,1},{3,2},{11,3},{10,11},{9,10},{8,9},{4,12},{5,4},{... | collective-permute-start | bytes 2949128 | tf_op jit(solution)/shard_map/ppermute | solution.py:1264
  582.4 19.4 %collective-permute-start.67 = (bf16[1280,384]{1,0:T(8,128)(2,1)S(1)}, bf16[1280,384]{1,0:T(8,128)(2,1)S(1)}, u32[]{:S(2)}, u32[]{:S(2)}) collective-permute-start(bf16[1280,384]{1,0:T(8,128)(2,1)S(1)} %add_convert_fusion.5), channel_id=1, source_target_pairs={{0,1},{1,2},{2,3},{3,11},{11,10},{10,9},{9,8},{8,0},{4,5},{5,6},{6... | collective-permute-start | bytes 2949128 | tf_op jit(solution)/shard_map/ppermute | solution.py:1264
  602.0 19.3 %collective-permute-start.70 = (bf16[1280,384]{1,0:T(8,128)(2,1)S(1)}, bf16[1280,384]{1,0:T(8,128)(2,1)S(1)}, u32[]{:S(2)}, u32[]{:S(2)}) collective-permute-start(bf16[1280,384]{1,0:T(8,128)(2,1)S(1)} %add_convert_fusion.2), channel_id=1, source_target_pairs={{0,8},{1,0},{2,1},{3,2},{11,3},{10,11},{9,10},{8,9},{4,12},{5,4},{... | collective-permute-start | bytes 2949128 | tf_op jit(solution)/shard_map/ppermute | solution.py:1264
  602.5 19.4 %collective-permute-start.69 = (bf16[1280,384]{1,0:T(8,128)(2,1)S(1)}, bf16[1280,384]{1,0:T(8,128)(2,1)S(1)}, u32[]{:S(2)}, u32[]{:S(2)}) collective-permute-start(bf16[1280,384]{1,0:T(8,128)(2,1)S(1)} %add_convert_fusion.3), channel_id=1, source_target_pairs={{0,1},{1,2},{2,3},{3,11},{11,10},{10,9},{9,8},{8,0},{4,5},{5,6},{6... | collective-permute-start | bytes 2949128 | tf_op jit(solution)/shard_map/ppermute | solution.py:1264
  622.1 42.3 %collective-permute-start.75 = (bf16[1280,384]{1,0:T(8,128)(2,1)S(1)}, bf16[1280,384]{1,0:T(8,128)(2,1)S(1)}, u32[]{:S(2)}, u32[]{:S(2)}) collective-permute-start(bf16[1280,384]{1,0:T(8,128)(2,1)S(1)} %add_convert_fusion.1.refs_0_), channel_id=1, source_target_pairs={{0,8},{8,0},{1,9},{9,1},{2,10},{10,2},{3,11},{11,3},{4,12},{12,4},... | collective-permute-start | bytes 2949128 | tf_op jit(solution)/shard_map/ppermute | solution.py:1056
  622.7 42.1 %collective-permute-start.78 = (bf16[1280,384]{1,0:T(8,128)(2,1)S(1)}, bf16[1280,384]{1,0:T(8,128)(2,1)}, u32[]{:S(2)}, u32[]{:S(2)}) collective-permute-start(bf16[1280,384]{1,0:T(8,128)(2,1)S(1)} %add_convert_fusion.refs_4_), channel_id=1, source_target_pairs={{0,8},{8,0},{1,9},{9,1},{2,10},{10,2},{3,11},{11,3},{4,12},{12,4},... | collective-permute-start | bytes 2949128 | tf_op jit(solution)/shard_map/ppermute | solution.py:1056
  623.7 31.2 %collective-permute-start.71 = (bf16[256,1536]{1,0:T(8,128)(2,1)S(1)}, bf16[256,1536]{1,0:T(8,128)(2,1)S(1)}, u32[]{:S(2)}, u32[]{:S(2)}) collective-permute-start(bf16[256,1536]{1,0:T(8,128)(2,1)S(1)} %pick.2), channel_id=1, source_target_pairs={{0,0},{4,1},{1,4},{5,5},{8,8},{12,9},{9,12},{13,13},{16,16},{20,17... | collective-permute-start | bytes 2359304 | tf_op jit(solution)/shard_map/ppermute | solution.py:1131
  632.6 23.8 %collective-permute-start.72 = (bf16[256,1536]{1,0:T(8,128)(2,1)S(1)}, bf16[256,1536]{1,0:T(8,128)(2,1)S(1)}, u32[]{:S(2)}, u32[]{:S(2)}) collective-permute-start(bf16[256,1536]{1,0:T(8,128)(2,1)S(1)} %pick.2), channel_id=1, source_target_pairs={{2,0},{6,1},{3,4},{7,5},{10,8},{14,9},{11,12},{15,13},{18,16},{22,... | collective-permute-start | bytes 2359304 | tf_op jit(solution)/shard_map/ppermute | solution.py:1131
  633.9 30.4 %collective-permute-start.73 = (bf16[256,1536]{1,0:T(8,128)(2,1)}, bf16[256,1536]{1,0:T(8,128)(2,1)S(1)}, u32[]{:S(2)}, u32[]{:S(2)}) collective-permute-start(bf16[256,1536]{1,0:T(8,128)(2,1)} %pick.3), channel_id=1, source_target_pairs={{0,2},{4,3},{1,6},{5,7},{8,10},{12,11},{9,14},{13,15},{16,18},{20,... | collective-permute-start | bytes 2359304 | tf_op jit(solution)/shard_map/ppermute | solution.py:1131
  (72 other events, 1266.5 us)

commit v5 on v4

--- a/solution.py
+++ b/solution.py
@@ -101,13 +101,16 @@
     return out
 
 
-def pair_loop(step):
-    def two(turn, _):
-        step(2 * turn)
-        step(2 * turn + 1)
+def loop(count, step):
+    def turn(i, _):
+        step(i)
         return 0
 
-    lax.fori_loop(0, PAIRS // 2, two, 0)
+    lax.fori_loop(0, count, turn, 0)
+
+
+def by_blocks(total, step):
+    loop(total // 512, lambda i: step(pl.ds(pl.multiple_of(i * 512, 512), 512)))
 
 
 def aligned(value):
@@ -175,9 +178,10 @@
     stores.append(fetch(tl, tl_hbm.at[slot], sem.at[3]))
     xw[0:8, :] = tl[...]
 
-    for at in range(0, OWN_PROJ, 512):
-        cols = slice(at, min(at + 512, OWN_PROJ))
+    def project(cols):
         pr[:, cols] = dot_nt(normed[...], win[cols, :]).astype(BF16)
+
+    by_blocks(OWN_PROJ, project)
     stores.append(fetch(pr, pr_hbm.at[slot], sem.at[4]))
     tail_out[...] = pr[t - 8 : t, X_AT : X_AT + OWN_CONV].astype(F32)
 
@@ -226,15 +230,17 @@
         ss[...] += gated * gated
         q[:, sl] = (gated * chanp[1:2, sl]).astype(BF16)
 
-    pair_loop(pair_step)
+    loop(PAIRS, pair_step)
     stores.append(fetch(mx, mx_hbm.at[slot], sem.at[5]))
     stores.append(fetch(q, q_hbm.at[slot], sem.at[6]))
     total = jnp.sum(ss[...], axis=1, keepdims=True)
     high = total.astype(BF16).astype(F32)
     lane = lax.broadcasted_iota(jnp.int32, (t, LANES), 1)
     p[:, D:] = jnp.where(lane == 0, high, jnp.where(lane == 1, total - high, 0.0)).astype(BF16)
-    for at in range(0, D, 512):
-        p[:, at : at + 512] = dot(q[...], wout[:, at : at + 512]).astype(BF16)
+    def output(cols):
+        p[:, cols] = dot(q[...], wout[:, cols]).astype(BF16)
+
+    by_blocks(D, output)
     for store in stores:
         store.wait()
 
@@ -319,8 +325,10 @@
     def _():
         pltpu.make_async_copy(cot_hbm, g_ref, sem.at[0]).wait()
 
-    for at in range(0, OWN, 512):
-        gw[:, at : at + 512] = dot_nt(g_ref[...], wout[at : at + 512, :])
+    def output_back(cols):
+        gw[:, cols] = dot_nt(g_ref[...], wout[cols, :])
+
+    by_blocks(OWN, output_back)
     y_copy.wait()
     ri_copy.wait()
     rinv = ri[:, 0:1]
@@ -441,8 +449,8 @@
     zero = jnp.zeros((t, LANES), F32)
     ddt, dld, dval = lax.fori_loop(
         0,
-        PAIRS // 2,
-        lambda turn, carry: pair_step(2 * turn + 1, pair_step(2 * turn, carry)),
+        PAIRS,
+        pair_step,
         (zero, zero, jnp.zeros((8, LANES), F32)),
     )
 
@@ -465,11 +473,13 @@
     gp_store = fetch(gp, gp_hbm.at[sc[row, WRITE]], sem.at[0])
     dc_out[...] = dw[0:8, :]
     n_copy.wait()
-    for at in range(0, D, 512):
-        cols = slice(at, at + 512)
+
+    def project_back(cols):
         values = dot(gp[...], win[:, cols])
         gn[:, cols] = values.astype(BF16)
         add(9, cols, jnp.sum(values * normed[:, cols].astype(F32), axis=0, keepdims=True))
+
+    by_blocks(D, project_back)
     gp_store.wait()
     gs_store.wait()
     h_copy.wait()
@@ -1265,6 +1275,8 @@
                 block = (block.astype(F32) + came).astype(BF16)
             sums[i] = block
         if hop == 3:
+            owners, edge_held = lax.optimization_barrier((owners, edge_held))
+        if hop == 5:
             finished = pick(table, edge_held, 0), pick(table, edge_held, 2)
             owners, *finished = lax.optimization_barrier((owners, *finished))
     *sums, early, late = lax.optimization_barrier((*sums, *finished))

time: 693 us -> 717 us (1.035)
  waiting for transfers between devices: 243 us -> 254 us
  Pallas kernels: 265 us -> 275 us
    ppermute x4, waiting for transfers between devices: 39 us -> 50.3 us  [relay_shards(): moved[moment - 1] = lax.ppermute(result, 'section', [(1, 0)])]
    pallas_call x26, Pallas kernels: 175 us -> 185 us  [chunk_call(): pl.pallas_call(kernel, in_specs=in_specs, out_specs=out_specs, out_shape=...]
  transfers between devices with their start and end apart: 81 -> 81, of which waited for: 37 -> 36; matrix products, arithmetic and copies ran while one was open for 3% -> 2% of each run, Pallas kernels for 30% -> 30%
where the time goes in v5:
time: 717 us; the launch traced here: 705 us
  Pallas kernels  275 us (38%)
  waiting for transfers between devices  254 us (35%)
  starting transfers between devices  141 us (20%)
  local copies, waits for them, and re-layouts  21.9 us (3%)
  other arithmetic  10.3 us (1%)
    pallas_call x26, Pallas kernels, chunk_call(): pl.pallas_call(kernel, in_specs=in_specs, out_specs=out_specs, out_shape=...  185 us
    pallas_call x16, Pallas kernels, block_grad(): pl.pallas_call(functools.partial(block_grad_kernel, row), grid_spec=pltpu...  70.6 us
    ppermute x14, waiting for transfers between devices, relay_shards(): came = lax.ppermute(sums[i], ('y', 'fsdp'), path).astype(F32)  67.6 us
    ppermute x10, waiting for transfers between devices, along(): return lax.ppermute(value, ('y', 'fsdp'), path)  57.5 us
    ppermute x4, waiting for transfers between devices, relay_shards(): moved[moment - 1] = lax.ppermute(result, 'section', [(1, 0)])  50.3 us
    ppermute x28, starting transfers between devices, swap(): return lax.ppermute(value, axis, [(0, 1), (1, 0)])  38.7 us
    ppermute x4, starting transfers between devices, bring(): lax.ppermute(local[m], ('core', 'fsdp'), route(first, m))  26.9 us
    ppermute x28, waiting for transfers between devices, swap(): return lax.ppermute(value, axis, [(0, 1), (1, 0)])  20 us
  transfers between devices with their start and end apart: 81, of which 36 were waited for; matrix products, arithmetic and copies ran while one was open for 2% of the time, Pallas kernels for 30%

profile of v5, /device:TPU:1, one launch (start us, length us, event | category | flops | bytes accessed | tf_op | source)
XLA Modules:
  0.0 705.4 jit_solution(7332444498821016192)
XLA Ops:
  10.1 19.9 %collective-permute-done.refs_4_ = bf16[1280,384]{1,0:T(8,128)(2,1)} collective-permute-done((bf16[1280,384]{1,0:T(8,128)(2,1)S(1)}, bf16[1280,384]{1,0:T(8,128)(2,1)}, u32[]{:S(2)}, u32[]{:S(2)}) %collective-permute-start) | collective-permute-done | bytes 983072 | tf_op jit(solution)/shard_map/ppermute | solution.py:890
  40.1 16.1 %collective-permute-done.5 = bf16[5348]{0:T(1024)(128)(2,1)S(1)} collective-permute-done((bf16[5348]{0:T(1024)(128)(2,1)S(1)}, bf16[5348]{0:T(1024)(128)(2,1)S(1)}, u32[]{:S(2)}, u32[]{:S(2)}) %collective-permute-start.5) | collective-permute-done | bytes 10728 | tf_op jit(solution)/shard_map/ppermute | solution.py:1072
  62.4 16.1 %collective-permute-done.10.refs_7_ = bf16[1280,384]{1,0:T(8,128)(2,1)S(1)} collective-permute-done((bf16[1280,384]{1,0:T(8,128)(2,1)}, bf16[1280,384]{1,0:T(8,128)(2,1)S(1)}, u32[]{:S(2)}, u32[]{:S(2)}) %collective-permute-start.10) | collective-permute-done | bytes 983072 | tf_op jit(solution)/shard_map/ppermute | solution.py:894
  87.2 15.3 %collective-permute-done.11.refs_13_ = bf16[1280,384]{1,0:T(8,128)(2,1)S(1)} collective-permute-done((bf16[1280,384]{1,0:T(8,128)(2,1)}, bf16[1280,384]{1,0:T(8,128)(2,1)S(1)}, u32[]{:S(2)}, u32[]{:S(2)}) %collective-permute-start.11) | collective-permute-done | bytes 983072 | tf_op jit(solution)/shard_map/ppermute | solution.py:890
  108.4 19.4 %collective-permute-done.19.refs_4_ = bf16[1280,384]{1,0:T(8,128)(2,1)S(1)} collective-permute-done((bf16[1280,384]{1,0:T(8,128)(2,1)S(1)}, bf16[1280,384]{1,0:T(8,128)(2,1)S(1)}, u32[]{:S(2)}, u32[]{:S(2)}) %collective-permute-start.19) | collective-permute-done | bytes 983072 | tf_op jit(solution)/shard_map/ppermute | solution.py:890
  134.8 14.1 %collective-permute-start.15 = (bf16[256,1536]{1,0:T(8,128)(2,1)}, bf16[256,1536]{1,0:T(8,128)(2,1)}, u32[]{:S(2)}, u32[]{:S(2)}) collective-permute-start(bf16[256,1536]{1,0:T(8,128)(2,1)} %get-tuple-element.549), channel_id=1, source_target_pairs={{0,0},{1,4},{4,1},{5,5},{8,8},{9,12},{12,9},{13,13},{16,16},{17,20... | collective-permute-start | bytes 2359304 | tf_op jit(solution)/shard_map/ppermute | solution.py:1132
  154.9 10.0 %collective-permute-start.16 = (bf16[256,1536]{1,0:T(8,128)(2,1)}, bf16[256,1536]{1,0:T(8,128)(2,1)}, u32[]{:S(2)}, u32[]{:S(2)}) collective-permute-start(bf16[256,1536]{1,0:T(8,128)(2,1)} %get-tuple-element.548), channel_id=1, source_target_pairs={{0,2},{1,6},{4,3},{5,7},{8,10},{9,14},{12,11},{13,15},{16,18},{17,... | collective-permute-start | bytes 2359304 | tf_op jit(solution)/shard_map/ppermute | solution.py:1132
  175.8 5.4 place_weights.2
  182.5 15.3 %collective-permute-start.27 = (bf16[256,1536]{1,0:T(8,128)(2,1)S(1)}, bf16[256,1536]{1,0:T(8,128)(2,1)S(1)}, u32[]{:S(2)}, u32[]{:S(2)}) collective-permute-start(bf16[256,1536]{1,0:T(8,128)(2,1)S(1)} %broadcast_select_fusion.1), channel_id=1, source_target_pairs={{0,4},{4,0},{1,5},{5,1},{2,6},{6,2},{3,7},{7,3},{8,12},{12,8},{9,1... | collective-permute-start | bytes 2359304 | tf_op jit(solution)/shard_map/ppermute | solution.py:1066
  201.9 14.7 %forward_chunk.6 = (bf16[256,1664]{1,0:T(8,128)(2,1)S(1)}, bf16[256,1536]{1,0:T(8,128)(2,1)S(1)}, f32[128,1536]{1,0:T(8,128)S(1)}, f32[8,1792]{1,0:T(8,128)S(1)}...) custom-call(s32[12,7]{1,0:T(8,128)S(1)} %reshape.193.sc, ...), custom_call_target="tpu_custom_call" | custom-call | flops 1048576 | bytes 65536 | tf_op jit(solution)/shard_map/forward_chunk/pallas_call | solution.py:567
  222.6 15.0 %forward_chunk.7 = (bf16[256,1664]{1,0:T(8,128)(2,1)S(1)}, bf16[256,1536]{1,0:T(8,128)(2,1)S(1)}, f32[128,1536]{1,0:T(8,128)S(1)}, f32[8,1792]{1,0:T(8,128)S(1)}...) custom-call(s32[12,7]{1,0:T(8,128)S(1)} %reshape.193.sc, ...), custom_call_target="tpu_custom_call", output_to_operand_aliasing={{4}: (12, {}), {5}: (13, {}), {6}: (14, {}), {7}: (15, {}),... | custom-call | flops 1048576 | bytes 65536 | tf_op jit(solution)/shard_map/forward_chunk/pallas_call | solution.py:567
  243.7 14.7 %forward_chunk.8 = (bf16[256,1664]{1,0:T(8,128)(2,1)S(1)}, bf16[256,1536]{1,0:T(8,128)(2,1)S(1)}, f32[128,1536]{1,0:T(8,128)S(1)}, f32[8,1792]{1,0:T(8,128)S(1)}...) custom-call(s32[12,7]{1,0:T(8,128)S(1)} %reshape.193.sc, ...), custom_call_target="tpu_custom_call", output_to_operand_aliasing={{4}: (12, {}), {5}: (13, {}), {6}: (14, {}), {7}: (15, {}),... | custom-call | flops 1048576 | bytes 65536 | tf_op jit(solution)/shard_map/forward_chunk/pallas_call | solution.py:567
  264.4 14.7 %forward_chunk.9 = (bf16[256,1664]{1,0:T(8,128)(2,1)S(1)}, bf16[256,1536]{1,0:T(8,128)(2,1)S(1)}, f32[128,1536]{1,0:T(8,128)S(1)}, f32[8,1792]{1,0:T(8,128)S(1)}...) custom-call(s32[12,7]{1,0:T(8,128)S(1)} %reshape.193.sc, ...), custom_call_target="tpu_custom_call", output_to_operand_aliasing={{4}: (12, {}), {5}: (13, {}), {6}: (14, {}), {7}: (15, {}),... | custom-call | flops 1048576 | bytes 65536 | tf_op jit(solution)/shard_map/forward_chunk/pallas_call | solution.py:567
  286.0 7.8 %collective-permute-done.39.refs_0_ = bf16[128,1536]{1,0:T(8,128)(2,1)S(1)} collective-permute-done((bf16[128,1536]{1,0:T(8,128)(2,1)S(1)}, bf16[128,1536]{1,0:T(8,128)(2,1)S(1)}, u32[]{:S(2)}, u32[]{:S(2)}) %collective-permute-start.39) | collective-permute-done | bytes 393248 | tf_op jit(solution)/shard_map/ppermute | solution.py:1186
  297.9 11.5 %forward_join.10 = (bf16[128,1536]{1,0:T(8,128)(2,1)}, bf16[5,256,1536]{2,1,0:T(8,128)(2,1)}, f32[5,256,128]{2,1,0:T(8,128)}, bf16[5,256,1536]{2,1,0:T(8,128)(2,1)}) custom-call(s32[12,7]{1,0:T(8,128)S(1)} %reshape.193.sc, bf16[256,1664]{1,0:T(8,128)(2,1)S(1)} %get-tuple-element.419.own_ref, ...), custom_call_target="tpu_custom_call", output_to_operand_aliasing={{1}: (4, {}), {2}: (5, {}), {3}: (6, {})} | custom-call | flops 1048576 | bytes 65536 | tf_op jit(solution)/shard_map/forward_join/pallas_call | solution.py:567
  317.0 49.5 %collective-permute-done.44.refs_0_ = bf16[128,1536]{1,0:T(8,128)(2,1)S(1)} collective-permute-done((bf16[128,1536]{1,0:T(8,128)(2,1)S(1)}, bf16[128,1536]{1,0:T(8,128)(2,1)S(1)}, u32[]{:S(2)}, u32[]{:S(2)}) %collective-permute-start.44) | collective-permute-done | bytes 393248 | tf_op jit(solution)/shard_map/ppermute | solution.py:1224
  371.2 20.7 %backward_chunk.8 = (bf16[256,1536]{1,0:T(8,128)(2,1)S(1)}, bf16[256,1536]{1,0:T(8,128)(2,1)S(1)}, bf16[256,1536]{1,0:T(8,128)(2,1)S(1)}, f32[128,1536]{1,0:T(8,...) custom-call(s32[12,7]{1,0:T(8,128)S(1)} %reshape.193.sc, ...), custom_call_target="tpu_custom_call", output_to_operand_aliasing={{7}: (21, {}), {8}: (22, {})} | custom-call | flops 1048576 | bytes 65536 | tf_op jit(solution)/shard_map/backward_chunk/pallas_call | solution.py:567
  398.9 20.5 %backward_chunk.9 = (bf16[256,1536]{1,0:T(8,128)(2,1)S(1)}, bf16[256,1536]{1,0:T(8,128)(2,1)S(1)}, bf16[256,1536]{1,0:T(8,128)(2,1)S(1)}, f32[128,1536]{1,0:T(8,...) custom-call(s32[12,7]{1,0:T(8,128)S(1)} %reshape.193.sc, ...), custom_call_target="tpu_custom_call", output_to_operand_aliasing={{7}: (21, {}), {8}: (22, {})} | custom-call | flops 1048576 | bytes 65536 | tf_op jit(solution)/shard_map/backward_chunk/pallas_call | solution.py:567
  425.3 20.5 %backward_chunk.10 = (bf16[256,1536]{1,0:T(8,128)(2,1)S(1)}, bf16[256,1536]{1,0:T(8,128)(2,1)S(1)}, bf16[256,1536]{1,0:T(8,128)(2,1)S(1)}, f32[128,1536]{1,0:T(8...) custom-call(s32[12,7]{1,0:T(8,128)S(1)} %reshape.193.sc, ...), custom_call_target="tpu_custom_call", output_to_operand_aliasing={{7}: (21, {}), {8}: (22, {})} | custom-call | flops 1048576 | bytes 65536 | tf_op jit(solution)/shard_map/backward_chunk/pallas_call | solution.py:567
  447.6 21.9 %backward_chunk.11 = (bf16[256,1536]{1,0:T(8,128)(2,1)S(1)}, bf16[256,1536]{1,0:T(8,128)(2,1)S(1)}, bf16[256,1536]{1,0:T(8,128)(2,1)S(1)}, f32[128,1536]{1,0:T(8...) custom-call(s32[12,7]{1,0:T(8,128)S(1)} %reshape.193.sc, ...), custom_call_target="tpu_custom_call", output_to_operand_aliasing={{7}: (21, {}), {8}: (22, {})} | custom-call | flops 1048576 | bytes 65536 | tf_op jit(solution)/shard_map/backward_chunk/pallas_call | solution.py:567
  474.3 4.4 block_grad.16
  478.7 4.4 block_grad.17
  484.9 4.4 block_grad.19
  489.3 4.4 block_grad.18
  493.7 12.9 %collective-permute-done.56 = bf16[1280,384]{1,0:T(8,128)(2,1)S(1)} collective-permute-done((bf16[1280,384]{1,0:T(8,128)(2,1)S(1)}, bf16[1280,384]{1,0:T(8,128)(2,1)S(1)}, u32[]{:S(2)}, u32[]{:S(2)}) %collective-permute-start.56) | collective-permute-done | bytes 983072 | tf_op jit(solution)/shard_map/ppermute | solution.py:1274
  509.4 4.4 block_grad.21
  513.8 4.6 block_grad.20
  518.4 11.6 %collective-permute-done.58 = bf16[1280,384]{1,0:T(8,128)(2,1)S(1)} collective-permute-done((bf16[1280,384]{1,0:T(8,128)(2,1)S(1)}, bf16[1280,384]{1,0:T(8,128)(2,1)S(1)}, u32[]{:S(2)}, u32[]{:S(2)}) %collective-permute-start.58) | collective-permute-done | bytes 983072 | tf_op jit(solution)/shard_map/ppermute | solution.py:1274
  543.5 4.4 block_grad.23
  547.9 4.4 block_grad.22
  552.6 5.6 collective-permute-done.61
  560.0 4.4 block_grad.25
  564.4 4.4 block_grad.24
  568.7 11.6 %collective-permute-done.64 = bf16[1280,384]{1,0:T(8,128)(2,1)S(1)} collective-permute-done((bf16[1280,384]{1,0:T(8,128)(2,1)S(1)}, bf16[1280,384]{1,0:T(8,128)(2,1)S(1)}, u32[]{:S(2)}, u32[]{:S(2)}) %collective-permute-start.64) | collective-permute-done | bytes 983072 | tf_op jit(solution)/shard_map/ppermute | solution.py:1274
  587.0 4.4 block_grad.27
  595.8 5.9 collective-permute-done.66
  604.0 4.6 block_grad.29
  608.6 4.4 block_grad.28
  613.0 9.2 %collective-permute-done.68 = bf16[1280,384]{1,0:T(8,128)(2,1)S(1)} collective-permute-done((bf16[1280,384]{1,0:T(8,128)(2,1)S(1)}, bf16[1280,384]{1,0:T(8,128)(2,1)S(1)}, u32[]{:S(2)}, u32[]{:S(2)}) %collective-permute-start.68) | collective-permute-done | bytes 983072 | tf_op jit(solution)/shard_map/ppermute | solution.py:1274
  624.2 4.4 block_grad.31
  628.6 4.4 block_grad.30
  633.0 9.0 %collective-permute-done.70 = bf16[1280,384]{1,0:T(8,128)(2,1)S(1)} collective-permute-done((bf16[1280,384]{1,0:T(8,128)(2,1)S(1)}, bf16[1280,384]{1,0:T(8,128)(2,1)S(1)}, u32[]{:S(2)}, u32[]{:S(2)}) %collective-permute-start.70) | collective-permute-done | bytes 983072 | tf_op jit(solution)/shard_map/ppermute | solution.py:1274
  644.3 9.0 %collective-permute-start.71 = (bf16[256,1536]{1,0:T(8,128)(2,1)S(1)}, bf16[256,1536]{1,0:T(8,128)(2,1)S(1)}, u32[]{:S(2)}, u32[]{:S(2)}) collective-permute-start(bf16[256,1536]{1,0:T(8,128)(2,1)S(1)} %pick.2), channel_id=1, source_target_pairs={{0,0},{4,1},{1,4},{5,5},{8,8},{12,9},{9,12},{13,13},{16,16},{20,17... | collective-permute-start | bytes 2359304 | tf_op jit(solution)/shard_map/ppermute | solution.py:1141
  654.6 6.2 collective-permute-start.73
  660.8 14.8 %collective-permute-done.71 = bf16[256,1536]{1,0:T(8,128)(2,1)S(1)} collective-permute-done((bf16[256,1536]{1,0:T(8,128)(2,1)S(1)}, bf16[256,1536]{1,0:T(8,128)(2,1)S(1)}, u32[]{:S(2)}, u32[]{:S(2)}) %collective-permute-start.71) | collective-permute-done | bytes 786464 | tf_op jit(solution)/shard_map/ppermute | solution.py:1141
  677.1 7.9 %collective-permute-start.76 = (bf16[1280,384]{1,0:T(8,128)(2,1)S(1)}, bf16[1280,384]{1,0:T(8,128)(2,1)}, u32[]{:S(2)}, u32[]{:S(2)}) collective-permute-start(bf16[1280,384]{1,0:T(8,128)(2,1)S(1)} %add_convert_fusion.1.refs_0_), channel_id=1, source_target_pairs={{0,4},{4,0},{1,5},{5,1},{2,6},{6,2},{3,7},{7,3},{8,12},{12,8},{9,1... | collective-permute-start | bytes 2949128 | tf_op jit(solution)/shard_map/ppermute | solution.py:1066
  686.0 4.6 collective-permute-start.80
  693.9 7.9 %join_grads.1 = (f32[6448,384]{1,0:T(8,128)}, f32[768,1536]{1,0:T(8,128)}, f32[16,384]{1,0:T(8,128)S(1)}) custom-call(s32[2]{0:T(128)S(1)} %pad_add_fusion.sc, bf16[1280,384]{1,0:T(8,128)(2,1)S(1)} %add_convert_fusion.1.refs_0_, bf16[1280,384]{1,0:T(8,128)(2,1)S(1)} %collective-permute-done.75.refs_1_, bf16[1280,384]{1,0:T(8,128)(2,1)} %collective-permute-done.76.refs_2_, ...), custom_call_target="tpu_custom_call" | custom-call | flops 1048576 | bytes 65536 | tf_op jit(solution)/shard_map/join_grads/pallas_call | solution.py:1053
  (357 shorter events, 176.5 us)
Async XLA Ops:
  6.4 23.7 %collective-permute-start = (bf16[1280,384]{1,0:T(8,128)(2,1)S(1)}, bf16[1280,384]{1,0:T(8,128)(2,1)}, u32[]{:S(2)}, u32[]{:S(2)}) collective-permute-start(bf16[1280,384]{1,0:T(8,128)(2,1)S(1)} %get-tuple-element.278.refs_0_), channel_id=1, source_target_pairs={{0,1},{1,0},{2,3},{3,2},{8,9},{9,8},{10,11},{11,10},{4,5},{5,4},{6... | collective-permute-start | bytes 2949128 | tf_op jit(solution)/shard_map/ppermute | solution.py:890
  8.5 21.6 %collective-permute-start.1 = (bf16[1280,384]{1,0:T(8,128)(2,1)S(1)}, bf16[1280,384]{1,0:T(8,128)(2,1)}, u32[]{:S(2)}, u32[]{:S(2)}) collective-permute-start(bf16[1280,384]{1,0:T(8,128)(2,1)S(1)} %get-tuple-element.278.refs_0_), channel_id=1, source_target_pairs={{1,2},{2,1},{9,10},{10,9},{5,6},{6,5},{13,14},{14,13},{17,18},{18,... | collective-permute-start | bytes 2949128 | tf_op jit(solution)/shard_map/ppermute | solution.py:890
  30.1 29.0 %collective-permute-start.2 = (bf16[1280,384]{1,0:T(8,128)(2,1)S(1)}, bf16[1280,384]{1,0:T(8,128)(2,1)}, u32[]{:S(2)}, u32[]{:S(2)}) collective-permute-start(bf16[1280,384]{1,0:T(8,128)(2,1)S(1)} %get-tuple-element.282.refs_1_), channel_id=1, source_target_pairs={{0,1},{1,0},{2,3},{3,2},{8,9},{9,8},{10,11},{11,10},{4,5},{5,4},{6... | collective-permute-start | bytes 2949128 | tf_op jit(solution)/shard_map/ppermute | solution.py:890
  34.3 24.9 %collective-permute-start.3 = (bf16[1280,384]{1,0:T(8,128)(2,1)S(1)}, bf16[1280,384]{1,0:T(8,128)(2,1)}, u32[]{:S(2)}, u32[]{:S(2)}) collective-permute-start(bf16[1280,384]{1,0:T(8,128)(2,1)S(1)} %get-tuple-element.282.refs_1_), channel_id=1, source_target_pairs={{1,2},{2,1},{9,10},{10,9},{5,6},{6,5},{13,14},{14,13},{17,18},{18,... | collective-permute-start | bytes 2949128 | tf_op jit(solution)/shard_map/ppermute | solution.py:890
  35.9 23.3 %collective-permute-start.4 = (bf16[1280,384]{1,0:T(8,128)(2,1)}, bf16[1280,384]{1,0:T(8,128)(2,1)}, u32[]{:S(2)}, u32[]{:S(2)}) collective-permute-start(bf16[1280,384]{1,0:T(8,128)(2,1)} %collective-permute-done.refs_4_), channel_id=1, source_target_pairs={{0,8},{1,9},{2,10},{3,11},{8,0},{9,1},{10,2},{11,3},{4,12},{5,13},... | collective-permute-start | bytes 2949128 | tf_op jit(solution)/shard_map/ppermute | solution.py:894
  37.8 18.4 %collective-permute-start.5 = (bf16[5348]{0:T(1024)(128)(2,1)S(1)}, bf16[5348]{0:T(1024)(128)(2,1)S(1)}, u32[]{:S(2)}, u32[]{:S(2)}) collective-permute-start(bf16[5348]{0:T(1024)(128)(2,1)S(1)} %concatenate.29), channel_id=1, source_target_pairs={{0,1},{1,2},{2,3},{3,0},{4,5},{5,6},{6,7},{7,4},{8,9},{9,10},{10,1... | collective-permute-start | bytes 32096 | tf_op jit(solution)/shard_map/ppermute | solution.py:1072
  39.3 18.5 %collective-permute-start.6 = (bf16[5348]{0:T(1024)(128)(2,1)S(1)}, bf16[5348]{0:T(1024)(128)(2,1)S(1)}, u32[]{:S(2)}, u32[]{:S(2)}) collective-permute-start(bf16[5348]{0:T(1024)(128)(2,1)S(1)} %concatenate.29), channel_id=1, source_target_pairs={{0,2},{1,3},{2,0},{3,1},{4,6},{5,7},{6,4},{7,5},{8,10},{9,11},{10,... | collective-permute-start | bytes 32096 | tf_op jit(solution)/shard_map/ppermute | solution.py:1072
  59.2 19.4 %collective-permute-start.10 = (bf16[1280,384]{1,0:T(8,128)(2,1)}, bf16[1280,384]{1,0:T(8,128)(2,1)S(1)}, u32[]{:S(2)}, u32[]{:S(2)}) collective-permute-start(bf16[1280,384]{1,0:T(8,128)(2,1)} %collective-permute-done.2.refs_5_), channel_id=1, source_target_pairs={{0,8},{1,9},{2,10},{3,11},{8,0},{9,1},{10,2},{11,3},{4,12},{5,13},... | collective-permute-start | bytes 2949128 | tf_op jit(solution)/shard_map/ppermute | solution.py:894
  60.4 21.0 %collective-permute-start.8 = (bf16[1280,384]{1,0:T(8,128)(2,1)}, bf16[1280,384]{1,0:T(8,128)(2,1)S(1)}, u32[]{:S(2)}, u32[]{:S(2)}) collective-permute-start(bf16[1280,384]{1,0:T(8,128)(2,1)} %collective-permute-done.1.refs_8_), channel_id=1, source_target_pairs={{1,0},{2,3},{9,8},{10,11},{5,4},{6,7},{13,12},{14,15},{17,16},{18,... | collective-permute-start | bytes 2949128 | tf_op jit(solution)/shard_map/ppermute | solution.py:890
  61.7 19.7 %collective-permute-start.9 = (bf16[1280,384]{1,0:T(8,128)(2,1)}, bf16[1280,384]{1,0:T(8,128)(2,1)S(1)}, u32[]{:S(2)}, u32[]{:S(2)}) collective-permute-start(bf16[1280,384]{1,0:T(8,128)(2,1)} %collective-permute-done.refs_4_), channel_id=1, source_target_pairs={{1,2},{2,1},{9,10},{10,9},{5,6},{6,5},{13,14},{14,13},{17,18},{18,... | collective-permute-start | bytes 2949128 | tf_op jit(solution)/shard_map/ppermute | solution.py:890
  81.4 21.1 %collective-permute-start.11 = (bf16[1280,384]{1,0:T(8,128)(2,1)}, bf16[1280,384]{1,0:T(8,128)(2,1)S(1)}, u32[]{:S(2)}, u32[]{:S(2)}) collective-permute-start(bf16[1280,384]{1,0:T(8,128)(2,1)} %collective-permute-done.3.refs_9_), channel_id=1, source_target_pairs={{1,0},{2,3},{9,8},{10,11},{5,4},{6,7},{13,12},{14,15},{17,16},{18,... | collective-permute-start | bytes 2949128 | tf_op jit(solution)/shard_map/ppermute | solution.py:890
  82.7 19.8 %collective-permute-start.12 = (bf16[1280,384]{1,0:T(8,128)(2,1)}, bf16[1280,384]{1,0:T(8,128)(2,1)}, u32[]{:S(2)}, u32[]{:S(2)}) collective-permute-start(bf16[1280,384]{1,0:T(8,128)(2,1)} %collective-permute-done.2.refs_5_), channel_id=1, source_target_pairs={{1,2},{2,1},{9,10},{10,9},{5,6},{6,5},{13,14},{14,13},{17,18},{18,... | collective-permute-start | bytes 2949128 | tf_op jit(solution)/shard_map/ppermute | solution.py:890
  84.3 19.8 %collective-permute-start.13 = (bf16[1280,384]{1,0:T(8,128)(2,1)S(1)}, bf16[1280,384]{1,0:T(8,128)(2,1)S(1)}, u32[]{:S(2)}, u32[]{:S(2)}) collective-permute-start(bf16[1280,384]{1,0:T(8,128)(2,1)S(1)} %collective-permute-done.8.refs_12_), channel_id=1, source_target_pairs={{0,8},{3,11},{8,0},{11,3},{4,12},{7,15},{12,4},{15,7},{16,24},{19,... | collective-permute-start | bytes 2949128 | tf_op jit(solution)/shard_map/ppermute | solution.py:894
  86.5 17.7 %collective-permute-start.14 = (bf16[1280,384]{1,0:T(8,128)(2,1)}, bf16[1280,384]{1,0:T(8,128)(2,1)S(1)}, u32[]{:S(2)}, u32[]{:S(2)}) collective-permute-start(bf16[1280,384]{1,0:T(8,128)(2,1)} %collective-permute-done.1.refs_8_), channel_id=1, source_target_pairs={{1,9},{2,10},{9,1},{10,2},{5,13},{6,14},{13,5},{14,6},{17,25},{18,... | collective-permute-start | bytes 2949128 | tf_op jit(solution)/shard_map/ppermute | solution.py:894
  104.1 23.6 %collective-permute-start.19 = (bf16[1280,384]{1,0:T(8,128)(2,1)S(1)}, bf16[1280,384]{1,0:T(8,128)(2,1)S(1)}, u32[]{:S(2)}, u32[]{:S(2)}) collective-permute-start(bf16[1280,384]{1,0:T(8,128)(2,1)S(1)} %collective-permute-done.9.refs_0_), channel_id=1, source_target_pairs={{1,0},{2,3},{9,8},{10,11},{5,4},{6,7},{13,12},{14,15},{17,16},{18,... | collective-permute-start | bytes 2949128 | tf_op jit(solution)/shard_map/ppermute | solution.py:890
  105.4 22.3 %collective-permute-start.20 = (bf16[1280,384]{1,0:T(8,128)(2,1)S(1)}, bf16[1280,384]{1,0:T(8,128)(2,1)S(1)}, u32[]{:S(2)}, u32[]{:S(2)}) collective-permute-start(bf16[1280,384]{1,0:T(8,128)(2,1)S(1)} %collective-permute-done.11.refs_13_), channel_id=1, source_target_pairs={{0,8},{3,11},{8,0},{11,3},{4,12},{7,15},{12,4},{15,7},{16,24},{19,... | collective-permute-start | bytes 2949128 | tf_op jit(solution)/shard_map/ppermute | solution.py:894
  107.6 20.1 %collective-permute-start.21 = (bf16[1280,384]{1,0:T(8,128)(2,1)}, bf16[1280,384]{1,0:T(8,128)(2,1)S(1)}, u32[]{:S(2)}, u32[]{:S(2)}) collective-permute-start(bf16[1280,384]{1,0:T(8,128)(2,1)} %collective-permute-done.3.refs_9_), channel_id=1, source_target_pairs={{1,9},{2,10},{9,1},{10,2},{5,13},{6,14},{13,5},{14,6},{17,25},{18,... | collective-permute-start | bytes 2949128 | tf_op jit(solution)/shard_map/ppermute | solution.py:894
  127.8 21.1 %collective-permute-start.22 = (bf16[1280,384]{1,0:T(8,128)(2,1)}, bf16[1280,384]{1,0:T(8,128)(2,1)}, u32[]{:S(2)}, u32[]{:S(2)}) collective-permute-start(bf16[1280,384]{1,0:T(8,128)(2,1)} %collective-permute-done.12.refs_1_), channel_id=1, source_target_pairs={{1,0},{2,3},{9,8},{10,11},{5,4},{6,7},{13,12},{14,15},{17,16},{18,... | collective-permute-start | bytes 2949128 | tf_op jit(solution)/shard_map/ppermute | solution.py:890
  129.1 19.8 %collective-permute-start.23 = (bf16[1280,384]{1,0:T(8,128)(2,1)S(1)}, bf16[1280,384]{1,0:T(8,128)(2,1)S(1)}, u32[]{:S(2)}, u32[]{:S(2)}) collective-permute-start(bf16[1280,384]{1,0:T(8,128)(2,1)S(1)} %collective-permute-done.19.refs_4_), channel_id=1, source_target_pairs={{0,8},{3,11},{8,0},{11,3},{4,12},{7,15},{12,4},{15,7},{16,24},{19,... | collective-permute-start | bytes 2949128 | tf_op jit(solution)/shard_map/ppermute | solution.py:894
  134.8 30.2 %collective-permute-start.15 = (bf16[256,1536]{1,0:T(8,128)(2,1)}, bf16[256,1536]{1,0:T(8,128)(2,1)}, u32[]{:S(2)}, u32[]{:S(2)}) collective-permute-start(bf16[256,1536]{1,0:T(8,128)(2,1)} %get-tuple-element.549), channel_id=1, source_target_pairs={{0,0},{1,4},{4,1},{5,5},{8,8},{9,12},{12,9},{13,13},{16,16},{17,20... | collective-permute-start | bytes 2359304 | tf_op jit(solution)/shard_map/ppermute | solution.py:1132
  148.9 32.3 %collective-permute-start.25 = (bf16[1280,384]{1,0:T(8,128)(2,1)}, bf16[1280,384]{1,0:T(8,128)(2,1)}, u32[]{:S(2)}, u32[]{:S(2)}) collective-permute-start(bf16[1280,384]{1,0:T(8,128)(2,1)} %collective-permute-done.12.refs_1_), channel_id=1, source_target_pairs={{1,9},{2,10},{9,1},{10,2},{5,13},{6,14},{13,5},{14,6},{17,25},{18,... | collective-permute-start | bytes 2949128 | tf_op jit(solution)/shard_map/ppermute | solution.py:894
  150.5 30.7 %collective-permute-start.26 = (bf16[1280,384]{1,0:T(8,128)(2,1)}, bf16[1280,384]{1,0:T(8,128)(2,1)}, u32[]{:S(2)}, u32[]{:S(2)}) collective-permute-start(bf16[1280,384]{1,0:T(8,128)(2,1)} %collective-permute-done.22.refs_5_), channel_id=1, source_target_pairs={{0,8},{3,11},{8,0},{11,3},{4,12},{7,15},{12,4},{15,7},{16,24},{19,... | collective-permute-start | bytes 2949128 | tf_op jit(solution)/shard_map/ppermute | solution.py:894
  153.6 27.6 %collective-permute-start.17 = (bf16[256,1536]{1,0:T(8,128)(2,1)}, bf16[256,1536]{1,0:T(8,128)(2,1)S(1)}, u32[]{:S(2)}, u32[]{:S(2)}) collective-permute-start(bf16[256,1536]{1,0:T(8,128)(2,1)} %get-tuple-element.549), channel_id=1, source_target_pairs={{2,0},{3,4},{6,1},{7,5},{10,8},{11,12},{14,9},{15,13},{18,16},{19,... | collective-permute-start | bytes 2359304 | tf_op jit(solution)/shard_map/ppermute | solution.py:1132
  154.9 26.3 %collective-permute-start.16 = (bf16[256,1536]{1,0:T(8,128)(2,1)}, bf16[256,1536]{1,0:T(8,128)(2,1)}, u32[]{:S(2)}, u32[]{:S(2)}) collective-permute-start(bf16[256,1536]{1,0:T(8,128)(2,1)} %get-tuple-element.548), channel_id=1, source_target_pairs={{0,2},{1,6},{4,3},{5,7},{8,10},{9,14},{12,11},{13,15},{16,18},{17,... | collective-permute-start | bytes 2359304 | tf_op jit(solution)/shard_map/ppermute | solution.py:1132
  182.5 19.1 %collective-permute-start.27 = (bf16[256,1536]{1,0:T(8,128)(2,1)S(1)}, bf16[256,1536]{1,0:T(8,128)(2,1)S(1)}, u32[]{:S(2)}, u32[]{:S(2)}) collective-permute-start(bf16[256,1536]{1,0:T(8,128)(2,1)S(1)} %broadcast_select_fusion.1), channel_id=1, source_target_pairs={{0,4},{4,0},{1,5},{5,1},{2,6},{6,2},{3,7},{7,3},{8,12},{12,8},{9,1... | collective-permute-start | bytes 2359304 | tf_op jit(solution)/shard_map/ppermute | solution.py:1066
  314.9 51.7 %collective-permute-start.44 = (bf16[128,1536]{1,0:T(8,128)(2,1)S(1)}, bf16[128,1536]{1,0:T(8,128)(2,1)S(1)}, u32[]{:S(2)}, u32[]{:S(2)}) collective-permute-start(bf16[128,1536]{1,0:T(8,128)(2,1)S(1)} %get-tuple-element.442), channel_id=1, source_target_pairs={{16,0},{17,1},{18,2},{19,3},{20,4},{21,5},{22,6},{23,7},{24,8},{25... | collective-permute-start | bytes 1179656 | tf_op jit(solution)/shard_map/ppermute | solution.py:1224
  369.8 22.8 %collective-permute-start.47 = (bf16[128,1536]{1,0:T(8,128)(2,1)S(1)}, bf16[128,1536]{1,0:T(8,128)(2,1)S(1)}, u32[]{:S(2)}, u32[]{:S(2)}) collective-permute-start(bf16[128,1536]{1,0:T(8,128)(2,1)S(1)} %get-tuple-element.457), channel_id=1, source_target_pairs={{16,0},{17,1},{18,2},{19,3},{20,4},{21,5},{22,6},{23,7},{24,8},{25... | collective-permute-start | bytes 1179656 | tf_op jit(solution)/shard_map/ppermute | solution.py:1224
  397.6 21.8 %collective-permute-start.50 = (bf16[128,1536]{1,0:T(8,128)(2,1)S(1)}, bf16[128,1536]{1,0:T(8,128)(2,1)S(1)}, u32[]{:S(2)}, u32[]{:S(2)}) collective-permute-start(bf16[128,1536]{1,0:T(8,128)(2,1)S(1)} %get-tuple-element.472), channel_id=1, source_target_pairs={{16,0},{17,1},{18,2},{19,3},{20,4},{21,5},{22,6},{23,7},{24,8},{25... | collective-permute-start | bytes 1179656 | tf_op jit(solution)/shard_map/ppermute | solution.py:1224
  424.0 21.8 %collective-permute-start.53 = (bf16[128,1536]{1,0:T(8,128)(2,1)S(1)}, bf16[128,1536]{1,0:T(8,128)(2,1)S(1)}, u32[]{:S(2)}, u32[]{:S(2)}) collective-permute-start(bf16[128,1536]{1,0:T(8,128)(2,1)S(1)} %get-tuple-element.487), channel_id=1, source_target_pairs={{16,0},{17,1},{18,2},{19,3},{20,4},{21,5},{22,6},{23,7},{24,8},{25... | collective-permute-start | bytes 1179656 | tf_op jit(solution)/shard_map/ppermute | solution.py:1224
  483.1 23.6 %collective-permute-start.56 = (bf16[1280,384]{1,0:T(8,128)(2,1)S(1)}, bf16[1280,384]{1,0:T(8,128)(2,1)S(1)}, u32[]{:S(2)}, u32[]{:S(2)}) collective-permute-start(bf16[1280,384]{1,0:T(8,128)(2,1)S(1)} %block_grad.17), channel_id=1, source_target_pairs={{0,8},{1,0},{2,1},{3,2},{11,3},{10,11},{9,10},{8,9},{4,12},{5,4},{... | collective-permute-start | bytes 2949128 | tf_op jit(solution)/shard_map/ppermute | solution.py:1274
  484.3 23.4 %collective-permute-start.55 = (bf16[1280,384]{1,0:T(8,128)(2,1)S(1)}, bf16[1280,384]{1,0:T(8,128)(2,1)S(1)}, u32[]{:S(2)}, u32[]{:S(2)}) collective-permute-start(bf16[1280,384]{1,0:T(8,128)(2,1)S(1)} %block_grad.16), channel_id=1, source_target_pairs={{0,1},{1,2},{2,3},{3,11},{11,10},{10,9},{9,8},{8,0},{4,5},{5,6},{6... | collective-permute-start | bytes 2949128 | tf_op jit(solution)/shard_map/ppermute | solution.py:1274
  507.9 22.1 %collective-permute-start.58 = (bf16[1280,384]{1,0:T(8,128)(2,1)S(1)}, bf16[1280,384]{1,0:T(8,128)(2,1)S(1)}, u32[]{:S(2)}, u32[]{:S(2)}) collective-permute-start(bf16[1280,384]{1,0:T(8,128)(2,1)S(1)} %add_convert_fusion.12), channel_id=1, source_target_pairs={{0,8},{1,0},{2,1},{3,2},{11,3},{10,11},{9,10},{8,9},{4,12},{5,4},{... | collective-permute-start | bytes 2949128 | tf_op jit(solution)/shard_map/ppermute | solution.py:1274
  509.2 21.5 %collective-permute-start.57 = (bf16[1280,384]{1,0:T(8,128)(2,1)S(1)}, bf16[1280,384]{1,0:T(8,128)(2,1)S(1)}, u32[]{:S(2)}, u32[]{:S(2)}) collective-permute-start(bf16[1280,384]{1,0:T(8,128)(2,1)S(1)} %add_convert_fusion.13), channel_id=1, source_target_pairs={{0,1},{1,2},{2,3},{3,11},{11,10},{10,9},{9,8},{8,0},{4,5},{5,6},{6... | collective-permute-start | bytes 2949128 | tf_op jit(solution)/shard_map/ppermute | solution.py:1274
  530.9 21.4 %collective-permute-start.62 = (bf16[1280,384]{1,0:T(8,128)(2,1)S(1)}, bf16[1280,384]{1,0:T(8,128)(2,1)S(1)}, u32[]{:S(2)}, u32[]{:S(2)}) collective-permute-start(bf16[1280,384]{1,0:T(8,128)(2,1)S(1)} %add_convert_fusion.10), channel_id=1, source_target_pairs={{0,8},{1,0},{2,1},{3,2},{11,3},{10,11},{9,10},{8,9},{4,12},{5,4},{... | collective-permute-start | bytes 2949128 | tf_op jit(solution)/shard_map/ppermute | solution.py:1274
  535.4 22.8 %collective-permute-start.61 = (bf16[1280,384]{1,0:T(8,128)(2,1)S(1)}, bf16[1280,384]{1,0:T(8,128)(2,1)S(1)}, u32[]{:S(2)}, u32[]{:S(2)}) collective-permute-start(bf16[1280,384]{1,0:T(8,128)(2,1)S(1)} %add_convert_fusion.11), channel_id=1, source_target_pairs={{0,1},{1,2},{2,3},{3,11},{11,10},{10,9},{9,8},{8,0},{4,5},{5,6},{6... | collective-permute-start | bytes 2949128 | tf_op jit(solution)/shard_map/ppermute | solution.py:1274
  558.4 21.9 %collective-permute-start.64 = (bf16[1280,384]{1,0:T(8,128)(2,1)S(1)}, bf16[1280,384]{1,0:T(8,128)(2,1)S(1)}, u32[]{:S(2)}, u32[]{:S(2)}) collective-permute-start(bf16[1280,384]{1,0:T(8,128)(2,1)S(1)} %add_convert_fusion.8), channel_id=1, source_target_pairs={{0,8},{1,0},{2,1},{3,2},{11,3},{10,11},{9,10},{8,9},{4,12},{5,4},{... | collective-permute-start | bytes 2949128 | tf_op jit(solution)/shard_map/ppermute | solution.py:1274
  559.1 21.6 %collective-permute-start.63 = (bf16[1280,384]{1,0:T(8,128)(2,1)S(1)}, bf16[1280,384]{1,0:T(8,128)(2,1)S(1)}, u32[]{:S(2)}, u32[]{:S(2)}) collective-permute-start(bf16[1280,384]{1,0:T(8,128)(2,1)S(1)} %add_convert_fusion.9), channel_id=1, source_target_pairs={{0,1},{1,2},{2,3},{3,11},{11,10},{10,9},{9,8},{8,0},{4,5},{5,6},{6... | collective-permute-start | bytes 2949128 | tf_op jit(solution)/shard_map/ppermute | solution.py:1274
  581.0 20.7 %collective-permute-start.66 = (bf16[1280,384]{1,0:T(8,128)(2,1)S(1)}, bf16[1280,384]{1,0:T(8,128)(2,1)S(1)}, u32[]{:S(2)}, u32[]{:S(2)}) collective-permute-start(bf16[1280,384]{1,0:T(8,128)(2,1)S(1)} %add_convert_fusion.6), channel_id=1, source_target_pairs={{0,8},{1,0},{2,1},{3,2},{11,3},{10,11},{9,10},{8,9},{4,12},{5,4},{... | collective-permute-start | bytes 2949128 | tf_op jit(solution)/shard_map/ppermute | solution.py:1274
  581.6 20.6 %collective-permute-start.65 = (bf16[1280,384]{1,0:T(8,128)(2,1)S(1)}, bf16[1280,384]{1,0:T(8,128)(2,1)S(1)}, u32[]{:S(2)}, u32[]{:S(2)}) collective-permute-start(bf16[1280,384]{1,0:T(8,128)(2,1)S(1)} %add_convert_fusion.7), channel_id=1, source_target_pairs={{0,1},{1,2},{2,3},{3,11},{11,10},{10,9},{9,8},{8,0},{4,5},{5,6},{6... | collective-permute-start | bytes 2949128 | tf_op jit(solution)/shard_map/ppermute | solution.py:1274
  602.4 19.8 %collective-permute-start.68 = (bf16[1280,384]{1,0:T(8,128)(2,1)S(1)}, bf16[1280,384]{1,0:T(8,128)(2,1)S(1)}, u32[]{:S(2)}, u32[]{:S(2)}) collective-permute-start(bf16[1280,384]{1,0:T(8,128)(2,1)S(1)} %add_convert_fusion.4), channel_id=1, source_target_pairs={{0,8},{1,0},{2,1},{3,2},{11,3},{10,11},{9,10},{8,9},{4,12},{5,4},{... | collective-permute-start | bytes 2949128 | tf_op jit(solution)/shard_map/ppermute | solution.py:1274
  603.0 19.4 %collective-permute-start.67 = (bf16[1280,384]{1,0:T(8,128)(2,1)S(1)}, bf16[1280,384]{1,0:T(8,128)(2,1)S(1)}, u32[]{:S(2)}, u32[]{:S(2)}) collective-permute-start(bf16[1280,384]{1,0:T(8,128)(2,1)S(1)} %add_convert_fusion.5), channel_id=1, source_target_pairs={{0,1},{1,2},{2,3},{3,11},{11,10},{10,9},{9,8},{8,0},{4,5},{5,6},{6... | collective-permute-start | bytes 2949128 | tf_op jit(solution)/shard_map/ppermute | solution.py:1274
  622.7 19.3 %collective-permute-start.70 = (bf16[1280,384]{1,0:T(8,128)(2,1)S(1)}, bf16[1280,384]{1,0:T(8,128)(2,1)S(1)}, u32[]{:S(2)}, u32[]{:S(2)}) collective-permute-start(bf16[1280,384]{1,0:T(8,128)(2,1)S(1)} %add_convert_fusion.2), channel_id=1, source_target_pairs={{0,8},{1,0},{2,1},{3,2},{11,3},{10,11},{9,10},{8,9},{4,12},{5,4},{... | collective-permute-start | bytes 2949128 | tf_op jit(solution)/shard_map/ppermute | solution.py:1274
  623.2 19.4 %collective-permute-start.69 = (bf16[1280,384]{1,0:T(8,128)(2,1)S(1)}, bf16[1280,384]{1,0:T(8,128)(2,1)S(1)}, u32[]{:S(2)}, u32[]{:S(2)}) collective-permute-start(bf16[1280,384]{1,0:T(8,128)(2,1)S(1)} %add_convert_fusion.3), channel_id=1, source_target_pairs={{0,1},{1,2},{2,3},{3,11},{11,10},{10,9},{9,8},{8,0},{4,5},{5,6},{6... | collective-permute-start | bytes 2949128 | tf_op jit(solution)/shard_map/ppermute | solution.py:1274
  642.8 42.3 %collective-permute-start.75 = (bf16[1280,384]{1,0:T(8,128)(2,1)S(1)}, bf16[1280,384]{1,0:T(8,128)(2,1)S(1)}, u32[]{:S(2)}, u32[]{:S(2)}) collective-permute-start(bf16[1280,384]{1,0:T(8,128)(2,1)S(1)} %add_convert_fusion.1.refs_0_), channel_id=1, source_target_pairs={{0,8},{8,0},{1,9},{9,1},{2,10},{10,2},{3,11},{11,3},{4,12},{12,4},... | collective-permute-start | bytes 2949128 | tf_op jit(solution)/shard_map/ppermute | solution.py:1066
  643.4 42.1 %collective-permute-start.78 = (bf16[1280,384]{1,0:T(8,128)(2,1)S(1)}, bf16[1280,384]{1,0:T(8,128)(2,1)}, u32[]{:S(2)}, u32[]{:S(2)}) collective-permute-start(bf16[1280,384]{1,0:T(8,128)(2,1)S(1)} %add_convert_fusion.refs_4_), channel_id=1, source_target_pairs={{0,8},{8,0},{1,9},{9,1},{2,10},{10,2},{3,11},{11,3},{4,12},{12,4},... | collective-permute-start | bytes 2949128 | tf_op jit(solution)/shard_map/ppermute | solution.py:1066
  644.3 31.2 %collective-permute-start.71 = (bf16[256,1536]{1,0:T(8,128)(2,1)S(1)}, bf16[256,1536]{1,0:T(8,128)(2,1)S(1)}, u32[]{:S(2)}, u32[]{:S(2)}) collective-permute-start(bf16[256,1536]{1,0:T(8,128)(2,1)S(1)} %pick.2), channel_id=1, source_target_pairs={{0,0},{4,1},{1,4},{5,5},{8,8},{12,9},{9,12},{13,13},{16,16},{20,17... | collective-permute-start | bytes 2359304 | tf_op jit(solution)/shard_map/ppermute | solution.py:1141
  653.3 23.8 %collective-permute-start.72 = (bf16[256,1536]{1,0:T(8,128)(2,1)S(1)}, bf16[256,1536]{1,0:T(8,128)(2,1)S(1)}, u32[]{:S(2)}, u32[]{:S(2)}) collective-permute-start(bf16[256,1536]{1,0:T(8,128)(2,1)S(1)} %pick.2), channel_id=1, source_target_pairs={{2,0},{6,1},{3,4},{7,5},{10,8},{14,9},{11,12},{15,13},{18,16},{22,... | collective-permute-start | bytes 2359304 | tf_op jit(solution)/shard_map/ppermute | solution.py:1141
  654.6 30.4 %collective-permute-start.73 = (bf16[256,1536]{1,0:T(8,128)(2,1)}, bf16[256,1536]{1,0:T(8,128)(2,1)S(1)}, u32[]{:S(2)}, u32[]{:S(2)}) collective-permute-start(bf16[256,1536]{1,0:T(8,128)(2,1)} %pick.3), channel_id=1, source_target_pairs={{0,2},{4,3},{1,6},{5,7},{8,10},{12,11},{9,14},{13,15},{16,18},{20,... | collective-permute-start | bytes 2359304 | tf_op jit(solution)/shard_map/ppermute | solution.py:1141
  (72 other events, 1279.8 us)

commit v6 on v4

--- a/solution.py
+++ b/solution.py
@@ -102,12 +102,12 @@
 
 
 def pair_loop(step):
-    def two(turn, _):
-        step(2 * turn)
-        step(2 * turn + 1)
+    def three(turn, _):
+        for i in range(3):
+            step(3 * turn + i)
         return 0
 
-    lax.fori_loop(0, PAIRS // 2, two, 0)
+    lax.fori_loop(0, PAIRS // 3, three, 0)
 
 
 def aligned(value):
@@ -441,8 +441,10 @@
     zero = jnp.zeros((t, LANES), F32)
     ddt, dld, dval = lax.fori_loop(
         0,
-        PAIRS // 2,
-        lambda turn, carry: pair_step(2 * turn + 1, pair_step(2 * turn, carry)),
+        PAIRS // 3,
+        lambda turn, carry: functools.reduce(
+            lambda held, i: pair_step(3 * turn + i, held), range(3), carry
+        ),
         (zero, zero, jnp.zeros((8, LANES), F32)),
     )
 
@@ -1265,6 +1267,8 @@
                 block = (block.astype(F32) + came).astype(BF16)
             sums[i] = block
         if hop == 3:
+            owners, edge_held = lax.optimization_barrier((owners, edge_held))
+        if hop == 5:
             finished = pick(table, edge_held, 0), pick(table, edge_held, 2)
             owners, *finished = lax.optimization_barrier((owners, *finished))
     *sums, early, late = lax.optimization_barrier((*sums, *finished))

time: 693 us -> 679 us (0.980)
  Pallas kernels: 265 us -> 257 us
    pallas_call x26, Pallas kernels: 175 us -> 168 us  [chunk_call(): pl.pallas_call(kernel, in_specs=in_specs, out_specs=out_specs, out_shape=...]
  transfers between devices with their start and end apart: 81 -> 81, of which waited for: 37 -> 37; matrix products, arithmetic and copies ran while one was open for 3% -> 3% of each run, Pallas kernels for 30% -> 29%
where the time goes in v6:
time: 679 us; the launch traced here: 671 us
  Pallas kernels  257 us (38%)
  waiting for transfers between devices  237 us (35%)
  starting transfers between devices  141 us (21%)
  local copies, waits for them, and re-layouts  21.9 us (3%)
  other arithmetic  10.3 us (2%)
    pallas_call x26, Pallas kernels, chunk_call(): pl.pallas_call(kernel, in_specs=in_specs, out_specs=out_specs, out_shape=...  168 us
    pallas_call x16, Pallas kernels, block_grad(): pl.pallas_call(functools.partial(block_grad_kernel, row), grid_spec=pltpu...  70.7 us
    ppermute x14, waiting for transfers between devices, relay_shards(): came = lax.ppermute(sums[i], ('y', 'fsdp'), path).astype(F32)  67.7 us
    ppermute x10, waiting for transfers between devices, along(): return lax.ppermute(value, ('y', 'fsdp'), path)  57.5 us
    ppermute x28, starting transfers between devices, swap(): return lax.ppermute(value, axis, [(0, 1), (1, 0)])  38.9 us
    ppermute x4, waiting for transfers between devices, relay_shards(): moved[moment - 1] = lax.ppermute(result, 'section', [(1, 0)])  38 us
    ppermute x4, starting transfers between devices, bring(): lax.ppermute(local[m], ('core', 'fsdp'), route(first, m))  26.9 us
    ppermute x28, waiting for transfers between devices, swap(): return lax.ppermute(value, axis, [(0, 1), (1, 0)])  20.4 us
  transfers between devices with their start and end apart: 81, of which 37 were waited for; matrix products, arithmetic and copies ran while one was open for 3% of the time, Pallas kernels for 29%

profile of v6, /device:TPU:1, one launch (start us, length us, event | category | flops | bytes accessed | tf_op | source)
XLA Modules:
  0.0 670.6 jit_solution(8672814919831254053)
XLA Ops:
  10.1 19.9 %collective-permute-done.refs_4_ = bf16[1280,384]{1,0:T(8,128)(2,1)} collective-permute-done((bf16[1280,384]{1,0:T(8,128)(2,1)S(1)}, bf16[1280,384]{1,0:T(8,128)(2,1)}, u32[]{:S(2)}, u32[]{:S(2)}) %collective-permute-start) | collective-permute-done | bytes 983072 | tf_op jit(solution)/shard_map/ppermute | solution.py:882
  40.1 16.1 %collective-permute-done.5 = bf16[5348]{0:T(1024)(128)(2,1)S(1)} collective-permute-done((bf16[5348]{0:T(1024)(128)(2,1)S(1)}, bf16[5348]{0:T(1024)(128)(2,1)S(1)}, u32[]{:S(2)}, u32[]{:S(2)}) %collective-permute-start.5) | collective-permute-done | bytes 10728 | tf_op jit(solution)/shard_map/ppermute | solution.py:1064
  62.4 16.1 %collective-permute-done.10.refs_7_ = bf16[1280,384]{1,0:T(8,128)(2,1)S(1)} collective-permute-done((bf16[1280,384]{1,0:T(8,128)(2,1)}, bf16[1280,384]{1,0:T(8,128)(2,1)S(1)}, u32[]{:S(2)}, u32[]{:S(2)}) %collective-permute-start.10) | collective-permute-done | bytes 983072 | tf_op jit(solution)/shard_map/ppermute | solution.py:886
  87.2 15.3 %collective-permute-done.11.refs_13_ = bf16[1280,384]{1,0:T(8,128)(2,1)S(1)} collective-permute-done((bf16[1280,384]{1,0:T(8,128)(2,1)}, bf16[1280,384]{1,0:T(8,128)(2,1)S(1)}, u32[]{:S(2)}, u32[]{:S(2)}) %collective-permute-start.11) | collective-permute-done | bytes 983072 | tf_op jit(solution)/shard_map/ppermute | solution.py:882
  108.4 19.4 %collective-permute-done.19.refs_4_ = bf16[1280,384]{1,0:T(8,128)(2,1)S(1)} collective-permute-done((bf16[1280,384]{1,0:T(8,128)(2,1)S(1)}, bf16[1280,384]{1,0:T(8,128)(2,1)S(1)}, u32[]{:S(2)}, u32[]{:S(2)}) %collective-permute-start.19) | collective-permute-done | bytes 983072 | tf_op jit(solution)/shard_map/ppermute | solution.py:882
  134.8 14.1 %collective-permute-start.15 = (bf16[256,1536]{1,0:T(8,128)(2,1)}, bf16[256,1536]{1,0:T(8,128)(2,1)}, u32[]{:S(2)}, u32[]{:S(2)}) collective-permute-start(bf16[256,1536]{1,0:T(8,128)(2,1)} %get-tuple-element.549), channel_id=1, source_target_pairs={{0,0},{1,4},{4,1},{5,5},{8,8},{9,12},{12,9},{13,13},{16,16},{17,20... | collective-permute-start | bytes 2359304 | tf_op jit(solution)/shard_map/ppermute | solution.py:1124
  154.9 10.0 %collective-permute-start.16 = (bf16[256,1536]{1,0:T(8,128)(2,1)}, bf16[256,1536]{1,0:T(8,128)(2,1)}, u32[]{:S(2)}, u32[]{:S(2)}) collective-permute-start(bf16[256,1536]{1,0:T(8,128)(2,1)} %get-tuple-element.548), channel_id=1, source_target_pairs={{0,2},{1,6},{4,3},{5,7},{8,10},{9,14},{12,11},{13,15},{16,18},{17,... | collective-permute-start | bytes 2359304 | tf_op jit(solution)/shard_map/ppermute | solution.py:1124
  175.8 5.4 place_weights.2
  182.5 15.3 %collective-permute-start.27 = (bf16[256,1536]{1,0:T(8,128)(2,1)S(1)}, bf16[256,1536]{1,0:T(8,128)(2,1)S(1)}, u32[]{:S(2)}, u32[]{:S(2)}) collective-permute-start(bf16[256,1536]{1,0:T(8,128)(2,1)S(1)} %broadcast_select_fusion.1), channel_id=1, source_target_pairs={{0,4},{4,0},{1,5},{5,1},{2,6},{6,2},{3,7},{7,3},{8,12},{12,8},{9,1... | collective-permute-start | bytes 2359304 | tf_op jit(solution)/shard_map/ppermute | solution.py:1058
  201.9 12.3 %forward_chunk.6 = (bf16[256,1664]{1,0:T(8,128)(2,1)S(1)}, bf16[256,1536]{1,0:T(8,128)(2,1)S(1)}, f32[128,1536]{1,0:T(8,128)S(1)}, f32[8,1792]{1,0:T(8,128)S(1)}...) custom-call(s32[12,7]{1,0:T(8,128)S(1)} %reshape.193.sc, ...), custom_call_target="tpu_custom_call" | custom-call | flops 1048576 | bytes 65536 | tf_op jit(solution)/shard_map/forward_chunk/pallas_call | solution.py:559
  220.2 12.0 %forward_chunk.7 = (bf16[256,1664]{1,0:T(8,128)(2,1)S(1)}, bf16[256,1536]{1,0:T(8,128)(2,1)S(1)}, f32[128,1536]{1,0:T(8,128)S(1)}, f32[8,1792]{1,0:T(8,128)S(1)}...) custom-call(s32[12,7]{1,0:T(8,128)S(1)} %reshape.193.sc, ...), custom_call_target="tpu_custom_call", output_to_operand_aliasing={{4}: (12, {}), {5}: (13, {}), {6}: (14, {}), {7}: (15, {}),... | custom-call | flops 1048576 | bytes 65536 | tf_op jit(solution)/shard_map/forward_chunk/pallas_call | solution.py:559
  238.3 12.5 %forward_chunk.8 = (bf16[256,1664]{1,0:T(8,128)(2,1)S(1)}, bf16[256,1536]{1,0:T(8,128)(2,1)S(1)}, f32[128,1536]{1,0:T(8,128)S(1)}, f32[8,1792]{1,0:T(8,128)S(1)}...) custom-call(s32[12,7]{1,0:T(8,128)S(1)} %reshape.193.sc, ...), custom_call_target="tpu_custom_call", output_to_operand_aliasing={{4}: (12, {}), {5}: (13, {}), {6}: (14, {}), {7}: (15, {}),... | custom-call | flops 1048576 | bytes 65536 | tf_op jit(solution)/shard_map/forward_chunk/pallas_call | solution.py:559
  256.7 12.0 %forward_chunk.9 = (bf16[256,1664]{1,0:T(8,128)(2,1)S(1)}, bf16[256,1536]{1,0:T(8,128)(2,1)S(1)}, f32[128,1536]{1,0:T(8,128)S(1)}, f32[8,1792]{1,0:T(8,128)S(1)}...) custom-call(s32[12,7]{1,0:T(8,128)S(1)} %reshape.193.sc, ...), custom_call_target="tpu_custom_call", output_to_operand_aliasing={{4}: (12, {}), {5}: (13, {}), {6}: (14, {}), {7}: (15, {}),... | custom-call | flops 1048576 | bytes 65536 | tf_op jit(solution)/shard_map/forward_chunk/pallas_call | solution.py:559
  274.7 6.4 forward_chunk.10
  290.9 7.9 %backward_chunk.6 = (bf16[256,1536]{1,0:T(8,128)(2,1)S(1)}, bf16[256,1536]{1,0:T(8,128)(2,1)S(1)}, bf16[256,1536]{1,0:T(8,128)(2,1)S(1)}, f32[128,1536]{1,0:T(8,...) custom-call(s32[12,7]{1,0:T(8,128)S(1)} %reshape.193.sc, ...), custom_call_target="tpu_custom_call" | custom-call | flops 1048576 | bytes 65536 | tf_op jit(solution)/shard_map/backward_chunk/pallas_call | solution.py:559
  304.0 37.6 %collective-permute-done.44.refs_0_ = bf16[128,1536]{1,0:T(8,128)(2,1)S(1)} collective-permute-done((bf16[128,1536]{1,0:T(8,128)(2,1)S(1)}, bf16[128,1536]{1,0:T(8,128)(2,1)S(1)}, u32[]{:S(2)}, u32[]{:S(2)}) %collective-permute-start.44) | collective-permute-done | bytes 393248 | tf_op jit(solution)/shard_map/ppermute | solution.py:1216
  346.3 18.6 %backward_chunk.8 = (bf16[256,1536]{1,0:T(8,128)(2,1)S(1)}, bf16[256,1536]{1,0:T(8,128)(2,1)S(1)}, bf16[256,1536]{1,0:T(8,128)(2,1)S(1)}, f32[128,1536]{1,0:T(8,...) custom-call(s32[12,7]{1,0:T(8,128)S(1)} %reshape.193.sc, ...), custom_call_target="tpu_custom_call", output_to_operand_aliasing={{7}: (21, {}), {8}: (22, {})} | custom-call | flops 1048576 | bytes 65536 | tf_op jit(solution)/shard_map/backward_chunk/pallas_call | solution.py:559
  371.5 17.9 %backward_chunk.9 = (bf16[256,1536]{1,0:T(8,128)(2,1)S(1)}, bf16[256,1536]{1,0:T(8,128)(2,1)S(1)}, bf16[256,1536]{1,0:T(8,128)(2,1)S(1)}, f32[128,1536]{1,0:T(8,...) custom-call(s32[12,7]{1,0:T(8,128)S(1)} %reshape.193.sc, ...), custom_call_target="tpu_custom_call", output_to_operand_aliasing={{7}: (21, {}), {8}: (22, {})} | custom-call | flops 1048576 | bytes 65536 | tf_op jit(solution)/shard_map/backward_chunk/pallas_call | solution.py:559
  395.7 18.5 %backward_chunk.10 = (bf16[256,1536]{1,0:T(8,128)(2,1)S(1)}, bf16[256,1536]{1,0:T(8,128)(2,1)S(1)}, bf16[256,1536]{1,0:T(8,128)(2,1)S(1)}, f32[128,1536]{1,0:T(8...) custom-call(s32[12,7]{1,0:T(8,128)S(1)} %reshape.193.sc, ...), custom_call_target="tpu_custom_call", output_to_operand_aliasing={{7}: (21, {}), {8}: (22, {})} | custom-call | flops 1048576 | bytes 65536 | tf_op jit(solution)/shard_map/backward_chunk/pallas_call | solution.py:559
  416.0 18.8 %backward_chunk.11 = (bf16[256,1536]{1,0:T(8,128)(2,1)S(1)}, bf16[256,1536]{1,0:T(8,128)(2,1)S(1)}, bf16[256,1536]{1,0:T(8,128)(2,1)S(1)}, f32[128,1536]{1,0:T(8...) custom-call(s32[12,7]{1,0:T(8,128)S(1)} %reshape.193.sc, ...), custom_call_target="tpu_custom_call", output_to_operand_aliasing={{7}: (21, {}), {8}: (22, {})} | custom-call | flops 1048576 | bytes 65536 | tf_op jit(solution)/shard_map/backward_chunk/pallas_call | solution.py:559
  439.6 4.4 block_grad.16
  444.0 4.4 block_grad.17
  450.2 4.5 block_grad.19
  454.8 4.4 block_grad.18
  459.2 12.8 %collective-permute-done.56 = bf16[1280,384]{1,0:T(8,128)(2,1)S(1)} collective-permute-done((bf16[1280,384]{1,0:T(8,128)(2,1)S(1)}, bf16[1280,384]{1,0:T(8,128)(2,1)S(1)}, u32[]{:S(2)}, u32[]{:S(2)}) %collective-permute-start.56) | collective-permute-done | bytes 983072 | tf_op jit(solution)/shard_map/ppermute | solution.py:1266
  474.8 4.4 block_grad.21
  479.2 4.6 block_grad.20
  483.7 11.6 %collective-permute-done.58 = bf16[1280,384]{1,0:T(8,128)(2,1)S(1)} collective-permute-done((bf16[1280,384]{1,0:T(8,128)(2,1)S(1)}, bf16[1280,384]{1,0:T(8,128)(2,1)S(1)}, u32[]{:S(2)}, u32[]{:S(2)}) %collective-permute-start.58) | collective-permute-done | bytes 983072 | tf_op jit(solution)/shard_map/ppermute | solution.py:1266
  508.7 4.4 block_grad.23
  513.1 4.4 block_grad.22
  517.7 5.8 collective-permute-done.61
  525.3 4.6 block_grad.25
  529.9 4.4 block_grad.24
  534.3 11.4 %collective-permute-done.64 = bf16[1280,384]{1,0:T(8,128)(2,1)S(1)} collective-permute-done((bf16[1280,384]{1,0:T(8,128)(2,1)S(1)}, bf16[1280,384]{1,0:T(8,128)(2,1)S(1)}, u32[]{:S(2)}, u32[]{:S(2)}) %collective-permute-start.64) | collective-permute-done | bytes 983072 | tf_op jit(solution)/shard_map/ppermute | solution.py:1266
  552.3 4.4 block_grad.27
  556.7 4.4 block_grad.26
  561.1 5.9 collective-permute-done.66
  573.7 4.4 block_grad.28
  578.0 9.5 %collective-permute-done.68 = bf16[1280,384]{1,0:T(8,128)(2,1)S(1)} collective-permute-done((bf16[1280,384]{1,0:T(8,128)(2,1)S(1)}, bf16[1280,384]{1,0:T(8,128)(2,1)S(1)}, u32[]{:S(2)}, u32[]{:S(2)}) %collective-permute-start.68) | collective-permute-done | bytes 983072 | tf_op jit(solution)/shard_map/ppermute | solution.py:1266
  589.5 4.4 block_grad.31
  593.9 4.4 block_grad.30
  598.3 9.0 %collective-permute-done.70 = bf16[1280,384]{1,0:T(8,128)(2,1)S(1)} collective-permute-done((bf16[1280,384]{1,0:T(8,128)(2,1)S(1)}, bf16[1280,384]{1,0:T(8,128)(2,1)S(1)}, u32[]{:S(2)}, u32[]{:S(2)}) %collective-permute-start.70) | collective-permute-done | bytes 983072 | tf_op jit(solution)/shard_map/ppermute | solution.py:1266
  609.7 9.0 %collective-permute-start.71 = (bf16[256,1536]{1,0:T(8,128)(2,1)S(1)}, bf16[256,1536]{1,0:T(8,128)(2,1)S(1)}, u32[]{:S(2)}, u32[]{:S(2)}) collective-permute-start(bf16[256,1536]{1,0:T(8,128)(2,1)S(1)} %pick.2), channel_id=1, source_target_pairs={{0,0},{4,1},{1,4},{5,5},{8,8},{12,9},{9,12},{13,13},{16,16},{20,17... | collective-permute-start | bytes 2359304 | tf_op jit(solution)/shard_map/ppermute | solution.py:1133
  619.9 6.2 collective-permute-start.73
  626.1 14.8 %collective-permute-done.71 = bf16[256,1536]{1,0:T(8,128)(2,1)S(1)} collective-permute-done((bf16[256,1536]{1,0:T(8,128)(2,1)S(1)}, bf16[256,1536]{1,0:T(8,128)(2,1)S(1)}, u32[]{:S(2)}, u32[]{:S(2)}) %collective-permute-start.71) | collective-permute-done | bytes 786464 | tf_op jit(solution)/shard_map/ppermute | solution.py:1133
  642.7 7.6 %collective-permute-start.76 = (bf16[1280,384]{1,0:T(8,128)(2,1)S(1)}, bf16[1280,384]{1,0:T(8,128)(2,1)}, u32[]{:S(2)}, u32[]{:S(2)}) collective-permute-start(bf16[1280,384]{1,0:T(8,128)(2,1)S(1)} %add_convert_fusion.1.refs_0_), channel_id=1, source_target_pairs={{0,4},{4,0},{1,5},{5,1},{2,6},{6,2},{3,7},{7,3},{8,12},{12,8},{9,1... | collective-permute-start | bytes 2949128 | tf_op jit(solution)/shard_map/ppermute | solution.py:1058
  651.3 4.6 collective-permute-start.80
  659.3 7.9 %join_grads.1 = (f32[6448,384]{1,0:T(8,128)}, f32[768,1536]{1,0:T(8,128)}, f32[16,384]{1,0:T(8,128)S(1)}) custom-call(s32[2]{0:T(128)S(1)} %pad_add_fusion.sc, bf16[1280,384]{1,0:T(8,128)(2,1)S(1)} %add_convert_fusion.1.refs_0_, bf16[1280,384]{1,0:T(8,128)(2,1)S(1)} %collective-permute-done.75.refs_1_, bf16[1280,384]{1,0:T(8,128)(2,1)} %collective-permute-done.76.refs_2_, ...), custom_call_target="tpu_custom_call" | custom-call | flops 1048576 | bytes 65536 | tf_op jit(solution)/shard_map/join_grads/pallas_call | solution.py:1045
  (357 shorter events, 179.0 us)
Async XLA Ops:
  6.4 23.7 %collective-permute-start = (bf16[1280,384]{1,0:T(8,128)(2,1)S(1)}, bf16[1280,384]{1,0:T(8,128)(2,1)}, u32[]{:S(2)}, u32[]{:S(2)}) collective-permute-start(bf16[1280,384]{1,0:T(8,128)(2,1)S(1)} %get-tuple-element.278.refs_0_), channel_id=1, source_target_pairs={{0,1},{1,0},{2,3},{3,2},{8,9},{9,8},{10,11},{11,10},{4,5},{5,4},{6... | collective-permute-start | bytes 2949128 | tf_op jit(solution)/shard_map/ppermute | solution.py:882
  8.5 21.6 %collective-permute-start.1 = (bf16[1280,384]{1,0:T(8,128)(2,1)S(1)}, bf16[1280,384]{1,0:T(8,128)(2,1)}, u32[]{:S(2)}, u32[]{:S(2)}) collective-permute-start(bf16[1280,384]{1,0:T(8,128)(2,1)S(1)} %get-tuple-element.278.refs_0_), channel_id=1, source_target_pairs={{1,2},{2,1},{9,10},{10,9},{5,6},{6,5},{13,14},{14,13},{17,18},{18,... | collective-permute-start | bytes 2949128 | tf_op jit(solution)/shard_map/ppermute | solution.py:882
  30.1 29.0 %collective-permute-start.2 = (bf16[1280,384]{1,0:T(8,128)(2,1)S(1)}, bf16[1280,384]{1,0:T(8,128)(2,1)}, u32[]{:S(2)}, u32[]{:S(2)}) collective-permute-start(bf16[1280,384]{1,0:T(8,128)(2,1)S(1)} %get-tuple-element.282.refs_1_), channel_id=1, source_target_pairs={{0,1},{1,0},{2,3},{3,2},{8,9},{9,8},{10,11},{11,10},{4,5},{5,4},{6... | collective-permute-start | bytes 2949128 | tf_op jit(solution)/shard_map/ppermute | solution.py:882
  34.3 24.9 %collective-permute-start.3 = (bf16[1280,384]{1,0:T(8,128)(2,1)S(1)}, bf16[1280,384]{1,0:T(8,128)(2,1)}, u32[]{:S(2)}, u32[]{:S(2)}) collective-permute-start(bf16[1280,384]{1,0:T(8,128)(2,1)S(1)} %get-tuple-element.282.refs_1_), channel_id=1, source_target_pairs={{1,2},{2,1},{9,10},{10,9},{5,6},{6,5},{13,14},{14,13},{17,18},{18,... | collective-permute-start | bytes 2949128 | tf_op jit(solution)/shard_map/ppermute | solution.py:882
  35.9 23.3 %collective-permute-start.4 = (bf16[1280,384]{1,0:T(8,128)(2,1)}, bf16[1280,384]{1,0:T(8,128)(2,1)}, u32[]{:S(2)}, u32[]{:S(2)}) collective-permute-start(bf16[1280,384]{1,0:T(8,128)(2,1)} %collective-permute-done.refs_4_), channel_id=1, source_target_pairs={{0,8},{1,9},{2,10},{3,11},{8,0},{9,1},{10,2},{11,3},{4,12},{5,13},... | collective-permute-start | bytes 2949128 | tf_op jit(solution)/shard_map/ppermute | solution.py:886
  37.8 18.4 %collective-permute-start.5 = (bf16[5348]{0:T(1024)(128)(2,1)S(1)}, bf16[5348]{0:T(1024)(128)(2,1)S(1)}, u32[]{:S(2)}, u32[]{:S(2)}) collective-permute-start(bf16[5348]{0:T(1024)(128)(2,1)S(1)} %concatenate.29), channel_id=1, source_target_pairs={{0,1},{1,2},{2,3},{3,0},{4,5},{5,6},{6,7},{7,4},{8,9},{9,10},{10,1... | collective-permute-start | bytes 32096 | tf_op jit(solution)/shard_map/ppermute | solution.py:1064
  39.3 18.5 %collective-permute-start.6 = (bf16[5348]{0:T(1024)(128)(2,1)S(1)}, bf16[5348]{0:T(1024)(128)(2,1)S(1)}, u32[]{:S(2)}, u32[]{:S(2)}) collective-permute-start(bf16[5348]{0:T(1024)(128)(2,1)S(1)} %concatenate.29), channel_id=1, source_target_pairs={{0,2},{1,3},{2,0},{3,1},{4,6},{5,7},{6,4},{7,5},{8,10},{9,11},{10,... | collective-permute-start | bytes 32096 | tf_op jit(solution)/shard_map/ppermute | solution.py:1064
  59.2 19.4 %collective-permute-start.10 = (bf16[1280,384]{1,0:T(8,128)(2,1)}, bf16[1280,384]{1,0:T(8,128)(2,1)S(1)}, u32[]{:S(2)}, u32[]{:S(2)}) collective-permute-start(bf16[1280,384]{1,0:T(8,128)(2,1)} %collective-permute-done.2.refs_5_), channel_id=1, source_target_pairs={{0,8},{1,9},{2,10},{3,11},{8,0},{9,1},{10,2},{11,3},{4,12},{5,13},... | collective-permute-start | bytes 2949128 | tf_op jit(solution)/shard_map/ppermute | solution.py:886
  60.4 21.0 %collective-permute-start.8 = (bf16[1280,384]{1,0:T(8,128)(2,1)}, bf16[1280,384]{1,0:T(8,128)(2,1)S(1)}, u32[]{:S(2)}, u32[]{:S(2)}) collective-permute-start(bf16[1280,384]{1,0:T(8,128)(2,1)} %collective-permute-done.1.refs_8_), channel_id=1, source_target_pairs={{1,0},{2,3},{9,8},{10,11},{5,4},{6,7},{13,12},{14,15},{17,16},{18,... | collective-permute-start | bytes 2949128 | tf_op jit(solution)/shard_map/ppermute | solution.py:882
  61.7 19.7 %collective-permute-start.9 = (bf16[1280,384]{1,0:T(8,128)(2,1)}, bf16[1280,384]{1,0:T(8,128)(2,1)S(1)}, u32[]{:S(2)}, u32[]{:S(2)}) collective-permute-start(bf16[1280,384]{1,0:T(8,128)(2,1)} %collective-permute-done.refs_4_), channel_id=1, source_target_pairs={{1,2},{2,1},{9,10},{10,9},{5,6},{6,5},{13,14},{14,13},{17,18},{18,... | collective-permute-start | bytes 2949128 | tf_op jit(solution)/shard_map/ppermute | solution.py:882
  81.4 21.1 %collective-permute-start.11 = (bf16[1280,384]{1,0:T(8,128)(2,1)}, bf16[1280,384]{1,0:T(8,128)(2,1)S(1)}, u32[]{:S(2)}, u32[]{:S(2)}) collective-permute-start(bf16[1280,384]{1,0:T(8,128)(2,1)} %collective-permute-done.3.refs_9_), channel_id=1, source_target_pairs={{1,0},{2,3},{9,8},{10,11},{5,4},{6,7},{13,12},{14,15},{17,16},{18,... | collective-permute-start | bytes 2949128 | tf_op jit(solution)/shard_map/ppermute | solution.py:882
  82.7 19.8 %collective-permute-start.12 = (bf16[1280,384]{1,0:T(8,128)(2,1)}, bf16[1280,384]{1,0:T(8,128)(2,1)}, u32[]{:S(2)}, u32[]{:S(2)}) collective-permute-start(bf16[1280,384]{1,0:T(8,128)(2,1)} %collective-permute-done.2.refs_5_), channel_id=1, source_target_pairs={{1,2},{2,1},{9,10},{10,9},{5,6},{6,5},{13,14},{14,13},{17,18},{18,... | collective-permute-start | bytes 2949128 | tf_op jit(solution)/shard_map/ppermute | solution.py:882
  84.3 19.8 %collective-permute-start.13 = (bf16[1280,384]{1,0:T(8,128)(2,1)S(1)}, bf16[1280,384]{1,0:T(8,128)(2,1)S(1)}, u32[]{:S(2)}, u32[]{:S(2)}) collective-permute-start(bf16[1280,384]{1,0:T(8,128)(2,1)S(1)} %collective-permute-done.8.refs_12_), channel_id=1, source_target_pairs={{0,8},{3,11},{8,0},{11,3},{4,12},{7,15},{12,4},{15,7},{16,24},{19,... | collective-permute-start | bytes 2949128 | tf_op jit(solution)/shard_map/ppermute | solution.py:886
  86.5 17.7 %collective-permute-start.14 = (bf16[1280,384]{1,0:T(8,128)(2,1)}, bf16[1280,384]{1,0:T(8,128)(2,1)S(1)}, u32[]{:S(2)}, u32[]{:S(2)}) collective-permute-start(bf16[1280,384]{1,0:T(8,128)(2,1)} %collective-permute-done.1.refs_8_), channel_id=1, source_target_pairs={{1,9},{2,10},{9,1},{10,2},{5,13},{6,14},{13,5},{14,6},{17,25},{18,... | collective-permute-start | bytes 2949128 | tf_op jit(solution)/shard_map/ppermute | solution.py:886
  104.1 23.6 %collective-permute-start.19 = (bf16[1280,384]{1,0:T(8,128)(2,1)S(1)}, bf16[1280,384]{1,0:T(8,128)(2,1)S(1)}, u32[]{:S(2)}, u32[]{:S(2)}) collective-permute-start(bf16[1280,384]{1,0:T(8,128)(2,1)S(1)} %collective-permute-done.9.refs_0_), channel_id=1, source_target_pairs={{1,0},{2,3},{9,8},{10,11},{5,4},{6,7},{13,12},{14,15},{17,16},{18,... | collective-permute-start | bytes 2949128 | tf_op jit(solution)/shard_map/ppermute | solution.py:882
  105.4 22.3 %collective-permute-start.20 = (bf16[1280,384]{1,0:T(8,128)(2,1)S(1)}, bf16[1280,384]{1,0:T(8,128)(2,1)S(1)}, u32[]{:S(2)}, u32[]{:S(2)}) collective-permute-start(bf16[1280,384]{1,0:T(8,128)(2,1)S(1)} %collective-permute-done.11.refs_13_), channel_id=1, source_target_pairs={{0,8},{3,11},{8,0},{11,3},{4,12},{7,15},{12,4},{15,7},{16,24},{19,... | collective-permute-start | bytes 2949128 | tf_op jit(solution)/shard_map/ppermute | solution.py:886
  107.6 20.1 %collective-permute-start.21 = (bf16[1280,384]{1,0:T(8,128)(2,1)}, bf16[1280,384]{1,0:T(8,128)(2,1)S(1)}, u32[]{:S(2)}, u32[]{:S(2)}) collective-permute-start(bf16[1280,384]{1,0:T(8,128)(2,1)} %collective-permute-done.3.refs_9_), channel_id=1, source_target_pairs={{1,9},{2,10},{9,1},{10,2},{5,13},{6,14},{13,5},{14,6},{17,25},{18,... | collective-permute-start | bytes 2949128 | tf_op jit(solution)/shard_map/ppermute | solution.py:886
  127.8 21.1 %collective-permute-start.22 = (bf16[1280,384]{1,0:T(8,128)(2,1)}, bf16[1280,384]{1,0:T(8,128)(2,1)}, u32[]{:S(2)}, u32[]{:S(2)}) collective-permute-start(bf16[1280,384]{1,0:T(8,128)(2,1)} %collective-permute-done.12.refs_1_), channel_id=1, source_target_pairs={{1,0},{2,3},{9,8},{10,11},{5,4},{6,7},{13,12},{14,15},{17,16},{18,... | collective-permute-start | bytes 2949128 | tf_op jit(solution)/shard_map/ppermute | solution.py:882
  129.1 19.8 %collective-permute-start.23 = (bf16[1280,384]{1,0:T(8,128)(2,1)S(1)}, bf16[1280,384]{1,0:T(8,128)(2,1)S(1)}, u32[]{:S(2)}, u32[]{:S(2)}) collective-permute-start(bf16[1280,384]{1,0:T(8,128)(2,1)S(1)} %collective-permute-done.19.refs_4_), channel_id=1, source_target_pairs={{0,8},{3,11},{8,0},{11,3},{4,12},{7,15},{12,4},{15,7},{16,24},{19,... | collective-permute-start | bytes 2949128 | tf_op jit(solution)/shard_map/ppermute | solution.py:886
  134.8 30.2 %collective-permute-start.15 = (bf16[256,1536]{1,0:T(8,128)(2,1)}, bf16[256,1536]{1,0:T(8,128)(2,1)}, u32[]{:S(2)}, u32[]{:S(2)}) collective-permute-start(bf16[256,1536]{1,0:T(8,128)(2,1)} %get-tuple-element.549), channel_id=1, source_target_pairs={{0,0},{1,4},{4,1},{5,5},{8,8},{9,12},{12,9},{13,13},{16,16},{17,20... | collective-permute-start | bytes 2359304 | tf_op jit(solution)/shard_map/ppermute | solution.py:1124
  148.9 32.3 %collective-permute-start.25 = (bf16[1280,384]{1,0:T(8,128)(2,1)}, bf16[1280,384]{1,0:T(8,128)(2,1)}, u32[]{:S(2)}, u32[]{:S(2)}) collective-permute-start(bf16[1280,384]{1,0:T(8,128)(2,1)} %collective-permute-done.12.refs_1_), channel_id=1, source_target_pairs={{1,9},{2,10},{9,1},{10,2},{5,13},{6,14},{13,5},{14,6},{17,25},{18,... | collective-permute-start | bytes 2949128 | tf_op jit(solution)/shard_map/ppermute | solution.py:886
  150.5 30.7 %collective-permute-start.26 = (bf16[1280,384]{1,0:T(8,128)(2,1)}, bf16[1280,384]{1,0:T(8,128)(2,1)}, u32[]{:S(2)}, u32[]{:S(2)}) collective-permute-start(bf16[1280,384]{1,0:T(8,128)(2,1)} %collective-permute-done.22.refs_5_), channel_id=1, source_target_pairs={{0,8},{3,11},{8,0},{11,3},{4,12},{7,15},{12,4},{15,7},{16,24},{19,... | collective-permute-start | bytes 2949128 | tf_op jit(solution)/shard_map/ppermute | solution.py:886
  153.6 27.6 %collective-permute-start.17 = (bf16[256,1536]{1,0:T(8,128)(2,1)}, bf16[256,1536]{1,0:T(8,128)(2,1)S(1)}, u32[]{:S(2)}, u32[]{:S(2)}) collective-permute-start(bf16[256,1536]{1,0:T(8,128)(2,1)} %get-tuple-element.549), channel_id=1, source_target_pairs={{2,0},{3,4},{6,1},{7,5},{10,8},{11,12},{14,9},{15,13},{18,16},{19,... | collective-permute-start | bytes 2359304 | tf_op jit(solution)/shard_map/ppermute | solution.py:1124
  154.9 26.3 %collective-permute-start.16 = (bf16[256,1536]{1,0:T(8,128)(2,1)}, bf16[256,1536]{1,0:T(8,128)(2,1)}, u32[]{:S(2)}, u32[]{:S(2)}) collective-permute-start(bf16[256,1536]{1,0:T(8,128)(2,1)} %get-tuple-element.548), channel_id=1, source_target_pairs={{0,2},{1,6},{4,3},{5,7},{8,10},{9,14},{12,11},{13,15},{16,18},{17,... | collective-permute-start | bytes 2359304 | tf_op jit(solution)/shard_map/ppermute | solution.py:1124
  182.5 19.1 %collective-permute-start.27 = (bf16[256,1536]{1,0:T(8,128)(2,1)S(1)}, bf16[256,1536]{1,0:T(8,128)(2,1)S(1)}, u32[]{:S(2)}, u32[]{:S(2)}) collective-permute-start(bf16[256,1536]{1,0:T(8,128)(2,1)S(1)} %broadcast_select_fusion.1), channel_id=1, source_target_pairs={{0,4},{4,0},{1,5},{5,1},{2,6},{6,2},{3,7},{7,3},{8,12},{12,8},{9,1... | collective-permute-start | bytes 2359304 | tf_op jit(solution)/shard_map/ppermute | solution.py:1058
  301.9 39.7 %collective-permute-start.44 = (bf16[128,1536]{1,0:T(8,128)(2,1)S(1)}, bf16[128,1536]{1,0:T(8,128)(2,1)S(1)}, u32[]{:S(2)}, u32[]{:S(2)}) collective-permute-start(bf16[128,1536]{1,0:T(8,128)(2,1)S(1)} %get-tuple-element.442), channel_id=1, source_target_pairs={{16,0},{17,1},{18,2},{19,3},{20,4},{21,5},{22,6},{23,7},{24,8},{25... | collective-permute-start | bytes 1179656 | tf_op jit(solution)/shard_map/ppermute | solution.py:1216
  345.0 20.2 %collective-permute-start.47 = (bf16[128,1536]{1,0:T(8,128)(2,1)S(1)}, bf16[128,1536]{1,0:T(8,128)(2,1)S(1)}, u32[]{:S(2)}, u32[]{:S(2)}) collective-permute-start(bf16[128,1536]{1,0:T(8,128)(2,1)S(1)} %get-tuple-element.457), channel_id=1, source_target_pairs={{16,0},{17,1},{18,2},{19,3},{20,4},{21,5},{22,6},{23,7},{24,8},{25... | collective-permute-start | bytes 1179656 | tf_op jit(solution)/shard_map/ppermute | solution.py:1216
  370.2 19.3 %collective-permute-start.50 = (bf16[128,1536]{1,0:T(8,128)(2,1)S(1)}, bf16[128,1536]{1,0:T(8,128)(2,1)S(1)}, u32[]{:S(2)}, u32[]{:S(2)}) collective-permute-start(bf16[128,1536]{1,0:T(8,128)(2,1)S(1)} %get-tuple-element.472), channel_id=1, source_target_pairs={{16,0},{17,1},{18,2},{19,3},{20,4},{21,5},{22,6},{23,7},{24,8},{25... | collective-permute-start | bytes 1179656 | tf_op jit(solution)/shard_map/ppermute | solution.py:1216
  394.4 19.9 %collective-permute-start.53 = (bf16[128,1536]{1,0:T(8,128)(2,1)S(1)}, bf16[128,1536]{1,0:T(8,128)(2,1)S(1)}, u32[]{:S(2)}, u32[]{:S(2)}) collective-permute-start(bf16[128,1536]{1,0:T(8,128)(2,1)S(1)} %get-tuple-element.487), channel_id=1, source_target_pairs={{16,0},{17,1},{18,2},{19,3},{20,4},{21,5},{22,6},{23,7},{24,8},{25... | collective-permute-start | bytes 1179656 | tf_op jit(solution)/shard_map/ppermute | solution.py:1216
  448.4 23.6 %collective-permute-start.56 = (bf16[1280,384]{1,0:T(8,128)(2,1)S(1)}, bf16[1280,384]{1,0:T(8,128)(2,1)S(1)}, u32[]{:S(2)}, u32[]{:S(2)}) collective-permute-start(bf16[1280,384]{1,0:T(8,128)(2,1)S(1)} %block_grad.17), channel_id=1, source_target_pairs={{0,8},{1,0},{2,1},{3,2},{11,3},{10,11},{9,10},{8,9},{4,12},{5,4},{... | collective-permute-start | bytes 2949128 | tf_op jit(solution)/shard_map/ppermute | solution.py:1266
  449.6 23.4 %collective-permute-start.55 = (bf16[1280,384]{1,0:T(8,128)(2,1)S(1)}, bf16[1280,384]{1,0:T(8,128)(2,1)S(1)}, u32[]{:S(2)}, u32[]{:S(2)}) collective-permute-start(bf16[1280,384]{1,0:T(8,128)(2,1)S(1)} %block_grad.16), channel_id=1, source_target_pairs={{0,1},{1,2},{2,3},{3,11},{11,10},{10,9},{9,8},{8,0},{4,5},{5,6},{6... | collective-permute-start | bytes 2949128 | tf_op jit(solution)/shard_map/ppermute | solution.py:1266
  473.2 22.1 %collective-permute-start.58 = (bf16[1280,384]{1,0:T(8,128)(2,1)S(1)}, bf16[1280,384]{1,0:T(8,128)(2,1)S(1)}, u32[]{:S(2)}, u32[]{:S(2)}) collective-permute-start(bf16[1280,384]{1,0:T(8,128)(2,1)S(1)} %add_convert_fusion.12), channel_id=1, source_target_pairs={{0,8},{1,0},{2,1},{3,2},{11,3},{10,11},{9,10},{8,9},{4,12},{5,4},{... | collective-permute-start | bytes 2949128 | tf_op jit(solution)/shard_map/ppermute | solution.py:1266
  474.5 21.5 %collective-permute-start.57 = (bf16[1280,384]{1,0:T(8,128)(2,1)S(1)}, bf16[1280,384]{1,0:T(8,128)(2,1)S(1)}, u32[]{:S(2)}, u32[]{:S(2)}) collective-permute-start(bf16[1280,384]{1,0:T(8,128)(2,1)S(1)} %add_convert_fusion.13), channel_id=1, source_target_pairs={{0,1},{1,2},{2,3},{3,11},{11,10},{10,9},{9,8},{8,0},{4,5},{5,6},{6... | collective-permute-start | bytes 2949128 | tf_op jit(solution)/shard_map/ppermute | solution.py:1266
  496.2 21.3 %collective-permute-start.62 = (bf16[1280,384]{1,0:T(8,128)(2,1)S(1)}, bf16[1280,384]{1,0:T(8,128)(2,1)S(1)}, u32[]{:S(2)}, u32[]{:S(2)}) collective-permute-start(bf16[1280,384]{1,0:T(8,128)(2,1)S(1)} %add_convert_fusion.10), channel_id=1, source_target_pairs={{0,8},{1,0},{2,1},{3,2},{11,3},{10,11},{9,10},{8,9},{4,12},{5,4},{... | collective-permute-start | bytes 2949128 | tf_op jit(solution)/shard_map/ppermute | solution.py:1266
  500.7 22.8 %collective-permute-start.61 = (bf16[1280,384]{1,0:T(8,128)(2,1)S(1)}, bf16[1280,384]{1,0:T(8,128)(2,1)S(1)}, u32[]{:S(2)}, u32[]{:S(2)}) collective-permute-start(bf16[1280,384]{1,0:T(8,128)(2,1)S(1)} %add_convert_fusion.11), channel_id=1, source_target_pairs={{0,1},{1,2},{2,3},{3,11},{11,10},{10,9},{9,8},{8,0},{4,5},{5,6},{6... | collective-permute-start | bytes 2949128 | tf_op jit(solution)/shard_map/ppermute | solution.py:1266
  523.8 21.9 %collective-permute-start.64 = (bf16[1280,384]{1,0:T(8,128)(2,1)S(1)}, bf16[1280,384]{1,0:T(8,128)(2,1)S(1)}, u32[]{:S(2)}, u32[]{:S(2)}) collective-permute-start(bf16[1280,384]{1,0:T(8,128)(2,1)S(1)} %add_convert_fusion.8), channel_id=1, source_target_pairs={{0,8},{1,0},{2,1},{3,2},{11,3},{10,11},{9,10},{8,9},{4,12},{5,4},{... | collective-permute-start | bytes 2949128 | tf_op jit(solution)/shard_map/ppermute | solution.py:1266
  524.4 21.6 %collective-permute-start.63 = (bf16[1280,384]{1,0:T(8,128)(2,1)S(1)}, bf16[1280,384]{1,0:T(8,128)(2,1)S(1)}, u32[]{:S(2)}, u32[]{:S(2)}) collective-permute-start(bf16[1280,384]{1,0:T(8,128)(2,1)S(1)} %add_convert_fusion.9), channel_id=1, source_target_pairs={{0,1},{1,2},{2,3},{3,11},{11,10},{10,9},{9,8},{8,0},{4,5},{5,6},{6... | collective-permute-start | bytes 2949128 | tf_op jit(solution)/shard_map/ppermute | solution.py:1266
  546.3 20.7 %collective-permute-start.66 = (bf16[1280,384]{1,0:T(8,128)(2,1)S(1)}, bf16[1280,384]{1,0:T(8,128)(2,1)S(1)}, u32[]{:S(2)}, u32[]{:S(2)}) collective-permute-start(bf16[1280,384]{1,0:T(8,128)(2,1)S(1)} %add_convert_fusion.6), channel_id=1, source_target_pairs={{0,8},{1,0},{2,1},{3,2},{11,3},{10,11},{9,10},{8,9},{4,12},{5,4},{... | collective-permute-start | bytes 2949128 | tf_op jit(solution)/shard_map/ppermute | solution.py:1266
  546.9 20.6 %collective-permute-start.65 = (bf16[1280,384]{1,0:T(8,128)(2,1)S(1)}, bf16[1280,384]{1,0:T(8,128)(2,1)S(1)}, u32[]{:S(2)}, u32[]{:S(2)}) collective-permute-start(bf16[1280,384]{1,0:T(8,128)(2,1)S(1)} %add_convert_fusion.7), channel_id=1, source_target_pairs={{0,1},{1,2},{2,3},{3,11},{11,10},{10,9},{9,8},{8,0},{4,5},{5,6},{6... | collective-permute-start | bytes 2949128 | tf_op jit(solution)/shard_map/ppermute | solution.py:1266
  567.8 19.8 %collective-permute-start.68 = (bf16[1280,384]{1,0:T(8,128)(2,1)S(1)}, bf16[1280,384]{1,0:T(8,128)(2,1)S(1)}, u32[]{:S(2)}, u32[]{:S(2)}) collective-permute-start(bf16[1280,384]{1,0:T(8,128)(2,1)S(1)} %add_convert_fusion.4), channel_id=1, source_target_pairs={{0,8},{1,0},{2,1},{3,2},{11,3},{10,11},{9,10},{8,9},{4,12},{5,4},{... | collective-permute-start | bytes 2949128 | tf_op jit(solution)/shard_map/ppermute | solution.py:1266
  568.4 19.4 %collective-permute-start.67 = (bf16[1280,384]{1,0:T(8,128)(2,1)S(1)}, bf16[1280,384]{1,0:T(8,128)(2,1)S(1)}, u32[]{:S(2)}, u32[]{:S(2)}) collective-permute-start(bf16[1280,384]{1,0:T(8,128)(2,1)S(1)} %add_convert_fusion.5), channel_id=1, source_target_pairs={{0,1},{1,2},{2,3},{3,11},{11,10},{10,9},{9,8},{8,0},{4,5},{5,6},{6... | collective-permute-start | bytes 2949128 | tf_op jit(solution)/shard_map/ppermute | solution.py:1266
  588.0 19.3 %collective-permute-start.70 = (bf16[1280,384]{1,0:T(8,128)(2,1)S(1)}, bf16[1280,384]{1,0:T(8,128)(2,1)S(1)}, u32[]{:S(2)}, u32[]{:S(2)}) collective-permute-start(bf16[1280,384]{1,0:T(8,128)(2,1)S(1)} %add_convert_fusion.2), channel_id=1, source_target_pairs={{0,8},{1,0},{2,1},{3,2},{11,3},{10,11},{9,10},{8,9},{4,12},{5,4},{... | collective-permute-start | bytes 2949128 | tf_op jit(solution)/shard_map/ppermute | solution.py:1266
  588.5 19.4 %collective-permute-start.69 = (bf16[1280,384]{1,0:T(8,128)(2,1)S(1)}, bf16[1280,384]{1,0:T(8,128)(2,1)S(1)}, u32[]{:S(2)}, u32[]{:S(2)}) collective-permute-start(bf16[1280,384]{1,0:T(8,128)(2,1)S(1)} %add_convert_fusion.3), channel_id=1, source_target_pairs={{0,1},{1,2},{2,3},{3,11},{11,10},{10,9},{9,8},{8,0},{4,5},{5,6},{6... | collective-permute-start | bytes 2949128 | tf_op jit(solution)/shard_map/ppermute | solution.py:1266
  608.1 42.3 %collective-permute-start.75 = (bf16[1280,384]{1,0:T(8,128)(2,1)S(1)}, bf16[1280,384]{1,0:T(8,128)(2,1)S(1)}, u32[]{:S(2)}, u32[]{:S(2)}) collective-permute-start(bf16[1280,384]{1,0:T(8,128)(2,1)S(1)} %add_convert_fusion.1.refs_0_), channel_id=1, source_target_pairs={{0,8},{8,0},{1,9},{9,1},{2,10},{10,2},{3,11},{11,3},{4,12},{12,4},... | collective-permute-start | bytes 2949128 | tf_op jit(solution)/shard_map/ppermute | solution.py:1058
  608.7 42.1 %collective-permute-start.78 = (bf16[1280,384]{1,0:T(8,128)(2,1)S(1)}, bf16[1280,384]{1,0:T(8,128)(2,1)}, u32[]{:S(2)}, u32[]{:S(2)}) collective-permute-start(bf16[1280,384]{1,0:T(8,128)(2,1)S(1)} %add_convert_fusion.refs_4_), channel_id=1, source_target_pairs={{0,8},{8,0},{1,9},{9,1},{2,10},{10,2},{3,11},{11,3},{4,12},{12,4},... | collective-permute-start | bytes 2949128 | tf_op jit(solution)/shard_map/ppermute | solution.py:1058
  609.7 31.2 %collective-permute-start.71 = (bf16[256,1536]{1,0:T(8,128)(2,1)S(1)}, bf16[256,1536]{1,0:T(8,128)(2,1)S(1)}, u32[]{:S(2)}, u32[]{:S(2)}) collective-permute-start(bf16[256,1536]{1,0:T(8,128)(2,1)S(1)} %pick.2), channel_id=1, source_target_pairs={{0,0},{4,1},{1,4},{5,5},{8,8},{12,9},{9,12},{13,13},{16,16},{20,17... | collective-permute-start | bytes 2359304 | tf_op jit(solution)/shard_map/ppermute | solution.py:1133
  618.6 24.0 %collective-permute-start.72 = (bf16[256,1536]{1,0:T(8,128)(2,1)S(1)}, bf16[256,1536]{1,0:T(8,128)(2,1)S(1)}, u32[]{:S(2)}, u32[]{:S(2)}) collective-permute-start(bf16[256,1536]{1,0:T(8,128)(2,1)S(1)} %pick.2), channel_id=1, source_target_pairs={{2,0},{6,1},{3,4},{7,5},{10,8},{14,9},{11,12},{15,13},{18,16},{22,... | collective-permute-start | bytes 2359304 | tf_op jit(solution)/shard_map/ppermute | solution.py:1133
  619.9 30.4 %collective-permute-start.73 = (bf16[256,1536]{1,0:T(8,128)(2,1)}, bf16[256,1536]{1,0:T(8,128)(2,1)S(1)}, u32[]{:S(2)}, u32[]{:S(2)}) collective-permute-start(bf16[256,1536]{1,0:T(8,128)(2,1)} %pick.3), channel_id=1, source_target_pairs={{0,2},{4,3},{1,6},{5,7},{8,10},{12,11},{9,14},{13,15},{16,18},{20,... | collective-permute-start | bytes 2359304 | tf_op jit(solution)/shard_map/ppermute | solution.py:1133
  (72 other events, 1262.0 us)
